TPU v7x, 128 devices: a whole 4x4x4 slice. The times are simulated.
128 devices in a mesh: seq: 32 (over x, z, y_hi), head: 4 (over y_lo, core).
Axes of the slice: x: 4, y: 4 (y_hi: 2, y_lo: 2; y = y_hi * 2 + y_lo), z: 4, core: 2. Of those that a mesh axis runs over, the one named last changes fastest.
Arguments:
- inputs: bfloat16 [2, 4096, 2048], P(None, 'seq'), may hold values from -6 to 6
- doc_lengths: int32 [2, 8], replicated, may hold values from 1 to 4089, as said below
- norm_in: bfloat16 [2048], P('seq'), may hold values from 0.5 to 1.5
- query_weight: bfloat16 [2048, 2048], P('seq', 'head'), may hold values from -0.125 to 0.125
- key_weight: bfloat16 [2048, 2048], P('seq', 'head'), may hold values from -0.125 to 0.125
- value_weight: bfloat16 [2048, 2048], P('seq', 'head'), may hold values from -0.125 to 0.125
- outgate_weight: bfloat16 [2048, 2048], P('seq', 'head'), may hold values from -0.125 to 0.125
- scalar_weight: bfloat16 [2048, 2, 16], P('seq', None, 'head'), may hold values from -0.125 to 0.125
- conv_kernel: bfloat16 [3, 4, 2048], P(None, None, 'head'), may hold values from -3 to 3
- decay_rate: bfloat16 [16], P('head'), may hold values from 0.00029945374 to 0.049804688
- head_norm: bfloat16 [128], replicated, may hold values from 0.5 to 1.5
- output_weight: bfloat16 [2048, 2048], P('head', 'seq'), may hold values from -0.25 to 0.25
- norm_ffn: bfloat16 [2048], P('seq'), may hold values from 0.5 to 1.5
- gate_weight: bfloat16 [2048, 5632], P('seq', 'head'), may hold values from -0.125 to 0.125
- up_weight: bfloat16 [2048, 5632], P('seq', 'head'), may hold values from -0.125 to 0.125
- down_weight: bfloat16 [5632, 2048], P('head', 'seq'), may hold values from -0.15625 to 0.15625
- grad_out: bfloat16 [2, 4096, 2048], P(None, 'seq'), may hold values from -6 to 6
Outputs:
- outputs: bfloat16 [2, 4096, 2048], P(None, 'seq')
- grad_in: float32 [2, 4096, 2048], P(None, 'seq')
- grad_norm_in: float32 [2048], P('seq')
- grad_query: float32 [2048, 2048], P('seq', 'head')
- grad_key: float32 [2048, 2048], P('seq', 'head')
- grad_value: float32 [2048, 2048], P('seq', 'head')
- grad_outgate: float32 [2048, 2048], P('seq', 'head')
- grad_scalars: float32 [2048, 2, 16], P('seq', None, 'head')
- grad_conv: float32 [3, 4, 2048], P(None, None, 'head')
- grad_decay: float32 [16], P('head')
- grad_head_norm: float32 [128], replicated
- grad_output: float32 [2048, 2048], P('head', 'seq')
- grad_norm_ffn: float32 [2048], P('seq')
- grad_gate: float32 [2048, 5632], P('seq', 'head')
- grad_up: float32 [2048, 5632], P('seq', 'head')
- grad_down: float32 [5632, 2048], P('head', 'seq')
Inputs may be any that keep to these rules, and one draw needn't show every extreme that they name: `doc_lengths`: each row holds the lengths of 8 packed documents and sums to 4096; in every row the second document starts within the first 128 positions and ends within the last 128.
All inputs are finite; a program needn't handle non-finite values.
Results may differ from a plain program's by a relative error of at most 0.03145.
Values may be sent and summed in bfloat16 or wider, within the bound.
No kernel may reach another device: no remote copies, remote signals or barrier semaphores. Data moves between devices by JAX's collectives and lax.ppermute only.
A program may use at most 192 MiB of HBM per device.

v0:
```python
from functools import partial

import jax
import jax.numpy as jnp
from jax import lax
from jax.sharding import PartitionSpec as P

H = 16
DK = 128
GROUP = 64


highest = lax.Precision.HIGHEST
norm_eps = 1e-06
head_eps = 1e-05


def passed_along(array, axis, by):
    devices = lax.axis_size(axis)
    pairs = [(i, i + by) for i in range(devices) if 0 <= i + by < devices]
    return lax.ppermute(array, axis, pairs)


def doc_numbers(doc_lengths, first_place, count_places):
    doc_ends = jnp.cumsum(doc_lengths, axis=1)
    places = first_place + jnp.arange(count_places, dtype=jnp.int32)
    counted = jnp.sum((places[None, :, None] >= doc_ends[:, None, :]).astype(jnp.int32), axis=2)
    return jnp.where(places[None, :] >= 0, counted, -1)


def rounded_copy(values):
    return lax.optimization_barrier(values.astype(jnp.bfloat16)).astype(jnp.float32)


def prepare(extended, kernel, scalars, decay_scale, docs_ext):
    tap_count = kernel.shape[1]
    step_count = extended.shape[1] - tap_count + 1
    local_docs = docs_ext[:, tap_count - 1 :]
    weights = jnp.transpose(kernel, (1, 0, 2)).reshape(tap_count, -1)
    convolved = jnp.zeros((extended.shape[0], step_count, extended.shape[2]), jnp.float32)
    for offset in range(tap_count):
        keep_mask = (docs_ext[:, offset : offset + step_count] == local_docs).astype(jnp.float32)
        convolved = (
            convolved
            + extended[:, offset : offset + step_count] * keep_mask[:, :, None] * weights[offset]
        )
    active = jax.nn.silu(convolved)
    inner_width = kernel.shape[2]
    head_count = decay_scale.shape[0]
    head_shape = (extended.shape[0], step_count, head_count, inner_width // head_count)
    queries = active[..., :inner_width].reshape(head_shape)
    key_rows = active[..., inner_width : 2 * inner_width].reshape(head_shape)
    values = active[..., 2 * inner_width :].reshape(head_shape)
    queries = queries * lax.rsqrt(jnp.sum(queries * queries, axis=-1, keepdims=True) + norm_eps)
    key_rows = key_rows * lax.rsqrt(jnp.sum(key_rows * key_rows, axis=-1, keepdims=True) + norm_eps)
    strength = jax.nn.sigmoid(scalars[:, :, 0])
    log_decay = -decay_scale * jax.nn.softplus(scalars[:, :, 1])
    return (queries, key_rows, values, strength, log_decay)


def unit_inverse(strict):
    matrix_size = strict.shape[-1]
    identity = jnp.eye(matrix_size, dtype=jnp.float32)
    power_term = -strict
    result = identity + power_term
    for repeat_index in range(max(1, (matrix_size - 1).bit_length()) - 1):
        power_term = jnp.einsum("shij,shjk->shik", power_term, power_term, precision=highest)
        result = jnp.einsum("shij,shjk->shik", result, identity + power_term, precision=highest)
    return result


def run_groups(
    queries, key_rows, values, strength, log_decay, memory, docs_ext, group_len, tap_count
):
    step_count = queries.shape[1]
    local_docs = docs_ext[:, tap_count - 1 :]
    below_mask = jnp.arange(group_len)[:, None] > jnp.arange(group_len)[None, :]
    causal_base = jnp.arange(group_len)[:, None] >= jnp.arange(group_len)[None, :]
    pieces = []
    for block_index in range(step_count // group_len):
        block_start = block_index * group_len
        query_block = jnp.transpose(queries[:, block_start : block_start + group_len], (0, 2, 1, 3))
        key_block = jnp.transpose(key_rows[:, block_start : block_start + group_len], (0, 2, 1, 3))
        value_block = jnp.transpose(values[:, block_start : block_start + group_len], (0, 2, 1, 3))
        strength_block = jnp.transpose(
            strength[:, block_start : block_start + group_len], (0, 2, 1)
        )
        cumulated = jnp.cumsum(
            jnp.transpose(log_decay[:, block_start : block_start + group_len], (0, 2, 1)), axis=-1
        )
        block_docs = local_docs[:, block_start : block_start + group_len]
        before = docs_ext[:, tap_count - 2 + block_start]
        reached = (block_docs == before[:, None]).astype(jnp.float32)[:, None, :]
        same_doc = block_docs[:, :, None] == block_docs[:, None, :]
        strict_mask = (same_doc & below_mask[None])[:, None]
        causal_mask = (same_doc & causal_base[None])[:, None]
        spread = cumulated[..., :, None] - cumulated[..., None, :]
        strict_decay = jnp.where(strict_mask, jnp.exp(jnp.where(strict_mask, spread, 0.0)), 0.0)
        causal_decay = jnp.where(causal_mask, jnp.exp(jnp.where(causal_mask, spread, 0.0)), 0.0)
        key_gram = jnp.einsum("shik,shjk->shij", key_block, key_block, precision=highest)
        inverse = unit_inverse(strength_block[..., :, None] * key_gram * strict_decay)
        start_decay = jnp.exp(cumulated) * reached
        update = jnp.einsum(
            "shij,shjv->shiv", inverse, strength_block[..., None] * value_block, precision=highest
        )
        correction = jnp.einsum(
            "shij,shjk->shik",
            inverse,
            (strength_block * start_decay)[..., None] * key_block,
            precision=highest,
        )
        fresh_values = update - jnp.einsum("shik,shkv->shiv", correction, memory, precision=highest)
        scores = (
            jnp.einsum("shik,shjk->shij", query_block, key_block, precision=highest) * causal_decay
        )
        output = jnp.einsum(
            "shik,shkv->shiv", query_block * start_decay[..., None], memory, precision=highest
        )
        output = output + jnp.einsum("shij,shjv->shiv", scores, fresh_values, precision=highest)
        tail_mask = (block_docs == block_docs[:, -1:]).astype(jnp.float32)[:, None, :]
        carry_decay = jnp.exp(cumulated[..., -1:] - cumulated) * tail_mask
        memory = (jnp.exp(cumulated[..., -1]) * reached[..., -1])[..., None, None] * memory
        memory = memory + jnp.einsum(
            "shjk,shjv->shkv", key_block * carry_decay[..., None], fresh_values, precision=highest
        )
        pieces.append(output)
    return (jnp.transpose(jnp.concatenate(pieces, axis=2), (0, 2, 1, 3)), memory)


def gated_norm(heads_out, out_gate, gain):
    scaled = (
        heads_out
        * lax.rsqrt(jnp.mean(heads_out * heads_out, axis=-1, keepdims=True) + head_eps)
        * gain
    )
    return scaled.reshape(out_gate.shape) * jax.nn.silu(out_gate)


def reduce_ffn(gain_grad, gate_grad_w, up_grad_w, down_grad_w):
    return (
        lax.psum_scatter(
            gain_grad.astype(jnp.bfloat16), "seq", scatter_dimension=0, tiled=True
        ).astype(jnp.float32),
        lax.psum_scatter(
            gate_grad_w.astype(jnp.bfloat16), "seq", scatter_dimension=0, tiled=True
        ).astype(jnp.float32),
        lax.psum_scatter(
            up_grad_w.astype(jnp.bfloat16), "seq", scatter_dimension=0, tiled=True
        ).astype(jnp.float32),
        lax.psum_scatter(
            down_grad_w.astype(jnp.bfloat16), "seq", scatter_dimension=1, tiled=True
        ).astype(jnp.float32),
    )


def body(
    inputs,
    doc_lengths,
    norm_in,
    query_weight,
    key_weight,
    value_weight,
    outgate_weight,
    scalar_weight,
    conv_kernel,
    decay_rate,
    head_norm,
    output_weight,
    norm_ffn,
    gate_weight,
    up_weight,
    down_weight,
    grad_out,
):
    gathered = (
        lax.all_gather(norm_in, "seq", axis=0, tiled=True),
        lax.all_gather(query_weight, "seq", axis=0, tiled=True),
        lax.all_gather(key_weight, "seq", axis=0, tiled=True),
        lax.all_gather(value_weight, "seq", axis=0, tiled=True),
        lax.all_gather(outgate_weight, "seq", axis=0, tiled=True),
        lax.all_gather(scalar_weight, "seq", axis=0, tiled=True),
        lax.all_gather(output_weight, "seq", axis=1, tiled=True),
        lax.all_gather(norm_ffn, "seq", axis=0, tiled=True),
        lax.all_gather(gate_weight, "seq", axis=0, tiled=True),
        lax.all_gather(up_weight, "seq", axis=0, tiled=True),
        lax.all_gather(down_weight, "seq", axis=1, tiled=True),
    )
    (
        gain_in,
        w_query,
        w_key,
        w_value,
        w_outgate,
        w_scalars,
        w_output,
        gain_ffn,
        gate_full,
        up_full,
        down_full,
    ) = gathered
    seq_count, step_count, model_width = inputs.shape
    tap_count = conv_kernel.shape[1]
    head_count = decay_rate.shape[0]
    inner_width = conv_kernel.shape[2]
    first_place = lax.axis_index("seq") * step_count - (tap_count - 1)
    docs_ext = doc_numbers(doc_lengths, first_place, step_count + tap_count - 1)
    hidden_in = inputs.astype(jnp.float32)
    scale_in = lax.rsqrt(jnp.mean(hidden_in * hidden_in, axis=-1, keepdims=True) + norm_eps)
    normed_in = (hidden_in * scale_in * gain_in.astype(jnp.float32)).astype(jnp.bfloat16)
    pre_conv = jnp.concatenate(
        [
            jnp.einsum("std,dc->stc", normed_in, w_query, preferred_element_type=jnp.float32),
            jnp.einsum("std,dc->stc", normed_in, w_key, preferred_element_type=jnp.float32),
            jnp.einsum("std,dc->stc", normed_in, w_value, preferred_element_type=jnp.float32),
        ],
        axis=-1,
    ).astype(jnp.bfloat16)
    out_gate = jnp.einsum("std,dc->stc", normed_in, w_outgate, preferred_element_type=jnp.float32)
    scalars = jnp.einsum("std,dkh->stkh", normed_in, w_scalars, preferred_element_type=jnp.float32)
    rim_rows = passed_along(pre_conv[:, step_count - tap_count + 1 :], "seq", 1)
    extended = jnp.concatenate([rim_rows, pre_conv], axis=1).astype(jnp.float32)
    kernel = conv_kernel.astype(jnp.float32)
    decay_scale = decay_rate.astype(jnp.float32)
    prepared, prep_pull = jax.vjp(
        partial(prepare, docs_ext=docs_ext), extended, kernel, scalars, decay_scale
    )
    queries, key_rows, values, strength, log_decay = prepared
    query_round = rounded_copy(queries)
    key_round = rounded_copy(key_rows)
    value_round = rounded_copy(values)
    grouped = partial(run_groups, docs_ext=docs_ext, group_len=GROUP, tap_count=tap_count)
    zero_state = jnp.zeros((seq_count, head_count, DK, DK), jnp.float32)
    identity = jnp.broadcast_to(jnp.eye(DK, dtype=jnp.float32), zero_state.shape)
    offset_state = grouped(query_round, key_round, value_round, strength, log_decay, zero_state)[1]
    transfer = grouped(
        query_round, key_round, jnp.zeros_like(value_round), strength, log_decay, identity
    )[1]

    def forward_hop(turn_index, incoming):
        moved = jnp.einsum("shij,shjv->shiv", transfer, incoming, precision=highest) + offset_state
        return passed_along(moved, "seq", 1)

    state_in = lax.fori_loop(0, lax.axis_size("seq") - 1, forward_hop, zero_state)
    (heads_out, final_state), delta_pull = jax.vjp(
        grouped, query_round, key_round, value_round, strength, log_decay, state_in
    )
    attn_normed, norm_pull = jax.vjp(gated_norm, heads_out, out_gate, head_norm.astype(jnp.float32))
    gated_rows = attn_normed.astype(jnp.bfloat16)
    mixer_out = lax.psum(
        jnp.einsum("stc,cd->std", gated_rows, w_output, preferred_element_type=jnp.float32).astype(
            jnp.bfloat16
        ),
        "head",
    ).astype(jnp.float32)
    residual = hidden_in + mixer_out
    scale_ffn = lax.rsqrt(jnp.mean(residual * residual, axis=-1, keepdims=True) + norm_eps)
    normed_ffn = (residual * scale_ffn * gain_ffn.astype(jnp.float32)).astype(jnp.bfloat16)
    gate_proj = jnp.einsum("std,df->stf", normed_ffn, gate_full, preferred_element_type=jnp.float32)
    up_proj = jnp.einsum("std,df->stf", normed_ffn, up_full, preferred_element_type=jnp.float32)
    gate_sigmoid = jax.nn.sigmoid(gate_proj)
    gate_silu = gate_proj * gate_sigmoid
    product = (gate_silu * up_proj).astype(jnp.bfloat16)
    ffn_out = lax.psum(
        jnp.einsum("stf,fd->std", product, down_full, preferred_element_type=jnp.float32).astype(
            jnp.bfloat16
        ),
        "head",
    ).astype(jnp.float32)
    outputs = (residual + ffn_out).astype(jnp.bfloat16)
    grad_final = grad_out.astype(jnp.float32)
    grad_downw = jnp.einsum("stf,std->fd", product, grad_out, preferred_element_type=jnp.float32)
    grad_act = jnp.einsum("std,fd->stf", grad_out, down_full, preferred_element_type=jnp.float32)
    gate_grad = (
        grad_act * up_proj * gate_sigmoid * (1.0 + gate_proj * (1.0 - gate_sigmoid))
    ).astype(jnp.bfloat16)
    up_grad = (grad_act * gate_silu).astype(jnp.bfloat16)
    grad_gatew = jnp.einsum(
        "std,stf->df", normed_ffn, gate_grad, preferred_element_type=jnp.float32
    )
    grad_upw = jnp.einsum("std,stf->df", normed_ffn, up_grad, preferred_element_type=jnp.float32)
    ffn_part = jnp.einsum("stf,df->std", gate_grad, gate_full, preferred_element_type=jnp.float32)
    ffn_part = ffn_part + jnp.einsum(
        "stf,df->std", up_grad, up_full, preferred_element_type=jnp.float32
    )
    grad_normed_ffn = lax.psum(ffn_part, "head")
    unit_ffn = residual * scale_ffn
    scaled_ffn = grad_normed_ffn * gain_ffn.astype(jnp.float32)
    grad_gain_ffn = jnp.sum(grad_normed_ffn * unit_ffn, axis=(0, 1))
    ffn_reduced = None
    grad_residual = grad_final + scale_ffn * (
        scaled_ffn - unit_ffn * jnp.mean(scaled_ffn * unit_ffn, axis=-1, keepdims=True)
    )
    grad_mixer = grad_residual.astype(jnp.bfloat16)
    grad_wout = jnp.einsum(
        "stc,std->cd", gated_rows, grad_mixer, preferred_element_type=jnp.float32
    )
    grad_gated = jnp.einsum("std,cd->stc", grad_mixer, w_output, preferred_element_type=jnp.float32)
    grad_heads_out, grad_out_gate, grad_gain_head = norm_pull(grad_gated)
    first_pass = delta_pull((grad_heads_out, zero_state))
    local_grad = first_pass[5]

    def back_hop(turn_index, incoming):
        moved = jnp.einsum("shji,shjv->shiv", transfer, incoming, precision=highest) + local_grad
        return passed_along(moved.astype(jnp.bfloat16), "seq", -1).astype(moved.dtype)

    state_grad = lax.fori_loop(0, lax.axis_size("seq") - 1, back_hop, zero_state)
    second_pass = delta_pull((jnp.zeros_like(grad_heads_out), state_grad))
    delta_grads = tuple((first_pass[position] + second_pass[position] for position in range(5)))
    grad_extended, grad_kernel, grad_scalars, grad_decay_scale = prep_pull(delta_grads)
    rim_grad = passed_along(
        grad_extended[:, : tap_count - 1].astype(jnp.bfloat16), "seq", -1
    ).astype(jnp.float32)
    grad_pre = grad_extended[:, tap_count - 1 :]
    grad_pre = grad_pre.at[:, step_count - tap_count + 1 :].add(rim_grad).astype(jnp.bfloat16)
    gate_grad_mix = grad_out_gate.astype(jnp.bfloat16)
    scalar_grad = grad_scalars.astype(jnp.bfloat16)
    pre_query_grad = grad_pre[..., :inner_width]
    pre_key_grad = grad_pre[..., inner_width : 2 * inner_width]
    pre_value_grad = grad_pre[..., 2 * inner_width :]
    grad_queryw = jnp.einsum(
        "std,stc->dc", normed_in, pre_query_grad, preferred_element_type=jnp.float32
    )
    grad_keyw = jnp.einsum(
        "std,stc->dc", normed_in, pre_key_grad, preferred_element_type=jnp.float32
    )
    grad_valuew = jnp.einsum(
        "std,stc->dc", normed_in, pre_value_grad, preferred_element_type=jnp.float32
    )
    grad_outgatew = jnp.einsum(
        "std,stc->dc", normed_in, gate_grad_mix, preferred_element_type=jnp.float32
    )
    grad_scalarw = jnp.einsum(
        "std,stkh->dkh", normed_in, scalar_grad, preferred_element_type=jnp.float32
    )
    input_part = jnp.einsum(
        "stc,dc->std", pre_query_grad, w_query, preferred_element_type=jnp.float32
    )
    input_part = input_part + jnp.einsum(
        "stc,dc->std", pre_key_grad, w_key, preferred_element_type=jnp.float32
    )
    input_part = input_part + jnp.einsum(
        "stc,dc->std", pre_value_grad, w_value, preferred_element_type=jnp.float32
    )
    input_part = input_part + jnp.einsum(
        "stc,dc->std", gate_grad_mix, w_outgate, preferred_element_type=jnp.float32
    )
    input_part = input_part + jnp.einsum(
        "stkh,dkh->std", scalar_grad, w_scalars, preferred_element_type=jnp.float32
    )
    grad_normed_in = lax.psum(input_part.astype(jnp.bfloat16), "head").astype(jnp.float32)
    unit_in = hidden_in * scale_in
    scaled_in = grad_normed_in * gain_in.astype(jnp.float32)
    grad_gain_in = jnp.sum(grad_normed_in * unit_in, axis=(0, 1))
    grad_in = grad_residual + scale_in * (
        scaled_in - unit_in * jnp.mean(scaled_in * unit_in, axis=-1, keepdims=True)
    )
    mixer_reduced = (
        lax.psum_scatter(
            grad_gain_in.astype(jnp.bfloat16), "seq", scatter_dimension=0, tiled=True
        ).astype(jnp.float32),
        lax.psum_scatter(
            grad_queryw.astype(jnp.bfloat16), "seq", scatter_dimension=0, tiled=True
        ).astype(jnp.float32),
        lax.psum_scatter(
            grad_keyw.astype(jnp.bfloat16), "seq", scatter_dimension=0, tiled=True
        ).astype(jnp.float32),
        lax.psum_scatter(
            grad_valuew.astype(jnp.bfloat16), "seq", scatter_dimension=0, tiled=True
        ).astype(jnp.float32),
        lax.psum_scatter(
            grad_outgatew.astype(jnp.bfloat16), "seq", scatter_dimension=0, tiled=True
        ).astype(jnp.float32),
        lax.psum_scatter(
            grad_scalarw.astype(jnp.bfloat16), "seq", scatter_dimension=0, tiled=True
        ).astype(jnp.float32),
        lax.psum_scatter(
            grad_wout.astype(jnp.bfloat16), "seq", scatter_dimension=1, tiled=True
        ).astype(jnp.float32),
    )
    ffn_reduced = reduce_ffn(grad_gain_ffn, grad_gatew, grad_upw, grad_downw)
    head_index = lax.axis_index("head")
    full_kernel = lax.dynamic_update_slice(
        jnp.zeros((3, tap_count, H * DK), jnp.float32),
        grad_kernel,
        (0, 0, head_index * inner_width),
    )
    full_decay = lax.dynamic_update_slice(
        jnp.zeros((H,), jnp.float32), grad_decay_scale, (head_index * head_count,)
    )
    summed_kernel, summed_decay, summed_norm = lax.psum(
        (full_kernel, full_decay, grad_gain_head), ("seq", "head")
    )
    grad_conv = lax.dynamic_slice(
        summed_kernel, (0, 0, head_index * inner_width), (3, tap_count, inner_width)
    )
    grad_decay = lax.dynamic_slice(summed_decay, (head_index * head_count,), (head_count,))
    return (
        outputs,
        grad_in,
        mixer_reduced[0],
        mixer_reduced[1],
        mixer_reduced[2],
        mixer_reduced[3],
        mixer_reduced[4],
        mixer_reduced[5],
        grad_conv,
        grad_decay,
        summed_norm,
        mixer_reduced[6],
        ffn_reduced[0],
        ffn_reduced[1],
        ffn_reduced[2],
        ffn_reduced[3],
    )


def solution(mesh):
    placed = (
        P(None, "seq", None),
        P(),
        P("seq"),
        P("seq", "head"),
        P("seq", "head"),
        P("seq", "head"),
        P("seq", "head"),
        P("seq", None, "head"),
        P(None, None, "head"),
        P("head"),
        P(),
        P("head", "seq"),
        P("seq"),
        P("seq", "head"),
        P("seq", "head"),
        P("head", "seq"),
        P(None, "seq", None),
    )
    return jax.shard_map(
        body,
        mesh=mesh,
        in_specs=placed,
        out_specs=(
            P(None, "seq", None),
            P(None, "seq", None),
            P("seq"),
            P("seq", "head"),
            P("seq", "head"),
            P("seq", "head"),
            P("seq", "head"),
            P("seq", None, "head"),
            P(None, None, "head"),
            P("head"),
            P(),
            P("head", "seq"),
            P("seq"),
            P("seq", "head"),
            P("seq", "head"),
            P("head", "seq"),
        ),
        check_vma=False,
    )
```

profile of v0, /device:TPU:1, one launch (start us, length us, event | category | flops | bytes accessed | tf_op | source)
XLA Modules:
  0.0 3962.7 jit_solution(5476009365611088949)
XLA Ops:
  16.3 86.4 %all-reduce.47 = (bf16[2048]{0:T(1024)(128)(2,1)S(1)}, bf16[2048]{0:T(1024)(128)(2,1)}) all-reduce(bf16[2048]{0:T(1024)(128)(2,1)S(1)} %dynamic-update-slice.3, bf16[2048]{0:T(1024)(128)(2,1)S(1)} %dynamic-update-slice.4), channel_id=1, replica_groups=mesh['seq'=32,'head'=4] {'seq'}, use_global_device_ids=true, to_apply=%add.41 | all-reduce | flops 4096 | bytes 16384
  105.1 81.0 %all_gather.37 = bf16[2048,2,4]{2,1,0:T(2,128)(2,1)S(1)} all-gather(bf16[64,2,4]{2,1,0:T(2,128)(2,1)S(1)} %copy.1315), channel_id=1, replica_groups=mesh['seq'=32,'head'=4] {'seq'}, dimensions={0}, use_global_device_ids=true | all-gather | bytes 33792 | tf_op jit(solution)/shard_map/all_gather | solution.py:181
  200.2 30.2 all-gather.13.cloned.1.call-done
  314.1 548.5 %while.22 = (s32[]{:T(128)}, f32[2,4,128,128]{3,2,1,0:T(8,128)S(1)}, f32[2,4,128,128]{3,2,1,0:T(8,128)}, f32[2,4,128,128]{3,2,1,0:T(8,128)}, s32[]{:T(128)}) while((s32[]{:T(128)}, f32[2,4,128,128]{3,2,1,0:T(8,128)S(1)}, f32[2,4,128,128]{3,2,1,0:T(8,128)}, f32[2,4,128,128]{3,2,1,0:T(8,128)}, s32[]{:T(128)}) %tuple.178), condition=%wide.region_8.9_spmd, body=%wide.region_7.8_spmd.sunk | while | flops 201457664 | bytes 4194405 | solution.py:243
  338.9 11.8 collective-permute-done
  358.9 10.2 collective-permute-done
  440.3 10.3 collective-permute-done
  458.5 11.4 collective-permute-done
  477.8 11.4 collective-permute-done
  497.4 10.5 collective-permute-done
  641.7 21.2 collective-permute-start
  902.0 95.6 %all-reduce.54.cloned.1.call-done = bf16[2,128,2048]{2,1,0:T(8,128)(2,1)} async-done(((bf16[2,128,2048]{2,1,0:T(8,128)(2,1)}), bf16[2,128,2048]{2,1,0:T(8,128)(2,1)}) %all-reduce.54.cloned.1.call-update) | async-done | bytes 1048592 | tf_op jit(solution)/shard_map/psum | solution.py:249
  1001.3 88.9 %all-gather.21.cloned.1.call-done = bf16[2048,1408]{1,0:T(8,128)(2,1)} async-done(((bf16[64,1408]{1,0:T(8,128)(2,1)}), bf16[2048,1408]{1,0:T(8,128)(2,1)}) %all-gather.21.cloned.1.call-update) | async-done | bytes 5767184 | tf_op jit(solution)/shard_map/all_gather | solution.py:185
  1096.1 84.3 %all-gather.23.cloned.1.call-done = bf16[1408,2048]{0,1:T(8,128)(2,1)} async-done(((bf16[1408,64]{0,1:T(8,128)(2,1)}), bf16[1408,2048]{0,1:T(8,128)(2,1)}) %all-gather.23.cloned.1.call-update) | async-done | bytes 5767184 | tf_op jit(solution)/shard_map/all_gather | solution.py:186
  1186.4 84.4 %all-gather.19.cloned.1.call-done = bf16[2048,1408]{1,0:T(8,128)(2,1)} async-done(((bf16[64,1408]{1,0:T(8,128)(2,1)}), bf16[2048,1408]{1,0:T(8,128)(2,1)}) %all-gather.19.cloned.1.call-update) | async-done | bytes 5767184 | tf_op jit(solution)/shard_map/all_gather | solution.py:184
  1305.3 36.6 all-reduce.56.cloned.1.call-done
  1364.8 494.5 %while.23 = (s32[]{:T(128)}, f32[2,4,128,128]{3,2,1,0:T(8,128)}, f32[2,4,128,128]{2,3,1,0:T(8,128)}, f32[2,4,128,128]{3,2,1,0:T(8,128)}, s32[]{:T(128)}, /*index=5*/s32[]{:T(128)}) while((s32[]{:T(128)}, f32[2,4,128,128]{3,2,1,0:T(8,128)}, f32[2,4,128,128]{2,3,1,0:T(8,128)}, f32[2,4,128,128]{3,2,1,0:T(8,128)}, s32[]{:T(128)}, ...), condition=%wide.region_17.18_spmd.clone, body=%wide.region_16.17_spmd.clone.sunk | while | flops 201850880 | bytes 3670135 | solution.py:306
  1368.7 10.0 collective-permute-done.1
  1384.4 9.7 collective-permute-done.1
  1543.6 9.6 collective-permute-done.1
  1559.0 10.6 collective-permute-done.1
  1575.5 10.6 collective-permute-done.1
  1591.9 11.2 collective-permute-done.1
  1608.9 12.5 collective-permute-done.1
  1627.2 14.1 collective-permute-done.1
  1647.1 14.0 collective-permute-done.1
  1666.9 12.3 collective-permute-done.1
  1685.0 12.2 collective-permute-done.1
  1703.0 10.6 collective-permute-done.1
  1764.9 10.4 collective-permute-done.1
  1781.0 10.6 collective-permute-done.1
  1797.5 10.6 collective-permute-done.1
  1813.9 10.6 collective-permute-done.1
  1830.4 10.6 collective-permute-done.1
  1846.8 10.6 collective-permute-done.1
  2082.4 130.6 %all-reduce.45 = (f32[16]{0:T(128)S(1)}, f32[128]{0:T(128)}) all-reduce(f32[16]{0:T(128)S(1)} %negate_dynamic-update-slice_fusion, f32[128]{0:T(128)S(1)} %copy-done.295), channel_id=1, replica_groups=mesh['seq'=32,'head'=4] {'seq','head'}, use_global_device_ids=true, to_apply=%region_75.76 | all-reduce | flops 144 | bytes 1152 | tf_op jit(solution)/shard_map/psum | solution.py:390
  2213.6 16.0 all-reduce.58.cloned.1.call-done
  2230.9 157.0 %reduce-scatter.28.cloned.1.call-done = bf16[64,8]{1,0:T(8,128)(2,1)} async-done(((bf16[2048,8]{1,0:T(8,128)(2,1)}), bf16[64,8]{1,0:T(8,128)(2,1)}) %reduce-scatter.28.cloned.1.call-update) | async-done | bytes 1040
  2389.3 79.1 %all-reduce.60.cloned.1.call-done = (bf16[2,128,2048]{2,1,0:T(8,128)(2,1)}, bf16[2,128,2048]{2,1,0:T(8,128)(2,1)}) async-done(((bf16[2,128,2048]{2,1,0:T(8,128)(2,1)}, bf16[2,128,2048]{2,1,0:T(8,128)(2,1)}), (bf16[2,128,2048]{2,1,0:T(8,128)(2,1)}, bf16[2,128,2048]{2,1,0:T(8,128)(2,1)})) %all-reduce.60.cloned.1.call-update) | async-done | bytes 2097168 | tf_op jit(solution)/shard_map/psum | solution.py:263
  2470.3 84.8 %all-reduce.46 = (bf16[2048]{0:T(1024)(128)(2,1)S(1)}, bf16[2048]{0:T(1024)(128)(2,1)S(1)}) all-reduce(bf16[2048]{0:T(1024)(128)(2,1)S(1)} %get-tuple-element.127, bf16[2048]{0:T(1024)(128)(2,1)S(1)} %copy-done.271), channel_id=2, replica_groups=mesh['seq'=32,'head'=4] {'seq'}, use_global_device_ids=true, to_apply=%region_63.64.clone | all-reduce | flops 4096 | bytes 16384
  2561.3 74.5 %reduce-scatter.20.cloned.1.call-done = bf16[512,64]{0,1:T(8,128)(2,1)} async-done(((bf16[512,2048]{0,1:T(8,128)(2,1)}), bf16[512,64]{0,1:T(8,128)(2,1)}) %reduce-scatter.20.cloned.1.call-update) | async-done | bytes 65552 | tf_op jit(solution)/shard_map/reduce_scatter | solution.py:376
  2637.3 181.9 %reduce-scatter.18.cloned.1.call-done = bf16[64,512]{1,0:T(8,128)(2,1)} async-done(((bf16[2048,512]{1,0:T(8,128)(2,1)}), bf16[64,512]{1,0:T(8,128)(2,1)}) %reduce-scatter.18.cloned.1.call-update) | async-done | bytes 65552 | tf_op jit(solution)/shard_map/reduce_scatter | solution.py:370
  2820.7 182.2 %reduce-scatter.12.cloned.1.call-done = bf16[64,512]{1,0:T(8,128)(2,1)} async-done(((bf16[2048,512]{1,0:T(8,128)(2,1)}), bf16[64,512]{1,0:T(8,128)(2,1)}) %reduce-scatter.12.cloned.1.call-update) | async-done | bytes 65552 | tf_op jit(solution)/shard_map/reduce_scatter | solution.py:361
  3004.4 182.6 %reduce-scatter.14.cloned.1.call-done = bf16[64,512]{1,0:T(8,128)(2,1)} async-done(((bf16[2048,512]{1,0:T(8,128)(2,1)}), bf16[64,512]{1,0:T(8,128)(2,1)}) %reduce-scatter.14.cloned.1.call-update) | async-done | bytes 65552 | tf_op jit(solution)/shard_map/reduce_scatter | solution.py:364
  3188.5 182.1 %reduce-scatter.16.cloned.1.call-done = bf16[64,512]{1,0:T(8,128)(2,1)} async-done(((bf16[2048,512]{1,0:T(8,128)(2,1)}), bf16[64,512]{1,0:T(8,128)(2,1)}) %reduce-scatter.16.cloned.1.call-update) | async-done | bytes 65552 | tf_op jit(solution)/shard_map/reduce_scatter | solution.py:367
  3372.1 193.2 %reduce-scatter.22.cloned.1.call-done = bf16[64,1408]{1,0:T(8,128)(2,1)} async-done(((bf16[2048,1408]{1,0:T(8,128)(2,1)}), bf16[64,1408]{1,0:T(8,128)(2,1)}) %reduce-scatter.22.cloned.1.call-update) | async-done | bytes 180240 | tf_op jit(solution)/shard_map/reduce_scatter | solution.py:144
  3567.0 192.5 %reduce-scatter.24.cloned.1.call-done = bf16[64,1408]{1,0:T(8,128)(2,1)} async-done(((bf16[2048,1408]{1,0:T(8,128)(2,1)}), bf16[64,1408]{1,0:T(8,128)(2,1)}) %reduce-scatter.24.cloned.1.call-update) | async-done | bytes 180240 | tf_op jit(solution)/shard_map/reduce_scatter | solution.py:147
  3761.2 192.8 %reduce-scatter.26.cloned.1.call-done = bf16[1408,64]{0,1:T(8,128)(2,1)} async-done(((bf16[1408,2048]{0,1:T(8,128)(2,1)}), bf16[1408,64]{0,1:T(8,128)(2,1)}) %reduce-scatter.26.cloned.1.call-update) | async-done | bytes 180240 | tf_op jit(solution)/shard_map/reduce_scatter | solution.py:150
  (1277 shorter events, 1216.1 us)
Async XLA Ops:
  7.2 188.1 %all-gather.9.cloned.1.call-start = ((), (), s32[]{:S(2)}) async-start(), calls=%async_computation.9 | async-start | bytes 2162688 | tf_op jit(solution)/shard_map/all_gather | solution.py:177
  7.9 189.9 %all-gather.11.cloned.1.call-start = ((), (), s32[]{:S(2)}) async-start(), calls=%async_computation.10 | async-start | bytes 2162688 | tf_op jit(solution)/shard_map/all_gather | solution.py:178
  8.7 221.7 %all-gather.13.cloned.1.call-start = ((), (), s32[]{:S(2)}) async-start(), calls=%async_computation.11 | async-start | bytes 2162688 | tf_op jit(solution)/shard_map/all_gather | solution.py:179
  9.4 867.1 %all-gather.15.cloned.1.call-start = ((), (), s32[]{:S(2)}) async-start(), calls=%async_computation.12 | async-start | bytes 2162688 | tf_op jit(solution)/shard_map/all_gather | solution.py:180
  10.0 869.9 %all-gather.17.cloned.1.call-start = ((), (), s32[]{:S(2)}) async-start(), calls=%async_computation.13 | async-start | bytes 2162688 | tf_op jit(solution)/shard_map/all_gather | solution.py:182
  10.6 986.9 %all-reduce.54.cloned.1.call-start = ((), (), s32[]{:S(2)}) async-start(), calls=%async_computation.14 | async-start | bytes 2097152 | tf_op jit(solution)/shard_map/psum | solution.py:249
  316.9 13.8 collective-permute-start
  333.4 17.4 collective-permute-start
  353.4 15.7 collective-permute-start
  418.0 14.5 collective-permute-start
  435.1 15.6 collective-permute-start
  453.3 16.6 collective-permute-start
  472.6 16.7 collective-permute-start
  491.9 16.1 collective-permute-start
  510.6 15.1 collective-permute-start
  528.4 14.4 collective-permute-start
  545.4 15.4 collective-permute-start
  563.5 13.9 collective-permute-start
  641.7 29.6 collective-permute-start
  673.9 14.4 collective-permute-start
  722.7 14.9 collective-permute-start
  740.3 14.9 collective-permute-start
  757.9 14.9 collective-permute-start
  775.5 14.9 collective-permute-start
  793.0 14.9 collective-permute-start
  810.6 14.9 collective-permute-start
  828.2 15.3 collective-permute-start
  846.1 16.6 collective-permute-start
  883.3 207.0 %all-gather.21.cloned.1.call-start = ((), (), s32[]{:S(2)}) async-start(), calls=%async_computation.16 | async-start | bytes 5947392 | tf_op jit(solution)/shard_map/all_gather | solution.py:185
  884.0 296.4 %all-gather.23.cloned.1.call-start = ((), (), s32[]{:S(2)}) async-start(), calls=%async_computation.17 | async-start | bytes 5947392 | tf_op jit(solution)/shard_map/all_gather | solution.py:186
  884.8 385.9 %all-gather.19.cloned.1.call-start = ((), (), s32[]{:S(2)}) async-start(), calls=%async_computation.15 | async-start | bytes 5947392 | tf_op jit(solution)/shard_map/all_gather | solution.py:184
  885.5 456.4 %all-reduce.56.cloned.1.call-start = ((), (), s32[]{:S(2)}) async-start(), calls=%async_computation.18 | async-start | bytes 4194304 | tf_op jit(solution)/shard_map/psum | solution.py:285
  1285.9 943.7 %all-reduce.58.cloned.1.call-start = ((), (), s32[]{:S(2)}) async-start(), calls=%async_computation.23 | async-start | bytes 196608 | tf_op jit(solution)/shard_map/psum | solution.py:390
  1607.6 13.8 collective-permute-start.1
  1625.9 15.4 collective-permute-start.1
  1645.8 15.3 collective-permute-start.1
  1665.6 13.6 collective-permute-start.1
  1683.7 13.5 collective-permute-start.1
  2027.7 360.2 %reduce-scatter.28.cloned.1.call-start = ((), (), s32[]{:S(2)}) async-start(), calls=%async_computation.28 | async-start | bytes 540672
  2040.9 427.5 %all-reduce.60.cloned.1.call-start = ((), (), s32[]{:S(2)}) async-start(), calls=%async_computation.29 | async-start | bytes 4194304 | tf_op jit(solution)/shard_map/psum | solution.py:263
  2051.0 584.8 %reduce-scatter.20.cloned.1.call-start = ((), (), s32[]{:S(2)}) async-start(), calls=%async_computation.24 | async-start | bytes 2162688 | tf_op jit(solution)/shard_map/reduce_scatter | solution.py:376
  2055.7 763.4 %reduce-scatter.18.cloned.1.call-start = ((), (), s32[]{:S(2)}) async-start(), calls=%async_computation.22 | async-start | bytes 2162688 | tf_op jit(solution)/shard_map/reduce_scatter | solution.py:370
  2058.0 944.9 %reduce-scatter.12.cloned.1.call-start = ((), (), s32[]{:S(2)}) async-start(), calls=%async_computation.19 | async-start | bytes 2162688 | tf_op jit(solution)/shard_map/reduce_scatter | solution.py:361
  2060.3 1126.7 %reduce-scatter.14.cloned.1.call-start = ((), (), s32[]{:S(2)}) async-start(), calls=%async_computation.20 | async-start | bytes 2162688 | tf_op jit(solution)/shard_map/reduce_scatter | solution.py:364
  2062.6 1308.0 %reduce-scatter.16.cloned.1.call-start = ((), (), s32[]{:S(2)}) async-start(), calls=%async_computation.21 | async-start | bytes 2162688 | tf_op jit(solution)/shard_map/reduce_scatter | solution.py:367
  2064.9 1500.4 %reduce-scatter.22.cloned.1.call-start = ((), (), s32[]{:S(2)}) async-start(), calls=%async_computation.25 | async-start | bytes 5947392 | tf_op jit(solution)/shard_map/reduce_scatter | solution.py:144
  2070.3 1689.2 %reduce-scatter.24.cloned.1.call-start = ((), (), s32[]{:S(2)}) async-start(), calls=%async_computation.26 | async-start | bytes 5947392 | tf_op jit(solution)/shard_map/reduce_scatter | solution.py:147
  2075.8 1878.1 %reduce-scatter.26.cloned.1.call-start = ((), (), s32[]{:S(2)}) async-start(), calls=%async_computation.27 | async-start | bytes 5947392 | tf_op jit(solution)/shard_map/reduce_scatter | solution.py:150
  (337 other events, 3129.1 us)
Sparse Core Ops, SparseCore 0:
  11.0 73.3 all-gather.8
  87.4 70.8 all-gather.10
  161.3 69.0 all-gather.12
  233.2 67.6 all-gather.14
  303.7 89.4 all-gather.16
  883.4 114.0 all-reduce.53
  1001.0 89.1 all-gather.20
  1093.8 86.6 all-gather.22
  1184.0 86.6 all-gather.18
  1286.0 55.8 all-reduce.55
  2027.8 201.7 all-reduce.57
  2231.9 155.9 reduce-scatter.27
  2390.5 77.8 all-reduce.59
  2470.7 165.0 reduce-scatter.19
  2638.0 181.1 reduce-scatter.17
  2821.5 181.3 reduce-scatter.11
  3005.1 181.8 reduce-scatter.13
  3189.3 181.2 reduce-scatter.15
  3373.0 192.2 reduce-scatter.21
  3567.5 191.8 reduce-scatter.23
  3761.9 192.0 reduce-scatter.25
where the time goes:
time: 4000 us; the launch traced here: 3960 us
  waiting for transfers between devices  2620 us (66%)
  matrix products  415 us (10%)
  blocking collectives  383 us (10%)
  starting transfers between devices  264 us (7%)
  other arithmetic  148 us (4%)
  local copies, waits for them, and re-layouts  110 us (3%)
    ppermute x64, waiting for transfers between devices, passed_along(): return lax.ppermute(array, axis, pairs)  563 us
    ppermute x64, starting transfers between devices, passed_along(): return lax.ppermute(array, axis, pairs)  262 us
    reduce_scatter x1, waiting for transfers between devices, reduce_ffn(): lax.psum_scatter(gate_grad_w.astype(jnp.bfloat16), 'seq', scatter_dimensi...  193 us
    reduce_scatter x1, waiting for transfers between devices, reduce_ffn(): lax.psum_scatter(down_grad_w.astype(jnp.bfloat16), 'seq', scatter_dimensi...  193 us
    reduce_scatter x1, waiting for transfers between devices, reduce_ffn(): lax.psum_scatter(up_grad_w.astype(jnp.bfloat16), 'seq', scatter_dimension...  193 us
    reduce_scatter x1, waiting for transfers between devices, body(): lax.psum_scatter(grad_keyw.astype(jnp.bfloat16), 'seq', scatter_dimension...  183 us
    reduce_scatter x1, waiting for transfers between devices, body(): lax.psum_scatter(grad_queryw.astype(jnp.bfloat16), 'seq', scatter_dimensi...  182 us
    reduce_scatter x1, waiting for transfers between devices, body(): lax.psum_scatter(grad_valuew.astype(jnp.bfloat16), 'seq', scatter_dimensi...  182 us
  transfers between devices with their start and end apart: 85, of which 80 were waited for; matrix products, arithmetic and copies ran while one was open for 8% of the time, Pallas kernels for 0%

commit v1 on v0

v1 whole, which is shorter than its diff:
```python
from functools import partial

import jax
import jax.numpy as jnp
from jax import lax
from jax.experimental import pallas as pl
from jax.experimental.pallas import tpu as pltpu
from jax.sharding import PartitionSpec as P

f32 = jnp.float32
bf16 = jnp.bfloat16
norm_eps = 1e-06
head_eps = 1e-05
SEQ = 32
HEADS = 4
DK = 128
TOK = 128
TAPS = 4
HALO = 16
VMEM = 56 * 1024 * 1024

NN = (((1,), (0,)), ((), ()))
NT = (((1,), (1,)), ((), ()))
TN = (((0,), (0,)), ((), ()))


def dot1(a, b, dims=NN):
    return lax.dot_general(a.astype(bf16), b.astype(bf16), dims, preferred_element_type=f32)


def split(a):
    high = a.astype(bf16)
    return high, (a - high.astype(f32)).astype(bf16)


def dot3(a, b, dims=NN):
    ah, al = split(a)
    bh, bl = split(b)
    return dot1(ah, bh, dims) + (dot1(ah, bl, dims) + dot1(al, bh, dims))


def dot2(exact, b, dims=NN):
    high = b.astype(bf16)
    rest = b - high.astype(f32)
    mid = rest.astype(bf16)
    low = (rest - mid.astype(f32)).astype(bf16)
    return dot1(exact, high, dims) + (dot1(exact, mid, dims) + dot1(exact, low, dims))


def sigmoid(x):
    return 1.0 / (1.0 + jnp.exp(-x))


def softplus(x):
    return jnp.maximum(x, 0.0) + jnp.log1p(jnp.exp(-jnp.abs(x)))


def iotas():
    rows = lax.broadcasted_iota(jnp.int32, (TOK, TOK), 0)
    cols = lax.broadcasted_iota(jnp.int32, (TOK, TOK), 1)
    return rows, cols


def unit_inverses(stricts):
    rows, cols = iotas()
    eye = (rows == cols).astype(f32)
    apart = jnp.bitwise_xor(rows, cols)
    results = []
    first = (apart == 1) & (rows > cols)
    results = [eye - jnp.where(first, a, 0.0) for a in stricts]
    size = 2
    while size < TOK:
        corner = (apart >= size) & (apart < 2 * size) & (rows > cols)
        parts = [dot3(jnp.where(corner, a, 0.0), x) for a, x in zip(stricts, results)]
        results = [x - dot3(x, c) for x, c in zip(results, parts)]
        size *= 2
    return results


def decays(scal, rates, marks, docs_row):
    rows, cols = iotas()
    strength = sigmoid(scal)
    log_decay = -rates * softplus(scal)
    lower = (rows >= cols).astype(bf16)
    total = dot2(lower, log_decay)
    total_t = jnp.transpose(total)
    same = marks[:, 5:6] == docs_row
    causal = same & (rows >= cols)
    return strength, total, total_t, causal, rows > cols


def conv_parts(ext_ref, weights, marks, lane):
    out = None
    for tap in range(TAPS):
        piece = ext_ref[pl.ds(HALO - TAPS + 1 + tap, TOK), pl.ds(lane, DK)]
        if tap < TAPS - 1:
            piece = piece * marks[:, tap : tap + 1]
        piece = piece * weights[tap : tap + 1, lane : lane + DK]
        out = piece if out is None else out + piece
    return out


def unit_scale(x):
    return lax.rsqrt(jnp.sum(x * x, axis=-1, keepdims=True) + norm_eps)


def chunk_forward(
    pre_ref, rim_ref, scal_ref, rate_ref, taps_ref, marks_ref, docs_ref,
    send_ref, p_ref, z_ref, x_ref, uw_ref, ext_ref,
):
    inner = HEADS * DK
    ext_ref[0:HALO, :] = rim_ref[...].astype(f32)
    ext_ref[HALO:, :] = pre_ref[...].astype(f32)
    marks = marks_ref[0]
    weights = taps_ref[...]
    strength, total, total_t, causal, below = decays(
        scal_ref[...], rate_ref[...], marks, docs_ref[0]
    )
    rows, cols = iotas()
    reached, tail = marks[:, 3:4], marks[:, 4:5]
    heads = []
    for h in range(HEADS):
        acts = []
        for c in range(3):
            conv = conv_parts(ext_ref, weights, marks, c * inner + h * DK)
            acts.append(conv * sigmoid(conv))
        q = (acts[0] * unit_scale(acts[0])).astype(bf16)
        k = (acts[1] * unit_scale(acts[1])).astype(bf16)
        v = acts[2].astype(bf16)
        c_col = total[:, HEADS + h : HEADS + h + 1]
        c_row = total_t[HEADS + h : HEADS + h + 1, :]
        decay = jnp.where(causal, jnp.exp(jnp.where(causal, c_col - c_row, 0.0)), 0.0)
        b = strength[:, h : h + 1]
        gram = dot1(k, k, NT)
        strict = jnp.where(below, b * gram * decay, 0.0)
        heads.append((q, k, v, c_col, decay, b, strict))
    inverses = unit_inverses([head[6] for head in heads])
    for h in range(HEADS):
        q, k, v, c_col, decay, b, strict = heads[h]
        x = inverses[h]
        start = jnp.exp(c_col) * reached
        kf = k.astype(f32)
        uw = dot3(x, jnp.concatenate([b * v.astype(f32), (b * start) * kf], axis=1))
        scores = dot1(q, k, NT) * decay
        suw = dot3(scores, uw)
        last = c_col[TOK - 1 : TOK, :]
        tail_k = kf * (jnp.exp(last - c_col) * tail)
        carry = jnp.exp(last) * reached[TOK - 1 : TOK, :]
        u, w = uw[:, :DK], uw[:, DK:]
        move = jnp.where(rows == cols, carry, 0.0) - dot3(tail_k, w, TN)
        offset_t = dot3(u, tail_k, TN)
        p_ref[h] = (q.astype(f32) * start - suw[:, DK:]).astype(bf16)
        z_ref[h] = suw[:, :DK]
        x_ref[h] = x.astype(bf16)
        uw_ref[h] = uw
        quarter = DK // HEADS
        for j in range(HEADS):
            send_ref[HEADS * h + j, 0:DK, :] = move.astype(bf16)
            send_ref[HEADS * h + j, DK : DK + quarter, :] = offset_t[
                j * quarter : (j + 1) * quarter
            ].astype(bf16)


def scan_forward(got_ref, out_ref):
    state = jnp.zeros((DK // HEADS, DK), f32)
    for i in range(SEQ):
        out_ref[i] = state.astype(bf16)
        if i + 1 < SEQ:
            high, low = split(state)
            both = dot1(jnp.concatenate([high, low], axis=0), got_ref[i, 0:DK, :], NT)
            half = DK // HEADS
            state = both[:half] + both[half:] + got_ref[i, DK : DK + half, :].astype(f32)


def scan_backward(got_ref, local_ref, out_ref):
    state = jnp.zeros((DK // HEADS, DK), f32)
    for i in range(SEQ - 1, -1, -1):
        out_ref[i] = state.astype(bf16)
        if i > 0:
            high, low = split(state)
            both = dot1(jnp.concatenate([high, low], axis=0), got_ref[i, 0:DK, :])
            half = DK // HEADS
            state = both[:half] + both[half:] + local_ref[i].astype(f32)


def gate_forward(p_ref, z_ref, s_ref, og_ref, gain_ref, heads_ref, gated_ref):
    gain = gain_ref[...]
    for h in range(HEADS):
        lanes = slice(h * DK, (h + 1) * DK)
        out = dot1(p_ref[h], s_ref[h], NT) + z_ref[h]
        heads_ref[:, lanes] = out
        r = lax.rsqrt(jnp.mean(out * out, axis=-1, keepdims=True) + head_eps)
        og = og_ref[:, lanes]
        gated_ref[:, lanes] = (out * r * gain * (og * sigmoid(og))).astype(bf16)


def gate_backward(
    gg_ref, heads_ref, og_ref, gain_ref, p_ref, do_ref, mix_ref, local_ref, gain_out_ref
):
    gain = gain_ref[...]
    total = jnp.zeros((1, DK), f32)
    quarter = DK // HEADS
    for h in range(HEADS):
        lanes = slice(h * DK, (h + 1) * DK)
        out = heads_ref[:, lanes]
        og = og_ref[:, lanes]
        gg = gg_ref[:, lanes]
        r = lax.rsqrt(jnp.mean(out * out, axis=-1, keepdims=True) + head_eps)
        u = out * r
        sig = sigmoid(og)
        w = og * sig
        ggw = gg * w
        g = ggw * gain
        total = total + jnp.sum(ggw * u, axis=0, keepdims=True)
        grad = r * (g - u * jnp.mean(g * u, axis=-1, keepdims=True))
        do_ref[:, lanes] = grad
        mix_ref[:, lanes] = (gg * gain * u * sig * (1.0 + og * (1.0 - sig))).astype(bf16)
        local = dot1(grad, p_ref[h], TN).astype(bf16)
        for j in range(HEADS):
            local_ref[HEADS * h + j] = local[j * quarter : (j + 1) * quarter]

    @pl.when(pl.program_id(0) == 0)
    def _():
        gain_out_ref[...] = jnp.zeros_like(gain_out_ref)

    gain_out_ref[0:1, :] += total


def chunk_backward(
    pre_ref, rim_ref, scal_ref, rate_ref, taps_ref, marks_ref, docs_ref,
    x_ref, uw_ref, s_ref, d_ref, do_ref,
    gpre_ref, grim_ref, gscal_ref, gtaps_ref, grate_ref, ext_ref, gext_ref,
):
    inner = HEADS * DK
    ext_ref[0:HALO, :] = rim_ref[...].astype(f32)
    ext_ref[HALO:, :] = pre_ref[...].astype(f32)
    gext_ref[...] = jnp.zeros_like(gext_ref)

    @pl.when(pl.program_id(0) == 0)
    def _():
        gtaps_ref[...] = jnp.zeros_like(gtaps_ref)
        grate_ref[...] = jnp.zeros_like(grate_ref)

    marks = marks_ref[0]
    weights = taps_ref[...]
    scal = scal_ref[...]
    rates = rate_ref[...]
    strength, total, total_t, causal, below = decays(scal, rates, marks, docs_ref[0])
    rows, cols = iotas()
    reached, tail = marks[:, 3:4], marks[:, 4:5]
    grad_b = jnp.zeros((TOK, TOK), f32)
    grad_c = jnp.zeros((TOK, TOK), f32)
    for h in range(HEADS):
        convs, sigs, acts = [], [], []
        for c in range(3):
            conv = conv_parts(ext_ref, weights, marks, c * inner + h * DK)
            sig = sigmoid(conv)
            convs.append(conv)
            sigs.append(sig)
            acts.append(conv * sig)
        nq, nk = unit_scale(acts[0]), unit_scale(acts[1])
        q_hat, k_hat = acts[0] * nq, acts[1] * nk
        q, k, v = q_hat.astype(bf16), k_hat.astype(bf16), acts[2].astype(bf16)
        qf, kf, vf = q.astype(f32), k.astype(f32), v.astype(f32)
        c_col = total[:, HEADS + h : HEADS + h + 1]
        c_row = total_t[HEADS + h : HEADS + h + 1, :]
        decay = jnp.where(causal, jnp.exp(jnp.where(causal, c_col - c_row, 0.0)), 0.0)
        strict_decay = jnp.where(below, decay, 0.0)
        b = strength[:, h : h + 1]
        gram_decay = dot1(k, k, NT) * strict_decay
        scores = dot1(q, k, NT) * decay
        start = jnp.exp(c_col) * reached
        last = c_col[TOK - 1 : TOK, :]
        tail_decay = jnp.exp(last - c_col) * tail
        tail_k = kf * tail_decay
        carry = jnp.exp(last) * reached[TOK - 1 : TOK, :]
        state, adj = s_ref[h], d_ref[h]
        do = do_ref[:, h * DK : (h + 1) * DK].astype(bf16)
        fresh = uw_ref[h, :, :DK] - dot1(uw_ref[h, :, DK:], state, NT)
        fresh = fresh.astype(bf16)
        recalled = dot1(k, state, NT)
        d_fresh = dot1(scores, do, TN) + dot1(tail_k, adj, NT)
        d_scores = dot1(do, fresh, NT)
        score_pull = d_scores * scores
        d_qk = (d_scores * decay).astype(bf16)
        do_state = dot1(do, state)
        d_q = dot1(d_qk, k) + start * do_state
        d_start = jnp.sum(qf * do_state, axis=-1, keepdims=True)
        d_r = dot1(x_ref[h], d_fresh, TN)
        d_v = b * d_r
        d_b = jnp.sum(d_r * (vf - start * recalled), axis=-1, keepdims=True)
        d_start = d_start - jnp.sum(d_v * recalled, axis=-1, keepdims=True)
        d_k = -start * dot1(d_v, state)
        d_strict = -dot1(d_r, fresh, NT)
        strict_pull = d_strict * gram_decay
        d_b = d_b + jnp.sum(strict_pull, axis=-1, keepdims=True)
        d_gram = (d_strict * (b * strict_decay)).astype(bf16)
        d_k = d_k + dot1(d_gram, k) + dot1(d_gram, k, TN) + dot1(d_qk, q, TN)
        fresh_adj = dot1(fresh, adj)
        d_k = d_k + tail_decay * fresh_adj
        d_tail = jnp.sum(kf * fresh_adj, axis=-1, keepdims=True) * tail_decay
        d_carry = jnp.sum(
            jnp.sum(adj.astype(f32) * state.astype(f32), axis=-1, keepdims=True),
            axis=0, keepdims=True,
        )
        pull = score_pull + b * strict_pull
        d_c = jnp.sum(pull - jnp.transpose(pull), axis=-1, keepdims=True)
        d_c = d_c + d_start * start - d_tail
        d_last = d_carry * carry + jnp.sum(d_tail, axis=0, keepdims=True)
        d_c = d_c + jnp.where(rows[:, 0:1] == TOK - 1, d_last, 0.0)
        grad_b = jnp.where(cols == h, d_b, grad_b)
        grad_c = jnp.where(cols == HEADS + h, d_c, grad_c)
        d_acts = (
            nq * (d_q - q_hat * jnp.sum(d_q * q_hat, axis=-1, keepdims=True)),
            nk * (d_k - k_hat * jnp.sum(d_k * k_hat, axis=-1, keepdims=True)),
            d_v,
        )
        for c in range(3):
            lane = c * inner + h * DK
            d_conv = d_acts[c] * sigs[c] * (1.0 + convs[c] * (1.0 - sigs[c]))
            for tap in range(TAPS):
                kept = d_conv * marks[:, tap : tap + 1] if tap < TAPS - 1 else d_conv
                place = (pl.ds(HALO - TAPS + 1 + tap, TOK), pl.ds(lane, DK))
                gtaps_ref[tap : tap + 1, lane : lane + DK] += jnp.sum(
                    kept * ext_ref[place], axis=0, keepdims=True
                )
                gext_ref[place] += kept * weights[tap : tap + 1, lane : lane + DK]
    upper = (cols >= rows).astype(bf16)
    grad_ld = dot2(upper, grad_c)
    decay_side = -grad_ld * rates * sigmoid(scal)
    gscal_ref[...] = jnp.where(
        cols < HEADS,
        grad_b * strength * (1.0 - strength),
        jnp.where(cols < 2 * HEADS, decay_side, 0.0),
    ).astype(bf16)
    grate_ref[0:1, :] += -jnp.sum(grad_ld * softplus(scal), axis=0, keepdims=True)
    gpre_ref[...] = gext_ref[HALO:, :]
    grim_ref[...] = gext_ref[0:HALO, :].astype(bf16)


def cost(flops, moved):
    return pl.CostEstimate(flops=flops, bytes_accessed=moved, transcendentals=0)


def params():
    return pltpu.CompilerParams(vmem_limit_bytes=VMEM)


def whole(shape):
    return pl.BlockSpec(shape, lambda s: (0,) * len(shape))


def by_rows(rows, cols, base=0, lane=0):
    return pl.BlockSpec((rows, cols), lambda s: (base + s, lane))


def by_lead(*shape):
    return pl.BlockSpec(shape, lambda s: (s,) + (0,) * (len(shape) - 1))


def mixer_specs():
    wide = 3 * HEADS * DK
    return [
        by_rows(TOK, wide),
        by_rows(HALO, wide, 2 * TOK // HALO),
        by_rows(TOK, 128),
        whole((1, 128)),
        whole((TAPS, wide)),
        by_lead(1, TOK, 8),
        by_lead(1, 1, TOK),
    ]


def run_chunk_forward(pre, scal, rates, taps, marks, docs):
    quarter = DK // HEADS
    wide = 3 * HEADS * DK
    return pl.pallas_call(
        chunk_forward,
        grid=(2,),
        in_specs=mixer_specs(),
        out_specs=[
            by_lead(16, DK + quarter, DK),
            by_lead(HEADS, TOK, DK),
            by_lead(HEADS, TOK, DK),
            by_lead(HEADS, TOK, DK),
            by_lead(HEADS, TOK, 2 * DK),
        ],
        out_shape=[
            jax.ShapeDtypeStruct((SEQ, DK + quarter, DK), bf16),
            jax.ShapeDtypeStruct((8, TOK, DK), bf16),
            jax.ShapeDtypeStruct((8, TOK, DK), f32),
            jax.ShapeDtypeStruct((8, TOK, DK), bf16),
            jax.ShapeDtypeStruct((8, TOK, 2 * DK), f32),
        ],
        scratch_shapes=[pltpu.VMEM((HALO + TOK, wide), f32)],
        compiler_params=params(),
        cost_estimate=cost(10**10, 6 * 10**6),
    )(pre, pre, scal, rates, taps, marks, docs)


def run_scan_forward(got):
    return pl.pallas_call(
        scan_forward,
        out_shape=jax.ShapeDtypeStruct((SEQ, DK // HEADS, DK), bf16),
        compiler_params=params(),
        cost_estimate=cost(10**9, 3 * 10**6),
    )(got)


def run_scan_backward(got, local):
    return pl.pallas_call(
        scan_backward,
        out_shape=jax.ShapeDtypeStruct((SEQ, DK // HEADS, DK), bf16),
        compiler_params=params(),
        cost_estimate=cost(10**9, 3 * 10**6),
    )(got, local)


def run_gate_forward(p, z, state, og, gain):
    inner = HEADS * DK
    return pl.pallas_call(
        gate_forward,
        grid=(2,),
        in_specs=[
            by_lead(HEADS, TOK, DK),
            by_lead(HEADS, TOK, DK),
            by_lead(HEADS, DK, DK),
            by_rows(TOK, inner),
            whole((1, DK)),
        ],
        out_specs=[by_rows(TOK, inner), by_rows(TOK, inner)],
        out_shape=[
            jax.ShapeDtypeStruct((2 * TOK, inner), f32),
            jax.ShapeDtypeStruct((2 * TOK, inner), bf16),
        ],
        compiler_params=params(),
        cost_estimate=cost(10**9, 3 * 10**6),
    )(p, z, state, og, gain)


def run_gate_backward(gg, heads_out, og, gain, p):
    inner = HEADS * DK
    return pl.pallas_call(
        gate_backward,
        grid=(2,),
        in_specs=[
            by_rows(TOK, inner),
            by_rows(TOK, inner),
            by_rows(TOK, inner),
            whole((1, DK)),
            by_lead(HEADS, TOK, DK),
        ],
        out_specs=[
            by_rows(TOK, inner),
            by_rows(TOK, inner),
            by_lead(16, DK // HEADS, DK),
            whole((8, DK)),
        ],
        out_shape=[
            jax.ShapeDtypeStruct((2 * TOK, inner), f32),
            jax.ShapeDtypeStruct((2 * TOK, inner), bf16),
            jax.ShapeDtypeStruct((SEQ, DK // HEADS, DK), bf16),
            jax.ShapeDtypeStruct((8, DK), f32),
        ],
        compiler_params=params(),
        cost_estimate=cost(10**9, 3 * 10**6),
    )(gg, heads_out, og, gain, p)


def run_chunk_backward(pre, scal, rates, taps, marks, docs, x, uw, state, adj, do):
    inner = HEADS * DK
    wide = 3 * inner
    return pl.pallas_call(
        chunk_backward,
        grid=(2,),
        in_specs=mixer_specs()
        + [
            by_lead(HEADS, TOK, DK),
            by_lead(HEADS, TOK, 2 * DK),
            by_lead(HEADS, DK, DK),
            by_lead(HEADS, DK, DK),
            by_rows(TOK, inner),
        ],
        out_specs=[
            by_rows(TOK, wide),
            by_rows(HALO, wide),
            by_rows(TOK, 128),
            whole((TAPS, wide)),
            whole((8, 128)),
        ],
        out_shape=[
            jax.ShapeDtypeStruct((2 * TOK, wide), f32),
            jax.ShapeDtypeStruct((2 * HALO, wide), bf16),
            jax.ShapeDtypeStruct((2 * TOK, 128), bf16),
            jax.ShapeDtypeStruct((TAPS, wide), f32),
            jax.ShapeDtypeStruct((8, 128), f32),
        ],
        scratch_shapes=[
            pltpu.VMEM((HALO + TOK, wide), f32),
            pltpu.VMEM((HALO + TOK, wide), f32),
        ],
        compiler_params=params(),
        cost_estimate=cost(10**10, 10**7),
    )(pre, pre, scal, rates, taps, marks, docs, x, uw, state, adj, do)


def passed_along(array, by):
    pairs = [(i, i + by) for i in range(SEQ) if 0 <= i + by < SEQ]
    return lax.ppermute(array, "seq", pairs)


STRIDE = {"x": (8, 4), "z": (2, 4), "y": (1, 2)}


def along(array, axis, by):
    stride, count = STRIDE[axis]
    pairs = []
    for i in range(SEQ):
        place = (i // stride) % count
        pairs.append((i, i + ((place + by) % count - place) * stride))
    return lax.ppermute(array, "seq", pairs)


def place_of(axis):
    stride, count = STRIDE[axis]
    return (lax.axis_index("seq") // stride) % count


def gather_pair(array):
    other = along(array, "y", 1)
    first = place_of("y") == 0
    return jnp.concatenate(
        [jnp.where(first, array, other), jnp.where(first, other, array)], axis=0
    )


def gather_four(array, axis, dim):
    half = array.shape[0] // 2
    left = along(array, axis, 1)
    right = along(array, axis, -1)
    far = jnp.concatenate(
        [along(left[:half], axis, 1), along(right[half:], axis, -1)], axis=0
    )
    place = place_of(axis)
    shape = list(array.shape)
    shape.insert(dim, 4)
    out = jnp.zeros(shape, array.dtype)
    for offset, block in ((0, array), (-1, left), (-2, far), (1, right)):
        out = lax.dynamic_update_index_in_dim(out, block, (place + offset) % 4, dim)
    return out


def gather_rows(left, right):
    left, right = gather_pair(left), gather_pair(right)
    left = gather_four(left, "x", 0)
    right = gather_four(right, "z", 0)
    left = gather_four(left, "z", 1)
    right = gather_four(right, "x", 0)
    return (
        left.reshape(-1, left.shape[-1]),
        right.reshape(-1, right.shape[-1]),
    )


def exchange(array, axis):
    return lax.all_to_all(array, axis, split_axis=0, concat_axis=0, tiled=True)


def head_scatter(partial_rows):
    rows = partial_rows.shape[0] // 4
    got = exchange(partial_rows.astype(bf16).reshape(4, rows, -1), "head")
    return jnp.sum(got.astype(f32), axis=0)


def head_gather(rows):
    got = exchange(jnp.broadcast_to(rows[None], (4,) + rows.shape), "head")
    return got.reshape(4 * rows.shape[0], -1)


def seq_scatter(partial_rows):
    rows = partial_rows.shape[0] // SEQ
    got = exchange(partial_rows.reshape(SEQ, rows, -1), "seq")
    return jnp.sum(got.astype(f32), axis=0)


def mm(a, b, dims="ij,jk->ik"):
    return jnp.einsum(dims, a, b, preferred_element_type=f32)


def row_scale(x):
    return lax.rsqrt(jnp.mean(x * x, axis=-1, keepdims=True) + norm_eps)


def norm_pull(x, scale, gain, grad):
    unit = x * scale
    scaled = grad * gain
    back = scale * (scaled - unit * jnp.mean(scaled * unit, axis=-1, keepdims=True))
    return back, jnp.sum(grad * unit, axis=0)


def doc_tables(doc_lengths):
    first = lax.axis_index("seq") * TOK - (TAPS - 1)
    ends = jnp.cumsum(doc_lengths, axis=1)
    places = first + jnp.arange(TOK + TAPS - 1, dtype=jnp.int32)
    counted = jnp.sum((places[None, :, None] >= ends[:, None, :]).astype(jnp.int32), axis=2)
    ext = jnp.where(places[None, :] >= 0, counted, -1)
    local = ext[:, TAPS - 1 :]
    columns = [(ext[:, o : o + TOK] == local) for o in range(TAPS - 1)]
    columns.append(local == ext[:, TAPS - 2 : TAPS - 1])
    columns.append(local == local[:, -1:])
    columns.append(local)
    columns += [jnp.zeros_like(local)] * 2
    marks = jnp.stack([c.astype(f32) for c in columns], axis=-1)
    return marks, local.astype(f32)[:, None, :]


def body(
    inputs, doc_lengths, norm_in, query_weight, key_weight, value_weight, outgate_weight,
    scalar_weight, conv_kernel, decay_rate, head_norm, output_weight, norm_ffn, gate_weight,
    up_weight, down_weight, grad_out,
):
    width = inputs.shape[2]
    inner = HEADS * DK
    hidden = gate_weight.shape[1]
    head_index = lax.axis_index("head")
    quarter = 2 * TOK // HEADS

    gains = jnp.stack([norm_in, norm_ffn] + [jnp.zeros_like(norm_in)] * 14)
    gains = exchange(jnp.broadcast_to(gains[None], (SEQ,) + gains.shape), "seq")
    gain_in = gains[:, 0].reshape(1, width).astype(f32)
    gain_ffn = gains[:, 1].reshape(1, width).astype(f32)

    misc = jnp.pad(scalar_weight.reshape(-1, 2 * HEADS), ((0, 0), (0, 128 - 2 * HEADS)))
    w_left, w_right = gather_rows(
        jnp.concatenate([query_weight, key_weight, misc], axis=1),
        jnp.concatenate([value_weight, outgate_weight], axis=1),
    )
    packed = jnp.concatenate(
        [gate_weight, up_weight, down_weight.T, output_weight.T], axis=1
    )
    w_late = lax.all_gather(packed, "seq", axis=0, tiled=True)
    w_gateup = w_late[:, : 2 * hidden]
    w_down_t = w_late[:, 2 * hidden : 3 * hidden]
    w_out_t = w_late[:, 3 * hidden :]

    marks, docs_row = doc_tables(doc_lengths)
    taps = jnp.transpose(conv_kernel.astype(f32), (1, 0, 2)).reshape(TAPS, 3 * inner)
    rates = jnp.zeros((1, 128), f32)
    rates = rates.at[0, HEADS : 2 * HEADS].set(decay_rate.astype(f32))
    gain_head = head_norm.astype(f32).reshape(1, DK)

    halo = passed_along(inputs[:, TOK - HALO :], 1)
    tokens = inputs.reshape(2 * TOK, width)
    all_rows = jnp.concatenate([tokens, halo.reshape(2 * HALO, width)], axis=0).astype(f32)
    normed_all = (all_rows * row_scale(all_rows) * gain_in).astype(bf16)
    normed_in = normed_all[: 2 * TOK]

    qk_misc = mm(normed_all, w_left)
    v_gate = mm(normed_all, w_right)
    pre = jnp.concatenate(
        [qk_misc[:, : 2 * inner].astype(bf16), v_gate[:, :inner].astype(bf16)], axis=1
    )
    scal = qk_misc[: 2 * TOK, 2 * inner :]
    out_gate = v_gate[: 2 * TOK, inner:]

    send, p, z, x, uw = run_chunk_forward(pre, scal, rates, taps, marks, docs_row)
    got = exchange(send, "seq")
    state = exchange(run_scan_forward(got), "seq").reshape(8, DK, DK)
    heads_out, gated_rows = run_gate_forward(p, z, state, out_gate, gain_head)

    mine = partial(lax.dynamic_slice_in_dim, start_index=head_index * quarter, slice_size=quarter)
    residual = mine(tokens).astype(f32) + head_scatter(mm(gated_rows, w_out_t, "ij,kj->ik"))
    scale_ffn = row_scale(residual)
    normed_ffn = head_gather((residual * scale_ffn * gain_ffn).astype(bf16))

    grad_rows = grad_out.reshape(2 * TOK, width)
    grad_act = mm(grad_rows, w_down_t)
    gate_up = mm(normed_ffn, w_gateup)
    gate, up = gate_up[:, :hidden], gate_up[:, hidden:]
    sig = sigmoid(gate)
    silu = gate * sig
    product = (silu * up).astype(bf16)
    gu_grad = jnp.concatenate(
        [
            (grad_act * up * sig * (1.0 + gate * (1.0 - sig))).astype(bf16),
            (grad_act * silu).astype(bf16),
        ],
        axis=1,
    )
    grad_normed = head_scatter(mm(gu_grad, w_gateup, "ij,kj->ik"))
    back, part_gain_ffn = norm_pull(residual, scale_ffn, gain_ffn, grad_normed)
    grad_residual = mine(grad_rows).astype(f32) + back
    grad_mixer = head_gather(grad_residual.astype(bf16))

    outputs = residual + head_scatter(mm(product, w_down_t, "ij,kj->ik"))
    outputs = head_gather(outputs.astype(bf16))

    grad_gated = mm(grad_mixer, w_out_t)
    do, gate_grad_mix, local, part_gain_head = run_gate_backward(
        grad_gated, heads_out, out_gate, gain_head, p
    )
    adj = exchange(run_scan_backward(got, exchange(local, "seq")), "seq").reshape(8, DK, DK)
    gpre, grim, gscal, gtaps, grate = run_chunk_backward(
        pre, scal, rates, taps, marks, docs_row, x, uw, state, adj, do
    )
    rim = passed_along(grim, -1).astype(f32).reshape(2, HALO, 3 * inner)
    gpre = gpre.reshape(2, TOK, 3 * inner).at[:, TOK - HALO :].add(rim)
    gpre = gpre.astype(bf16).reshape(2 * TOK, 3 * inner)

    input_part = mm(
        jnp.concatenate([gpre[:, : 2 * inner], gscal], axis=1), w_left, "ij,kj->ik"
    ) + mm(jnp.concatenate([gpre[:, 2 * inner :], gate_grad_mix], axis=1), w_right, "ij,kj->ik")
    grad_normed_in = head_scatter(input_part)
    own = mine(tokens).astype(f32)
    back_in, part_gain_in = norm_pull(own, row_scale(own), gain_in, grad_normed_in)
    grad_in = head_gather((grad_residual + back_in).astype(bf16)).astype(f32)

    grad_down = seq_scatter(mm(grad_rows, product, "ti,tj->ij").astype(bf16))
    grad_gateup = seq_scatter(mm(normed_ffn, gu_grad, "ti,tj->ij").astype(bf16))
    grad_out_w = seq_scatter(mm(grad_mixer, gated_rows, "ti,tj->ij").astype(bf16))
    grad_mix = seq_scatter(
        mm(
            normed_in, jnp.concatenate([gpre, gate_grad_mix, gscal], axis=1), "ti,tj->ij"
        ).astype(bf16)
    )

    small = jnp.concatenate([gtaps.reshape(12, inner), jnp.zeros((4, inner), f32)], axis=0)
    tail = jnp.concatenate([part_gain_head[0], grate[0], jnp.zeros((inner - 256,), f32)])
    small = jnp.broadcast_to(small.at[12].set(tail)[None], (SEQ, 16, inner))
    own_gains = jnp.pad(
        jnp.stack([part_gain_in.reshape(SEQ, -1), part_gain_ffn.reshape(SEQ, -1)], axis=1),
        ((0, 0), (0, 0), (0, inner - width // SEQ)),
    )
    small = small.at[:, 13:15].set(own_gains)
    small = jnp.sum(exchange(small, "seq"), axis=0)
    across = jnp.pad(small[12:15], ((0, 5), (0, 0)))
    across = jnp.sum(exchange(jnp.broadcast_to(across[None], (4, 8, inner)), "head"), axis=0)
    grad_conv = jnp.transpose(small[:12].reshape(TAPS, 3, inner), (1, 0, 2))
    rows = width // SEQ
    return (
        outputs.reshape(inputs.shape),
        grad_in.reshape(inputs.shape),
        across[1, :rows],
        grad_mix[:, :inner],
        grad_mix[:, inner : 2 * inner],
        grad_mix[:, 2 * inner : 3 * inner],
        grad_mix[:, 3 * inner : 4 * inner],
        grad_mix[:, 4 * inner : 4 * inner + 2 * HEADS].reshape(rows, 2, HEADS),
        grad_conv,
        small[12, DK + HEADS : DK + 2 * HEADS],
        across[0, :DK],
        grad_out_w.T,
        across[2, :rows],
        grad_gateup[:, :hidden],
        grad_gateup[:, hidden:],
        grad_down.T,
    )


def solution(mesh):
    weight = P("seq", "head")
    weight_t = P("head", "seq")
    tokens = P(None, "seq", None)
    scalars = P("seq", None, "head")
    taps = P(None, None, "head")
    return jax.shard_map(
        body,
        mesh=mesh,
        in_specs=(
            tokens, P(), P("seq"), weight, weight, weight, weight, scalars, taps, P("head"), P(),
            weight_t, P("seq"), weight, weight, weight_t, tokens,
        ),
        out_specs=(
            tokens, tokens, P("seq"), weight, weight, weight, weight, scalars, taps, P("head"),
            P(), weight_t, P("seq"), weight, weight, weight_t,
        ),
        check_vma=False,
    )
```

time: 4000 us -> 1010 us (0.25)
  waiting for transfers between devices: 2620 us -> 567 us
  matrix products: 415 us -> 60.4 us
  blocking collectives: 383 us -> 127 us
  starting transfers between devices: 264 us -> 111 us
  other arithmetic: 148 us -> 38.1 us
  local copies, waits for them, and re-layouts: 110 us -> 35 us
  Pallas kernels: 0 us -> 41.2 us
    reduce_scatter x8 -> x0, waiting for transfers between devices: 1380 us -> none  [the longest x1 193 us: reduce_ffn(): lax.psum_scatter(gate_grad_w.astype(jnp.bfloat16), 'seq', scatter_dimensi...]
    ppermute x64 -> x20, waiting for transfers between devices: 563 us -> 56 us  [the longest x18 56 us: along(): return lax.ppermute(array, 'seq', pairs)]
    all_to_all x0 -> x12, waiting for transfers between devices: none -> 464 us  [exchange(): return lax.all_to_all(array, axis, split_axis=0, concat_axis=0, tiled=True)]
    dot_general x276 -> x14, matrix products: 415 us -> 60.4 us  [mm(): return jnp.einsum(dims, a, b, preferred_element_type=f32)]
    all_gather x8 -> x1, waiting for transfers between devices: 288 us -> 46.5 us  [body(): w_late = lax.all_gather(packed, 'seq', axis=0, tiled=True)]
    ppermute x64 -> x20, starting transfers between devices: 262 us -> 30.9 us  [the longest x18 25 us: along(): return lax.ppermute(array, 'seq', pairs)]
    psum x4 -> x0, waiting for transfers between devices: 227 us -> none  [the longest x1 95.6 us: body(): lax.psum(jnp.einsum('stc,cd->std', gated_rows, w_output, preferred_elemen...]
    unnamed x2 -> x0, blocking collectives: 171 us -> none
  transfers between devices with their start and end apart: 85 -> 33, of which waited for: 80 -> 18; matrix products, arithmetic and copies ran while one was open for 8% -> 9% of each run, Pallas kernels for 0% -> 2%
where the time goes in v1:
time: 1010 us; the launch traced here: 994 us
  waiting for transfers between devices  567 us (56%)
  blocking collectives  127 us (13%)
  starting transfers between devices  111 us (11%)
  matrix products  60.4 us (6%)
  Pallas kernels  41.2 us (4%)
  other arithmetic  38.1 us (4%)
  local copies, waits for them, and re-layouts  35 us (3%)
  between operations  15.8 us (2%)
    all_to_all x12, waiting for transfers between devices, exchange(): return lax.all_to_all(array, axis, split_axis=0, concat_axis=0, tiled=True)  464 us
    all_to_all x7, blocking collectives, exchange(): return lax.all_to_all(array, axis, split_axis=0, concat_axis=0, tiled=True)  127 us
    all_to_all x12, starting transfers between devices, exchange(): return lax.all_to_all(array, axis, split_axis=0, concat_axis=0, tiled=True)  79.7 us
    dot_general x14, matrix products, mm(): return jnp.einsum(dims, a, b, preferred_element_type=f32)  60.4 us
    ppermute x18, waiting for transfers between devices, along(): return lax.ppermute(array, 'seq', pairs)  56 us
    all_gather x1, waiting for transfers between devices, body(): w_late = lax.all_gather(packed, 'seq', axis=0, tiled=True)  46.5 us
    ppermute x18, starting transfers between devices, along(): return lax.ppermute(array, 'seq', pairs)  25 us
  transfers between devices with their start and end apart: 33, of which 18 were waited for; matrix products, arithmetic and copies ran while one was open for 9% of the time, Pallas kernels for 2%

profile of v1, /device:TPU:1, one launch (start us, length us, event | category | flops | bytes accessed | tf_op | source)
XLA Modules:
  0.0 994.2 jit_solution(3990540490033023295)
XLA Ops:
  15.7 7.9 all-to-all-start
  23.6 4.6 collective-permute-start
  43.0 4.8 collective-permute-done.13
  61.5 39.9 %collective-permute-done.17 = bf16[4,128,1024]{2,1,0:T(8,128)(2,1)S(1)} collective-permute-done((bf16[4,128,1024]{2,1,0:T(8,128)(2,1)S(1)}, bf16[4,128,1024]{2,1,0:T(8,128)(2,1)S(1)}, u32[]{:S(2)}, u32[]{:S(2)}) %collective-permute-start.17) | collective-permute-done | bytes 1048608 | tf_op jit(solution)/shard_map/ppermute | solution.py:521
  107.4 5.5 collective-permute-done.18
  122.9 11.0 %shard_map.288 = (bf16[32,160,128]{2,1,0:T(8,128)(2,1)}, bf16[8,128,128]{2,1,0:T(8,128)(2,1)}, f32[8,128,128]{2,1,0:T(8,128)}, bf16[8,128,128]{2,1,0:T(8,128)(2,1)}, f32[8,128,256]{2,1,0:T(8,128)}) custom-call(bf16[288,1536]{1,0:T(8,128)(2,1)} %pad_maximum_fusion.4.pre_ref.rim_ref, bf16[288,1536]{1,0:T(8,128)(2,1)} %pad_maximum_fusion.4.pre_ref.rim_ref, ...), custom_call_target="tpu_custom_call" | custom-call | flops 10000000000 | bytes 6000000 | tf_op jit(solution)/shard_map/pallas_call | solution.py:377
  133.9 22.3 %all_to_all.95.got_ref = bf16[32,160,128]{2,1,0:T(8,128)(2,1)} all-to-all(bf16[32,160,128]{2,1,0:T(8,128)(2,1)} %get-tuple-element.82), channel_id=1, replica_groups=mesh['seq'=32,'head'=4] {'seq'}, dimensions={0} | all-to-all | bytes 2621440 | tf_op jit(solution)/shard_map/all_to_all | solution.py:566
  156.2 5.9 shard_map.289
  167.6 9.3 all-to-all-done.2
  180.0 46.5 %all-gather.2.cloned.1.call-done = bf16[2048,4736]{1,0:T(8,128)(2,1)} async-done(((bf16[64,4736]{1,0:T(8,128)(2,1)}), bf16[2048,4736]{1,0:T(8,128)(2,1)}) %all-gather.2.cloned.1.call-update) | async-done | bytes 19398672 | tf_op jit(solution)/shard_map/all_gather | solution.py:641
  229.9 4.6 all-to-all-start.3
  234.5 13.5 %all-to-all-done.3 = bf16[4,64,2048]{2,1,0:T(8,128)(2,1)S(1)} async-done(((bf16[4,64,2048]{2,1,0:T(8,128)(2,1)}), bf16[4,64,2048]{2,1,0:T(8,128)(2,1)S(1)}, u32[]{:S(2)}, u32[]{:S(2)}) %all-to-all-start.3) | async-done | bytes 1048608 | tf_op jit(solution)/shard_map/all_to_all | solution.py:566
  248.7 17.1 %all_to_all.96 = bf16[4,64,2048]{2,1,0:T(8,128)(2,1)S(1)} all-to-all(bf16[4,64,2048]{2,1,0:T(8,128)(2,1)S(1)} %broadcast_in_dim.163), channel_id=1, replica_groups=mesh['seq'=32,'head'=4] {'head'}, dimensions={0} | all-to-all | bytes 2097152 | tf_op jit(solution)/shard_map/all_to_all | solution.py:566
  265.8 6.7 fusion.2
  272.5 4.7 multiply_convert_fusion.1
  277.3 8.2 fusion.13
  285.5 16.9 %all_to_all.97 = bf16[4,64,2048]{2,1,0:T(8,128)(2,1)S(1)} all-to-all(bf16[4,64,2048]{2,1,0:T(8,128)(2,1)S(1)} %bitcast.166), channel_id=1, replica_groups=mesh['seq'=32,'head'=4] {'head'}, dimensions={0} | all-to-all | bytes 2097152 | tf_op jit(solution)/shard_map/all_to_all | solution.py:566
  303.2 16.9 %all_to_all.98 = bf16[4,64,2048]{2,1,0:T(8,128)(2,1)S(1)} all-to-all(bf16[4,64,2048]{2,1,0:T(8,128)(2,1)S(1)} %broadcast_in_dim.165), channel_id=1, replica_groups=mesh['seq'=32,'head'=4] {'head'}, dimensions={0} | all-to-all | bytes 2097152 | tf_op jit(solution)/shard_map/all_to_all | solution.py:566
  326.1 14.9 %all_to_all.99.local_ref = bf16[32,32,128]{2,1,0:T(8,128)(2,1)} all-to-all(bf16[32,32,128]{2,1,0:T(8,128)(2,1)} %get-tuple-element.87), channel_id=1, replica_groups=mesh['seq'=32,'head'=4] {'seq'}, dimensions={0} | all-to-all | bytes 524288 | tf_op jit(solution)/shard_map/all_to_all | solution.py:566
  341.0 5.9 shard_map.292
  346.9 14.3 %all_to_all.100 = bf16[32,32,128]{2,1,0:T(8,128)(2,1)} all-to-all(bf16[32,32,128]{2,1,0:T(8,128)(2,1)} %shard_map.292), channel_id=1, replica_groups=mesh['seq'=32,'head'=4] {'seq'}, dimensions={0} | all-to-all | bytes 524288 | tf_op jit(solution)/shard_map/all_to_all | solution.py:566
  361.2 13.0 %shard_map.293 = (f32[256,1536]{1,0:T(8,128)}, bf16[32,1536]{1,0:T(8,128)(2,1)}, bf16[256,128]{1,0:T(8,128)(2,1)}, f32[4,1536]{1,0:T(4,128)}, f32[8,128]{1,0:T(8,128)}) custom-call(bf16[288,1536]{1,0:T(8,128)(2,1)} %pad_maximum_fusion.4.pre_ref.rim_ref, bf16[288,1536]{1,0:T(8,128)(2,1)} %pad_maximum_fusion.4.pre_ref.rim_ref, f32[256,128]{1,0:T(8,128)} %slice.273.scal_ref, ...), custom_call_target="tpu_custom_call" | custom-call | flops 10000000000 | bytes 10000000 | tf_op jit(solution)/shard_map/pallas_call | solution.py:473
  375.5 5.4 fusion.16
  380.9 7.9 all-to-all-start.5
  394.4 4.9 fusion.12
  402.5 5.1 all-to-all-start.11
  409.7 11.6 %all-to-all-done.11 = bf16[4,64,2048]{2,1,0:T(8,128)(2,1)} async-done(((bf16[4,64,2048]{2,1,0:T(8,128)(2,1)}), bf16[4,64,2048]{2,1,0:T(8,128)(2,1)}, u32[]{:S(2)}, u32[]{:S(2)}) %all-to-all-start.11) | async-done | bytes 1048608 | tf_op jit(solution)/shard_map/all_to_all | solution.py:566
  421.3 7.3 all-to-all-start.16
  433.7 24.0 %all-to-all-done.16 = bf16[32,64,512]{2,1,0:T(8,128)(2,1)} async-done(((bf16[32,64,512]{2,1,0:T(8,128)(2,1)}), bf16[32,64,512]{2,1,0:T(8,128)(2,1)}, u32[]{:S(2)}, u32[]{:S(2)}) %all-to-all-start.16) | async-done | bytes 2097184 | tf_op jit(solution)/shard_map/all_to_all | solution.py:566
  459.8 5.2 all-to-all-start.6
  467.9 10.7 %all-to-all-done.6 = bf16[4,64,2048]{2,1,0:T(8,128)(2,1)S(1)} async-done(((bf16[4,64,2048]{2,1,0:T(8,128)(2,1)}), bf16[4,64,2048]{2,1,0:T(8,128)(2,1)S(1)}, u32[]{:S(2)}, u32[]{:S(2)}) %all-to-all-start.6) | async-done | bytes 1048608 | tf_op jit(solution)/shard_map/all_to_all | solution.py:566
  478.6 24.2 %all_to_all.101 = f32[32,16,512]{2,1,0:T(8,128)} all-to-all(f32[32,16,512]{2,1,0:T(8,128)S(1)} %scatter.14), channel_id=1, replica_groups=mesh['seq'=32,'head'=4] {'seq'}, dimensions={0} | all-to-all | bytes 2097152 | tf_op jit(solution)/shard_map/all_to_all | solution.py:566
  503.9 6.1 all-to-all-start.12
  511.3 12.3 %all-to-all-done.12 = bf16[4,64,2048]{2,1,0:T(8,128)(2,1)S(1)} async-done(((bf16[4,64,2048]{2,1,0:T(8,128)(2,1)}), bf16[4,64,2048]{2,1,0:T(8,128)(2,1)S(1)}, u32[]{:S(2)}, u32[]{:S(2)}) %all-to-all-start.12) | async-done | bytes 1048608 | tf_op jit(solution)/shard_map/all_to_all | solution.py:566
  524.2 4.1 all-to-all-start.14
  528.4 5.4 fusion.4
  533.8 8.4 copy.98
  542.2 5.0 all-to-all-start.18
  547.3 4.9 convolution_convert_fusion.1
  552.2 82.5 %all-to-all-done.18 = bf16[32,64,1408]{2,1,0:T(8,128)(2,1)} async-done(((bf16[32,64,1408]{2,1,0:T(8,128)(2,1)}), bf16[32,64,1408]{2,1,0:T(8,128)(2,1)}, u32[]{:S(2)}, u32[]{:S(2)}) %all-to-all-start.18) | async-done | bytes 5767200 | tf_op jit(solution)/shard_map/all_to_all | solution.py:566
  634.7 7.3 all-to-all-start.15
  642.1 7.2 convolution_convert_fusion
  649.2 128.2 %all-to-all-done.15 = bf16[32,64,2176]{2,1,0:T(8,128)(2,1)} async-done(((bf16[32,64,2176]{2,1,0:T(8,128)(2,1)}), bf16[32,64,2176]{2,1,0:T(8,128)(2,1)}, u32[]{:S(2)}, u32[]{:S(2)}) %all-to-all-start.15) | async-done | bytes 8912928 | tf_op jit(solution)/shard_map/all_to_all | solution.py:566
  777.4 15.1 %all-to-all-start.17 = ((bf16[32,64,2816]{2,1,0:T(8,128)(2,1)}), bf16[32,64,2816]{2,1,0:T(8,128)(2,1)}, u32[]{:S(2)}, u32[]{:S(2)}) async-start(bf16[32,64,2816]{2,1,0:T(8,128)(2,1)} %bitcast.137), calls=%async_computation.17 | async-start | bytes 23068672 | tf_op jit(solution)/shard_map/all_to_all | solution.py:566
  798.9 4.2 convert_reduce_fusion.2
  803.1 5.0 convert_reduce_fusion.1
  809.5 168.8 %all-to-all-done.17 = bf16[32,64,2816]{2,1,0:T(8,128)(2,1)} async-done(((bf16[32,64,2816]{2,1,0:T(8,128)(2,1)}), bf16[32,64,2816]{2,1,0:T(8,128)(2,1)}, u32[]{:S(2)}, u32[]{:S(2)}) %all-to-all-start.17) | async-done | bytes 11534368 | tf_op jit(solution)/shard_map/all_to_all | solution.py:566
  978.3 6.2 convert_reduce_fusion
  (249 shorter events, 107.1 us)
Async XLA Ops:
  7.2 16.4 %copy-start = (bf16[2,128,2048]{2,1,0:T(8,128)(2,1)S(1)}, bf16[2,128,2048]{2,1,0:T(8,128)(2,1)}, u32[]{:S(2)}) copy-start(bf16[2,128,2048]{2,1,0:T(8,128)(2,1)} %param.25) | copy-start | bytes 3145732
  7.2 21.1 %copy-start.27 = (bf16[64,2,4]{0,2,1:T(4,128)(2,1)S(1)}, bf16[64,2,4]{0,2,1:T(4,128)(2,1)}, u32[]{:S(2)}) copy-start(bf16[64,2,4]{0,2,1:T(4,128)(2,1)} %param.32) | copy-start | bytes 3076
  7.2 21.2 %copy-start.22 = (bf16[64,512]{1,0:T(8,128)(2,1)S(1)}, bf16[64,512]{1,0:T(8,128)(2,1)}, u32[]{:S(2)}) copy-start(bf16[64,512]{1,0:T(8,128)(2,1)} %param.29) | copy-start | bytes 196612
  7.2 21.2 %copy-start.23 = (bf16[64,512]{1,0:T(8,128)(2,1)S(1)}, bf16[64,512]{1,0:T(8,128)(2,1)}, u32[]{:S(2)}) copy-start(bf16[64,512]{1,0:T(8,128)(2,1)} %param.28) | copy-start | bytes 196612
  7.2 22.5 %copy-start.28 = (s32[2,8]{1,0:T(2,128)S(1)}, s32[2,8]{1,0:T(2,128)}, u32[]{:S(2)}) copy-start(s32[2,8]{1,0:T(2,128)} %param.26) | copy-start | bytes 196
  7.3 23.6 %copy-start.31 = (bf16[4]{0:T(256)(128)(2,1)S(1)}, bf16[4]{0:T(256)(128)(2,1)}, u32[]{:S(2)}) copy-start(bf16[4]{0:T(256)(128)(2,1)} %param.34) | copy-start | bytes 28
  7.3 25.7 %copy-start.26 = (bf16[3,4,512]{2,1,0:T(4,128)(2,1)S(1)}, bf16[3,4,512]{2,1,0:T(4,128)(2,1)}, u32[]{:S(2)}) copy-start(bf16[3,4,512]{2,1,0:T(4,128)(2,1)} %param.33) | copy-start | bytes 36868
  7.3 219.2 %all-gather.2.cloned.1.call-start = ((), (), s32[]{:S(2)}) async-start(), calls=%async_computation.19 | async-start | bytes 20004864 | tf_op jit(solution)/shard_map/all_gather | solution.py:641
  11.1 25.6 %collective-permute-start.10 = (bf16[64,1024]{1,0:T(8,128)(2,1)S(1)}, bf16[64,1024]{1,0:T(8,128)(2,1)S(1)}, u32[]{:S(2)}, u32[]{:S(2)}) collective-permute-start(bf16[64,1024]{1,0:T(8,128)(2,1)S(1)} %constant_dynamic-update-slice_fusion), channel_id=1, source_target_pairs={{0,4},{4,0},{8,12},{12,8},{16,20},{20,16},{24,28},{28,24},{32,36},... | collective-permute-start | bytes 393224 | tf_op jit(solution)/shard_map/ppermute | solution.py:521
  15.7 20.6 %all-to-all-start = ((bf16[32,2,512]{2,1,0:T(2,128)(2,1)}), bf16[32,2,512]{2,1,0:T(2,128)(2,1)S(1)}, u32[]{:S(2)}, u32[]{:S(2)}) async-start(bf16[32,2,512]{2,1,0:T(2,128)(2,1)} %reshape.367), calls=%async_computation | async-start | bytes 131072 | tf_op jit(solution)/shard_map/all_to_all | solution.py:566
  23.6 15.9 %collective-permute-start = (bf16[2,16,2048]{2,1,0:T(8,128)(2,1)S(1)}, bf16[2,16,2048]{2,1,0:T(8,128)(2,1)S(1)}, u32[]{:S(2)}, u32[]{:S(2)}) collective-permute-start(bf16[2,16,2048]{2,1,0:T(8,128)(2,1)S(1)} %slice.216), channel_id=1, source_target_pairs={{0,4},{4,8},{8,12},{12,16},{16,20},{20,24},{24,28},{28,32},{32,36}... | collective-permute-start | bytes 393224 | tf_op jit(solution)/shard_map/ppermute | solution.py:509
  28.4 11.6 %collective-permute-start.1 = (bf16[64,1152]{1,0:T(8,128)(2,1)S(1)}, bf16[64,1152]{1,0:T(8,128)(2,1)S(1)}, u32[]{:S(2)}, u32[]{:S(2)}) collective-permute-start(bf16[64,1152]{1,0:T(8,128)(2,1)S(1)} %fusion.55), channel_id=1, source_target_pairs={{0,4},{4,0},{8,12},{12,8},{16,20},{20,16},{24,28},{28,24},{32,36},... | collective-permute-start | bytes 442376 | tf_op jit(solution)/shard_map/ppermute | solution.py:521
  36.8 11.7 %collective-permute-start.11 = (bf16[128,1024]{1,0:T(8,128)(2,1)S(1)}, bf16[128,1024]{1,0:T(8,128)(2,1)S(1)}, u32[]{:S(2)}, u32[]{:S(2)}) collective-permute-start(bf16[128,1024]{1,0:T(8,128)(2,1)S(1)} %pad_maximum_fusion.7), channel_id=1, source_target_pairs={{0,8},{4,12},{8,16},{12,20},{16,24},{20,28},{24,0},{28,4},{32,40},... | collective-permute-start | bytes 786440 | tf_op jit(solution)/shard_map/ppermute | solution.py:521
  38.0 9.8 collective-permute-start.13
  40.1 11.2 %collective-permute-start.2 = (bf16[128,1152]{1,0:T(8,128)(2,1)S(1)}, bf16[128,1152]{1,0:T(8,128)(2,1)S(1)}, u32[]{:S(2)}, u32[]{:S(2)}) collective-permute-start(bf16[128,1152]{1,0:T(8,128)(2,1)S(1)} %pad_maximum_fusion.6), channel_id=1, source_target_pairs={{0,32},{4,36},{8,40},{12,44},{16,48},{20,52},{24,56},{28,60},{32,6... | collective-permute-start | bytes 884744 | tf_op jit(solution)/shard_map/ppermute | solution.py:521
  41.4 8.1 collective-permute-start.4
  47.8 3.9 collective-permute-start.14
  48.4 5.1 collective-permute-start.12
  49.5 6.9 collective-permute-start.5
  51.3 5.5 collective-permute-start.3
  53.6 51.4 %collective-permute-start.15 = (bf16[4,128,1024]{2,1,0:T(8,128)(2,1)S(1)}, bf16[4,128,1024]{2,1,0:T(8,128)(2,1)S(1)}, u32[]{:S(2)}, u32[]{:S(2)}) collective-permute-start(bf16[4,128,1024]{2,1,0:T(8,128)(2,1)S(1)} %bitcast_dynamic-update-slice_fusion.9), channel_id=1, source_target_pairs={{0,32},{4,36},{8,40},{12,44},{16,48},{20,52},{24,56},{28,60},{32,6... | collective-permute-start | bytes 3145736 | tf_op jit(solution)/shard_map/ppermute | solution.py:521
  54.2 47.1 %collective-permute-start.17 = (bf16[4,128,1024]{2,1,0:T(8,128)(2,1)S(1)}, bf16[4,128,1024]{2,1,0:T(8,128)(2,1)S(1)}, u32[]{:S(2)}, u32[]{:S(2)}) collective-permute-start(bf16[4,128,1024]{2,1,0:T(8,128)(2,1)S(1)} %bitcast_dynamic-update-slice_fusion.9), channel_id=1, source_target_pairs={{0,96},{4,100},{8,104},{12,108},{16,112},{20,116},{24,120},{28,124... | collective-permute-start | bytes 3145736 | tf_op jit(solution)/shard_map/ppermute | solution.py:521
  56.9 48.5 %collective-permute-start.6 = (bf16[4,128,1152]{2,1,0:T(8,128)(2,1)S(1)}, bf16[4,128,1152]{2,1,0:T(8,128)(2,1)S(1)}, u32[]{:S(2)}, u32[]{:S(2)}) collective-permute-start(bf16[4,128,1152]{2,1,0:T(8,128)(2,1)S(1)} %bitcast_dynamic-update-slice_fusion.6), channel_id=1, source_target_pairs={{0,8},{4,12},{8,16},{12,20},{16,24},{20,28},{24,0},{28,4},{32,40},... | collective-permute-start | bytes 3538952 | tf_op jit(solution)/shard_map/ppermute | solution.py:521
  58.2 47.1 %collective-permute-start.8 = (bf16[4,128,1152]{2,1,0:T(8,128)(2,1)S(1)}, bf16[4,128,1152]{2,1,0:T(8,128)(2,1)S(1)}, u32[]{:S(2)}, u32[]{:S(2)}) collective-permute-start(bf16[4,128,1152]{2,1,0:T(8,128)(2,1)S(1)} %bitcast_dynamic-update-slice_fusion.6), channel_id=1, source_target_pairs={{0,24},{4,28},{8,0},{12,4},{16,8},{20,12},{24,16},{28,20},{32,56},... | collective-permute-start | bytes 3538952 | tf_op jit(solution)/shard_map/ppermute | solution.py:521
  60.0 59.0 %copy-start.5 = (bf16[288,2048]{1,0:T(8,128)(2,1)}, bf16[288,2048]{1,0:T(8,128)(2,1)S(1)}, u32[]{:S(2)}) copy-start(bf16[288,2048]{1,0:T(8,128)(2,1)S(1)} %fusion.21) | copy-start | bytes 3538948
  101.4 11.4 %collective-permute-start.18 = (bf16[2,128,1024]{2,1,0:T(8,128)(2,1)S(1)}, bf16[2,128,1024]{2,1,0:T(8,128)(2,1)S(1)}, u32[]{:S(2)}, u32[]{:S(2)}) collective-permute-start(bf16[2,128,1024]{2,1,0:T(8,128)(2,1)S(1)} %slice.271), channel_id=1, source_target_pairs={{0,96},{4,100},{8,104},{12,108},{16,112},{20,116},{24,120},{28,124... | collective-permute-start | bytes 1572872 | tf_op jit(solution)/shard_map/ppermute | solution.py:521
  105.0 11.0 %collective-permute-start.16 = (bf16[2,128,1024]{2,1,0:T(8,128)(2,1)S(1)}, bf16[2,128,1024]{2,1,0:T(8,128)(2,1)S(1)}, u32[]{:S(2)}, u32[]{:S(2)}) collective-permute-start(bf16[2,128,1024]{2,1,0:T(8,128)(2,1)S(1)} %slice.270), channel_id=1, source_target_pairs={{0,32},{4,36},{8,40},{12,44},{16,48},{20,52},{24,56},{28,60},{32,6... | collective-permute-start | bytes 1572872 | tf_op jit(solution)/shard_map/ppermute | solution.py:521
  105.3 13.3 %collective-permute-start.9 = (bf16[2,128,1152]{2,1,0:T(8,128)(2,1)S(1)}, bf16[2,128,1152]{2,1,0:T(8,128)(2,1)S(1)}, u32[]{:S(2)}, u32[]{:S(2)}) collective-permute-start(bf16[2,128,1152]{2,1,0:T(8,128)(2,1)S(1)} %slice.266), channel_id=1, source_target_pairs={{0,24},{4,28},{8,0},{12,4},{16,8},{20,12},{24,16},{28,20},{32,56},... | collective-permute-start | bytes 1769480 | tf_op jit(solution)/shard_map/ppermute | solution.py:521
  105.5 13.2 %collective-permute-start.7 = (bf16[2,128,1152]{2,1,0:T(8,128)(2,1)S(1)}, bf16[2,128,1152]{2,1,0:T(8,128)(2,1)S(1)}, u32[]{:S(2)}, u32[]{:S(2)}) collective-permute-start(bf16[2,128,1152]{2,1,0:T(8,128)(2,1)S(1)} %slice.265), channel_id=1, source_target_pairs={{0,8},{4,12},{8,16},{12,20},{16,24},{20,28},{24,0},{28,4},{32,40},... | collective-permute-start | bytes 1769480 | tf_op jit(solution)/shard_map/ppermute | solution.py:521
  156.2 9.9 %copy-start.32 = (bf16[128]{0:T(256)(128)(2,1)S(1)}, bf16[128]{0:T(256)(128)(2,1)}, u32[]{:S(2)}) copy-start(bf16[128]{0:T(256)(128)(2,1)} %param.35) | copy-start | bytes 772
  162.1 14.7 %all-to-all-start.2 = ((bf16[32,32,128]{2,1,0:T(8,128)(2,1)}), bf16[32,32,128]{2,1,0:T(8,128)(2,1)S(1)}, u32[]{:S(2)}, u32[]{:S(2)}) async-start(bf16[32,32,128]{2,1,0:T(8,128)(2,1)} %shard_map.289), calls=%async_computation.2 | async-start | bytes 524288 | tf_op jit(solution)/shard_map/all_to_all | solution.py:566
  229.9 18.2 %all-to-all-start.3 = ((bf16[4,64,2048]{2,1,0:T(8,128)(2,1)}), bf16[4,64,2048]{2,1,0:T(8,128)(2,1)S(1)}, u32[]{:S(2)}, u32[]{:S(2)}) async-start(bf16[4,64,2048]{2,1,0:T(8,128)(2,1)} %bitcast.164), calls=%async_computation.3 | async-start | bytes 2097152 | tf_op jit(solution)/shard_map/all_to_all | solution.py:566
  277.3 98.2 %copy-start.13 = (bf16[256,1408]{1,0:T(8,128)(2,1)}, bf16[256,1408]{1,0:T(8,128)(2,1)S(1)}, u32[]{:S(2)}) copy-start(bf16[256,1408]{1,0:T(8,128)(2,1)S(1)} %get-tuple-element.172) | copy-start | bytes 2162692
  374.2 14.7 %collective-permute-start.19 = (bf16[32,1536]{1,0:T(8,128)(2,1)}, bf16[32,1536]{1,0:T(8,128)(2,1)S(1)}, u32[]{:S(2)}, u32[]{:S(2)}) collective-permute-start(bf16[32,1536]{1,0:T(8,128)(2,1)} %get-tuple-element.90), channel_id=1, source_target_pairs={{4,0},{8,4},{12,8},{16,12},{20,16},{24,20},{28,24},{32,28},{36,32}... | collective-permute-start | bytes 294920 | tf_op jit(solution)/shard_map/ppermute | solution.py:509
  380.9 12.2 %copy-start.18 = (bf16[256,512]{1,0:T(8,128)(2,1)S(1)}, bf16[256,512]{1,0:T(8,128)(2,1)}, u32[]{:S(2)}) copy-start(bf16[256,512]{1,0:T(8,128)(2,1)} %get-tuple-element.92) | copy-start | bytes 786436
  380.9 21.6 %all-to-all-start.5 = ((bf16[4,64,2048]{2,1,0:T(8,128)(2,1)}), bf16[4,64,2048]{2,1,0:T(8,128)(2,1)}, u32[]{:S(2)}, u32[]{:S(2)}) async-start(bf16[4,64,2048]{2,1,0:T(8,128)(2,1)} %bitcast.163), calls=%async_computation.5 | async-start | bytes 2097152 | tf_op jit(solution)/shard_map/all_to_all | solution.py:566
  399.3 8.3 copy-start.20
  402.5 18.8 %all-to-all-start.11 = ((bf16[4,64,2048]{2,1,0:T(8,128)(2,1)}), bf16[4,64,2048]{2,1,0:T(8,128)(2,1)}, u32[]{:S(2)}, u32[]{:S(2)}) async-start(bf16[4,64,2048]{2,1,0:T(8,128)(2,1)} %bitcast.165), calls=%async_computation.11 | async-start | bytes 2097152 | tf_op jit(solution)/shard_map/all_to_all | solution.py:566
  421.3 36.5 %all-to-all-start.16 = ((bf16[32,64,512]{2,1,0:T(8,128)(2,1)}), bf16[32,64,512]{2,1,0:T(8,128)(2,1)}, u32[]{:S(2)}, u32[]{:S(2)}) async-start(bf16[32,64,512]{2,1,0:T(8,128)(2,1)} %bitcast.66), calls=%async_computation.16 | async-start | bytes 4194304 | tf_op jit(solution)/shard_map/all_to_all | solution.py:566
  433.7 32.0 %copy-start.25 = (f32[4,1536]{1,0:T(4,128)S(1)}, f32[4,1536]{1,0:T(4,128)}, u32[]{:S(2)}) copy-start(f32[4,1536]{1,0:T(4,128)} %get-tuple-element.93) | copy-start | bytes 73732
  459.8 18.8 %all-to-all-start.6 = ((bf16[4,64,2048]{2,1,0:T(8,128)(2,1)}), bf16[4,64,2048]{2,1,0:T(8,128)(2,1)S(1)}, u32[]{:S(2)}, u32[]{:S(2)}) async-start(bf16[4,64,2048]{2,1,0:T(8,128)(2,1)} %broadcast_in_dim.164), calls=%async_computation.6 | async-start | bytes 2097152 | tf_op jit(solution)/shard_map/all_to_all | solution.py:566
  478.6 25.3 %copy-start.10 = (bf16[4,64,2048]{2,1,0:T(8,128)(2,1)}, bf16[4,64,2048]{2,1,0:T(8,128)(2,1)S(1)}, u32[]{:S(2)}) copy-start(bf16[4,64,2048]{2,1,0:T(8,128)(2,1)S(1)} %all-to-all-done.6) | copy-start | bytes 3145732
  502.8 25.6 %copy-start.14 = (bf16[256,1408]{1,0:T(8,128)(2,1)S(1)}, bf16[256,1408]{1,0:T(8,128)(2,1)}, u32[]{:S(2)}) copy-start(bf16[256,1408]{1,0:T(8,128)(2,1)} %copy-done.13) | copy-start | bytes 2162692
  503.9 19.7 %all-to-all-start.12 = ((bf16[4,64,2048]{2,1,0:T(8,128)(2,1)}), bf16[4,64,2048]{2,1,0:T(8,128)(2,1)S(1)}, u32[]{:S(2)}, u32[]{:S(2)}) async-start(bf16[4,64,2048]{2,1,0:T(8,128)(2,1)} %broadcast_in_dim.166), calls=%async_computation.12 | async-start | bytes 2097152 | tf_op jit(solution)/shard_map/all_to_all | solution.py:566
  524.2 17.9 %all-to-all-start.14 = ((f32[4,8,512]{2,1,0:T(8,128)}), f32[4,8,512]{2,1,0:T(8,128)S(1)}, u32[]{:S(2)}, u32[]{:S(2)}) async-start(f32[4,8,512]{2,1,0:T(8,128)} %broadcast_in_dim.170), calls=%async_computation.14 | async-start | bytes 131072 | tf_op jit(solution)/shard_map/all_to_all | solution.py:566
  542.2 92.5 %all-to-all-start.18 = ((bf16[32,64,1408]{2,1,0:T(8,128)(2,1)}), bf16[32,64,1408]{2,1,0:T(8,128)(2,1)}, u32[]{:S(2)}, u32[]{:S(2)}) async-start(bf16[32,64,1408]{2,1,0:T(8,128)(2,1)} %bitcast.139), calls=%async_computation.18 | async-start | bytes 11534336 | tf_op jit(solution)/shard_map/all_to_all | solution.py:566
  634.7 142.7 %all-to-all-start.15 = ((bf16[32,64,2176]{2,1,0:T(8,128)(2,1)}), bf16[32,64,2176]{2,1,0:T(8,128)(2,1)}, u32[]{:S(2)}, u32[]{:S(2)}) async-start(bf16[32,64,2176]{2,1,0:T(8,128)(2,1)} %bitcast.138), calls=%async_computation.15 | async-start | bytes 17825792 | tf_op jit(solution)/shard_map/all_to_all | solution.py:566
  777.4 200.9 %all-to-all-start.17 = ((bf16[32,64,2816]{2,1,0:T(8,128)(2,1)}), bf16[32,64,2816]{2,1,0:T(8,128)(2,1)}, u32[]{:S(2)}, u32[]{:S(2)}) async-start(bf16[32,64,2816]{2,1,0:T(8,128)(2,1)} %bitcast.137), calls=%async_computation.17 | async-start | bytes 23068672 | tf_op jit(solution)/shard_map/all_to_all | solution.py:566
  (19 other events, 92.9 us)
Sparse Core Ops, SparseCore 0:
  11.2 215.2 all-gather.1

commit v2 on v1

v2 whole, which is shorter than its diff:
```python
from functools import partial

import jax
import jax.numpy as jnp
from jax import lax
from jax.experimental import pallas as pl
from jax.experimental.pallas import tpu as pltpu
from jax.sharding import Mesh
from jax.sharding import PartitionSpec as P

f32 = jnp.float32
bf16 = jnp.bfloat16
norm_eps = 1e-06
head_eps = 1e-05
SEQ = 32
HEADS = 4
DK = 128
TOK = 128
TAPS = 4
HALO = 16
VMEM = 56 * 1024 * 1024

NN = (((1,), (0,)), ((), ()))
NT = (((1,), (1,)), ((), ()))
TN = (((0,), (0,)), ((), ()))


def dot1(a, b, dims=NN):
    return lax.dot_general(a.astype(bf16), b.astype(bf16), dims, preferred_element_type=f32)


def split(a):
    high = a.astype(bf16)
    return high, (a - high.astype(f32)).astype(bf16)


def dot3(a, b, dims=NN):
    ah, al = split(a)
    bh, bl = split(b)
    return dot1(ah, bh, dims) + (dot1(ah, bl, dims) + dot1(al, bh, dims))


def dot2(exact, b, dims=NN):
    high = b.astype(bf16)
    rest = b - high.astype(f32)
    mid = rest.astype(bf16)
    low = (rest - mid.astype(f32)).astype(bf16)
    return dot1(exact, high, dims) + (dot1(exact, mid, dims) + dot1(exact, low, dims))


def sigmoid(x):
    return 1.0 / (1.0 + jnp.exp(-x))


def softplus(x):
    return jnp.maximum(x, 0.0) + jnp.log1p(jnp.exp(-jnp.abs(x)))


def iotas():
    rows = lax.broadcasted_iota(jnp.int32, (TOK, TOK), 0)
    cols = lax.broadcasted_iota(jnp.int32, (TOK, TOK), 1)
    return rows, cols


def unit_inverses(stricts):
    rows, cols = iotas()
    eye = (rows == cols).astype(f32)
    apart = jnp.bitwise_xor(rows, cols)
    results = []
    first = (apart == 1) & (rows > cols)
    results = [eye - jnp.where(first, a, 0.0) for a in stricts]
    size = 2
    while size < TOK:
        corner = (apart >= size) & (apart < 2 * size) & (rows > cols)
        parts = [dot3(jnp.where(corner, a, 0.0), x) for a, x in zip(stricts, results)]
        results = [x - dot3(x, c) for x, c in zip(results, parts)]
        size *= 2
    return results


def decays(scal, rates, marks, docs_row):
    rows, cols = iotas()
    strength = sigmoid(scal)
    log_decay = -rates * softplus(scal)
    lower = (rows >= cols).astype(bf16)
    total = dot2(lower, log_decay)
    total_t = jnp.transpose(total)
    same = marks[:, 5:6] == docs_row
    causal = same & (rows >= cols)
    return strength, total, total_t, causal, rows > cols


def conv_parts(ext_ref, weights, marks, lane):
    out = None
    for tap in range(TAPS):
        piece = ext_ref[pl.ds(HALO - TAPS + 1 + tap, TOK), pl.ds(lane, DK)]
        if tap < TAPS - 1:
            piece = piece * marks[:, tap : tap + 1]
        piece = piece * weights[tap : tap + 1, lane : lane + DK]
        out = piece if out is None else out + piece
    return out


def unit_scale(x):
    return lax.rsqrt(jnp.sum(x * x, axis=-1, keepdims=True) + norm_eps)


def chunk_forward(
    pre_ref, rim_ref, scal_ref, rate_ref, taps_ref, marks_ref, docs_ref,
    send_ref, p_ref, z_ref, x_ref, uw_ref, ext_ref,
):
    inner = HEADS * DK
    ext_ref[0:HALO, :] = rim_ref[...].astype(f32)
    ext_ref[HALO:, :] = pre_ref[...].astype(f32)
    marks = marks_ref[0]
    weights = taps_ref[...]
    strength, total, total_t, causal, below = decays(
        scal_ref[...], rate_ref[...], marks, docs_ref[0]
    )
    rows, cols = iotas()
    reached, tail = marks[:, 3:4], marks[:, 4:5]
    heads = []
    for h in range(HEADS):
        acts = []
        for c in range(3):
            conv = conv_parts(ext_ref, weights, marks, c * inner + h * DK)
            acts.append(conv * sigmoid(conv))
        q = (acts[0] * unit_scale(acts[0])).astype(bf16)
        k = (acts[1] * unit_scale(acts[1])).astype(bf16)
        v = acts[2].astype(bf16)
        c_col = total[:, HEADS + h : HEADS + h + 1]
        c_row = total_t[HEADS + h : HEADS + h + 1, :]
        decay = jnp.where(causal, jnp.exp(jnp.where(causal, c_col - c_row, 0.0)), 0.0)
        b = strength[:, h : h + 1]
        gram = dot1(k, k, NT)
        strict = jnp.where(below, b * gram * decay, 0.0)
        heads.append((q, k, v, c_col, decay, b, strict))
    inverses = unit_inverses([head[6] for head in heads])
    for h in range(HEADS):
        q, k, v, c_col, decay, b, strict = heads[h]
        x = inverses[h]
        start = jnp.exp(c_col) * reached
        kf = k.astype(f32)
        uw = dot3(x, jnp.concatenate([b * v.astype(f32), (b * start) * kf], axis=1))
        scores = dot1(q, k, NT) * decay
        suw = dot3(scores, uw)
        last = c_col[TOK - 1 : TOK, :]
        tail_k = kf * (jnp.exp(last - c_col) * tail)
        carry = jnp.exp(last) * reached[TOK - 1 : TOK, :]
        u, w = uw[:, :DK], uw[:, DK:]
        move = jnp.where(rows == cols, carry, 0.0) - dot3(tail_k, w, TN)
        offset_t = dot3(u, tail_k, TN)
        p_ref[h] = (q.astype(f32) * start - suw[:, DK:]).astype(bf16)
        z_ref[h] = suw[:, :DK]
        x_ref[h] = x.astype(bf16)
        uw_ref[h] = uw
        quarter = DK // HEADS
        for j in range(HEADS):
            send_ref[HEADS * h + j, 0:DK, :] = move.astype(bf16)
            send_ref[HEADS * h + j, DK : DK + quarter, :] = offset_t[
                j * quarter : (j + 1) * quarter
            ].astype(bf16)


def scan_forward(got_ref, out_ref):
    state = jnp.zeros((DK // HEADS, DK), f32)
    for i in range(SEQ):
        out_ref[i] = state.astype(bf16)
        if i + 1 < SEQ:
            high, low = split(state)
            both = dot1(jnp.concatenate([high, low], axis=0), got_ref[i, 0:DK, :], NT)
            half = DK // HEADS
            state = both[:half] + both[half:] + got_ref[i, DK : DK + half, :].astype(f32)


def scan_backward(got_ref, local_ref, out_ref):
    state = jnp.zeros((DK // HEADS, DK), f32)
    for i in range(SEQ - 1, -1, -1):
        out_ref[i] = state.astype(bf16)
        if i > 0:
            high, low = split(state)
            both = dot1(jnp.concatenate([high, low], axis=0), got_ref[i, 0:DK, :])
            half = DK // HEADS
            state = both[:half] + both[half:] + local_ref[i].astype(f32)


def gate_forward(p_ref, z_ref, s_ref, og_ref, gain_ref, heads_ref, gated_ref):
    gain = gain_ref[...]
    for h in range(HEADS):
        lanes = slice(h * DK, (h + 1) * DK)
        out = dot1(p_ref[h], s_ref[h], NT) + z_ref[h]
        heads_ref[:, lanes] = out
        r = lax.rsqrt(jnp.mean(out * out, axis=-1, keepdims=True) + head_eps)
        og = og_ref[:, lanes]
        gated_ref[:, lanes] = (out * r * gain * (og * sigmoid(og))).astype(bf16)


def gate_backward(
    gg_ref, heads_ref, og_ref, gain_ref, p_ref, do_ref, mix_ref, local_ref, gain_out_ref
):
    gain = gain_ref[...]
    total = jnp.zeros((1, DK), f32)
    quarter = DK // HEADS
    for h in range(HEADS):
        lanes = slice(h * DK, (h + 1) * DK)
        out = heads_ref[:, lanes]
        og = og_ref[:, lanes]
        gg = gg_ref[:, lanes]
        r = lax.rsqrt(jnp.mean(out * out, axis=-1, keepdims=True) + head_eps)
        u = out * r
        sig = sigmoid(og)
        w = og * sig
        ggw = gg * w
        g = ggw * gain
        total = total + jnp.sum(ggw * u, axis=0, keepdims=True)
        grad = r * (g - u * jnp.mean(g * u, axis=-1, keepdims=True))
        do_ref[:, lanes] = grad
        mix_ref[:, lanes] = (gg * gain * u * sig * (1.0 + og * (1.0 - sig))).astype(bf16)
        local = dot1(grad, p_ref[h], TN).astype(bf16)
        for j in range(HEADS):
            local_ref[HEADS * h + j] = local[j * quarter : (j + 1) * quarter]

    @pl.when(pl.program_id(0) == 0)
    def _():
        gain_out_ref[...] = jnp.zeros_like(gain_out_ref)

    gain_out_ref[0:1, :] += total


def conv_acts(ext_ref, weights, marks, lane):
    conv = conv_parts(ext_ref, weights, marks, lane)
    sig = sigmoid(conv)
    return conv, sig, conv * sig


def conv_pull(d_act, conv, sig, ext_ref, gext_ref, gtaps_ref, weights, marks, lane):
    d_conv = d_act * sig * (1.0 + conv * (1.0 - sig))
    for tap in range(TAPS):
        kept = d_conv * marks[:, tap : tap + 1] if tap < TAPS - 1 else d_conv
        place = (pl.ds(HALO - TAPS + 1 + tap, TOK), pl.ds(lane, DK))
        gtaps_ref[tap : tap + 1, lane : lane + DK] += jnp.sum(
            kept * ext_ref[place], axis=0, keepdims=True
        )
        gext_ref[place] += kept * weights[tap : tap + 1, lane : lane + DK]


def store_rows(gpre_ref, gext_ref):
    s = pl.program_id(0)
    gpre_ref[pl.ds(pl.multiple_of(s * TOK, TOK), TOK), :] = gext_ref[HALO:, :].astype(bf16)
    halo = pl.multiple_of(2 * TOK + s * HALO, HALO)
    gpre_ref[pl.ds(halo, HALO), :] = gext_ref[0:HALO, :].astype(bf16)


def unit_pull(d, hat, scale):
    return scale * (d - hat * jnp.sum(d * hat, axis=-1, keepdims=True))


def chunk_backward_early(
    pre_ref, rim_ref, scal_ref, rate_ref, taps_ref, marks_ref, docs_ref,
    uw_ref, s_ref, do_ref,
    gpre_ref, gtaps_ref, fresh_ref, recalled_ref, df_ref, dk_ref, dc_ref, ext_ref, gext_ref,
):
    inner = HEADS * DK
    ext_ref[0:HALO, :] = rim_ref[...].astype(f32)
    ext_ref[HALO:, :] = pre_ref[...].astype(f32)
    gext_ref[...] = jnp.zeros_like(gext_ref)

    @pl.when(pl.program_id(0) == 0)
    def _():
        gtaps_ref[...] = jnp.zeros_like(gtaps_ref)

    marks = marks_ref[0]
    weights = taps_ref[...]
    strength, total, total_t, causal, below = decays(
        scal_ref[...], rate_ref[...], marks, docs_ref[0]
    )
    rows, cols = iotas()
    reached = marks[:, 3:4]
    grad_c = jnp.zeros((TOK, TOK), f32)
    for h in range(HEADS):
        conv, sig, act = conv_acts(ext_ref, weights, marks, h * DK)
        act_k = conv_acts(ext_ref, weights, marks, inner + h * DK)[2]
        nq = unit_scale(act)
        q_hat = act * nq
        q, k = q_hat.astype(bf16), (act_k * unit_scale(act_k)).astype(bf16)
        c_col = total[:, HEADS + h : HEADS + h + 1]
        c_row = total_t[HEADS + h : HEADS + h + 1, :]
        decay = jnp.where(causal, jnp.exp(jnp.where(causal, c_col - c_row, 0.0)), 0.0)
        scores = dot1(q, k, NT) * decay
        start = jnp.exp(c_col) * reached
        state = s_ref[h]
        do = do_ref[:, h * DK : (h + 1) * DK].astype(bf16)
        fresh = uw_ref[h, :, :DK] - dot1(uw_ref[h, :, DK:], state, NT)
        fresh = fresh.astype(bf16)
        fresh_ref[h] = fresh
        recalled_ref[h] = dot1(k, state, NT)
        df_ref[h] = dot1(scores, do, TN)
        d_scores = dot1(do, fresh, NT)
        pull = d_scores * scores
        d_qk = (d_scores * decay).astype(bf16)
        dk_ref[h] = dot1(d_qk, q, TN)
        do_state = dot1(do, state)
        d_q = dot1(d_qk, k) + start * do_state
        d_start = jnp.sum(q.astype(f32) * do_state, axis=-1, keepdims=True)
        d_c = jnp.sum(pull - jnp.transpose(pull), axis=-1, keepdims=True) + d_start * start
        grad_c = jnp.where(cols == HEADS + h, d_c, grad_c)
        conv_pull(
            unit_pull(d_q, q_hat, nq), conv, sig, ext_ref, gext_ref, gtaps_ref, weights, marks,
            h * DK,
        )
    dc_ref[...] = grad_c
    store_rows(gpre_ref, gext_ref)


def chunk_backward_late(
    pre_ref, rim_ref, scal_ref, rate_ref, taps_ref, marks_ref, docs_ref,
    x_ref, s_ref, d_ref, fresh_ref, recalled_ref, df_ref, dk_ref, dc_ref,
    gpre_ref, gscal_ref, gtaps_ref, grate_ref, ext_ref, gext_ref,
):
    inner = HEADS * DK
    ext_ref[0:HALO, :] = rim_ref[:, inner:].astype(f32)
    ext_ref[HALO:, :] = pre_ref[:, inner:].astype(f32)
    gext_ref[...] = jnp.zeros_like(gext_ref)

    @pl.when(pl.program_id(0) == 0)
    def _():
        gtaps_ref[...] = jnp.zeros_like(gtaps_ref)
        grate_ref[...] = jnp.zeros_like(grate_ref)

    marks = marks_ref[0]
    weights = taps_ref[:, inner:]
    scal = scal_ref[...]
    rates = rate_ref[...]
    strength, total, total_t, causal, below = decays(scal, rates, marks, docs_ref[0])
    rows, cols = iotas()
    reached, tail = marks[:, 3:4], marks[:, 4:5]
    grad_b = jnp.zeros((TOK, TOK), f32)
    grad_c = jnp.zeros((TOK, TOK), f32)
    for h in range(HEADS):
        conv_k, sig_k, act_k = conv_acts(ext_ref, weights, marks, h * DK)
        conv_v, sig_v, act_v = conv_acts(ext_ref, weights, marks, inner + h * DK)
        nk = unit_scale(act_k)
        k_hat = act_k * nk
        k, v = k_hat.astype(bf16), act_v.astype(bf16)
        kf, vf = k.astype(f32), v.astype(f32)
        c_col = total[:, HEADS + h : HEADS + h + 1]
        c_row = total_t[HEADS + h : HEADS + h + 1, :]
        strict = causal & below
        strict_decay = jnp.where(strict, jnp.exp(jnp.where(strict, c_col - c_row, 0.0)), 0.0)
        b = strength[:, h : h + 1]
        gram_decay = dot1(k, k, NT) * strict_decay
        start = jnp.exp(c_col) * reached
        last = c_col[TOK - 1 : TOK, :]
        tail_decay = jnp.exp(last - c_col) * tail
        carry = jnp.exp(last) * reached[TOK - 1 : TOK, :]
        state, adj = s_ref[h], d_ref[h]
        fresh, recalled = fresh_ref[h], recalled_ref[h]
        d_fresh = df_ref[h] + dot1(kf * tail_decay, adj, NT)
        d_r = dot1(x_ref[h], d_fresh, TN)
        d_v = b * d_r
        d_b = jnp.sum(d_r * (vf - start * recalled), axis=-1, keepdims=True)
        d_start = -jnp.sum(d_v * recalled, axis=-1, keepdims=True)
        d_strict = -dot1(d_r, fresh, NT)
        strict_pull = d_strict * gram_decay
        d_b = d_b + jnp.sum(strict_pull, axis=-1, keepdims=True)
        d_gram = (d_strict * (b * strict_decay)).astype(bf16)
        d_k = dk_ref[h] - start * dot1(d_v, state) + dot1(d_gram, k) + dot1(d_gram, k, TN)
        fresh_adj = dot1(fresh, adj)
        d_k = d_k + tail_decay * fresh_adj
        d_tail = jnp.sum(kf * fresh_adj, axis=-1, keepdims=True) * tail_decay
        d_carry = jnp.sum(
            jnp.sum(adj.astype(f32) * state.astype(f32), axis=-1, keepdims=True),
            axis=0, keepdims=True,
        )
        pull = b * strict_pull
        d_c = jnp.sum(pull - jnp.transpose(pull), axis=-1, keepdims=True)
        d_c = d_c + d_start * start - d_tail
        d_last = d_carry * carry + jnp.sum(d_tail, axis=0, keepdims=True)
        d_c = d_c + jnp.where(rows[:, 0:1] == TOK - 1, d_last, 0.0)
        grad_b = jnp.where(cols == h, d_b, grad_b)
        grad_c = jnp.where(cols == HEADS + h, d_c, grad_c)
        conv_pull(
            unit_pull(d_k, k_hat, nk), conv_k, sig_k, ext_ref, gext_ref, gtaps_ref, weights,
            marks, h * DK,
        )
        conv_pull(
            d_v, conv_v, sig_v, ext_ref, gext_ref, gtaps_ref, weights, marks, inner + h * DK
        )
    upper = (cols >= rows).astype(bf16)
    grad_ld = dot2(upper, grad_c + dc_ref[...])
    decay_side = -grad_ld * rates * sigmoid(scal)
    gscal_ref[...] = jnp.where(
        cols < HEADS,
        grad_b * strength * (1.0 - strength),
        jnp.where(cols < 2 * HEADS, decay_side, 0.0),
    ).astype(bf16)
    grate_ref[0:1, :] += -jnp.sum(grad_ld * softplus(scal), axis=0, keepdims=True)
    store_rows(gpre_ref, gext_ref)


def row_grads(groups, lhs_count, rhs_count, *refs):
    out_ref = refs[-1]
    lhs = [refs[i][...] for i in range(lhs_count)]
    rhs = refs[lhs_count : lhs_count + rhs_count]
    lane = 0
    for group in groups:
        total = None
        for i, j in group:
            part = dot1(lhs[i][: rhs[j].shape[0]], rhs[j][...], TN)
            total = part if total is None else total + part
        out_ref[:, lane : lane + total.shape[1]] = total.astype(bf16)
        lane += total.shape[1]


def mixer_grads(
    offsets, place_ref, normed_ref, mixer_ref, og_ref, gq_ref, gkv_ref, gscal_ref, gated_ref, *outs
):
    width = normed_ref.shape[1]
    part = HEADS * DK // 2
    tokens = 2 * TOK

    def rows_x(ref, offset):
        place = lax.rem(place_ref[0] + offset, 4)
        return ref[:, pl.ds(pl.multiple_of(place * (width // 4), 128), width // 4)]

    def rows_z(ref, offset):
        place = lax.rem(place_ref[1] + offset, 4)
        cut = width // 16
        pieces = [
            ref[:, pl.ds(pl.multiple_of((j * 4 + place) * cut, 128), cut)] for j in range(4)
        ]
        return jnp.concatenate(pieces, axis=1)

    def store(outs, columns):
        lane = 0
        for column in columns:
            column = column.astype(bf16)
            lanes = slice(lane, lane + column.shape[1])
            rows = column.shape[0] // len(outs)
            for i, out in enumerate(outs):
                out[:, lanes] = column[i * rows : (i + 1) * rows]
            lane += column.shape[1]

    count = len(outs) // (2 * len(offsets))
    for i, offset in enumerate(offsets):
        normed = rows_x(normed_ref, offset)
        store(
            outs[i * count : (i + 1) * count],
            [
                dot1(normed[:tokens], og_ref[...], TN),
                dot1(normed, gq_ref[...], TN),
                dot1(normed[:tokens], gscal_ref[...], TN),
                dot1(normed, gkv_ref[:, :part], TN),
            ],
        )
        normed = rows_z(normed_ref, offset)
        i += len(offsets)
        store(
            outs[i * count : (i + 1) * count],
            [
                dot1(normed, gkv_ref[:, part:], TN),
                dot1(rows_z(mixer_ref, offset), gated_ref[...], TN),
            ],
        )


def input_grads(
    rim_ref, gq_ref, gkv_ref, gscal_ref, og_ref, left_ref, right_ref, out_ref, first_ref, second_ref
):
    inner = HEADS * DK
    part = inner // 2
    tokens = 2 * TOK

    @pl.when(pl.program_id(0) == 0)
    def _():
        first_ref[:, :inner] = gq_ref[:tokens, :]
        first_ref[:, inner : inner + 128] = gscal_ref[...]
        first_ref[:, inner + 128 : inner + 128 + part] = gkv_ref[:tokens, :part]
        first_ref[:, inner + 128 + part :] = og_ref[...]
        second_ref[...] = gkv_ref[:tokens, part:]
        for s in range(2):
            rows = slice((s + 1) * TOK - HALO, (s + 1) * TOK)
            rim = rim_ref[s * HALO : (s + 1) * HALO, :].astype(f32)

            def put(ref, lanes, came):
                ref[rows, lanes] = (ref[rows, lanes].astype(f32) + came).astype(bf16)

            put(first_ref, slice(0, inner), rim[:, :inner])
            put(
                first_ref,
                slice(inner + 128, inner + 128 + part),
                rim[:, inner : inner + part],
            )
            put(second_ref, slice(0, inner + part), rim[:, inner + part :])

    total = dot1(first_ref[...], left_ref[...], NT)
    total = total + dot1(second_ref[...], right_ref[:, : inner + part], NT)
    out_ref[...] = total.astype(bf16)


def ignoring(kernel, at, count):
    def inner_kernel(*refs):
        kernel(*refs[:at], *refs[at + count :])

    return inner_kernel


def dep_specs(deps):
    return [pl.BlockSpec(memory_space=pl.ANY) for _ in deps]


def cost(flops, moved):
    return pl.CostEstimate(flops=flops, bytes_accessed=moved, transcendentals=0)


def params():
    return pltpu.CompilerParams(vmem_limit_bytes=VMEM)


def whole(shape):
    return pl.BlockSpec(shape, lambda s: (0,) * len(shape))


def by_rows(rows, cols, base=0, lane=0):
    return pl.BlockSpec((rows, cols), lambda s: (base + s, lane))


def by_lead(*shape):
    return pl.BlockSpec(shape, lambda s: (s,) + (0,) * (len(shape) - 1))


def mixer_specs():
    wide = 3 * HEADS * DK
    return [
        by_rows(TOK, wide),
        by_rows(HALO, wide, 2 * TOK // HALO),
        by_rows(TOK, 128),
        whole((1, 128)),
        whole((TAPS, wide)),
        by_lead(1, TOK, 8),
        by_lead(1, 1, TOK),
    ]


def run_chunk_forward(pre, scal, rates, taps, marks, docs):
    quarter = DK // HEADS
    wide = 3 * HEADS * DK
    return pl.pallas_call(
        chunk_forward,
        grid=(2,),
        in_specs=mixer_specs(),
        out_specs=[
            by_lead(16, DK + quarter, DK),
            by_lead(HEADS, TOK, DK),
            by_lead(HEADS, TOK, DK),
            by_lead(HEADS, TOK, DK),
            by_lead(HEADS, TOK, 2 * DK),
        ],
        out_shape=[
            jax.ShapeDtypeStruct((SEQ, DK + quarter, DK), bf16),
            jax.ShapeDtypeStruct((8, TOK, DK), bf16),
            jax.ShapeDtypeStruct((8, TOK, DK), f32),
            jax.ShapeDtypeStruct((8, TOK, DK), bf16),
            jax.ShapeDtypeStruct((8, TOK, 2 * DK), f32),
        ],
        scratch_shapes=[pltpu.VMEM((HALO + TOK, wide), f32)],
        compiler_params=params(),
        cost_estimate=cost(10**10, 6 * 10**6),
    )(pre, pre, scal, rates, taps, marks, docs)


def run_scan_forward(got):
    return pl.pallas_call(
        scan_forward,
        out_shape=jax.ShapeDtypeStruct((SEQ, DK // HEADS, DK), bf16),
        compiler_params=params(),
        cost_estimate=cost(10**9, 3 * 10**6),
    )(got)


def run_scan_backward(got, local, deps):
    vmem = pl.BlockSpec(memory_space=pltpu.VMEM)
    return pl.pallas_call(
        ignoring(scan_backward, 2, len(deps)),
        in_specs=[vmem, vmem] + dep_specs(deps),
        out_specs=vmem,
        out_shape=jax.ShapeDtypeStruct((SEQ, DK // HEADS, DK), bf16),
        compiler_params=params(),
        cost_estimate=cost(10**9, 3 * 10**6),
    )(got, local, *deps)


def run_gate_forward(p, z, state, og, gain, deps):
    inner = HEADS * DK
    return pl.pallas_call(
        ignoring(gate_forward, 5, len(deps)),
        grid=(2,),
        in_specs=[
            by_lead(HEADS, TOK, DK),
            by_lead(HEADS, TOK, DK),
            by_lead(HEADS, DK, DK),
            by_rows(TOK, inner),
            whole((1, DK)),
        ]
        + dep_specs(deps),
        out_specs=[by_rows(TOK, inner), by_rows(TOK, inner)],
        out_shape=[
            jax.ShapeDtypeStruct((2 * TOK, inner), f32),
            jax.ShapeDtypeStruct((2 * TOK, inner), bf16),
        ],
        compiler_params=params(),
        cost_estimate=cost(10**9, 3 * 10**6),
    )(p, z, state, og, gain, *deps)


def run_gate_backward(gg, heads_out, og, gain, p):
    inner = HEADS * DK
    return pl.pallas_call(
        gate_backward,
        grid=(2,),
        in_specs=[
            by_rows(TOK, inner),
            by_rows(TOK, inner),
            by_rows(TOK, inner),
            whole((1, DK)),
            by_lead(HEADS, TOK, DK),
        ],
        out_specs=[
            by_rows(TOK, inner),
            by_rows(TOK, inner),
            by_lead(16, DK // HEADS, DK),
            whole((8, DK)),
        ],
        out_shape=[
            jax.ShapeDtypeStruct((2 * TOK, inner), f32),
            jax.ShapeDtypeStruct((2 * TOK, inner), bf16),
            jax.ShapeDtypeStruct((SEQ, DK // HEADS, DK), bf16),
            jax.ShapeDtypeStruct((8, DK), f32),
        ],
        compiler_params=params(),
        cost_estimate=cost(10**9, 3 * 10**6),
    )(gg, heads_out, og, gain, p)


def run_chunk_backward_early(pre, scal, rates, taps, marks, docs, uw, state, do):
    inner = HEADS * DK
    wide = 3 * inner
    square = jax.ShapeDtypeStruct((8, TOK, DK), f32)
    return pl.pallas_call(
        chunk_backward_early,
        grid=(2,),
        in_specs=mixer_specs()
        + [
            by_lead(HEADS, TOK, 2 * DK),
            by_lead(HEADS, DK, DK),
            by_rows(TOK, inner),
        ],
        out_specs=[
            whole((2 * (TOK + HALO), inner)),
            whole((TAPS, inner)),
            by_lead(HEADS, TOK, DK),
            by_lead(HEADS, TOK, DK),
            by_lead(HEADS, TOK, DK),
            by_lead(HEADS, TOK, DK),
            by_rows(TOK, 128),
        ],
        out_shape=[
            jax.ShapeDtypeStruct((2 * (TOK + HALO), inner), bf16),
            jax.ShapeDtypeStruct((TAPS, inner), f32),
            jax.ShapeDtypeStruct((8, TOK, DK), bf16),
            square,
            square,
            square,
            jax.ShapeDtypeStruct((2 * TOK, 128), f32),
        ],
        scratch_shapes=[
            pltpu.VMEM((HALO + TOK, wide), f32),
            pltpu.VMEM((HALO + TOK, inner), f32),
        ],
        compiler_params=params(),
        cost_estimate=cost(5 * 10**9, 10**7),
    )(pre, pre, scal, rates, taps, marks, docs, uw, state, do)


def run_chunk_backward_late(
    pre, scal, rates, taps, marks, docs, x, state, adj, early, deps
):
    inner = HEADS * DK
    wide = 3 * inner
    return pl.pallas_call(
        ignoring(chunk_backward_late, 15, len(deps)),
        grid=(2,),
        in_specs=mixer_specs()
        + [
            by_lead(HEADS, TOK, DK),
            by_lead(HEADS, DK, DK),
            by_lead(HEADS, DK, DK),
            by_lead(HEADS, TOK, DK),
            by_lead(HEADS, TOK, DK),
            by_lead(HEADS, TOK, DK),
            by_lead(HEADS, TOK, DK),
            by_rows(TOK, 128),
        ]
        + dep_specs(deps),
        out_specs=[
            whole((2 * (TOK + HALO), 2 * inner)),
            by_rows(TOK, 128),
            whole((TAPS, 2 * inner)),
            whole((8, 128)),
        ],
        out_shape=[
            jax.ShapeDtypeStruct((2 * (TOK + HALO), 2 * inner), bf16),
            jax.ShapeDtypeStruct((2 * TOK, 128), bf16),
            jax.ShapeDtypeStruct((TAPS, 2 * inner), f32),
            jax.ShapeDtypeStruct((8, 128), f32),
        ],
        scratch_shapes=[
            pltpu.VMEM((HALO + TOK, 2 * inner), f32),
            pltpu.VMEM((HALO + TOK, 2 * inner), f32),
        ],
        compiler_params=params(),
        cost_estimate=cost(5 * 10**9, 10**7),
    )(pre, pre, scal, rates, taps, marks, docs, x, state, adj, *early, *deps)


def run_row_grads(lhs, rhs, groups, deps=()):
    width = lhs[0].shape[1]
    cols = sum(rhs[group[0][1]].shape[1] for group in groups)
    return pl.pallas_call(
        partial(row_grads, groups, len(lhs), len(rhs)),
        grid=(4,),
        in_specs=[pl.BlockSpec((m.shape[0], width // 4), lambda s: (0, s)) for m in lhs]
        + [whole(m.shape) for m in rhs]
        + dep_specs(deps),
        out_specs=pl.BlockSpec((width // 4, cols), lambda s: (s, 0)),
        out_shape=jax.ShapeDtypeStruct((width, cols), bf16),
        compiler_params=params(),
        cost_estimate=cost(2 * rhs[0].shape[0] * width * cols, 2 * width * cols),
    )(*lhs, *rhs, *deps)


def run_mixer_grads(offsets, halves, *arrays, deps=()):
    width = arrays[0].shape[1]
    inner = HEADS * DK
    vmem = pl.BlockSpec(memory_space=pltpu.VMEM)
    place = jnp.stack([place_of("x"), place_of("z")]).astype(jnp.int32)
    shapes = [
        (width // 4 // halves, cols)
        for cols in (2 * inner + inner // 2 + 128, 2 * inner + inner // 2)
        for _ in range(halves * len(offsets))
    ]
    return pl.pallas_call(
        ignoring(partial(mixer_grads, offsets), 8, len(deps)),
        in_specs=[pl.BlockSpec(memory_space=pltpu.SMEM)] + [vmem] * 7 + dep_specs(deps),
        out_specs=[vmem] * len(shapes),
        out_shape=[jax.ShapeDtypeStruct(shape, bf16) for shape in shapes],
        compiler_params=params(),
        cost_estimate=cost(2 * 256 * width * 5 * inner, 2 * width * 5 * inner),
    )(place, *arrays, *deps)


def run_input_grads(rim, gq, gkv, gscal, og, left, right):
    inner = HEADS * DK
    width = left.shape[0]
    tokens = 2 * TOK
    cut = width // 4
    return pl.pallas_call(
        input_grads,
        grid=(4,),
        in_specs=[whole(m.shape) for m in (rim, gq, gkv, gscal, og)]
        + [
            by_rows(cut, left.shape[1]),
            by_rows(cut, right.shape[1]),
        ],
        out_specs=pl.BlockSpec((tokens, cut), lambda s: (0, s)),
        out_shape=jax.ShapeDtypeStruct((tokens, width), bf16),
        scratch_shapes=[
            pltpu.VMEM((tokens, left.shape[1]), bf16),
            pltpu.VMEM((tokens, inner + inner // 2), bf16),
        ],
        compiler_params=params(),
        cost_estimate=cost(2 * tokens * width * 5 * inner, 2 * width * 5 * inner),
    )(rim, gq, gkv, gscal, og, left, right)


SEQ_AXES = ("x", "z", "y")
GROUP_AXES = ("y", "head")


def passed_along(array, by):
    pairs = [(i, i + by) for i in range(SEQ) if 0 <= i + by < SEQ]
    return lax.ppermute(array, SEQ_AXES, pairs)


def along(array, axis, by):
    count = lax.axis_size(axis)
    return lax.ppermute(array, axis, [(i, (i + by) % count) for i in range(count)])


def place_of(axis):
    return lax.axis_index(axis)


def flipped(array, axes, mask):
    count = lax.axis_size(axes)
    return lax.ppermute(array, axes, [(i, i ^ mask) for i in range(count)])


def pick(array, index, dim):
    return lax.dynamic_index_in_dim(array, index, dim, keepdims=False)


def ordered(mine, other, place, axis=0):
    first = place == 0
    return jnp.concatenate(
        [jnp.where(first, mine, other), jnp.where(first, other, mine)], axis=axis
    )


def later(array, *deps):
    for dep in deps:
        first = lax.slice(dep, (0,) * dep.ndim, (1,) * dep.ndim).reshape(())
        array = array + (first * 0).astype(array.dtype)
    return array


def gather_last(first, second):
    near, far, halfway = near_and_far(first, second, ("z", "x"))
    outs = []
    for i, (array, axis, dim) in enumerate(((first, "z", 1), (second, "x", 0))):
        place = place_of(axis)
        shape = list(array.shape)
        shape.insert(dim, 4)
        out = jnp.zeros(shape, array.dtype)
        block = jnp.concatenate(far[2 * i : 2 * i + 2], axis=0)
        for offset, block in ((0, array), (-1, near[2 * i]), (-2, block), (1, near[2 * i + 1])):
            out = lax.dynamic_update_index_in_dim(out, block, (place + offset) % 4, dim)
        outs.append(out.reshape(-1, array.shape[-1]))
    return outs[0], outs[1], halfway


def exchange(array, axis):
    return lax.all_to_all(array, axis, split_axis=0, concat_axis=0, tiled=True)


def head_place():
    index = lax.axis_index("head")
    return index // 2, index % 2


def core_scatter(partial_rows):
    core = head_place()[1]
    rows = partial_rows.shape[0] // HEADS
    blocks = partial_rows.astype(bf16).reshape(2, 2, rows, -1)
    got = flipped(pick(blocks, 1 - core, 1), "head", 1)
    return pick(blocks, core, 1).astype(f32) + got.astype(f32), got


def chip_scatter(both, *gates):
    chip = head_place()[0]
    got = flipped(later(pick(both, 1 - chip, 0), *gates).astype(bf16), "head", 2)
    return pick(both, chip, 0) + got.astype(f32)


def head_gather(rows):
    chip, core = head_place()
    got = flipped(rows, "head", 2)
    first = chip == 0
    chips = jnp.stack([jnp.where(first, rows, got), jnp.where(first, got, rows)])
    got = flipped(chips, "head", 1)
    first = core == 0
    cores = [jnp.where(first, chips, got), jnp.where(first, got, chips)]
    return jnp.stack(cores, axis=1).reshape(HEADS * rows.shape[0], -1)


def group_scatter(partial_rows):
    chip, core = head_place()
    place = place_of("y") * 2 + chip
    blocks = partial_rows.astype(bf16).reshape(4, 2, -1, partial_rows.shape[1])
    got = flipped(pick(blocks, 1 - core, 1), GROUP_AXES, 1)
    both = pick(blocks, core, 1).astype(f32) + got.astype(f32)
    total = pick(both, place, 0)
    for mask in (2, 1, 3):
        part = pick(both, jnp.bitwise_xor(place, mask), 0).astype(bf16)
        total = total + flipped(part, GROUP_AXES, 2 * mask).astype(f32)
    return total, got


def group_gather(rows):
    chip, core = head_place()
    place = place_of("y") * 2 + chip
    out = jnp.zeros((4,) + rows.shape, rows.dtype)
    for mask in (2, 1, 3, 0):
        got = flipped(rows, GROUP_AXES, 2 * mask) if mask else rows
        out = lax.dynamic_update_index_in_dim(out, got, jnp.bitwise_xor(place, mask), 0)
    got = flipped(out, GROUP_AXES, 1)
    first = core == 0
    cores = [jnp.where(first, out, got), jnp.where(first, got, out)]
    return jnp.stack(cores, axis=1).reshape(8 * rows.shape[0], -1)


def in_vmem(kernel, shapes, place, *arrays, deps=()):
    vmem = pl.BlockSpec(memory_space=pltpu.VMEM)
    moved = sum(2 * a.size for a in arrays)
    return pl.pallas_call(
        ignoring(kernel, 1 + len(arrays), len(deps)),
        in_specs=[pl.BlockSpec(memory_space=pltpu.SMEM)] + [vmem] * len(arrays) + dep_specs(deps),
        out_specs=[vmem] * len(shapes),
        out_shape=[jax.ShapeDtypeStruct(shape, kind) for shape, kind in shapes],
        compiler_params=params(),
        cost_estimate=cost(moved, moved),
    )(place, *arrays, *deps)


def add_far(place_ref, *refs):
    for i in range(2):
        right, left, ahead, behind = refs[4 * i : 4 * i + 4]
        right_out, left_out = refs[8 + 2 * i : 10 + 2 * i]
        half = ahead.shape[0]
        total = right[:half].astype(f32) + ahead[...].astype(f32)
        right_out[:half] = total.astype(bf16)
        right_out[half:] = right[half:]
        left_out[:half] = left[:half]
        total = left[half:].astype(f32) + behind[...].astype(f32)
        left_out[half:] = total.astype(bf16)


def add_and_cut(place_ref, *refs):
    for i in range(2):
        members = refs[3 * i : 3 * i + 3]
        outs = refs[6 + 4 * i : 10 + 4 * i]
        rows = members[0].shape[0] // 4
        for out, by in zip(outs, (0, 2, 1, 3)):
            start = pl.multiple_of(lax.rem(place_ref[1 - i] + by, 4) * rows, rows)
            total = members[0][pl.ds(start, rows), :].astype(f32)
            for member in members[1:]:
                total = total + member[pl.ds(start, rows), :].astype(f32)
            out[...] = total.astype(bf16)


def add_and_halve(place_ref, *refs):
    kept, sent = refs[8:]
    rows = kept.shape[0]
    lane = 0
    for i in range(2):
        parts = refs[4 * i : 4 * i + 4]
        lanes = slice(lane, lane + parts[0].shape[1])
        lane += parts[0].shape[1]
        for out, at in ((kept, place_ref[2]), (sent, 1 - place_ref[2])):
            start = pl.multiple_of(at * rows, rows)
            total = parts[0][pl.ds(start, rows), :].astype(f32)
            for part in parts[1:]:
                total = total + part[pl.ds(start, rows), :].astype(f32)
            out[:, lanes] = total.astype(out.dtype)


def places():
    return jnp.stack([place_of(axis) for axis in SEQ_AXES]).astype(jnp.int32)


def reduce_near(owns, arrays, deps):
    shapes = [(arrays[i].shape, bf16) for i in (0, 1, 4, 5)]
    sums = in_vmem(add_far, shapes, places(), *arrays, deps=deps)
    gate = sums[0]
    arrays = []
    for i, axis in enumerate(("x", "z")):
        arrays += [owns[i], along(sums[2 * i], axis, 1), along(sums[2 * i + 1], axis, -1)]
    return arrays, gate


def reduce_cross(arrays, deps):
    shapes = []
    for own in (arrays[0], arrays[3]):
        shapes += [((own.shape[0] // 4, own.shape[1]), bf16)] * 4
    cut = in_vmem(add_and_cut, shapes, places(), *arrays, deps=deps)
    arrays = []
    for i, axis in enumerate(("z", "x")):
        own, two, one, three = cut[4 * i : 4 * i + 4]
        arrays += [own, along(two, axis, 2), along(one, axis, 1), along(three, axis, -1)]
    return arrays, cut[0]


def reduce_end(arrays, deps):
    rows, cols = arrays[0].shape[0] // 2, arrays[0].shape[1] + arrays[4].shape[1]
    shapes = [((rows, cols), f32), ((rows, cols), bf16)]
    kept, sent = in_vmem(add_and_halve, shapes, places(), *arrays, deps=deps)
    return kept + along(sent, "y", 1).astype(f32)


def pair_up(place_ref, left, left_other, right, right_other, left_out, right_out):
    rows = left.shape[0]
    mine = pl.multiple_of(place_ref[2] * rows, rows)
    other = pl.multiple_of((1 - place_ref[2]) * rows, rows)
    left_out[pl.ds(mine, rows), :] = left[...]
    left_out[pl.ds(other, rows), :] = left_other[...]
    right_out[pl.ds(mine, rows), :] = right[...]
    right_out[pl.ds(other, rows), :] = right_other[...]


def pass_on(place_ref, *refs):
    for i in range(2):
        half = refs[4 + 2 * i].shape[0]
        refs[4 + 2 * i][...] = refs[2 * i][:half]
        refs[5 + 2 * i][...] = refs[2 * i + 1][half:]


def put_in_place(axes, place_ref, *refs):
    for i in range(2):
        out = refs[10 + i]
        own, left, right, far_a, far_b = refs[5 * i : 5 * i + 5]
        place = place_ref[axes[i]]
        half = far_a.shape[0]
        out[place] = own[...]
        out[lax.rem(place + 3, 4)] = left[...]
        out[lax.rem(place + 1, 4)] = right[...]
        out[lax.rem(place + 2, 4), :half] = far_a[...]
        out[lax.rem(place + 2, 4), half:] = far_b[...]


def near_and_far(first, second, axes):
    near = []
    for array, axis in ((first, axes[0]), (second, axes[1])):
        near += [along(array, axis, 1), along(array, axis, -1)]
    shapes = []
    for array in (first, second):
        shapes += [((array.shape[0] // 2,) + array.shape[1:], bf16)] * 2
    halves = in_vmem(pass_on, shapes, places(), *near)
    far = []
    for i in range(2):
        far += [along(halves[2 * i], axes[i], 1), along(halves[2 * i + 1], axes[i], -1)]
    return near, far, halves[0]


def sum_along(array, axis):
    total = array
    for by in range(1, lax.axis_size(axis)):
        total = total + along(array, axis, by)
    return total


def mm(a, b, dims="ij,jk->ik"):
    return jnp.einsum(dims, a, b, preferred_element_type=f32)


def row_scale(x):
    return lax.rsqrt(jnp.mean(x * x, axis=-1, keepdims=True) + norm_eps)


def norm_pull(x, scale, gain, grad):
    unit = x * scale
    scaled = grad * gain
    return scale * (scaled - unit * jnp.mean(scaled * unit, axis=-1, keepdims=True))


def doc_tables(doc_lengths):
    first = lax.axis_index(SEQ_AXES) * TOK - (TAPS - 1)
    ends = jnp.cumsum(doc_lengths, axis=1)
    places = first + jnp.arange(TOK + TAPS - 1, dtype=jnp.int32)
    counted = jnp.sum((places[None, :, None] >= ends[:, None, :]).astype(jnp.int32), axis=2)
    ext = jnp.where(places[None, :] >= 0, counted, -1)
    local = ext[:, TAPS - 1 :]
    columns = [(ext[:, o : o + TOK] == local) for o in range(TAPS - 1)]
    columns.append(local == ext[:, TAPS - 2 : TAPS - 1])
    columns.append(local == local[:, -1:])
    columns.append(local)
    columns += [jnp.zeros_like(local)] * 2
    marks = jnp.stack([c.astype(f32) for c in columns], axis=-1)
    return marks, local.astype(f32)[:, None, :]


def body(
    inputs, doc_lengths, norm_in, query_weight, key_weight, value_weight, outgate_weight,
    scalar_weight, conv_kernel, decay_rate, head_norm, output_weight, norm_ffn, gate_weight,
    up_weight, down_weight, grad_out,
):
    width = inputs.shape[2]
    inner = HEADS * DK
    hidden = gate_weight.shape[1]
    head_index = lax.axis_index("head")
    quarter = 2 * TOK // HEADS

    gains = jnp.stack([norm_in, norm_ffn], axis=1)
    misc = jnp.concatenate([scalar_weight.reshape(-1, 2 * HEADS), gains], axis=1)
    misc = jnp.pad(misc, ((0, 0), (0, 128 - misc.shape[1])))
    part = inner // 2
    left = jnp.concatenate([query_weight, misc, key_weight[:, :part], outgate_weight], axis=1)
    right = jnp.concatenate([key_weight[:, part:], value_weight, output_weight.T], axis=1)
    y_place = place_of("y")
    rows = left.shape[0]
    left, right = in_vmem(
        pair_up,
        [((2 * rows, left.shape[1]), bf16), ((2 * rows, right.shape[1]), bf16)],
        places(),
        left, along(left, "y", 1), right, along(right, "y", 1),
    )
    near, far, _ = near_and_far(left, right, ("x", "z"))
    left, right = in_vmem(
        partial(put_in_place, (0, 1)),
        [((4, 2 * rows, part.shape[1]), bf16) for part in (left, right)],
        places(),
        left, *near[:2], *far[:2], right, *near[2:], *far[2:],
    )
    all_left, all_right, halfway = gather_last(left, right)
    w_gate, w_out_t = all_left[:, -inner:], all_right[:, -inner:]
    w_left, w_right = all_left[:, :-inner], all_right[:, :-inner]
    gains = w_left[:, inner : inner + 128].T[2 * HEADS : 2 * HEADS + 2].astype(f32)
    gain_in, gain_ffn = gains[0:1], gains[1:2]

    units = hidden // 2
    span = -(-units // 128) * 128

    def in_halves(weight):
        halves = weight.reshape(weight.shape[0], 2, units)
        return jnp.pad(halves, ((0, 0), (0, 0), (0, span - units)))

    packed = jnp.concatenate(
        [in_halves(gate_weight), in_halves(up_weight), in_halves(down_weight.T)], axis=2
    )
    other = along(later(pick(packed, 1 - y_place, 1), left), "y", 1)
    packed = later(ordered(pick(packed, y_place, 1), other, y_place), halfway)
    w_ffn = lax.all_gather(packed, ("x", "z"), axis=0, tiled=True)
    w_gateup = w_ffn[:, : 2 * span]
    w_down_t = w_ffn[:, 2 * span :]

    marks, docs_row = doc_tables(doc_lengths)
    taps = jnp.transpose(conv_kernel.astype(f32), (1, 0, 2)).reshape(TAPS, 3 * inner)
    rates = jnp.zeros((1, 128), f32)
    rates = rates.at[0, HEADS : 2 * HEADS].set(decay_rate.astype(f32))
    gain_head = head_norm.astype(f32).reshape(1, DK)

    halo = passed_along(inputs[:, TOK - HALO :], 1)
    tokens = inputs.reshape(2 * TOK, width)
    all_rows = jnp.concatenate([tokens, halo.reshape(2 * HALO, width)], axis=0).astype(f32)
    scale_in = row_scale(all_rows)
    normed_all = (all_rows * scale_in * gain_in).astype(bf16)
    normed_in = normed_all[: 2 * TOK]

    left = mm(normed_all, w_left)
    right = mm(normed_all, w_right)
    pre = jnp.concatenate(
        [left[:, :inner].astype(bf16), left[:, inner + 128 :].astype(bf16), right.astype(bf16)],
        axis=1,
    )
    scal = left[: 2 * TOK, inner : inner + 128]

    grad_rows = grad_out.reshape(2 * TOK, width)
    grad_other = along(grad_rows, "y", 1)
    send, p, z, x, uw = run_chunk_forward(pre, scal, rates, taps, marks, docs_row)
    out_gate = mm(normed_in, w_gate)
    got = exchange(send, SEQ_AXES)
    state = exchange(run_scan_forward(got), SEQ_AXES).reshape(8, DK, DK)
    heads_out, gated_rows = run_gate_forward(
        p, z, state, out_gate, gain_head, (grad_other,)
    )

    mine = partial(lax.dynamic_slice_in_dim, start_index=head_index * quarter, slice_size=quarter)
    residual = mine(tokens).astype(f32) + chip_scatter(
        core_scatter(mm(gated_rows, w_out_t, "ij,kj->ik"))[0]
    )
    scale_ffn = row_scale(residual)
    normed_ffn = group_gather((residual * scale_ffn * gain_ffn).astype(bf16))

    group_grads = ordered(grad_rows, grad_other, y_place)
    grad_act = mm(group_grads, w_down_t)
    gate_up = mm(normed_ffn, w_gateup)
    gate, up = gate_up[:, :span], gate_up[:, span:]
    sig = sigmoid(gate)
    silu = gate * sig
    product = (silu * up).astype(bf16)
    gu_grad = jnp.concatenate(
        [
            (grad_act * up * sig * (1.0 + gate * (1.0 - sig))).astype(bf16),
            (grad_act * silu).astype(bf16),
        ],
        axis=1,
    )
    ffn_part = mm(gu_grad, w_gateup, "ij,kj->ik").astype(bf16)
    grad_normed = group_scatter(ffn_part)[0]
    back = norm_pull(residual, scale_ffn, gain_ffn, grad_normed)
    grad_residual = mine(grad_rows).astype(f32) + back
    grad_mixer = head_gather(grad_residual.astype(bf16))

    grad_gated = mm(grad_mixer, w_out_t)
    do, gate_grad_mix, local, part_gain_head = run_gate_backward(
        grad_gated, heads_out, out_gate, gain_head, p
    )
    local_got = exchange(local, SEQ_AXES)
    early = run_chunk_backward_early(pre, scal, rates, taps, marks, docs_row, uw, state, do)
    gq, gtaps_q = early[:2]
    ffn_all = run_row_grads(
        [normed_ffn, group_grads], [gu_grad, product], (((0, 0),), ((1, 1),)), (gq,)
    )
    ffn = lax.psum_scatter(ffn_all, ("x", "z"), scatter_dimension=0, tiled=True)
    adj_out = run_scan_backward(got, local_got, (ffn_all,))
    ffn_out, ffn_got = group_scatter(mm(later(product, local), w_down_t, "ij,kj->ik"))
    adj = exchange(adj_out, SEQ_AXES).reshape(8, DK, DK)
    gkv, gscal, gtaps_kv, grate = run_chunk_backward_late(
        pre, scal, rates, taps, marks, docs_row, x, state, adj, early[2:], (ffn_got,)
    )

    arrays = (normed_all, grad_mixer, gate_grad_mix, gq, gkv, gscal, gated_rows)
    far = run_mixer_grads((2,), 2, *arrays, deps=(ffn_out,))
    blocks = run_mixer_grads((1, 3, 0), 1, *arrays, deps=(far[0],))
    owns, partials = (blocks[2], blocks[5]), []
    for i, axis in enumerate(("x", "z")):
        partials += blocks[3 * i : 3 * i + 2]
        partials += [along(far[2 * i], axis, 1), along(far[2 * i + 1], axis, -1)]

    gtaps = jnp.concatenate([gtaps_q, gtaps_kv], axis=1).reshape(12, inner)
    tail = jnp.concatenate([part_gain_head[:1], grate[:1]], axis=1)
    tail = jnp.pad(tail, ((0, 3), (0, inner - tail.shape[1])))
    small = sum_along(jnp.concatenate([gtaps, tail], axis=0), "x")
    rim = jnp.concatenate([gq[2 * TOK :], gkv[2 * TOK :]], axis=1)
    rim = passed_along(later(rim, blocks[0]), -1)
    input_sent = run_input_grads(
        rim, gq, gkv, gscal, gate_grad_mix, all_left, all_right
    )
    partials, near_gate = reduce_near(owns, partials, (small, input_sent))
    small = sum_along(later(small, near_gate), "z")
    by_core = core_scatter(later(input_sent, near_gate))[0]
    grad_normed_in = chip_scatter(by_core)
    own = mine(tokens).astype(f32)
    back_in = norm_pull(own, row_scale(own), gain_in, grad_normed_in)
    both = jnp.concatenate([residual + ffn_out, grad_residual + back_in], axis=1)
    both = both.astype(bf16)
    partials, cross_gate = reduce_cross(partials, (both, small, ffn))
    small = sum_along(later(small, cross_gate), "y")
    mixer_w = reduce_end(partials, ())
    both = head_gather(later(both, cross_gate))
    outputs, grad_in = both[:, :width], both[:, width:].astype(f32)

    ffn = ffn.reshape(2, -1, 3, span)[..., :units]
    ffn_other = along(pick(ffn, 1 - y_place, 0), "y", 1)
    ffn = ordered(pick(ffn, y_place, 0), ffn_other, y_place, 2).astype(f32)

    rows = width // SEQ
    key_at = 2 * inner + 128
    grad_conv = jnp.transpose(small[:12].reshape(TAPS, 3, inner), (1, 0, 2))

    def gain_grad(gain, weights, grads):
        total = 0.0
        for weight, grad in zip(weights, grads):
            total = total + jnp.sum(weight.astype(f32) * grad, axis=1)
        return total / gain.astype(f32)

    grad_scalar = mixer_w[:, 2 * inner : 2 * inner + 2 * HEADS]
    gain_parts = jnp.concatenate(
        [
            gain_grad(
                norm_in,
                (outgate_weight, query_weight, scalar_weight.reshape(rows, -1), key_weight, value_weight),
                (
                    mixer_w[:, :inner],
                    mixer_w[:, inner : 2 * inner],
                    grad_scalar,
                    mixer_w[:, key_at : key_at + inner],
                    mixer_w[:, key_at + inner : key_at + 2 * inner],
                ),
            ),
            gain_grad(norm_ffn, (gate_weight, up_weight), (ffn[:, 0], ffn[:, 1])),
            small[12, :DK],
        ]
    )
    shared = sum_along(gain_parts[None], "head")[0]
    return (
        outputs.reshape(inputs.shape),
        grad_in.reshape(inputs.shape),
        shared[:rows],
        mixer_w[:, inner : 2 * inner],
        mixer_w[:, key_at : key_at + inner],
        mixer_w[:, key_at + inner : key_at + 2 * inner],
        mixer_w[:, :inner],
        grad_scalar.reshape(rows, 2, HEADS),
        grad_conv,
        small[12, DK + HEADS : DK + 2 * HEADS],
        shared[2 * rows :],
        mixer_w[:, key_at + 2 * inner :].T,
        shared[rows : 2 * rows],
        ffn[:, 0],
        ffn[:, 1],
        ffn[:, 2].T,
    )


def solution(mesh):
    mesh = Mesh(mesh.devices.reshape(4, 4, 2, HEADS), ("x", "z", "y", "head"))
    seq = SEQ_AXES
    weight = P(seq, "head")
    weight_t = P("head", seq)
    tokens = P(None, seq, None)
    scalars = P(seq, None, "head")
    taps = P(None, None, "head")
    return jax.shard_map(
        body,
        mesh=mesh,
        in_specs=(
            tokens, P(), P(seq), weight, weight, weight, weight, scalars, taps, P("head"), P(),
            weight_t, P(seq), weight, weight, weight_t, tokens,
        ),
        out_specs=(
            tokens, tokens, P(seq), weight, weight, weight, weight, scalars, taps, P("head"),
            P(), weight_t, P(seq), weight, weight, weight_t,
        ),
        check_vma=False,
    )
```

time: 1010 us -> 569 us (0.56)
  waiting for transfers between devices: 567 us -> 175 us
  blocking collectives: 127 us -> 0 us
  Pallas kernels: 41.2 us -> 102 us
  starting transfers between devices: 111 us -> 145 us
  matrix products: 60.4 us -> 28.6 us
  local copies, waits for them, and re-layouts: 35 us -> 49.9 us
    all_to_all x12 -> x4, waiting for transfers between devices: 464 us -> 45.3 us  [exchange(): return lax.all_to_all(array, axis, split_axis=0, concat_axis=0, tiled=True)]
    all_to_all x7 -> x0, blocking collectives: 127 us -> none  [exchange(): return lax.all_to_all(array, axis, split_axis=0, concat_axis=0, tiled=True)]
    ppermute x20 -> x68, starting transfers between devices: 30.9 us -> 119 us  [the longest x46 77.6 us: along(): lax.ppermute(array, axis, [(i, (i + by) % count) for i in range(count)])]
    ppermute x20 -> x68, waiting for transfers between devices: 56 us -> 130 us  [the longest x46 82 us: along(): lax.ppermute(array, axis, [(i, (i + by) % count) for i in range(count)])]
    pallas_call x3 -> x15, Pallas kernels: 21.3 us -> 82.3 us  [the longest x7 26.5 us: in_vmem(): pl.pallas_call(ignoring(kernel, 1 + len(arrays), len(deps)), in_specs=[pl...]
    all_to_all x12 -> x4, starting transfers between devices: 79.7 us -> 26.2 us  [exchange(): return lax.all_to_all(array, axis, split_axis=0, concat_axis=0, tiled=True)]
    all_gather x1, waiting for transfers between devices: 46.5 us -> 0.01 us  [body(): w_ffn = lax.all_gather(packed, ('x', 'z'), axis=0, tiled=True)]
    dot_general x14 -> x9, matrix products: 60.4 us -> 28.6 us  [mm(): return jnp.einsum(dims, a, b, preferred_element_type=f32)]
  transfers between devices with their start and end apart: 33 -> 74, of which waited for: 18 -> 34; matrix products, arithmetic and copies ran while one was open for 9% -> 13% of each run, Pallas kernels for 2% -> 12%
where the time goes in v2:
time: 569 us; the launch traced here: 561 us
  waiting for transfers between devices  175 us (31%)
  starting transfers between devices  145 us (25%)
  Pallas kernels  102 us (18%)
  local copies, waits for them, and re-layouts  49.9 us (9%)
  other arithmetic  38.9 us (7%)
  matrix products  28.6 us (5%)
  between operations  20 us (4%)
    ppermute x46, waiting for transfers between devices, along(): lax.ppermute(array, axis, [(i, (i + by) % count) for i in range(count)])  82 us
    ppermute x46, starting transfers between devices, along(): lax.ppermute(array, axis, [(i, (i + by) % count) for i in range(count)])  77.6 us
    all_to_all x4, waiting for transfers between devices, exchange(): return lax.all_to_all(array, axis, split_axis=0, concat_axis=0, tiled=True)  45.3 us
    ppermute x20, waiting for transfers between devices, flipped(): return lax.ppermute(array, axes, [(i, i ^ mask) for i in range(count)])  43.5 us
    ppermute x20, starting transfers between devices, flipped(): return lax.ppermute(array, axes, [(i, i ^ mask) for i in range(count)])  34.5 us
    dot_general x9, matrix products, mm(): return jnp.einsum(dims, a, b, preferred_element_type=f32)  28.6 us
    pallas_call x7, Pallas kernels, in_vmem(): pl.pallas_call(ignoring(kernel, 1 + len(arrays), len(deps)), in_specs=[pl...  26.5 us
    all_to_all x4, starting transfers between devices, exchange(): return lax.all_to_all(array, axis, split_axis=0, concat_axis=0, tiled=True)  26.2 us
  transfers between devices with their start and end apart: 74, of which 34 were waited for; matrix products, arithmetic and copies ran while one was open for 13% of the time, Pallas kernels for 12%

profile of v2, /device:TPU:1, one launch (start us, length us, event | category | flops | bytes accessed | tf_op | source)
XLA Modules:
  0.0 560.5 jit_solution(6273728471244164879)
XLA Ops:
  9.9 3.8 collective-permute-start.1
  15.3 5.6 %collective-permute-done.2.refs_4_ = bf16[64,1280]{1,0:T(8,128)(2,1)S(1)} collective-permute-done((bf16[64,1280]{1,0:T(8,128)(2,1)S(1)}, bf16[64,1280]{1,0:T(8,128)(2,1)S(1)}, u32[]{:S(2)}, u32[]{:S(2)}) %collective-permute-start.2) | collective-permute-done | bytes 163872 | tf_op jit(solution)/shard_map/ppermute | solution.py:797
  30.8 5.8 %collective-permute-done.5.refs_3_.refs_7_ = bf16[128,1280]{1,0:T(8,128)(2,1)S(1)} collective-permute-done((bf16[128,1280]{1,0:T(8,128)(2,1)}, bf16[128,1280]{1,0:T(8,128)(2,1)S(1)}, u32[]{:S(2)}, u32[]{:S(2)}) %collective-permute-start.5) | collective-permute-done | bytes 327712 | tf_op jit(solution)/shard_map/ppermute | solution.py:797
  65.4 3.6 collective-permute-start.26
  69.1 4.0 collective-permute-done.26
  73.2 5.5 collective-permute-start
  78.7 6.7 %collective-permute-done.13.refs_3_ = bf16[4,128,1280]{2,1,0:T(8,128)(2,1)S(1)} collective-permute-done((bf16[4,128,1280]{2,1,0:T(8,128)(2,1)}, bf16[4,128,1280]{2,1,0:T(8,128)(2,1)S(1)}, u32[]{:S(2)}, u32[]{:S(2)}) %collective-permute-start.13) | collective-permute-done | bytes 1310752 | tf_op jit(solution)/shard_map/ppermute | solution.py:797
  88.0 4.2 shard_map.291
  111.9 6.5 %collective-permute-done.17 = bf16[2,128,1280]{2,1,0:T(8,128)(2,1)S(1)} collective-permute-done((bf16[2,128,1280]{2,1,0:T(8,128)(2,1)S(1)}, bf16[2,128,1280]{2,1,0:T(8,128)(2,1)S(1)}, u32[]{:S(2)}, u32[]{:S(2)}) %collective-permute-start.17) | collective-permute-done | bytes 655392 | tf_op jit(solution)/shard_map/ppermute | solution.py:797
  118.4 5.0 collective-permute-done.18
  123.6 6.2 %collective-permute-done.15 = bf16[2,128,1408]{2,1,0:T(8,128)(2,1)S(1)} collective-permute-done((bf16[2,128,1408]{2,1,0:T(8,128)(2,1)S(1)}, bf16[2,128,1408]{2,1,0:T(8,128)(2,1)S(1)}, u32[]{:S(2)}, u32[]{:S(2)}) %collective-permute-start.15) | collective-permute-done | bytes 720928 | tf_op jit(solution)/shard_map/ppermute | solution.py:797
  139.1 11.0 %shard_map.292 = (bf16[32,160,128]{2,1,0:T(8,128)(2,1)}, bf16[8,128,128]{2,1,0:T(8,128)(2,1)}, f32[8,128,128]{2,1,0:T(8,128)}, bf16[8,128,128]{2,1,0:T(8,128)(2,1)}, f32[8,128,256]{2,1,0:T(8,128)}) custom-call(bf16[288,1536]{1,0:T(8,128)(2,1)} %pad_maximum_fusion.7.pre_ref.rim_ref.refs_0_.refs_1_, ...), custom_call_target="tpu_custom_call" | custom-call | flops 10000000000 | bytes 6000000 | tf_op jit(solution)/shard_map/pallas_call | solution.py:548
  150.1 9.6 %all-to-all-start = ((bf16[32,160,128]{2,1,0:T(8,128)(2,1)}), bf16[32,160,128]{2,1,0:T(8,128)(2,1)S(1)}, u32[]{:S(2)}, u32[]{:S(2)}) async-start(bf16[32,160,128]{2,1,0:T(8,128)(2,1)} %get-tuple-element.100), calls=%async_computation | async-start | bytes 2621440 | tf_op jit(solution)/shard_map/all_to_all | solution.py:843
  163.1 27.4 %all-to-all-done.got_ref.refs_0_ = bf16[32,160,128]{2,1,0:T(8,128)(2,1)S(1)} async-done(((bf16[32,160,128]{2,1,0:T(8,128)(2,1)}), bf16[32,160,128]{2,1,0:T(8,128)(2,1)S(1)}, u32[]{:S(2)}, u32[]{:S(2)}) %all-to-all-start) | async-done | bytes 1310752 | tf_op jit(solution)/shard_map/all_to_all | solution.py:843
  191.5 5.9 %shard_map.293 = bf16[32,32,128]{2,1,0:T(8,128)(2,1)} custom-call(bf16[32,160,128]{2,1,0:T(8,128)(2,1)} %copy-done.11), custom_call_target="tpu_custom_call" | custom-call | flops 1000000000 | bytes 3000000 | tf_op jit(solution)/shard_map/pallas_call | solution.py:573
  197.4 7.2 %all-to-all-start.1 = ((bf16[32,32,128]{2,1,0:T(8,128)(2,1)}), bf16[32,32,128]{2,1,0:T(8,128)(2,1)S(1)}, u32[]{:S(2)}, u32[]{:S(2)}) async-start(bf16[32,32,128]{2,1,0:T(8,128)(2,1)} %shard_map.293), calls=%async_computation.1 | async-start | bytes 524288 | tf_op jit(solution)/shard_map/all_to_all | solution.py:843
  208.1 6.0 %all-to-all-done.1 = bf16[32,32,128]{2,1,0:T(8,128)(2,1)S(1)} async-done(((bf16[32,32,128]{2,1,0:T(8,128)(2,1)}), bf16[32,32,128]{2,1,0:T(8,128)(2,1)S(1)}, u32[]{:S(2)}, u32[]{:S(2)}) %all-to-all-start.1) | async-done | bytes 262176 | tf_op jit(solution)/shard_map/all_to_all | solution.py:843
  220.8 6.5 %collective-permute-start.20 = (bf16[2,64,2048]{2,1,0:T(8,128)(2,1)S(1)}, bf16[2,64,2048]{2,1,0:T(8,128)(2,1)S(1)}, u32[]{:S(2)}, u32[]{:S(2)}) collective-permute-start(bf16[2,64,2048]{2,1,0:T(8,128)(2,1)S(1)} %dynamic-slice_bitcast_fusion.3), channel_id=1, source_target_pairs={{0,1},{1,0},{2,3},{3,2},{4,5},{5,4},{6,7},{7,6},{8,9},{9,8},{10,11... | collective-permute-start | bytes 1572872 | tf_op jit(solution)/shard_map/ppermute | solution.py:806
  230.9 7.1 %collective-permute-done.21 = bf16[64,2048]{1,0:T(8,128)(2,1)S(1)} collective-permute-done((bf16[64,2048]{1,0:T(8,128)(2,1)S(1)}, bf16[64,2048]{1,0:T(8,128)(2,1)S(1)}, u32[]{:S(2)}, u32[]{:S(2)}) %collective-permute-start.21) | collective-permute-done | bytes 262176 | tf_op jit(solution)/shard_map/ppermute | solution.py:806
  241.7 4.9 collective-permute-done.22
  250.2 3.6 collective-permute-done.24
  260.5 6.3 %fusion.2 = f32[512,1536]{1,0:T(8,128)S(1)} fusion(bf16[512,2048]{1,0:T(8,128)(2,1)} %bitcast.258, bf16[2048,2304]{1,0:T(8,128)(2,1)} %all-gather.2.cloned.1.call-done), kind=kOutput, calls=%fused_computation.2 | convolution fusion | flops 3221225472 | bytes 11534336 | tf_op jit(solution)/shard_map/ij,jk->ik/dot_general | solution.py:1042
  270.4 3.7 fusion.8
  280.7 6.1 %collective-permute-done.28 = bf16[64,2048]{1,0:T(8,128)(2,1)S(1)} collective-permute-done((bf16[64,2048]{1,0:T(8,128)(2,1)S(1)}, bf16[64,2048]{1,0:T(8,128)(2,1)S(1)}, u32[]{:S(2)}, u32[]{:S(2)}) %collective-permute-start.28) | collective-permute-done | bytes 262176 | tf_op jit(solution)/shard_map/ppermute | solution.py:806
  286.8 3.6 collective-permute-done.29
  294.8 7.1 %collective-permute-done.31 = bf16[64,2048]{1,0:T(8,128)(2,1)} collective-permute-done((bf16[64,2048]{1,0:T(8,128)(2,1)S(1)}, bf16[64,2048]{1,0:T(8,128)(2,1)}, u32[]{:S(2)}, u32[]{:S(2)}) %collective-permute-start.31) | collective-permute-done | bytes 262176 | tf_op jit(solution)/shard_map/ppermute | solution.py:806
  307.7 3.5 fusion.19.gg_ref
  314.1 7.9 %shard_map.296 = (bf16[288,512]{1,0:T(8,128)(2,1)}, f32[4,512]{1,0:T(4,128)}, bf16[8,128,128]{2,1,0:T(8,128)(2,1)}, f32[8,128,128]{2,1,0:T(8,128)}, f32[8,128,12...) custom-call(bf16[288,1536]{1,0:T(8,128)(2,1)} %pad_maximum_fusion.7.pre_ref.rim_ref.refs_0_.refs_1_, ...), custom_call_target="tpu_custom_call" | custom-call | flops 5000000000 | bytes 10000000 | tf_op jit(solution)/shard_map/pallas_call | solution.py:649
  322.0 9.8 %shard_map.297.refs_2_ = bf16[2048,2304]{1,0:T(8,128)(2,1)} custom-call(bf16[512,2048]{1,0:T(8,128)(2,1)} %bitcast.259, bf16[512,2048]{1,0:T(8,128)(2,1)} %pad_maximum_fusion.1.refs_1_, bf16[512,1536]{1,0:T(8,128)(2,1)} %pad_maximum_fusion.3.refs_2_, bf16[512,768]{1,0:T(8,128)(2,1)} %get-tuple-element.264.refs_3_, ...), custom_call_target="tpu_custom_call" | custom-call | flops 4831838208 | bytes 9437184 | tf_op jit(solution)/shard_map/pallas_call | solution.py:729
  333.8 3.7 convolution_convert_fusion
  339.9 4.4 all-to-all-start.2
  346.4 9.0 %all-to-all-done.2.refs_1_ = bf16[32,32,128]{2,1,0:T(8,128)(2,1)S(1)} async-done(((bf16[32,32,128]{2,1,0:T(8,128)(2,1)}), bf16[32,32,128]{2,1,0:T(8,128)(2,1)S(1)}, u32[]{:S(2)}, u32[]{:S(2)}) %all-to-all-start.2) | async-done | bytes 262176 | tf_op jit(solution)/shard_map/all_to_all | solution.py:843
  356.1 5.9 %shard_map.298 = bf16[32,32,128]{2,1,0:T(8,128)(2,1)} custom-call(bf16[32,160,128]{2,1,0:T(8,128)(2,1)} %copy-done.11, bf16[32,32,128]{2,1,0:T(8,128)(2,1)} %copy-done.26, bf16[2048,2304]{1,0:T(8,128)(2,1)} %shard_map.297.refs_2_), custom_call_target="tpu_custom_call" | custom-call | flops 1000000000 | bytes 3000000 | tf_op jit(solution)/shard_map/pallas_call | solution.py:583
  362.1 4.9 all-to-all-start.3
  377.5 10.3 %shard_map.299 = (bf16[288,1024]{1,0:T(8,128)(2,1)}, bf16[256,128]{1,0:T(8,128)(2,1)}, f32[4,1024]{1,0:T(4,128)}, f32[8,128]{1,0:T(8,128)}) custom-call(bf16[288,1536]{1,0:T(8,128)(2,1)} %pad_maximum_fusion.7.pre_ref.rim_ref.refs_0_.refs_1_, bf16[288,1536]{1,0:T(8,128)(2,1)} %pad_maximum_fusion.7.pre_ref.rim_ref.refs_0_.refs_1_, ...), custom_call_target="tpu_custom_call" | custom-call | flops 5000000000 | bytes 10000000 | tf_op jit(solution)/shard_map/pallas_call | solution.py:690
  389.6 3.5 collective-permute-start.43
  396.0 4.4 shard_map.300
  403.2 7.5 %shard_map.301 = (bf16[512,1408]{1,0:T(8,128)(2,1)}, bf16[512,1408]{1,0:T(8,128)(2,1)}, bf16[512,1408]{1,0:T(8,128)(2,1)}, bf16[512,1280]{1,0:T(8,128)(2,1)}, bf...) custom-call(s32[2]{0:T(128)} %pad_add_fusion.1.refs_0_, bf16[288,2048]{1,0:T(8,128)(2,1)} %copy-done.24, ...), custom_call_target="tpu_custom_call" | custom-call | flops 2684354560 | bytes 10485760 | tf_op jit(solution)/shard_map/pallas_call | solution.py:752
  417.5 4.7 collective-permute-done.37.rim_ref
  422.8 7.5 %shard_map.302.refs_10_ = bf16[256,2048]{1,0:T(8,128)(2,1)} custom-call(bf16[32,1536]{1,0:T(8,128)(2,1)} %copy-done.64, bf16[288,512]{1,0:T(8,128)(2,1)} %get-tuple-element.106.refs_4_.gq_ref, bf16[288,1024]{1,0:T(8,128)(2,1)} %get-tuple-element.113.refs_5_.gkv_ref, bf16[256,128]{1,0:T(8,128)(2,1)} %get-tuple-element.115.refs_6_.gscal_ref, ...), custom_call_target="tpu_custom_call" | custom-call | flops 2684354560 | bytes 10485760 | tf_op jit(solution)/shard_map/pallas_call | solution.py:767
  432.3 6.1 %shard_map.303 = (bf16[512,1408]{1,0:T(8,128)(2,1)}, bf16[512,1408]{1,0:T(8,128)(2,1)}, bf16[512,1280]{1,0:T(8,128)(2,1)}, bf16[512,1280]{1,0:T(8,128)(2,1)}) custom-call(s32[3]{0:T(128)} %pad_add_fusion.refs_0_, bf16[512,1408]{1,0:T(8,128)(2,1)} %get-tuple-element.117.refs_1_, bf16[512,1408]{1,0:T(8,128)(2,1)} %get-tuple-element.118.refs_2_, ...), custom_call_target="tpu_custom_call" | custom-call | flops 8257536 | bytes 8257536 | tf_op jit(solution)/shard_map/pallas_call | solution.py:905
  441.2 6.4 %collective-permute-start.45 = (bf16[2,64,2048]{2,1,0:T(8,128)(2,1)}, bf16[2,64,2048]{2,1,0:T(8,128)(2,1)}, u32[]{:S(2)}, u32[]{:S(2)}) collective-permute-start(bf16[2,64,2048]{2,1,0:T(8,128)(2,1)} %dynamic-slice_bitcast_fusion.2), channel_id=1, source_target_pairs={{0,1},{1,0},{2,3},{3,2},{4,5},{5,4},{6,7},{7,6},{8,9},{9,8},{10,11... | collective-permute-start | bytes 1572872 | tf_op jit(solution)/shard_map/ppermute | solution.py:806
  460.6 24.8 %collective-permute-done.49.refs_5_ = bf16[512,1280]{1,0:T(8,128)(2,1)} collective-permute-done((bf16[512,1280]{1,0:T(8,128)(2,1)}, bf16[512,1280]{1,0:T(8,128)(2,1)}, u32[]{:S(2)}, u32[]{:S(2)}) %collective-permute-start.49) | collective-permute-done | bytes 1310752 | tf_op jit(solution)/shard_map/ppermute | solution.py:797
  486.6 5.6 shard_map.304
  498.1 6.9 %collective-permute-start.64 = (f32[16,512]{1,0:T(8,128)S(1)}, f32[16,512]{1,0:T(8,128)S(1)}, u32[]{:S(2)}, u32[]{:S(2)}) collective-permute-start(f32[16,512]{1,0:T(8,128)S(1)} %broadcast_add_fusion.2), channel_id=1, source_target_pairs={{0,4},{4,0},{1,5},{5,1},{2,6},{6,2},{3,7},{7,3},{8,12},{12,8},{9,1... | collective-permute-start | bytes 98312 | tf_op jit(solution)/shard_map/ppermute | solution.py:797
  518.6 4.0 collective-permute-done.61.refs_8_
  530.3 7.9 %collective-permute-start.55 = (bf16[2,64,4096]{2,1,0:T(8,128)(2,1)S(1)}, bf16[2,64,4096]{2,1,0:T(8,128)(2,1)S(1)}, u32[]{:S(2)}, u32[]{:S(2)}) collective-permute-start(bf16[2,64,4096]{2,1,0:T(8,128)(2,1)S(1)} %pad_maximum_fusion.6), channel_id=1, source_target_pairs={{0,1},{1,0},{2,3},{3,2},{4,5},{5,4},{6,7},{7,6},{8,9},{9,8},{10,11... | collective-permute-start | bytes 3145736 | tf_op jit(solution)/shard_map/ppermute | solution.py:806
  539.5 5.3 collective-permute-start.65
  (444 shorter events, 213.5 us)
Async XLA Ops:
  7.2 253.3 %all-gather.2.cloned.1.call-start = ((), (), s32[]{:S(2)}) async-start(), calls=%async_computation.5 | async-start | bytes 10027008 | tf_op jit(solution)/shard_map/all_gather | solution.py:1121
  9.9 11.1 %collective-permute-start.1 = (bf16[64,1408]{1,0:T(8,128)(2,1)S(1)}, bf16[64,1408]{1,0:T(8,128)(2,1)S(1)}, u32[]{:S(2)}, u32[]{:S(2)}) collective-permute-start(bf16[64,1408]{1,0:T(8,128)(2,1)S(1)} %fusion.59.refs_1_), channel_id=1, source_target_pairs={{0,4},{4,0},{1,5},{5,1},{2,6},{6,2},{3,7},{7,3},{8,12},{12,8},{9,1... | collective-permute-start | bytes 540680 | tf_op jit(solution)/shard_map/ppermute | solution.py:797
  24.4 12.3 %collective-permute-start.3 = (bf16[128,1408]{1,0:T(8,128)(2,1)}, bf16[128,1408]{1,0:T(8,128)(2,1)S(1)}, u32[]{:S(2)}, u32[]{:S(2)}) collective-permute-start(bf16[128,1408]{1,0:T(8,128)(2,1)} %get-tuple-element.86.refs_1_), channel_id=1, source_target_pairs={{0,32},{32,64},{64,96},{96,0},{1,33},{33,65},{65,97},{97,1},{2,34}... | collective-permute-start | bytes 1081352 | tf_op jit(solution)/shard_map/ppermute | solution.py:797
  25.6 11.1 %collective-permute-start.4 = (bf16[128,1408]{1,0:T(8,128)(2,1)}, bf16[128,1408]{1,0:T(8,128)(2,1)S(1)}, u32[]{:S(2)}, u32[]{:S(2)}) collective-permute-start(bf16[128,1408]{1,0:T(8,128)(2,1)} %get-tuple-element.86.refs_1_), channel_id=1, source_target_pairs={{0,96},{32,0},{64,32},{96,64},{1,97},{33,1},{65,33},{97,65},{2,98}... | collective-permute-start | bytes 1081352 | tf_op jit(solution)/shard_map/ppermute | solution.py:797
  40.4 10.6 %collective-permute-start.7 = (bf16[64,1408]{1,0:T(8,128)(2,1)}, bf16[64,1408]{1,0:T(8,128)(2,1)S(1)}, u32[]{:S(2)}, u32[]{:S(2)}) collective-permute-start(bf16[64,1408]{1,0:T(8,128)(2,1)} %get-tuple-element.88), channel_id=1, source_target_pairs={{0,32},{32,64},{64,96},{96,0},{1,33},{33,65},{65,97},{97,1},{2,34}... | collective-permute-start | bytes 540680 | tf_op jit(solution)/shard_map/ppermute | solution.py:797
  40.4 10.6 %collective-permute-start.8 = (bf16[64,1408]{1,0:T(8,128)(2,1)}, bf16[64,1408]{1,0:T(8,128)(2,1)S(1)}, u32[]{:S(2)}, u32[]{:S(2)}) collective-permute-start(bf16[64,1408]{1,0:T(8,128)(2,1)} %get-tuple-element.89), channel_id=1, source_target_pairs={{0,96},{32,0},{64,32},{96,64},{1,97},{33,1},{65,33},{97,65},{2,98}... | collective-permute-start | bytes 540680 | tf_op jit(solution)/shard_map/ppermute | solution.py:797
  55.9 29.5 %collective-permute-start.11 = (bf16[4,128,1408]{2,1,0:T(8,128)(2,1)}, bf16[4,128,1408]{2,1,0:T(8,128)(2,1)}, u32[]{:S(2)}, u32[]{:S(2)}) collective-permute-start(bf16[4,128,1408]{2,1,0:T(8,128)(2,1)} %get-tuple-element.92), channel_id=1, source_target_pairs={{0,8},{8,16},{16,24},{24,0},{1,9},{9,17},{17,25},{25,1},{2,10},{10... | collective-permute-start | bytes 4325384 | tf_op jit(solution)/shard_map/ppermute | solution.py:797
  55.9 29.5 %collective-permute-start.12 = (bf16[4,128,1408]{2,1,0:T(8,128)(2,1)}, bf16[4,128,1408]{2,1,0:T(8,128)(2,1)S(1)}, u32[]{:S(2)}, u32[]{:S(2)}) collective-permute-start(bf16[4,128,1408]{2,1,0:T(8,128)(2,1)} %get-tuple-element.92), channel_id=1, source_target_pairs={{0,24},{8,0},{16,8},{24,16},{1,25},{9,1},{17,9},{25,17},{2,26},{10... | collective-permute-start | bytes 4325384 | tf_op jit(solution)/shard_map/ppermute | solution.py:797
  59.5 25.9 %collective-permute-start.13 = (bf16[4,128,1280]{2,1,0:T(8,128)(2,1)}, bf16[4,128,1280]{2,1,0:T(8,128)(2,1)S(1)}, u32[]{:S(2)}, u32[]{:S(2)}) collective-permute-start(bf16[4,128,1280]{2,1,0:T(8,128)(2,1)} %get-tuple-element.93), channel_id=1, source_target_pairs={{0,32},{32,64},{64,96},{96,0},{1,33},{33,65},{65,97},{97,1},{2,34}... | collective-permute-start | bytes 3932168 | tf_op jit(solution)/shard_map/ppermute | solution.py:797
  59.5 25.9 %collective-permute-start.14 = (bf16[4,128,1280]{2,1,0:T(8,128)(2,1)}, bf16[4,128,1280]{2,1,0:T(8,128)(2,1)S(1)}, u32[]{:S(2)}, u32[]{:S(2)}) collective-permute-start(bf16[4,128,1280]{2,1,0:T(8,128)(2,1)} %get-tuple-element.93), channel_id=1, source_target_pairs={{0,96},{32,0},{64,32},{96,64},{1,97},{33,1},{65,33},{97,65},{2,98}... | collective-permute-start | bytes 3932168 | tf_op jit(solution)/shard_map/ppermute | solution.py:797
  73.2 28.0 %collective-permute-start = (bf16[2,16,2048]{2,1,0:T(8,128)(2,1)S(1)}, bf16[2,16,2048]{2,1,0:T(8,128)(2,1)S(1)}, u32[]{:S(2)}, u32[]{:S(2)}) collective-permute-start(bf16[2,16,2048]{2,1,0:T(8,128)(2,1)S(1)} %slice.200), channel_id=1, source_target_pairs={{0,4},{4,8},{8,12},{12,16},{16,20},{20,24},{24,28},{28,32},{32,36}... | collective-permute-start | bytes 393224 | tf_op jit(solution)/shard_map/ppermute | solution.py:792
  104.6 13.7 %collective-permute-start.17 = (bf16[2,128,1280]{2,1,0:T(8,128)(2,1)S(1)}, bf16[2,128,1280]{2,1,0:T(8,128)(2,1)S(1)}, u32[]{:S(2)}, u32[]{:S(2)}) collective-permute-start(bf16[2,128,1280]{2,1,0:T(8,128)(2,1)S(1)} %copy-done.76), channel_id=1, source_target_pairs={{0,32},{32,64},{64,96},{96,0},{1,33},{33,65},{65,97},{97,1},{2,34}... | collective-permute-start | bytes 1966088 | tf_op jit(solution)/shard_map/ppermute | solution.py:797
  104.8 18.5 %collective-permute-start.18 = (bf16[2,128,1280]{2,1,0:T(8,128)(2,1)S(1)}, bf16[2,128,1280]{2,1,0:T(8,128)(2,1)S(1)}, u32[]{:S(2)}, u32[]{:S(2)}) collective-permute-start(bf16[2,128,1280]{2,1,0:T(8,128)(2,1)S(1)} %copy-done.75), channel_id=1, source_target_pairs={{0,96},{32,0},{64,32},{96,64},{1,97},{33,1},{65,33},{97,65},{2,98}... | collective-permute-start | bytes 1966088 | tf_op jit(solution)/shard_map/ppermute | solution.py:797
  107.5 22.3 %collective-permute-start.15 = (bf16[2,128,1408]{2,1,0:T(8,128)(2,1)S(1)}, bf16[2,128,1408]{2,1,0:T(8,128)(2,1)S(1)}, u32[]{:S(2)}, u32[]{:S(2)}) collective-permute-start(bf16[2,128,1408]{2,1,0:T(8,128)(2,1)S(1)} %copy-done.74), channel_id=1, source_target_pairs={{0,8},{8,16},{16,24},{24,0},{1,9},{9,17},{17,25},{25,1},{2,10},{10... | collective-permute-start | bytes 2162696 | tf_op jit(solution)/shard_map/ppermute | solution.py:797
  107.6 24.3 %collective-permute-start.16 = (bf16[2,128,1408]{2,1,0:T(8,128)(2,1)S(1)}, bf16[2,128,1408]{2,1,0:T(8,128)(2,1)S(1)}, u32[]{:S(2)}, u32[]{:S(2)}) collective-permute-start(bf16[2,128,1408]{2,1,0:T(8,128)(2,1)S(1)} %copy-done.73), channel_id=1, source_target_pairs={{0,24},{8,0},{16,8},{24,16},{1,25},{9,1},{17,9},{25,17},{2,26},{10... | collective-permute-start | bytes 2162696 | tf_op jit(solution)/shard_map/ppermute | solution.py:797
  150.1 40.3 %all-to-all-start = ((bf16[32,160,128]{2,1,0:T(8,128)(2,1)}), bf16[32,160,128]{2,1,0:T(8,128)(2,1)S(1)}, u32[]{:S(2)}, u32[]{:S(2)}) async-start(bf16[32,160,128]{2,1,0:T(8,128)(2,1)} %get-tuple-element.100), calls=%async_computation | async-start | bytes 2621440 | tf_op jit(solution)/shard_map/all_to_all | solution.py:843
  159.7 48.4 %collective-permute-start.19 = (bf16[256,2048]{1,0:T(8,128)(2,1)S(1)}, bf16[256,2048]{1,0:T(8,128)(2,1)}, u32[]{:S(2)}, u32[]{:S(2)}) collective-permute-start(bf16[256,2048]{1,0:T(8,128)(2,1)S(1)} %bitcast.261), channel_id=1, source_target_pairs={{0,4},{4,0},{1,5},{5,1},{2,6},{6,2},{3,7},{7,3},{8,12},{12,8},{9,1... | collective-permute-start | bytes 3145736 | tf_op jit(solution)/shard_map/ppermute | solution.py:797
  197.4 16.8 %all-to-all-start.1 = ((bf16[32,32,128]{2,1,0:T(8,128)(2,1)}), bf16[32,32,128]{2,1,0:T(8,128)(2,1)S(1)}, u32[]{:S(2)}, u32[]{:S(2)}) async-start(bf16[32,32,128]{2,1,0:T(8,128)(2,1)} %shard_map.293), calls=%async_computation.1 | async-start | bytes 524288 | tf_op jit(solution)/shard_map/all_to_all | solution.py:843
  204.7 281.9 %reduce-scatter.2.cloned.1.call-start = ((), (), s32[]{:S(2)}) async-start(), calls=%async_computation.6 | async-start | bytes 10027008 | tf_op jit(solution)/shard_map/reduce_scatter | solution.py:1193
  239.1 11.1 %collective-permute-start.23 = (bf16[64,2048]{1,0:T(8,128)(2,1)S(1)}, bf16[64,2048]{1,0:T(8,128)(2,1)S(1)}, u32[]{:S(2)}, u32[]{:S(2)}) collective-permute-start(bf16[64,2048]{1,0:T(8,128)(2,1)S(1)} %multiply_convert_fusion.3), channel_id=1, source_target_pairs={{0,2},{1,3},{2,0},{3,1},{4,6},{5,7},{6,4},{7,5},{8,10},{9,11},{10,... | collective-permute-start | bytes 786440 | tf_op jit(solution)/shard_map/ppermute | solution.py:806
  239.5 14.4 %collective-permute-start.24 = (bf16[64,2048]{1,0:T(8,128)(2,1)S(1)}, bf16[64,2048]{1,0:T(8,128)(2,1)S(1)}, u32[]{:S(2)}, u32[]{:S(2)}) collective-permute-start(bf16[64,2048]{1,0:T(8,128)(2,1)S(1)} %multiply_convert_fusion.3), channel_id=1, source_target_pairs={{0,6},{1,7},{2,4},{3,5},{4,2},{5,3},{6,0},{7,1},{8,14},{9,15},{10,... | collective-permute-start | bytes 786440 | tf_op jit(solution)/shard_map/ppermute | solution.py:806
  278.5 11.9 %collective-permute-start.29 = (bf16[64,2048]{1,0:T(8,128)(2,1)S(1)}, bf16[64,2048]{1,0:T(8,128)(2,1)S(1)}, u32[]{:S(2)}, u32[]{:S(2)}) collective-permute-start(bf16[64,2048]{1,0:T(8,128)(2,1)S(1)} %get-tuple-element.274), channel_id=1, source_target_pairs={{0,2},{1,3},{2,0},{3,1},{4,6},{5,7},{6,4},{7,5},{8,10},{9,11},{10,... | collective-permute-start | bytes 786440 | tf_op jit(solution)/shard_map/ppermute | solution.py:806
  278.5 14.3 %collective-permute-start.30 = (bf16[64,2048]{1,0:T(8,128)(2,1)S(1)}, bf16[64,2048]{1,0:T(8,128)(2,1)S(1)}, u32[]{:S(2)}, u32[]{:S(2)}) collective-permute-start(bf16[64,2048]{1,0:T(8,128)(2,1)S(1)} %get-tuple-element.273), channel_id=1, source_target_pairs={{0,6},{1,7},{2,4},{3,5},{4,2},{5,3},{6,0},{7,1},{8,14},{9,15},{10,... | collective-permute-start | bytes 786440 | tf_op jit(solution)/shard_map/ppermute | solution.py:806
  339.9 27.1 %collective-permute-start.33 = (bf16[4,64,2048]{2,1,0:T(8,128)(2,1)}, bf16[4,64,2048]{2,1,0:T(8,128)(2,1)S(1)}, u32[]{:S(2)}, u32[]{:S(2)}) collective-permute-start(bf16[4,64,2048]{2,1,0:T(8,128)(2,1)} %dynamic-slice_bitcast_fusion), channel_id=1, source_target_pairs={{0,1},{1,0},{2,3},{3,2},{4,5},{5,4},{6,7},{7,6},{8,9},{9,8},{10,11... | collective-permute-start | bytes 3145736 | tf_op jit(solution)/shard_map/ppermute | solution.py:806
  339.9 15.5 %all-to-all-start.2 = ((bf16[32,32,128]{2,1,0:T(8,128)(2,1)}), bf16[32,32,128]{2,1,0:T(8,128)(2,1)S(1)}, u32[]{:S(2)}, u32[]{:S(2)}) async-start(bf16[32,32,128]{2,1,0:T(8,128)(2,1)} %get-tuple-element.103), calls=%async_computation.2 | async-start | bytes 524288 | tf_op jit(solution)/shard_map/all_to_all | solution.py:843
  362.1 15.4 %all-to-all-start.3 = ((bf16[32,32,128]{2,1,0:T(8,128)(2,1)}), bf16[32,32,128]{2,1,0:T(8,128)(2,1)}, u32[]{:S(2)}, u32[]{:S(2)}) async-start(bf16[32,32,128]{2,1,0:T(8,128)(2,1)} %shard_map.298), calls=%async_computation.3 | async-start | bytes 524288 | tf_op jit(solution)/shard_map/all_to_all | solution.py:843
  371.2 22.7 %collective-permute-start.34 = (bf16[64,2048]{1,0:T(8,128)(2,1)}, bf16[64,2048]{1,0:T(8,128)(2,1)S(1)}, u32[]{:S(2)}, u32[]{:S(2)}) collective-permute-start(bf16[64,2048]{1,0:T(8,128)(2,1)} %get-tuple-element.269), channel_id=1, source_target_pairs={{0,4},{1,5},{2,6},{3,7},{4,0},{5,1},{6,2},{7,3},{8,12},{9,13},{10,... | collective-permute-start | bytes 786440 | tf_op jit(solution)/shard_map/ppermute | solution.py:806
  373.9 20.1 %collective-permute-start.35 = (bf16[64,2048]{1,0:T(8,128)(2,1)}, bf16[64,2048]{1,0:T(8,128)(2,1)S(1)}, u32[]{:S(2)}, u32[]{:S(2)}) collective-permute-start(bf16[64,2048]{1,0:T(8,128)(2,1)} %get-tuple-element.271), channel_id=1, source_target_pairs={{0,2},{1,3},{2,0},{3,1},{4,6},{5,7},{6,4},{7,5},{8,10},{9,11},{10,... | collective-permute-start | bytes 786440 | tf_op jit(solution)/shard_map/ppermute | solution.py:806
  374.1 19.9 %collective-permute-start.36 = (bf16[64,2048]{1,0:T(8,128)(2,1)S(1)}, bf16[64,2048]{1,0:T(8,128)(2,1)}, u32[]{:S(2)}, u32[]{:S(2)}) collective-permute-start(bf16[64,2048]{1,0:T(8,128)(2,1)S(1)} %get-tuple-element.270), channel_id=1, source_target_pairs={{0,6},{1,7},{2,4},{3,5},{4,2},{5,3},{6,0},{7,1},{8,14},{9,15},{10,... | collective-permute-start | bytes 786440 | tf_op jit(solution)/shard_map/ppermute | solution.py:806
  389.3 23.2 %collective-permute-start.42 = (f32[16,512]{1,0:T(8,128)S(1)}, f32[16,512]{1,0:T(8,128)S(1)}, u32[]{:S(2)}, u32[]{:S(2)}) collective-permute-start(f32[16,512]{1,0:T(8,128)S(1)} %pad_maximum_fusion.11), channel_id=1, source_target_pairs={{0,32},{32,64},{64,96},{96,0},{1,33},{33,65},{65,97},{97,1},{2,34}... | collective-permute-start | bytes 98312 | tf_op jit(solution)/shard_map/ppermute | solution.py:797
  389.6 23.8 %collective-permute-start.43 = (f32[16,512]{1,0:T(8,128)S(1)}, f32[16,512]{1,0:T(8,128)S(1)}, u32[]{:S(2)}, u32[]{:S(2)}) collective-permute-start(f32[16,512]{1,0:T(8,128)S(1)} %pad_maximum_fusion.11), channel_id=1, source_target_pairs={{0,64},{32,96},{64,0},{96,32},{1,65},{33,97},{65,1},{97,33},{2,66}... | collective-permute-start | bytes 98312 | tf_op jit(solution)/shard_map/ppermute | solution.py:797
  393.9 21.3 %collective-permute-start.44 = (f32[16,512]{1,0:T(8,128)S(1)}, f32[16,512]{1,0:T(8,128)S(1)}, u32[]{:S(2)}, u32[]{:S(2)}) collective-permute-start(f32[16,512]{1,0:T(8,128)S(1)} %pad_maximum_fusion.11), channel_id=1, source_target_pairs={{0,96},{32,0},{64,32},{96,64},{1,97},{33,1},{65,33},{97,65},{2,98}... | collective-permute-start | bytes 98312 | tf_op jit(solution)/shard_map/ppermute | solution.py:797
  400.5 30.3 %collective-permute-start.38 = (bf16[256,1408]{1,0:T(8,128)(2,1)}, bf16[256,1408]{1,0:T(8,128)(2,1)S(1)}, u32[]{:S(2)}, u32[]{:S(2)}) collective-permute-start(bf16[256,1408]{1,0:T(8,128)(2,1)} %get-tuple-element.116.refs_8_), channel_id=1, source_target_pairs={{0,32},{32,64},{64,96},{96,0},{1,33},{33,65},{65,97},{97,1},{2,34}... | collective-permute-start | bytes 2162696 | tf_op jit(solution)/shard_map/ppermute | solution.py:797
  401.9 28.8 %collective-permute-start.39 = (bf16[256,1408]{1,0:T(8,128)(2,1)}, bf16[256,1408]{1,0:T(8,128)(2,1)S(1)}, u32[]{:S(2)}, u32[]{:S(2)}) collective-permute-start(bf16[256,1408]{1,0:T(8,128)(2,1)} %get-tuple-element.119), channel_id=1, source_target_pairs={{0,96},{32,0},{64,32},{96,64},{1,97},{33,1},{65,33},{97,65},{2,98}... | collective-permute-start | bytes 2162696 | tf_op jit(solution)/shard_map/ppermute | solution.py:797
  412.5 18.2 %collective-permute-start.40 = (bf16[256,1280]{1,0:T(8,128)(2,1)S(1)}, bf16[256,1280]{1,0:T(8,128)(2,1)S(1)}, u32[]{:S(2)}, u32[]{:S(2)}) collective-permute-start(bf16[256,1280]{1,0:T(8,128)(2,1)S(1)} %copy-done.78), channel_id=1, source_target_pairs={{0,8},{8,16},{16,24},{24,0},{1,9},{9,17},{17,25},{25,1},{2,10},{10... | collective-permute-start | bytes 1966088 | tf_op jit(solution)/shard_map/ppermute | solution.py:797
  413.4 17.3 %collective-permute-start.41 = (bf16[256,1280]{1,0:T(8,128)(2,1)S(1)}, bf16[256,1280]{1,0:T(8,128)(2,1)S(1)}, u32[]{:S(2)}, u32[]{:S(2)}) collective-permute-start(bf16[256,1280]{1,0:T(8,128)(2,1)S(1)} %copy-done.77), channel_id=1, source_target_pairs={{0,24},{8,0},{16,8},{24,16},{1,25},{9,1},{17,9},{25,17},{2,26},{10... | collective-permute-start | bytes 1966088 | tf_op jit(solution)/shard_map/ppermute | solution.py:797
  441.2 9.8 %collective-permute-start.45 = (bf16[2,64,2048]{2,1,0:T(8,128)(2,1)}, bf16[2,64,2048]{2,1,0:T(8,128)(2,1)}, u32[]{:S(2)}, u32[]{:S(2)}) collective-permute-start(bf16[2,64,2048]{2,1,0:T(8,128)(2,1)} %dynamic-slice_bitcast_fusion.2), channel_id=1, source_target_pairs={{0,1},{1,0},{2,3},{3,2},{4,5},{5,4},{6,7},{7,6},{8,9},{9,8},{10,11... | collective-permute-start | bytes 1572872 | tf_op jit(solution)/shard_map/ppermute | solution.py:806
  452.2 33.9 %collective-permute-start.47 = (bf16[512,1408]{1,0:T(8,128)(2,1)}, bf16[512,1408]{1,0:T(8,128)(2,1)}, u32[]{:S(2)}, u32[]{:S(2)}) collective-permute-start(bf16[512,1408]{1,0:T(8,128)(2,1)} %get-tuple-element.128), channel_id=1, source_target_pairs={{0,32},{32,64},{64,96},{96,0},{1,33},{33,65},{65,97},{97,1},{2,34}... | collective-permute-start | bytes 4325384 | tf_op jit(solution)/shard_map/ppermute | solution.py:797
  454.5 32.1 %collective-permute-start.48 = (bf16[512,1408]{1,0:T(8,128)(2,1)S(1)}, bf16[512,1408]{1,0:T(8,128)(2,1)}, u32[]{:S(2)}, u32[]{:S(2)}) collective-permute-start(bf16[512,1408]{1,0:T(8,128)(2,1)S(1)} %copy-done.72), channel_id=1, source_target_pairs={{0,96},{32,0},{64,32},{96,64},{1,97},{33,1},{65,33},{97,65},{2,98}... | collective-permute-start | bytes 4325384 | tf_op jit(solution)/shard_map/ppermute | solution.py:797
  455.0 30.4 %collective-permute-start.49 = (bf16[512,1280]{1,0:T(8,128)(2,1)}, bf16[512,1280]{1,0:T(8,128)(2,1)}, u32[]{:S(2)}, u32[]{:S(2)}) collective-permute-start(bf16[512,1280]{1,0:T(8,128)(2,1)} %get-tuple-element.132), channel_id=1, source_target_pairs={{0,8},{8,16},{16,24},{24,0},{1,9},{9,17},{17,25},{25,1},{2,10},{10... | collective-permute-start | bytes 3932168 | tf_op jit(solution)/shard_map/ppermute | solution.py:797
  455.2 30.2 %collective-permute-start.50 = (bf16[512,1280]{1,0:T(8,128)(2,1)}, bf16[512,1280]{1,0:T(8,128)(2,1)}, u32[]{:S(2)}, u32[]{:S(2)}) collective-permute-start(bf16[512,1280]{1,0:T(8,128)(2,1)} %get-tuple-element.133), channel_id=1, source_target_pairs={{0,24},{8,0},{16,8},{24,16},{1,25},{9,1},{17,9},{25,17},{2,26},{10... | collective-permute-start | bytes 3932168 | tf_op jit(solution)/shard_map/ppermute | solution.py:797
  494.1 28.5 %collective-permute-start.56 = (bf16[128,1408]{1,0:T(8,128)(2,1)}, bf16[128,1408]{1,0:T(8,128)(2,1)S(1)}, u32[]{:S(2)}, u32[]{:S(2)}) collective-permute-start(bf16[128,1408]{1,0:T(8,128)(2,1)} %get-tuple-element.135), channel_id=1, source_target_pairs={{0,16},{8,24},{16,0},{24,8},{1,17},{9,25},{17,1},{25,9},{2,18},{10... | collective-permute-start | bytes 1081352 | tf_op jit(solution)/shard_map/ppermute | solution.py:797
  496.3 26.3 %collective-permute-start.57 = (bf16[128,1408]{1,0:T(8,128)(2,1)}, bf16[128,1408]{1,0:T(8,128)(2,1)S(1)}, u32[]{:S(2)}, u32[]{:S(2)}) collective-permute-start(bf16[128,1408]{1,0:T(8,128)(2,1)} %get-tuple-element.136), channel_id=1, source_target_pairs={{0,8},{8,16},{16,24},{24,0},{1,9},{9,17},{17,25},{25,1},{2,10},{10... | collective-permute-start | bytes 1081352 | tf_op jit(solution)/shard_map/ppermute | solution.py:797
  496.3 20.1 %collective-permute-start.59 = (bf16[128,1280]{1,0:T(8,128)(2,1)}, bf16[128,1280]{1,0:T(8,128)(2,1)S(1)}, u32[]{:S(2)}, u32[]{:S(2)}) collective-permute-start(bf16[128,1280]{1,0:T(8,128)(2,1)} %get-tuple-element.139), channel_id=1, source_target_pairs={{0,64},{32,96},{64,0},{96,32},{1,65},{33,97},{65,1},{97,33},{2,66}... | collective-permute-start | bytes 983048 | tf_op jit(solution)/shard_map/ppermute | solution.py:797
  497.4 20.0 %collective-permute-start.60 = (bf16[128,1280]{1,0:T(8,128)(2,1)}, bf16[128,1280]{1,0:T(8,128)(2,1)}, u32[]{:S(2)}, u32[]{:S(2)}) collective-permute-start(bf16[128,1280]{1,0:T(8,128)(2,1)} %get-tuple-element.140), channel_id=1, source_target_pairs={{0,32},{32,64},{64,96},{96,0},{1,33},{33,65},{65,97},{97,1},{2,34}... | collective-permute-start | bytes 983048 | tf_op jit(solution)/shard_map/ppermute | solution.py:797
  517.4 12.6 %collective-permute-start.54 = (bf16[64,4096]{1,0:T(8,128)(2,1)S(1)}, bf16[64,4096]{1,0:T(8,128)(2,1)S(1)}, u32[]{:S(2)}, u32[]{:S(2)}) collective-permute-start(bf16[64,4096]{1,0:T(8,128)(2,1)S(1)} %broadcast_add_fusion.1), channel_id=1, source_target_pairs={{0,2},{1,3},{2,0},{3,1},{4,6},{5,7},{6,4},{7,5},{8,10},{9,11},{10,... | collective-permute-start | bytes 1572872 | tf_op jit(solution)/shard_map/ppermute | solution.py:806
  526.6 11.5 %collective-permute-start.62 = (bf16[64,2688]{1,0:T(8,128)(2,1)}, bf16[64,2688]{1,0:T(8,128)(2,1)S(1)}, u32[]{:S(2)}, u32[]{:S(2)}) collective-permute-start(bf16[64,2688]{1,0:T(8,128)(2,1)} %get-tuple-element.143), channel_id=1, source_target_pairs={{0,4},{4,0},{1,5},{5,1},{2,6},{6,2},{3,7},{7,3},{8,12},{12,8},{9,1... | collective-permute-start | bytes 1032200 | tf_op jit(solution)/shard_map/ppermute | solution.py:797
  530.3 19.8 %collective-permute-start.55 = (bf16[2,64,4096]{2,1,0:T(8,128)(2,1)S(1)}, bf16[2,64,4096]{2,1,0:T(8,128)(2,1)S(1)}, u32[]{:S(2)}, u32[]{:S(2)}) collective-permute-start(bf16[2,64,4096]{2,1,0:T(8,128)(2,1)S(1)} %pad_maximum_fusion.6), channel_id=1, source_target_pairs={{0,1},{1,0},{2,3},{3,2},{4,5},{5,4},{6,7},{7,6},{8,9},{9,8},{10,11... | collective-permute-start | bytes 3145736 | tf_op jit(solution)/shard_map/ppermute | solution.py:806
  (109 other events, 701.2 us)
Sparse Core Ops, SparseCore 0:
  95.2 100.5 all-gather.1
  332.0 92.0 reduce-scatter.1

commit v3 on v2

--- a/solution.py
+++ b/solution.py
@@ -642,19 +642,20 @@
     )(gg, heads_out, og, gain, p)
 
 
-def run_chunk_backward_early(pre, scal, rates, taps, marks, docs, uw, state, do):
+def run_chunk_backward_early(pre, scal, rates, taps, marks, docs, uw, state, do, deps):
     inner = HEADS * DK
     wide = 3 * inner
     square = jax.ShapeDtypeStruct((8, TOK, DK), f32)
     return pl.pallas_call(
-        chunk_backward_early,
+        ignoring(chunk_backward_early, 10, len(deps)),
         grid=(2,),
         in_specs=mixer_specs()
         + [
             by_lead(HEADS, TOK, 2 * DK),
             by_lead(HEADS, DK, DK),
             by_rows(TOK, inner),
-        ],
+        ]
+        + dep_specs(deps),
         out_specs=[
             whole((2 * (TOK + HALO), inner)),
             whole((TAPS, inner)),
@@ -679,7 +680,7 @@
         ],
         compiler_params=params(),
         cost_estimate=cost(5 * 10**9, 10**7),
-    )(pre, pre, scal, rates, taps, marks, docs, uw, state, do)
+    )(pre, pre, scal, rates, taps, marks, docs, uw, state, do, *deps)
 
 
 def run_chunk_backward_late(
@@ -984,7 +985,7 @@
     rows, cols = arrays[0].shape[0] // 2, arrays[0].shape[1] + arrays[4].shape[1]
     shapes = [((rows, cols), f32), ((rows, cols), bf16)]
     kept, sent = in_vmem(add_and_halve, shapes, places(), *arrays, deps=deps)
-    return kept + along(sent, "y", 1).astype(f32)
+    return kept + along(sent, "y", 1).astype(f32), sent
 
 
 def pair_up(place_ref, left, left_other, right, right_other, left_out, right_out):
@@ -1185,13 +1186,15 @@
         grad_gated, heads_out, out_gate, gain_head, p
     )
     local_got = exchange(local, SEQ_AXES)
-    early = run_chunk_backward_early(pre, scal, rates, taps, marks, docs_row, uw, state, do)
+    early = run_chunk_backward_early(
+        pre, scal, rates, taps, marks, docs_row, uw, state, do, ()
+    )
     gq, gtaps_q = early[:2]
     ffn_all = run_row_grads(
-        [normed_ffn, group_grads], [gu_grad, product], (((0, 0),), ((1, 1),)), (gq,)
+        [normed_ffn, group_grads], [gu_grad, product], (((0, 0),), ((1, 1),)), (local,)
     )
     ffn = lax.psum_scatter(ffn_all, ("x", "z"), scatter_dimension=0, tiled=True)
-    adj_out = run_scan_backward(got, local_got, (ffn_all,))
+    adj_out = run_scan_backward(got, local_got, (gq,))
     ffn_out, ffn_got = group_scatter(mm(later(product, local), w_down_t, "ij,kj->ik"))
     adj = exchange(adj_out, SEQ_AXES).reshape(8, DK, DK)
     gkv, gscal, gtaps_kv, grate = run_chunk_backward_late(
@@ -1199,8 +1202,8 @@
     )
 
     arrays = (normed_all, grad_mixer, gate_grad_mix, gq, gkv, gscal, gated_rows)
-    far = run_mixer_grads((2,), 2, *arrays, deps=(ffn_out,))
-    blocks = run_mixer_grads((1, 3, 0), 1, *arrays, deps=(far[0],))
+    far = run_mixer_grads((2,), 2, *arrays)
+    blocks = run_mixer_grads((1, 3, 0), 1, *arrays, deps=(far[0], ffn_out))
     owns, partials = (blocks[2], blocks[5]), []
     for i, axis in enumerate(("x", "z")):
         partials += blocks[3 * i : 3 * i + 2]
@@ -1209,29 +1212,28 @@
     gtaps = jnp.concatenate([gtaps_q, gtaps_kv], axis=1).reshape(12, inner)
     tail = jnp.concatenate([part_gain_head[:1], grate[:1]], axis=1)
     tail = jnp.pad(tail, ((0, 3), (0, inner - tail.shape[1])))
-    small = sum_along(jnp.concatenate([gtaps, tail], axis=0), "x")
+    small = sum_along(later(jnp.concatenate([gtaps, tail], axis=0), blocks[0]), "x")
     rim = jnp.concatenate([gq[2 * TOK :], gkv[2 * TOK :]], axis=1)
-    rim = passed_along(later(rim, blocks[0]), -1)
+    rim = passed_along(rim, -1)
     input_sent = run_input_grads(
         rim, gq, gkv, gscal, gate_grad_mix, all_left, all_right
     )
     partials, near_gate = reduce_near(owns, partials, (small, input_sent))
-    small = sum_along(later(small, near_gate), "z")
+    ffn = ffn.reshape(2, -1, 3, span)[..., :units]
+    ffn_other = along(later(pick(ffn, 1 - y_place, 0), near_gate), "y", 1)
+    ffn = ordered(pick(ffn, y_place, 0), ffn_other, y_place, 2).astype(f32)
     by_core = core_scatter(later(input_sent, near_gate))[0]
     grad_normed_in = chip_scatter(by_core)
     own = mine(tokens).astype(f32)
     back_in = norm_pull(own, row_scale(own), gain_in, grad_normed_in)
     both = jnp.concatenate([residual + ffn_out, grad_residual + back_in], axis=1)
     both = both.astype(bf16)
-    partials, cross_gate = reduce_cross(partials, (both, small, ffn))
-    small = sum_along(later(small, cross_gate), "y")
-    mixer_w = reduce_end(partials, ())
+    partials, cross_gate = reduce_cross(partials, (both, ffn_other))
+    small = sum_along(later(small, cross_gate), "z")
+    mixer_w, end_gate = reduce_end(partials, ())
+    small = sum_along(later(small, end_gate), "y")
     both = head_gather(later(both, cross_gate))
     outputs, grad_in = both[:, :width], both[:, width:].astype(f32)
-
-    ffn = ffn.reshape(2, -1, 3, span)[..., :units]
-    ffn_other = along(pick(ffn, 1 - y_place, 0), "y", 1)
-    ffn = ordered(pick(ffn, y_place, 0), ffn_other, y_place, 2).astype(f32)
 
     rows = width // SEQ
     key_at = 2 * inner + 128

time: 569 us -> 565 us (level)
  waiting for transfers between devices: 175 us -> 163 us
    ppermute x2, starting transfers between devices: 7.02 us -> 18.3 us  [passed_along(): return lax.ppermute(array, SEQ_AXES, pairs)]
    all_to_all x4, waiting for transfers between devices: 45.3 us -> 38.7 us  [exchange(): return lax.all_to_all(array, axis, split_axis=0, concat_axis=0, tiled=True)]
    ppermute x46, starting transfers between devices: 77.6 us -> 71.8 us  [along(): lax.ppermute(array, axis, [(i, (i + by) % count) for i in range(count)])]
    unnamed x168 -> x155, local copies, waits for them, and re-layouts: 20.2 us -> 19.5 us
  transfers between devices with their start and end apart: 74 -> 74, of which waited for: 34 -> 31; matrix products, arithmetic and copies ran while one was open for 13% -> 14% of each run, Pallas kernels for 12% -> 14%
where the time goes in v3:
time: 565 us; the launch traced here: 558 us
  waiting for transfers between devices  163 us (29%)
  starting transfers between devices  149 us (26%)
  Pallas kernels  102 us (18%)
  local copies, waits for them, and re-layouts  51.9 us (9%)
  other arithmetic  42.3 us (7%)
  matrix products  28.6 us (5%)
  between operations  20.8 us (4%)
    ppermute x46, waiting for transfers between devices, along(): lax.ppermute(array, axis, [(i, (i + by) % count) for i in range(count)])  79.5 us
    ppermute x46, starting transfers between devices, along(): lax.ppermute(array, axis, [(i, (i + by) % count) for i in range(count)])  71.8 us
    ppermute x20, waiting for transfers between devices, flipped(): return lax.ppermute(array, axes, [(i, i ^ mask) for i in range(count)])  44.5 us
    all_to_all x4, waiting for transfers between devices, exchange(): return lax.all_to_all(array, axis, split_axis=0, concat_axis=0, tiled=True)  38.7 us
    ppermute x20, starting transfers between devices, flipped(): return lax.ppermute(array, axes, [(i, i ^ mask) for i in range(count)])  33.1 us
    dot_general x9, matrix products, mm(): return jnp.einsum(dims, a, b, preferred_element_type=f32)  28.6 us
    pallas_call x7, Pallas kernels, in_vmem(): pl.pallas_call(ignoring(kernel, 1 + len(arrays), len(deps)), in_specs=[pl...  26.4 us
    all_to_all x4, starting transfers between devices, exchange(): return lax.all_to_all(array, axis, split_axis=0, concat_axis=0, tiled=True)  25.9 us
  transfers between devices with their start and end apart: 74, of which 31 were waited for; matrix products, arithmetic and copies ran while one was open for 14% of the time, Pallas kernels for 14%

profile of v3, /device:TPU:1, one launch (start us, length us, event | category | flops | bytes accessed | tf_op | source)
XLA Modules:
  0.0 557.7 jit_solution(7057335425510648901)
XLA Ops:
  9.9 3.8 collective-permute-start.1
  15.3 5.6 %collective-permute-done.2.refs_4_ = bf16[64,1280]{1,0:T(8,128)(2,1)S(1)} collective-permute-done((bf16[64,1280]{1,0:T(8,128)(2,1)S(1)}, bf16[64,1280]{1,0:T(8,128)(2,1)S(1)}, u32[]{:S(2)}, u32[]{:S(2)}) %collective-permute-start.2) | collective-permute-done | bytes 163872 | tf_op jit(solution)/shard_map/ppermute | solution.py:798
  30.8 5.8 %collective-permute-done.5.refs_3_.refs_7_ = bf16[128,1280]{1,0:T(8,128)(2,1)S(1)} collective-permute-done((bf16[128,1280]{1,0:T(8,128)(2,1)}, bf16[128,1280]{1,0:T(8,128)(2,1)S(1)}, u32[]{:S(2)}, u32[]{:S(2)}) %collective-permute-start.5) | collective-permute-done | bytes 327712 | tf_op jit(solution)/shard_map/ppermute | solution.py:798
  50.5 3.4 shard_map.290
  64.2 3.6 collective-permute-start.26
  71.9 17.0 %collective-permute-start = (bf16[2,16,2048]{2,1,0:T(8,128)(2,1)S(1)}, bf16[2,16,2048]{2,1,0:T(8,128)(2,1)S(1)}, u32[]{:S(2)}, u32[]{:S(2)}) collective-permute-start(bf16[2,16,2048]{2,1,0:T(8,128)(2,1)S(1)} %slice.203), channel_id=1, source_target_pairs={{0,4},{4,8},{8,12},{12,16},{16,20},{20,24},{24,28},{28,32},{32,36}... | collective-permute-start | bytes 393224 | tf_op jit(solution)/shard_map/ppermute | solution.py:793
  91.3 4.2 shard_map.291
  114.1 8.2 %collective-permute-done.18 = bf16[2,128,1280]{2,1,0:T(8,128)(2,1)S(1)} collective-permute-done((bf16[2,128,1280]{2,1,0:T(8,128)(2,1)S(1)}, bf16[2,128,1280]{2,1,0:T(8,128)(2,1)S(1)}, u32[]{:S(2)}, u32[]{:S(2)}) %collective-permute-start.18) | collective-permute-done | bytes 655392 | tf_op jit(solution)/shard_map/ppermute | solution.py:798
  122.3 4.9 collective-permute-done.17
  128.8 5.5 collective-permute-done.16
  141.6 11.1 %shard_map.292 = (bf16[32,160,128]{2,1,0:T(8,128)(2,1)}, bf16[8,128,128]{2,1,0:T(8,128)(2,1)}, f32[8,128,128]{2,1,0:T(8,128)}, bf16[8,128,128]{2,1,0:T(8,128)(2,1)}, f32[8,128,256]{2,1,0:T(8,128)}) custom-call(bf16[288,1536]{1,0:T(8,128)(2,1)} %pad_maximum_fusion.7.pre_ref.rim_ref.refs_0_.refs_1_, ...), custom_call_target="tpu_custom_call" | custom-call | flops 10000000000 | bytes 6000000 | tf_op jit(solution)/shard_map/pallas_call | solution.py:548
  152.8 7.6 %all-to-all-start = ((bf16[32,160,128]{2,1,0:T(8,128)(2,1)}), bf16[32,160,128]{2,1,0:T(8,128)(2,1)S(1)}, u32[]{:S(2)}, u32[]{:S(2)}) async-start(bf16[32,160,128]{2,1,0:T(8,128)(2,1)} %get-tuple-element.100), calls=%async_computation | async-start | bytes 2621440 | tf_op jit(solution)/shard_map/all_to_all | solution.py:844
  163.7 27.6 %all-to-all-done.got_ref.refs_0_ = bf16[32,160,128]{2,1,0:T(8,128)(2,1)S(1)} async-done(((bf16[32,160,128]{2,1,0:T(8,128)(2,1)}), bf16[32,160,128]{2,1,0:T(8,128)(2,1)S(1)}, u32[]{:S(2)}, u32[]{:S(2)}) %all-to-all-start) | async-done | bytes 1310752 | tf_op jit(solution)/shard_map/all_to_all | solution.py:844
  192.4 5.9 %shard_map.293 = bf16[32,32,128]{2,1,0:T(8,128)(2,1)} custom-call(bf16[32,160,128]{2,1,0:T(8,128)(2,1)} %copy-done.18), custom_call_target="tpu_custom_call" | custom-call | flops 1000000000 | bytes 3000000 | tf_op jit(solution)/shard_map/pallas_call | solution.py:573
  198.3 7.0 %all-to-all-start.1 = ((bf16[32,32,128]{2,1,0:T(8,128)(2,1)}), bf16[32,32,128]{2,1,0:T(8,128)(2,1)S(1)}, u32[]{:S(2)}, u32[]{:S(2)}) async-start(bf16[32,32,128]{2,1,0:T(8,128)(2,1)} %shard_map.293), calls=%async_computation.1 | async-start | bytes 524288 | tf_op jit(solution)/shard_map/all_to_all | solution.py:844
  205.3 3.4 fusion.17.refs_3_.og_ref
  208.8 6.0 %all-to-all-done.1 = bf16[32,32,128]{2,1,0:T(8,128)(2,1)S(1)} async-done(((bf16[32,32,128]{2,1,0:T(8,128)(2,1)}), bf16[32,32,128]{2,1,0:T(8,128)(2,1)S(1)}, u32[]{:S(2)}, u32[]{:S(2)}) %all-to-all-start.1) | async-done | bytes 262176 | tf_op jit(solution)/shard_map/all_to_all | solution.py:844
  221.4 6.1 %collective-permute-start.20 = (bf16[2,64,2048]{2,1,0:T(8,128)(2,1)S(1)}, bf16[2,64,2048]{2,1,0:T(8,128)(2,1)S(1)}, u32[]{:S(2)}, u32[]{:S(2)}) collective-permute-start(bf16[2,64,2048]{2,1,0:T(8,128)(2,1)S(1)} %dynamic-slice_bitcast_fusion.3), channel_id=1, source_target_pairs={{0,1},{1,0},{2,3},{3,2},{4,5},{5,4},{6,7},{7,6},{8,9},{9,8},{10,11... | collective-permute-start | bytes 1572872 | tf_op jit(solution)/shard_map/ppermute | solution.py:807
  230.7 7.4 %collective-permute-done.21 = bf16[64,2048]{1,0:T(8,128)(2,1)S(1)} collective-permute-done((bf16[64,2048]{1,0:T(8,128)(2,1)S(1)}, bf16[64,2048]{1,0:T(8,128)(2,1)S(1)}, u32[]{:S(2)}, u32[]{:S(2)}) %collective-permute-start.21) | collective-permute-done | bytes 262176 | tf_op jit(solution)/shard_map/ppermute | solution.py:807
  241.8 4.9 collective-permute-done.22
  250.0 3.8 collective-permute-done.24
  260.5 6.3 %fusion.2 = f32[512,1536]{1,0:T(8,128)S(1)} fusion(bf16[512,2048]{1,0:T(8,128)(2,1)} %bitcast.262, bf16[2048,2304]{1,0:T(8,128)(2,1)} %all-gather.2.cloned.1.call-done), kind=kOutput, calls=%fused_computation.2 | convolution fusion | flops 3221225472 | bytes 11534336 | tf_op jit(solution)/shard_map/ij,jk->ik/dot_general | solution.py:1043
  270.4 3.7 fusion.8
  278.0 3.3 collective-permute-start.28
  281.3 5.1 collective-permute-done.30
  286.5 6.5 %collective-permute-done.28 = bf16[64,2048]{1,0:T(8,128)(2,1)S(1)} collective-permute-done((bf16[64,2048]{1,0:T(8,128)(2,1)S(1)}, bf16[64,2048]{1,0:T(8,128)(2,1)S(1)}, u32[]{:S(2)}, u32[]{:S(2)}) %collective-permute-start.28) | collective-permute-done | bytes 262176 | tf_op jit(solution)/shard_map/ppermute | solution.py:807
  294.6 6.6 %collective-permute-done.31 = bf16[64,2048]{1,0:T(8,128)(2,1)} collective-permute-done((bf16[64,2048]{1,0:T(8,128)(2,1)S(1)}, bf16[64,2048]{1,0:T(8,128)(2,1)}, u32[]{:S(2)}, u32[]{:S(2)}) %collective-permute-start.31) | collective-permute-done | bytes 262176 | tf_op jit(solution)/shard_map/ppermute | solution.py:807
  308.1 3.5 fusion.19.gg_ref
  314.5 9.8 %shard_map.303 = bf16[2048,2304]{1,0:T(8,128)(2,1)} custom-call(bf16[512,2048]{1,0:T(8,128)(2,1)} %bitcast.263, bf16[512,2048]{1,0:T(8,128)(2,1)} %pad_maximum_fusion.1.refs_1_, bf16[512,1536]{1,0:T(8,128)(2,1)} %pad_maximum_fusion.3.refs_2_, bf16[512,768]{1,0:T(8,128)(2,1)} %get-tuple-element.264.refs_3_, bf16[32,32,128]{2,1,0:T(8,128)(2,1)} %get-tuple-element.103.refs_4_), custom_call_target="tpu_custom_call" | custom-call | flops 4831838208 | bytes 9437184 | tf_op jit(solution)/shard_map/pallas_call | solution.py:730
  326.3 3.7 convolution_convert_fusion
  333.0 3.9 all-to-all-start.2
  337.6 7.9 %shard_map.296 = (bf16[288,512]{1,0:T(8,128)(2,1)}, f32[4,512]{1,0:T(4,128)}, bf16[8,128,128]{2,1,0:T(8,128)(2,1)}, f32[8,128,128]{2,1,0:T(8,128)}, f32[8,128,12...) custom-call(bf16[288,1536]{1,0:T(8,128)(2,1)} %pad_maximum_fusion.7.pre_ref.rim_ref.refs_0_.refs_1_, ...), custom_call_target="tpu_custom_call" | custom-call | flops 5000000000 | bytes 10000000 | tf_op jit(solution)/shard_map/pallas_call | solution.py:649
  348.8 5.9 %shard_map.297 = bf16[32,32,128]{2,1,0:T(8,128)(2,1)} custom-call(bf16[32,160,128]{2,1,0:T(8,128)(2,1)} %copy-done.18, bf16[32,32,128]{2,1,0:T(8,128)(2,1)} %copy-done.47, bf16[288,512]{1,0:T(8,128)(2,1)} %get-tuple-element.106.refs_2_.gq_ref.refs_4_), custom_call_target="tpu_custom_call" | custom-call | flops 1000000000 | bytes 3000000 | tf_op jit(solution)/shard_map/pallas_call | solution.py:583
  354.7 7.4 %all-to-all-start.3 = ((bf16[32,32,128]{2,1,0:T(8,128)(2,1)}), bf16[32,32,128]{2,1,0:T(8,128)(2,1)}, u32[]{:S(2)}, u32[]{:S(2)}) async-start(bf16[32,32,128]{2,1,0:T(8,128)(2,1)} %shard_map.297), calls=%async_computation.3 | async-start | bytes 524288 | tf_op jit(solution)/shard_map/all_to_all | solution.py:844
  373.7 10.2 %shard_map.298 = (bf16[288,1024]{1,0:T(8,128)(2,1)}, bf16[256,128]{1,0:T(8,128)(2,1)}, f32[4,1024]{1,0:T(4,128)}, f32[8,128]{1,0:T(8,128)}) custom-call(bf16[288,1536]{1,0:T(8,128)(2,1)} %pad_maximum_fusion.7.pre_ref.rim_ref.refs_0_.refs_1_, bf16[288,1536]{1,0:T(8,128)(2,1)} %pad_maximum_fusion.7.pre_ref.rim_ref.refs_0_.refs_1_, ...), custom_call_target="tpu_custom_call" | custom-call | flops 5000000000 | bytes 10000000 | tf_op jit(solution)/shard_map/pallas_call | solution.py:691
  383.9 4.5 shard_map.300
  399.5 7.5 %shard_map.301 = (bf16[512,1408]{1,0:T(8,128)(2,1)}, bf16[512,1408]{1,0:T(8,128)(2,1)}, bf16[512,1408]{1,0:T(8,128)(2,1)}, bf16[512,1280]{1,0:T(8,128)(2,1)}, bf...) custom-call(s32[2]{0:T(128)} %pad_add_fusion.1.refs_0_, bf16[288,2048]{1,0:T(8,128)(2,1)} %copy-done.20, ...), custom_call_target="tpu_custom_call" | custom-call | flops 2684354560 | bytes 10485760 | tf_op jit(solution)/shard_map/pallas_call | solution.py:753
  408.9 5.3 collective-permute-start.44
  423.0 7.5 %shard_map.299.refs_10_ = bf16[256,2048]{1,0:T(8,128)(2,1)} custom-call(bf16[32,1536]{1,0:T(8,128)(2,1)} %copy-done.58, bf16[288,512]{1,0:T(8,128)(2,1)} %get-tuple-element.106.refs_2_.gq_ref.refs_4_, bf16[288,1024]{1,0:T(8,128)(2,1)} %get-tuple-element.113.gkv_ref.refs_5_, bf16[256,128]{1,0:T(8,128)(2,1)} %get-tuple-element.114.gscal_ref.refs_6_, ...), custom_call_target="tpu_custom_call" | custom-call | flops 2684354560 | bytes 10485760 | tf_op jit(solution)/shard_map/pallas_call | solution.py:768
  432.0 6.1 %shard_map.302 = (bf16[512,1408]{1,0:T(8,128)(2,1)}, bf16[512,1408]{1,0:T(8,128)(2,1)}, bf16[512,1280]{1,0:T(8,128)(2,1)}, bf16[512,1280]{1,0:T(8,128)(2,1)}) custom-call(s32[3]{0:T(128)} %pad_add_fusion.refs_0_, bf16[512,1408]{1,0:T(8,128)(2,1)} %get-tuple-element.117.refs_1_, bf16[512,1408]{1,0:T(8,128)(2,1)} %get-tuple-element.118.refs_2_, ...), custom_call_target="tpu_custom_call" | custom-call | flops 8257536 | bytes 8257536 | tf_op jit(solution)/shard_map/pallas_call | solution.py:906
  440.0 5.8 %collective-permute-start.45 = (bf16[2,64,2048]{2,1,0:T(8,128)(2,1)S(1)}, bf16[2,64,2048]{2,1,0:T(8,128)(2,1)S(1)}, u32[]{:S(2)}, u32[]{:S(2)}) collective-permute-start(bf16[2,64,2048]{2,1,0:T(8,128)(2,1)S(1)} %dynamic-slice_bitcast_fusion.2), channel_id=1, source_target_pairs={{0,1},{1,0},{2,3},{3,2},{4,5},{5,4},{6,7},{7,6},{8,9},{9,8},{10,11... | collective-permute-start | bytes 1572872 | tf_op jit(solution)/shard_map/ppermute | solution.py:807
  461.1 20.8 %collective-permute-done.49.refs_5_ = bf16[512,1280]{1,0:T(8,128)(2,1)} collective-permute-done((bf16[512,1280]{1,0:T(8,128)(2,1)}, bf16[512,1280]{1,0:T(8,128)(2,1)}, u32[]{:S(2)}, u32[]{:S(2)}) %collective-permute-start.49) | collective-permute-done | bytes 1310752 | tf_op jit(solution)/shard_map/ppermute | solution.py:798
  483.4 5.5 shard_map.304
  502.5 8.5 %collective-permute-done.58.refs_7_ = bf16[128,1280]{1,0:T(8,128)(2,1)S(1)} collective-permute-done((bf16[128,1280]{1,0:T(8,128)(2,1)}, bf16[128,1280]{1,0:T(8,128)(2,1)S(1)}, u32[]{:S(2)}, u32[]{:S(2)}) %collective-permute-start.58) | collective-permute-done | bytes 327712 | tf_op jit(solution)/shard_map/ppermute | solution.py:798
  521.7 4.2 collective-permute-start.64
  526.7 4.8 collective-permute-done.64
  531.8 4.0 collective-permute-start.53
  535.8 3.4 collective-permute-done.60
  (430 shorter events, 212.3 us)
Async XLA Ops:
  7.2 253.3 %all-gather.2.cloned.1.call-start = ((), (), s32[]{:S(2)}) async-start(), calls=%async_computation.5 | async-start | bytes 10027008 | tf_op jit(solution)/shard_map/all_gather | solution.py:1122
  9.9 11.1 %collective-permute-start.1 = (bf16[64,1408]{1,0:T(8,128)(2,1)S(1)}, bf16[64,1408]{1,0:T(8,128)(2,1)S(1)}, u32[]{:S(2)}, u32[]{:S(2)}) collective-permute-start(bf16[64,1408]{1,0:T(8,128)(2,1)S(1)} %fusion.60.refs_1_), channel_id=1, source_target_pairs={{0,4},{4,0},{1,5},{5,1},{2,6},{6,2},{3,7},{7,3},{8,12},{12,8},{9,1... | collective-permute-start | bytes 540680 | tf_op jit(solution)/shard_map/ppermute | solution.py:798
  24.4 12.3 %collective-permute-start.3 = (bf16[128,1408]{1,0:T(8,128)(2,1)}, bf16[128,1408]{1,0:T(8,128)(2,1)S(1)}, u32[]{:S(2)}, u32[]{:S(2)}) collective-permute-start(bf16[128,1408]{1,0:T(8,128)(2,1)} %get-tuple-element.86.refs_1_), channel_id=1, source_target_pairs={{0,32},{32,64},{64,96},{96,0},{1,33},{33,65},{65,97},{97,1},{2,34}... | collective-permute-start | bytes 1081352 | tf_op jit(solution)/shard_map/ppermute | solution.py:798
  25.6 11.1 %collective-permute-start.4 = (bf16[128,1408]{1,0:T(8,128)(2,1)}, bf16[128,1408]{1,0:T(8,128)(2,1)S(1)}, u32[]{:S(2)}, u32[]{:S(2)}) collective-permute-start(bf16[128,1408]{1,0:T(8,128)(2,1)} %get-tuple-element.86.refs_1_), channel_id=1, source_target_pairs={{0,96},{32,0},{64,32},{96,64},{1,97},{33,1},{65,33},{97,65},{2,98}... | collective-permute-start | bytes 1081352 | tf_op jit(solution)/shard_map/ppermute | solution.py:798
  27.0 9.6 %collective-permute-start.5 = (bf16[128,1280]{1,0:T(8,128)(2,1)}, bf16[128,1280]{1,0:T(8,128)(2,1)S(1)}, u32[]{:S(2)}, u32[]{:S(2)}) collective-permute-start(bf16[128,1280]{1,0:T(8,128)(2,1)} %get-tuple-element.87.refs_6_), channel_id=1, source_target_pairs={{0,8},{8,16},{16,24},{24,0},{1,9},{9,17},{17,25},{25,1},{2,10},{10... | collective-permute-start | bytes 983048 | tf_op jit(solution)/shard_map/ppermute | solution.py:798
  53.9 36.2 %collective-permute-start.11 = (bf16[4,128,1408]{2,1,0:T(8,128)(2,1)}, bf16[4,128,1408]{2,1,0:T(8,128)(2,1)}, u32[]{:S(2)}, u32[]{:S(2)}) collective-permute-start(bf16[4,128,1408]{2,1,0:T(8,128)(2,1)} %get-tuple-element.92), channel_id=1, source_target_pairs={{0,8},{8,16},{16,24},{24,0},{1,9},{9,17},{17,25},{25,1},{2,10},{10... | collective-permute-start | bytes 4325384 | tf_op jit(solution)/shard_map/ppermute | solution.py:798
  54.3 35.8 %collective-permute-start.12 = (bf16[4,128,1408]{2,1,0:T(8,128)(2,1)}, bf16[4,128,1408]{2,1,0:T(8,128)(2,1)S(1)}, u32[]{:S(2)}, u32[]{:S(2)}) collective-permute-start(bf16[4,128,1408]{2,1,0:T(8,128)(2,1)} %get-tuple-element.92), channel_id=1, source_target_pairs={{0,24},{8,0},{16,8},{24,16},{1,25},{9,1},{17,9},{25,17},{2,26},{10... | collective-permute-start | bytes 4325384 | tf_op jit(solution)/shard_map/ppermute | solution.py:798
  57.4 32.7 %collective-permute-start.13 = (bf16[4,128,1280]{2,1,0:T(8,128)(2,1)}, bf16[4,128,1280]{2,1,0:T(8,128)(2,1)}, u32[]{:S(2)}, u32[]{:S(2)}) collective-permute-start(bf16[4,128,1280]{2,1,0:T(8,128)(2,1)} %get-tuple-element.93), channel_id=1, source_target_pairs={{0,32},{32,64},{64,96},{96,0},{1,33},{33,65},{65,97},{97,1},{2,34}... | collective-permute-start | bytes 3932168 | tf_op jit(solution)/shard_map/ppermute | solution.py:798
  57.4 32.6 %collective-permute-start.14 = (bf16[4,128,1280]{2,1,0:T(8,128)(2,1)}, bf16[4,128,1280]{2,1,0:T(8,128)(2,1)}, u32[]{:S(2)}, u32[]{:S(2)}) collective-permute-start(bf16[4,128,1280]{2,1,0:T(8,128)(2,1)} %get-tuple-element.93), channel_id=1, source_target_pairs={{0,96},{32,0},{64,32},{96,64},{1,97},{33,1},{65,33},{97,65},{2,98}... | collective-permute-start | bytes 3932168 | tf_op jit(solution)/shard_map/ppermute | solution.py:798
  71.9 31.5 %collective-permute-start = (bf16[2,16,2048]{2,1,0:T(8,128)(2,1)S(1)}, bf16[2,16,2048]{2,1,0:T(8,128)(2,1)S(1)}, u32[]{:S(2)}, u32[]{:S(2)}) collective-permute-start(bf16[2,16,2048]{2,1,0:T(8,128)(2,1)S(1)} %slice.203), channel_id=1, source_target_pairs={{0,4},{4,8},{8,12},{12,16},{16,20},{20,24},{24,28},{28,32},{32,36}... | collective-permute-start | bytes 393224 | tf_op jit(solution)/shard_map/ppermute | solution.py:793
  106.8 15.5 %collective-permute-start.18 = (bf16[2,128,1280]{2,1,0:T(8,128)(2,1)S(1)}, bf16[2,128,1280]{2,1,0:T(8,128)(2,1)S(1)}, u32[]{:S(2)}, u32[]{:S(2)}) collective-permute-start(bf16[2,128,1280]{2,1,0:T(8,128)(2,1)S(1)} %copy-done.70), channel_id=1, source_target_pairs={{0,96},{32,0},{64,32},{96,64},{1,97},{33,1},{65,33},{97,65},{2,98}... | collective-permute-start | bytes 1966088 | tf_op jit(solution)/shard_map/ppermute | solution.py:798
  107.7 19.5 %collective-permute-start.17 = (bf16[2,128,1280]{2,1,0:T(8,128)(2,1)S(1)}, bf16[2,128,1280]{2,1,0:T(8,128)(2,1)S(1)}, u32[]{:S(2)}, u32[]{:S(2)}) collective-permute-start(bf16[2,128,1280]{2,1,0:T(8,128)(2,1)S(1)} %copy-done.69), channel_id=1, source_target_pairs={{0,32},{32,64},{64,96},{96,0},{1,33},{33,65},{65,97},{97,1},{2,34}... | collective-permute-start | bytes 1966088 | tf_op jit(solution)/shard_map/ppermute | solution.py:798
  109.7 24.8 %collective-permute-start.15 = (bf16[2,128,1408]{2,1,0:T(8,128)(2,1)S(1)}, bf16[2,128,1408]{2,1,0:T(8,128)(2,1)S(1)}, u32[]{:S(2)}, u32[]{:S(2)}) collective-permute-start(bf16[2,128,1408]{2,1,0:T(8,128)(2,1)S(1)} %copy-done.67), channel_id=1, source_target_pairs={{0,8},{8,16},{16,24},{24,0},{1,9},{9,17},{17,25},{25,1},{2,10},{10... | collective-permute-start | bytes 2162696 | tf_op jit(solution)/shard_map/ppermute | solution.py:798
  109.8 24.5 %collective-permute-start.16 = (bf16[2,128,1408]{2,1,0:T(8,128)(2,1)S(1)}, bf16[2,128,1408]{2,1,0:T(8,128)(2,1)S(1)}, u32[]{:S(2)}, u32[]{:S(2)}) collective-permute-start(bf16[2,128,1408]{2,1,0:T(8,128)(2,1)S(1)} %copy-done.68), channel_id=1, source_target_pairs={{0,24},{8,0},{16,8},{24,16},{1,25},{9,1},{17,9},{25,17},{2,26},{10... | collective-permute-start | bytes 2162696 | tf_op jit(solution)/shard_map/ppermute | solution.py:798
  152.8 38.5 %all-to-all-start = ((bf16[32,160,128]{2,1,0:T(8,128)(2,1)}), bf16[32,160,128]{2,1,0:T(8,128)(2,1)S(1)}, u32[]{:S(2)}, u32[]{:S(2)}) async-start(bf16[32,160,128]{2,1,0:T(8,128)(2,1)} %get-tuple-element.100), calls=%async_computation | async-start | bytes 2621440 | tf_op jit(solution)/shard_map/all_to_all | solution.py:844
  160.4 48.4 %collective-permute-start.19 = (bf16[256,2048]{1,0:T(8,128)(2,1)S(1)}, bf16[256,2048]{1,0:T(8,128)(2,1)}, u32[]{:S(2)}, u32[]{:S(2)}) collective-permute-start(bf16[256,2048]{1,0:T(8,128)(2,1)S(1)} %bitcast.265), channel_id=1, source_target_pairs={{0,4},{4,0},{1,5},{5,1},{2,6},{6,2},{3,7},{7,3},{8,12},{12,8},{9,1... | collective-permute-start | bytes 3145736 | tf_op jit(solution)/shard_map/ppermute | solution.py:798
  198.3 16.5 %all-to-all-start.1 = ((bf16[32,32,128]{2,1,0:T(8,128)(2,1)}), bf16[32,32,128]{2,1,0:T(8,128)(2,1)S(1)}, u32[]{:S(2)}, u32[]{:S(2)}) async-start(bf16[32,32,128]{2,1,0:T(8,128)(2,1)} %shard_map.293), calls=%async_computation.1 | async-start | bytes 524288 | tf_op jit(solution)/shard_map/all_to_all | solution.py:844
  205.3 250.5 %reduce-scatter.2.cloned.1.call-start = ((), (), s32[]{:S(2)}) async-start(), calls=%async_computation.6 | async-start | bytes 10027008 | tf_op jit(solution)/shard_map/reduce_scatter | solution.py:1196
  239.1 10.9 %collective-permute-start.23 = (bf16[64,2048]{1,0:T(8,128)(2,1)S(1)}, bf16[64,2048]{1,0:T(8,128)(2,1)S(1)}, u32[]{:S(2)}, u32[]{:S(2)}) collective-permute-start(bf16[64,2048]{1,0:T(8,128)(2,1)S(1)} %multiply_convert_fusion.3), channel_id=1, source_target_pairs={{0,2},{1,3},{2,0},{3,1},{4,6},{5,7},{6,4},{7,5},{8,10},{9,11},{10,... | collective-permute-start | bytes 786440 | tf_op jit(solution)/shard_map/ppermute | solution.py:807
  239.2 14.6 %collective-permute-start.24 = (bf16[64,2048]{1,0:T(8,128)(2,1)S(1)}, bf16[64,2048]{1,0:T(8,128)(2,1)S(1)}, u32[]{:S(2)}, u32[]{:S(2)}) collective-permute-start(bf16[64,2048]{1,0:T(8,128)(2,1)S(1)} %multiply_convert_fusion.3), channel_id=1, source_target_pairs={{0,6},{1,7},{2,4},{3,5},{4,2},{5,3},{6,0},{7,1},{8,14},{9,15},{10,... | collective-permute-start | bytes 786440 | tf_op jit(solution)/shard_map/ppermute | solution.py:807
  278.0 14.9 %collective-permute-start.28 = (bf16[64,2048]{1,0:T(8,128)(2,1)S(1)}, bf16[64,2048]{1,0:T(8,128)(2,1)S(1)}, u32[]{:S(2)}, u32[]{:S(2)}) collective-permute-start(bf16[64,2048]{1,0:T(8,128)(2,1)S(1)} %get-tuple-element.272), channel_id=1, source_target_pairs={{0,4},{1,5},{2,6},{3,7},{4,0},{5,1},{6,2},{7,3},{8,12},{9,13},{10,... | collective-permute-start | bytes 786440 | tf_op jit(solution)/shard_map/ppermute | solution.py:807
  332.4 29.8 %collective-permute-start.33 = (bf16[4,64,2048]{2,1,0:T(8,128)(2,1)}, bf16[4,64,2048]{2,1,0:T(8,128)(2,1)S(1)}, u32[]{:S(2)}, u32[]{:S(2)}) collective-permute-start(bf16[4,64,2048]{2,1,0:T(8,128)(2,1)} %dynamic-slice_bitcast_fusion), channel_id=1, source_target_pairs={{0,1},{1,0},{2,3},{3,2},{4,5},{5,4},{6,7},{7,6},{8,9},{9,8},{10,11... | collective-permute-start | bytes 3145736 | tf_op jit(solution)/shard_map/ppermute | solution.py:807
  333.0 15.1 %all-to-all-start.2 = ((bf16[32,32,128]{2,1,0:T(8,128)(2,1)}), bf16[32,32,128]{2,1,0:T(8,128)(2,1)S(1)}, u32[]{:S(2)}, u32[]{:S(2)}) async-start(bf16[32,32,128]{2,1,0:T(8,128)(2,1)} %get-tuple-element.103.refs_4_), calls=%async_computation.2 | async-start | bytes 524288 | tf_op jit(solution)/shard_map/all_to_all | solution.py:844
  354.7 18.9 %all-to-all-start.3 = ((bf16[32,32,128]{2,1,0:T(8,128)(2,1)}), bf16[32,32,128]{2,1,0:T(8,128)(2,1)}, u32[]{:S(2)}, u32[]{:S(2)}) async-start(bf16[32,32,128]{2,1,0:T(8,128)(2,1)} %shard_map.297), calls=%async_computation.3 | async-start | bytes 524288 | tf_op jit(solution)/shard_map/all_to_all | solution.py:844
  366.4 26.9 %collective-permute-start.36 = (bf16[64,2048]{1,0:T(8,128)(2,1)}, bf16[64,2048]{1,0:T(8,128)(2,1)S(1)}, u32[]{:S(2)}, u32[]{:S(2)}) collective-permute-start(bf16[64,2048]{1,0:T(8,128)(2,1)} %get-tuple-element.270), channel_id=1, source_target_pairs={{0,6},{1,7},{2,4},{3,5},{4,2},{5,3},{6,0},{7,1},{8,14},{9,15},{10,... | collective-permute-start | bytes 786440 | tf_op jit(solution)/shard_map/ppermute | solution.py:807
  369.0 24.4 %collective-permute-start.35 = (bf16[64,2048]{1,0:T(8,128)(2,1)}, bf16[64,2048]{1,0:T(8,128)(2,1)}, u32[]{:S(2)}, u32[]{:S(2)}) collective-permute-start(bf16[64,2048]{1,0:T(8,128)(2,1)} %get-tuple-element.271), channel_id=1, source_target_pairs={{0,2},{1,3},{2,0},{3,1},{4,6},{5,7},{6,4},{7,5},{8,10},{9,11},{10,... | collective-permute-start | bytes 786440 | tf_op jit(solution)/shard_map/ppermute | solution.py:807
  369.0 27.0 %collective-permute-start.34 = (bf16[64,2048]{1,0:T(8,128)(2,1)S(1)}, bf16[64,2048]{1,0:T(8,128)(2,1)}, u32[]{:S(2)}, u32[]{:S(2)}) collective-permute-start(bf16[64,2048]{1,0:T(8,128)(2,1)S(1)} %get-tuple-element.269), channel_id=1, source_target_pairs={{0,4},{1,5},{2,6},{3,7},{4,0},{5,1},{6,2},{7,3},{8,12},{9,13},{10,... | collective-permute-start | bytes 786440 | tf_op jit(solution)/shard_map/ppermute | solution.py:807
  388.4 42.7 %collective-permute-start.38 = (bf16[256,1408]{1,0:T(8,128)(2,1)}, bf16[256,1408]{1,0:T(8,128)(2,1)S(1)}, u32[]{:S(2)}, u32[]{:S(2)}) collective-permute-start(bf16[256,1408]{1,0:T(8,128)(2,1)} %get-tuple-element.116.refs_8_), channel_id=1, source_target_pairs={{0,32},{32,64},{64,96},{96,0},{1,33},{33,65},{65,97},{97,1},{2,34}... | collective-permute-start | bytes 2162696 | tf_op jit(solution)/shard_map/ppermute | solution.py:798
  388.8 42.3 %collective-permute-start.39 = (bf16[256,1408]{1,0:T(8,128)(2,1)}, bf16[256,1408]{1,0:T(8,128)(2,1)}, u32[]{:S(2)}, u32[]{:S(2)}) collective-permute-start(bf16[256,1408]{1,0:T(8,128)(2,1)} %get-tuple-element.119), channel_id=1, source_target_pairs={{0,96},{32,0},{64,32},{96,64},{1,97},{33,1},{65,33},{97,65},{2,98}... | collective-permute-start | bytes 2162696 | tf_op jit(solution)/shard_map/ppermute | solution.py:798
  393.3 37.7 %collective-permute-start.40 = (bf16[256,1280]{1,0:T(8,128)(2,1)}, bf16[256,1280]{1,0:T(8,128)(2,1)}, u32[]{:S(2)}, u32[]{:S(2)}) collective-permute-start(bf16[256,1280]{1,0:T(8,128)(2,1)} %get-tuple-element.122), channel_id=1, source_target_pairs={{0,8},{8,16},{16,24},{24,0},{1,9},{9,17},{17,25},{25,1},{2,10},{10... | collective-permute-start | bytes 1966088 | tf_op jit(solution)/shard_map/ppermute | solution.py:798
  393.4 37.7 %collective-permute-start.41 = (bf16[256,1280]{1,0:T(8,128)(2,1)}, bf16[256,1280]{1,0:T(8,128)(2,1)}, u32[]{:S(2)}, u32[]{:S(2)}) collective-permute-start(bf16[256,1280]{1,0:T(8,128)(2,1)} %get-tuple-element.123), channel_id=1, source_target_pairs={{0,24},{8,0},{16,8},{24,16},{1,25},{9,1},{17,9},{25,17},{2,26},{10... | collective-permute-start | bytes 1966088 | tf_op jit(solution)/shard_map/ppermute | solution.py:798
  396.0 12.8 %collective-permute-start.37 = (bf16[32,1536]{1,0:T(8,128)(2,1)}, bf16[32,1536]{1,0:T(8,128)(2,1)S(1)}, u32[]{:S(2)}, u32[]{:S(2)}) collective-permute-start(bf16[32,1536]{1,0:T(8,128)(2,1)} %pad_maximum_fusion.12), channel_id=1, source_target_pairs={{4,0},{8,4},{12,8},{16,12},{20,16},{24,20},{28,24},{32,28},{36,32}... | collective-permute-start | bytes 294920 | tf_op jit(solution)/shard_map/ppermute | solution.py:793
  448.6 34.0 %collective-permute-start.47 = (bf16[512,1408]{1,0:T(8,128)(2,1)}, bf16[512,1408]{1,0:T(8,128)(2,1)}, u32[]{:S(2)}, u32[]{:S(2)}) collective-permute-start(bf16[512,1408]{1,0:T(8,128)(2,1)} %get-tuple-element.128), channel_id=1, source_target_pairs={{0,32},{32,64},{64,96},{96,0},{1,33},{33,65},{65,97},{97,1},{2,34}... | collective-permute-start | bytes 4325384 | tf_op jit(solution)/shard_map/ppermute | solution.py:798
  449.2 33.5 %collective-permute-start.48 = (bf16[512,1408]{1,0:T(8,128)(2,1)}, bf16[512,1408]{1,0:T(8,128)(2,1)}, u32[]{:S(2)}, u32[]{:S(2)}) collective-permute-start(bf16[512,1408]{1,0:T(8,128)(2,1)} %get-tuple-element.130), channel_id=1, source_target_pairs={{0,96},{32,0},{64,32},{96,64},{1,97},{33,1},{65,33},{97,65},{2,98}... | collective-permute-start | bytes 4325384 | tf_op jit(solution)/shard_map/ppermute | solution.py:798
  451.3 30.6 %collective-permute-start.49 = (bf16[512,1280]{1,0:T(8,128)(2,1)}, bf16[512,1280]{1,0:T(8,128)(2,1)}, u32[]{:S(2)}, u32[]{:S(2)}) collective-permute-start(bf16[512,1280]{1,0:T(8,128)(2,1)} %get-tuple-element.132), channel_id=1, source_target_pairs={{0,8},{8,16},{16,24},{24,0},{1,9},{9,17},{17,25},{25,1},{2,10},{10... | collective-permute-start | bytes 3932168 | tf_op jit(solution)/shard_map/ppermute | solution.py:798
  451.3 30.6 %collective-permute-start.50 = (bf16[512,1280]{1,0:T(8,128)(2,1)}, bf16[512,1280]{1,0:T(8,128)(2,1)}, u32[]{:S(2)}, u32[]{:S(2)}) collective-permute-start(bf16[512,1280]{1,0:T(8,128)(2,1)} %get-tuple-element.133), channel_id=1, source_target_pairs={{0,24},{8,0},{16,8},{24,16},{1,25},{9,1},{17,9},{25,17},{2,26},{10... | collective-permute-start | bytes 3932168 | tf_op jit(solution)/shard_map/ppermute | solution.py:798
  457.2 25.4 %collective-permute-start.51 = (bf16[64,3,704]{2,1,0:T(4,128)(2,1)S(1)}, bf16[64,3,704]{2,1,0:T(4,128)(2,1)S(1)}, u32[]{:S(2)}, u32[]{:S(2)}) collective-permute-start(bf16[64,3,704]{2,1,0:T(4,128)(2,1)S(1)} %add_bitcast_fusion), channel_id=1, source_target_pairs={{0,4},{4,0},{1,5},{5,1},{2,6},{6,2},{3,7},{7,3},{8,12},{12,8},{9,1... | collective-permute-start | bytes 811016 | tf_op jit(solution)/shard_map/ppermute | solution.py:798
  490.9 22.9 %collective-permute-start.54 = (bf16[128,1408]{1,0:T(8,128)(2,1)}, bf16[128,1408]{1,0:T(8,128)(2,1)S(1)}, u32[]{:S(2)}, u32[]{:S(2)}) collective-permute-start(bf16[128,1408]{1,0:T(8,128)(2,1)} %get-tuple-element.135), channel_id=1, source_target_pairs={{0,16},{8,24},{16,0},{24,8},{1,17},{9,25},{17,1},{25,9},{2,18},{10... | collective-permute-start | bytes 1081352 | tf_op jit(solution)/shard_map/ppermute | solution.py:798
  491.5 23.4 %collective-permute-start.55 = (bf16[128,1408]{1,0:T(8,128)(2,1)}, bf16[128,1408]{1,0:T(8,128)(2,1)S(1)}, u32[]{:S(2)}, u32[]{:S(2)}) collective-permute-start(bf16[128,1408]{1,0:T(8,128)(2,1)} %get-tuple-element.136), channel_id=1, source_target_pairs={{0,8},{8,16},{16,24},{24,0},{1,9},{9,17},{17,25},{25,1},{2,10},{10... | collective-permute-start | bytes 1081352 | tf_op jit(solution)/shard_map/ppermute | solution.py:798
  494.8 16.1 %collective-permute-start.58 = (bf16[128,1280]{1,0:T(8,128)(2,1)}, bf16[128,1280]{1,0:T(8,128)(2,1)S(1)}, u32[]{:S(2)}, u32[]{:S(2)}) collective-permute-start(bf16[128,1280]{1,0:T(8,128)(2,1)} %get-tuple-element.140), channel_id=1, source_target_pairs={{0,32},{32,64},{64,96},{96,0},{1,33},{33,65},{65,97},{97,1},{2,34}... | collective-permute-start | bytes 983048 | tf_op jit(solution)/shard_map/ppermute | solution.py:798
  494.8 17.3 %collective-permute-start.59 = (bf16[128,1280]{1,0:T(8,128)(2,1)}, bf16[128,1280]{1,0:T(8,128)(2,1)S(1)}, u32[]{:S(2)}, u32[]{:S(2)}) collective-permute-start(bf16[128,1280]{1,0:T(8,128)(2,1)} %get-tuple-element.141), channel_id=1, source_target_pairs={{0,96},{32,0},{64,32},{96,64},{1,97},{33,1},{65,33},{97,65},{2,98}... | collective-permute-start | bytes 983048 | tf_op jit(solution)/shard_map/ppermute | solution.py:798
  501.3 14.8 %collective-permute-start.56 = (bf16[128,1408]{1,0:T(8,128)(2,1)S(1)}, bf16[128,1408]{1,0:T(8,128)(2,1)S(1)}, u32[]{:S(2)}, u32[]{:S(2)}) collective-permute-start(bf16[128,1408]{1,0:T(8,128)(2,1)S(1)} %copy-done.71), channel_id=1, source_target_pairs={{0,24},{8,0},{16,8},{24,16},{1,25},{9,1},{17,9},{25,17},{2,26},{10... | collective-permute-start | bytes 1081352 | tf_op jit(solution)/shard_map/ppermute | solution.py:798
  510.9 10.7 %collective-permute-start.63 = (f32[16,512]{1,0:T(8,128)S(1)}, f32[16,512]{1,0:T(8,128)S(1)}, u32[]{:S(2)}, u32[]{:S(2)}) collective-permute-start(f32[16,512]{1,0:T(8,128)S(1)} %broadcast_add_fusion.2), channel_id=1, source_target_pairs={{0,24},{8,0},{16,8},{24,16},{1,25},{9,1},{17,9},{25,17},{2,26},{10... | collective-permute-start | bytes 98312 | tf_op jit(solution)/shard_map/ppermute | solution.py:798
  512.1 9.5 %collective-permute-start.62 = (f32[16,512]{1,0:T(8,128)S(1)}, f32[16,512]{1,0:T(8,128)S(1)}, u32[]{:S(2)}, u32[]{:S(2)}) collective-permute-start(f32[16,512]{1,0:T(8,128)S(1)} %broadcast_add_fusion.2), channel_id=1, source_target_pairs={{0,16},{8,24},{16,0},{24,8},{1,17},{9,25},{17,1},{25,9},{2,18},{10... | collective-permute-start | bytes 98312 | tf_op jit(solution)/shard_map/ppermute | solution.py:798
  514.9 16.6 %collective-permute-start.52 = (bf16[64,4096]{1,0:T(8,128)(2,1)S(1)}, bf16[64,4096]{1,0:T(8,128)(2,1)S(1)}, u32[]{:S(2)}, u32[]{:S(2)}) collective-permute-start(bf16[64,4096]{1,0:T(8,128)(2,1)S(1)} %broadcast_add_fusion.1), channel_id=1, source_target_pairs={{0,2},{1,3},{2,0},{3,1},{4,6},{5,7},{6,4},{7,5},{8,10},{9,11},{10,... | collective-permute-start | bytes 1572872 | tf_op jit(solution)/shard_map/ppermute | solution.py:807
  521.7 9.8 %collective-permute-start.64 = (f32[16,512]{1,0:T(8,128)S(1)}, f32[16,512]{1,0:T(8,128)S(1)}, u32[]{:S(2)}, u32[]{:S(2)}) collective-permute-start(f32[16,512]{1,0:T(8,128)S(1)} %add_add_fusion), channel_id=1, source_target_pairs={{0,4},{4,0},{1,5},{5,1},{2,6},{6,2},{3,7},{7,3},{8,12},{12,8},{9,1... | collective-permute-start | bytes 98312 | tf_op jit(solution)/shard_map/ppermute | solution.py:798
  526.7 12.5 %collective-permute-start.60 = (bf16[64,2688]{1,0:T(8,128)(2,1)}, bf16[64,2688]{1,0:T(8,128)(2,1)S(1)}, u32[]{:S(2)}, u32[]{:S(2)}) collective-permute-start(bf16[64,2688]{1,0:T(8,128)(2,1)} %get-tuple-element.143), channel_id=1, source_target_pairs={{0,4},{4,0},{1,5},{5,1},{2,6},{6,2},{3,7},{7,3},{8,12},{12,8},{9,1... | collective-permute-start | bytes 1032200 | tf_op jit(solution)/shard_map/ppermute | solution.py:798
  531.8 15.4 %collective-permute-start.53 = (bf16[2,64,4096]{2,1,0:T(8,128)(2,1)S(1)}, bf16[2,64,4096]{2,1,0:T(8,128)(2,1)S(1)}, u32[]{:S(2)}, u32[]{:S(2)}) collective-permute-start(bf16[2,64,4096]{2,1,0:T(8,128)(2,1)S(1)} %pad_maximum_fusion.6), channel_id=1, source_target_pairs={{0,1},{1,0},{2,3},{3,2},{4,5},{5,4},{6,7},{7,6},{8,9},{9,8},{10,11... | collective-permute-start | bytes 3145736 | tf_op jit(solution)/shard_map/ppermute | solution.py:807
  (102 other events, 683.5 us)
Sparse Core Ops, SparseCore 0:
  98.4 98.0 all-gather.1
  324.5 93.1 reduce-scatter.1

commit v4 on v3

--- a/solution.py
+++ b/solution.py
@@ -760,19 +760,20 @@
     )(place, *arrays, *deps)
 
 
-def run_input_grads(rim, gq, gkv, gscal, og, left, right):
+def run_input_grads(rim, gq, gkv, gscal, og, left, right, deps):
     inner = HEADS * DK
     width = left.shape[0]
     tokens = 2 * TOK
     cut = width // 4
     return pl.pallas_call(
-        input_grads,
+        ignoring(input_grads, 7, len(deps)),
         grid=(4,),
         in_specs=[whole(m.shape) for m in (rim, gq, gkv, gscal, og)]
         + [
             by_rows(cut, left.shape[1]),
             by_rows(cut, right.shape[1]),
-        ],
+        ]
+        + dep_specs(deps),
         out_specs=pl.BlockSpec((tokens, cut), lambda s: (0, s)),
         out_shape=jax.ShapeDtypeStruct((tokens, width), bf16),
         scratch_shapes=[
@@ -781,7 +782,7 @@
         ],
         compiler_params=params(),
         cost_estimate=cost(2 * tokens * width * 5 * inner, 2 * width * 5 * inner),
-    )(rim, gq, gkv, gscal, og, left, right)
+    )(rim, gq, gkv, gscal, og, left, right, *deps)
 
 
 SEQ_AXES = ("x", "z", "y")
@@ -865,13 +866,14 @@
 
 def head_gather(rows):
     chip, core = head_place()
-    got = flipped(rows, "head", 2)
+    chip_got = flipped(rows, "head", 2)
     first = chip == 0
-    chips = jnp.stack([jnp.where(first, rows, got), jnp.where(first, got, rows)])
+    chips = [jnp.where(first, rows, chip_got), jnp.where(first, chip_got, rows)]
+    chips = jnp.stack(chips)
     got = flipped(chips, "head", 1)
     first = core == 0
     cores = [jnp.where(first, chips, got), jnp.where(first, got, chips)]
-    return jnp.stack(cores, axis=1).reshape(HEADS * rows.shape[0], -1)
+    return jnp.stack(cores, axis=1).reshape(HEADS * rows.shape[0], -1), chip_got
 
 
 def group_scatter(partial_rows):
@@ -985,7 +987,7 @@
     rows, cols = arrays[0].shape[0] // 2, arrays[0].shape[1] + arrays[4].shape[1]
     shapes = [((rows, cols), f32), ((rows, cols), bf16)]
     kept, sent = in_vmem(add_and_halve, shapes, places(), *arrays, deps=deps)
-    return kept + along(sent, "y", 1).astype(f32), sent
+    return kept + along(sent, "y", 1).astype(f32)
 
 
 def pair_up(place_ref, left, left_other, right, right_other, left_out, right_out):
@@ -1179,7 +1181,7 @@
     grad_normed = group_scatter(ffn_part)[0]
     back = norm_pull(residual, scale_ffn, gain_ffn, grad_normed)
     grad_residual = mine(grad_rows).astype(f32) + back
-    grad_mixer = head_gather(grad_residual.astype(bf16))
+    grad_mixer = head_gather(grad_residual.astype(bf16))[0]
 
     grad_gated = mm(grad_mixer, w_out_t)
     do, gate_grad_mix, local, part_gain_head = run_gate_backward(
@@ -1212,13 +1214,13 @@
     gtaps = jnp.concatenate([gtaps_q, gtaps_kv], axis=1).reshape(12, inner)
     tail = jnp.concatenate([part_gain_head[:1], grate[:1]], axis=1)
     tail = jnp.pad(tail, ((0, 3), (0, inner - tail.shape[1])))
-    small = sum_along(later(jnp.concatenate([gtaps, tail], axis=0), blocks[0]), "x")
+    small = jnp.concatenate([gtaps, tail], axis=0)
     rim = jnp.concatenate([gq[2 * TOK :], gkv[2 * TOK :]], axis=1)
     rim = passed_along(rim, -1)
     input_sent = run_input_grads(
-        rim, gq, gkv, gscal, gate_grad_mix, all_left, all_right
-    )
-    partials, near_gate = reduce_near(owns, partials, (small, input_sent))
+        rim, gq, gkv, gscal, gate_grad_mix, all_left, all_right, (blocks[0],)
+    )
+    partials, near_gate = reduce_near(owns, partials, (input_sent,))
     ffn = ffn.reshape(2, -1, 3, span)[..., :units]
     ffn_other = along(later(pick(ffn, 1 - y_place, 0), near_gate), "y", 1)
     ffn = ordered(pick(ffn, y_place, 0), ffn_other, y_place, 2).astype(f32)
@@ -1228,11 +1230,11 @@
     back_in = norm_pull(own, row_scale(own), gain_in, grad_normed_in)
     both = jnp.concatenate([residual + ffn_out, grad_residual + back_in], axis=1)
     both = both.astype(bf16)
-    partials, cross_gate = reduce_cross(partials, (both, ffn_other))
-    small = sum_along(later(small, cross_gate), "z")
-    mixer_w, end_gate = reduce_end(partials, ())
-    small = sum_along(later(small, end_gate), "y")
-    both = head_gather(later(both, cross_gate))
+    small = sum_along(later(small, ffn_other), "x")
+    partials, cross_gate = reduce_cross(partials, (both, ffn_other, small))
+    mixer_w = reduce_end(partials, ())
+    both, chip_got = head_gather(later(both, cross_gate))
+    small = sum_along(sum_along(later(small, chip_got), "z"), "y")
     outputs, grad_in = both[:, :width], both[:, width:].astype(f32)
 
     rows = width // SEQ

time: 565 us -> 568 us (level)
    unnamed x155 -> x169, local copies, waits for them, and re-layouts: 19.5 us -> 20.9 us
  transfers between devices with their start and end apart: 74 -> 74, of which waited for: 31 -> 33; matrix products, arithmetic and copies ran while one was open for 14% -> 14% of each run, Pallas kernels for 14% -> 14%
where the time goes in v4:
time: 568 us; the launch traced here: 560 us
  waiting for transfers between devices  164 us (29%)
  starting transfers between devices  149 us (26%)
  Pallas kernels  102 us (18%)
  local copies, waits for them, and re-layouts  52.7 us (9%)
  other arithmetic  42.9 us (8%)
  matrix products  28.6 us (5%)
  between operations  20.8 us (4%)
    ppermute x46, waiting for transfers between devices, along(): lax.ppermute(array, axis, [(i, (i + by) % count) for i in range(count)])  82.4 us
    ppermute x46, starting transfers between devices, along(): lax.ppermute(array, axis, [(i, (i + by) % count) for i in range(count)])  74.9 us
    ppermute x20, waiting for transfers between devices, flipped(): return lax.ppermute(array, axes, [(i, i ^ mask) for i in range(count)])  42.5 us
    all_to_all x4, waiting for transfers between devices, exchange(): return lax.all_to_all(array, axis, split_axis=0, concat_axis=0, tiled=True)  38.7 us
    ppermute x20, starting transfers between devices, flipped(): return lax.ppermute(array, axes, [(i, i ^ mask) for i in range(count)])  30.7 us
    dot_general x9, matrix products, mm(): return jnp.einsum(dims, a, b, preferred_element_type=f32)  28.6 us
    pallas_call x7, Pallas kernels, in_vmem(): pl.pallas_call(ignoring(kernel, 1 + len(arrays), len(deps)), in_specs=[pl...  26.4 us
    all_to_all x4, starting transfers between devices, exchange(): return lax.all_to_all(array, axis, split_axis=0, concat_axis=0, tiled=True)  25.2 us
  transfers between devices with their start and end apart: 74, of which 33 were waited for; matrix products, arithmetic and copies ran while one was open for 14% of the time, Pallas kernels for 14%

profile of v4, /device:TPU:1, one launch (start us, length us, event | category | flops | bytes accessed | tf_op | source)
XLA Modules:
  0.0 560.0 jit_solution(14643706255515664917)
XLA Ops:
  9.9 3.8 collective-permute-start.1
  15.3 5.6 %collective-permute-done.2.refs_4_ = bf16[64,1280]{1,0:T(8,128)(2,1)S(1)} collective-permute-done((bf16[64,1280]{1,0:T(8,128)(2,1)S(1)}, bf16[64,1280]{1,0:T(8,128)(2,1)S(1)}, u32[]{:S(2)}, u32[]{:S(2)}) %collective-permute-start.2) | collective-permute-done | bytes 163872 | tf_op jit(solution)/shard_map/ppermute | solution.py:799
  30.8 5.8 %collective-permute-done.5.refs_3_.refs_7_ = bf16[128,1280]{1,0:T(8,128)(2,1)S(1)} collective-permute-done((bf16[128,1280]{1,0:T(8,128)(2,1)}, bf16[128,1280]{1,0:T(8,128)(2,1)S(1)}, u32[]{:S(2)}, u32[]{:S(2)}) %collective-permute-start.5) | collective-permute-done | bytes 327712 | tf_op jit(solution)/shard_map/ppermute | solution.py:799
  50.5 3.5 shard_map.290
  64.2 3.6 collective-permute-start.26
  71.9 17.0 %collective-permute-start = (bf16[2,16,2048]{2,1,0:T(8,128)(2,1)S(1)}, bf16[2,16,2048]{2,1,0:T(8,128)(2,1)S(1)}, u32[]{:S(2)}, u32[]{:S(2)}) collective-permute-start(bf16[2,16,2048]{2,1,0:T(8,128)(2,1)S(1)} %slice.202), channel_id=1, source_target_pairs={{0,4},{4,8},{8,12},{12,16},{16,20},{20,24},{24,28},{28,32},{32,36}... | collective-permute-start | bytes 393224 | tf_op jit(solution)/shard_map/ppermute | solution.py:794
  91.3 4.2 shard_map.291
  114.1 8.2 %collective-permute-done.18 = bf16[2,128,1280]{2,1,0:T(8,128)(2,1)S(1)} collective-permute-done((bf16[2,128,1280]{2,1,0:T(8,128)(2,1)S(1)}, bf16[2,128,1280]{2,1,0:T(8,128)(2,1)S(1)}, u32[]{:S(2)}, u32[]{:S(2)}) %collective-permute-start.18) | collective-permute-done | bytes 655392 | tf_op jit(solution)/shard_map/ppermute | solution.py:799
  122.3 4.9 collective-permute-done.17
  128.8 5.4 collective-permute-done.16
  141.7 11.1 %shard_map.292 = (bf16[32,160,128]{2,1,0:T(8,128)(2,1)}, bf16[8,128,128]{2,1,0:T(8,128)(2,1)}, f32[8,128,128]{2,1,0:T(8,128)}, bf16[8,128,128]{2,1,0:T(8,128)(2,1)}, f32[8,128,256]{2,1,0:T(8,128)}) custom-call(bf16[288,1536]{1,0:T(8,128)(2,1)} %pad_maximum_fusion.7.pre_ref.rim_ref.refs_0_.refs_1_, ...), custom_call_target="tpu_custom_call" | custom-call | flops 10000000000 | bytes 6000000 | tf_op jit(solution)/shard_map/pallas_call | solution.py:548
  152.8 7.6 %all-to-all-start = ((bf16[32,160,128]{2,1,0:T(8,128)(2,1)}), bf16[32,160,128]{2,1,0:T(8,128)(2,1)S(1)}, u32[]{:S(2)}, u32[]{:S(2)}) async-start(bf16[32,160,128]{2,1,0:T(8,128)(2,1)} %get-tuple-element.100), calls=%async_computation | async-start | bytes 2621440 | tf_op jit(solution)/shard_map/all_to_all | solution.py:845
  163.7 27.6 %all-to-all-done.got_ref.refs_0_ = bf16[32,160,128]{2,1,0:T(8,128)(2,1)S(1)} async-done(((bf16[32,160,128]{2,1,0:T(8,128)(2,1)}), bf16[32,160,128]{2,1,0:T(8,128)(2,1)S(1)}, u32[]{:S(2)}, u32[]{:S(2)}) %all-to-all-start) | async-done | bytes 1310752 | tf_op jit(solution)/shard_map/all_to_all | solution.py:845
  192.4 5.9 %shard_map.293 = bf16[32,32,128]{2,1,0:T(8,128)(2,1)} custom-call(bf16[32,160,128]{2,1,0:T(8,128)(2,1)} %copy-done.19), custom_call_target="tpu_custom_call" | custom-call | flops 1000000000 | bytes 3000000 | tf_op jit(solution)/shard_map/pallas_call | solution.py:573
  198.3 7.0 %all-to-all-start.1 = ((bf16[32,32,128]{2,1,0:T(8,128)(2,1)}), bf16[32,32,128]{2,1,0:T(8,128)(2,1)S(1)}, u32[]{:S(2)}, u32[]{:S(2)}) async-start(bf16[32,32,128]{2,1,0:T(8,128)(2,1)} %shard_map.293), calls=%async_computation.1 | async-start | bytes 524288 | tf_op jit(solution)/shard_map/all_to_all | solution.py:845
  208.8 6.0 %all-to-all-done.1 = bf16[32,32,128]{2,1,0:T(8,128)(2,1)S(1)} async-done(((bf16[32,32,128]{2,1,0:T(8,128)(2,1)}), bf16[32,32,128]{2,1,0:T(8,128)(2,1)S(1)}, u32[]{:S(2)}, u32[]{:S(2)}) %all-to-all-start.1) | async-done | bytes 262176 | tf_op jit(solution)/shard_map/all_to_all | solution.py:845
  221.4 6.1 %collective-permute-start.20 = (bf16[2,64,2048]{2,1,0:T(8,128)(2,1)S(1)}, bf16[2,64,2048]{2,1,0:T(8,128)(2,1)S(1)}, u32[]{:S(2)}, u32[]{:S(2)}) collective-permute-start(bf16[2,64,2048]{2,1,0:T(8,128)(2,1)S(1)} %dynamic-slice_bitcast_fusion.3), channel_id=1, source_target_pairs={{0,1},{1,0},{2,3},{3,2},{4,5},{5,4},{6,7},{7,6},{8,9},{9,8},{10,11... | collective-permute-start | bytes 1572872 | tf_op jit(solution)/shard_map/ppermute | solution.py:808
  230.7 7.4 %collective-permute-done.21 = bf16[64,2048]{1,0:T(8,128)(2,1)S(1)} collective-permute-done((bf16[64,2048]{1,0:T(8,128)(2,1)S(1)}, bf16[64,2048]{1,0:T(8,128)(2,1)S(1)}, u32[]{:S(2)}, u32[]{:S(2)}) %collective-permute-start.21) | collective-permute-done | bytes 262176 | tf_op jit(solution)/shard_map/ppermute | solution.py:808
  241.8 4.9 collective-permute-done.22
  250.1 3.8 collective-permute-done.24
  260.5 6.3 %fusion.2 = f32[512,1536]{1,0:T(8,128)S(1)} fusion(bf16[512,2048]{1,0:T(8,128)(2,1)} %bitcast.262, bf16[2048,2304]{1,0:T(8,128)(2,1)} %all-gather.2.cloned.1.call-done), kind=kOutput, calls=%fused_computation.2 | convolution fusion | flops 3221225472 | bytes 11534336 | tf_op jit(solution)/shard_map/ij,jk->ik/dot_general | solution.py:1045
  270.4 3.7 fusion.8
  281.3 5.1 collective-permute-done.30
  286.4 6.5 %collective-permute-done.28 = bf16[64,2048]{1,0:T(8,128)(2,1)S(1)} collective-permute-done((bf16[64,2048]{1,0:T(8,128)(2,1)S(1)}, bf16[64,2048]{1,0:T(8,128)(2,1)S(1)}, u32[]{:S(2)}, u32[]{:S(2)}) %collective-permute-start.28) | collective-permute-done | bytes 262176 | tf_op jit(solution)/shard_map/ppermute | solution.py:808
  295.2 6.5 %collective-permute-done.31 = bf16[64,2048]{1,0:T(8,128)(2,1)S(1)} collective-permute-done((bf16[64,2048]{1,0:T(8,128)(2,1)S(1)}, bf16[64,2048]{1,0:T(8,128)(2,1)S(1)}, u32[]{:S(2)}, u32[]{:S(2)}) %collective-permute-start.31) | collective-permute-done | bytes 262176 | tf_op jit(solution)/shard_map/ppermute | solution.py:808
  307.7 3.5 fusion.19.gg_ref
  314.1 9.8 %shard_map.303 = bf16[2048,2304]{1,0:T(8,128)(2,1)} custom-call(bf16[512,2048]{1,0:T(8,128)(2,1)} %bitcast.263, bf16[512,2048]{1,0:T(8,128)(2,1)} %pad_maximum_fusion.1.refs_1_, bf16[512,1536]{1,0:T(8,128)(2,1)} %pad_maximum_fusion.3.refs_2_, bf16[512,768]{1,0:T(8,128)(2,1)} %get-tuple-element.264.refs_3_, bf16[32,32,128]{2,1,0:T(8,128)(2,1)} %get-tuple-element.103.refs_4_), custom_call_target="tpu_custom_call" | custom-call | flops 4831838208 | bytes 9437184 | tf_op jit(solution)/shard_map/pallas_call | solution.py:730
  325.9 3.7 convolution_convert_fusion
  332.6 3.9 all-to-all-start.2
  336.5 7.9 %shard_map.296 = (bf16[288,512]{1,0:T(8,128)(2,1)}, f32[4,512]{1,0:T(4,128)}, bf16[8,128,128]{2,1,0:T(8,128)(2,1)}, f32[8,128,128]{2,1,0:T(8,128)}, f32[8,128,12...) custom-call(bf16[288,1536]{1,0:T(8,128)(2,1)} %pad_maximum_fusion.7.pre_ref.rim_ref.refs_0_.refs_1_, ...), custom_call_target="tpu_custom_call" | custom-call | flops 5000000000 | bytes 10000000 | tf_op jit(solution)/shard_map/pallas_call | solution.py:649
  348.5 5.9 %shard_map.297 = bf16[32,32,128]{2,1,0:T(8,128)(2,1)} custom-call(bf16[32,160,128]{2,1,0:T(8,128)(2,1)} %copy-done.19, bf16[32,32,128]{2,1,0:T(8,128)(2,1)} %copy-done.51, bf16[288,512]{1,0:T(8,128)(2,1)} %get-tuple-element.106.refs_2_.refs_4_.refs_1_), custom_call_target="tpu_custom_call" | custom-call | flops 1000000000 | bytes 3000000 | tf_op jit(solution)/shard_map/pallas_call | solution.py:583
  354.4 6.8 %all-to-all-start.3 = ((bf16[32,32,128]{2,1,0:T(8,128)(2,1)}), bf16[32,32,128]{2,1,0:T(8,128)(2,1)}, u32[]{:S(2)}, u32[]{:S(2)}) async-start(bf16[32,32,128]{2,1,0:T(8,128)(2,1)} %shard_map.297), calls=%async_computation.3 | async-start | bytes 524288 | tf_op jit(solution)/shard_map/all_to_all | solution.py:845
  371.8 10.2 %shard_map.298 = (bf16[288,1024]{1,0:T(8,128)(2,1)}, bf16[256,128]{1,0:T(8,128)(2,1)}, f32[4,1024]{1,0:T(4,128)}, f32[8,128]{1,0:T(8,128)}) custom-call(bf16[288,1536]{1,0:T(8,128)(2,1)} %pad_maximum_fusion.7.pre_ref.rim_ref.refs_0_.refs_1_, bf16[288,1536]{1,0:T(8,128)(2,1)} %pad_maximum_fusion.7.pre_ref.rim_ref.refs_0_.refs_1_, ...), custom_call_target="tpu_custom_call" | custom-call | flops 5000000000 | bytes 10000000 | tf_op jit(solution)/shard_map/pallas_call | solution.py:691
  382.0 4.5 shard_map.299
  396.4 7.4 %shard_map.300 = (bf16[512,1408]{1,0:T(8,128)(2,1)}, bf16[512,1408]{1,0:T(8,128)(2,1)}, bf16[512,1408]{1,0:T(8,128)(2,1)}, bf16[512,1280]{1,0:T(8,128)(2,1)}, bf...) custom-call(s32[2]{0:T(128)} %pad_add_fusion.1.refs_0_, bf16[288,2048]{1,0:T(8,128)(2,1)} %copy-done.21, ...), custom_call_target="tpu_custom_call" | custom-call | flops 2684354560 | bytes 10485760 | tf_op jit(solution)/shard_map/pallas_call | solution.py:753
  404.5 7.6 %shard_map.301.refs_9_ = bf16[256,2048]{1,0:T(8,128)(2,1)} custom-call(bf16[32,1536]{1,0:T(8,128)(2,1)} %copy-done.61, bf16[288,512]{1,0:T(8,128)(2,1)} %get-tuple-element.106.refs_2_.refs_4_.refs_1_, bf16[288,1024]{1,0:T(8,128)(2,1)} %get-tuple-element.113.refs_5_.refs_2_, bf16[256,128]{1,0:T(8,128)(2,1)} %get-tuple-element.114.refs_6_.refs_3_, ...), custom_call_target="tpu_custom_call" | custom-call | flops 2684354560 | bytes 10485760 | tf_op jit(solution)/shard_map/pallas_call | solution.py:768
  416.9 6.1 %shard_map.302 = (bf16[512,1408]{1,0:T(8,128)(2,1)}, bf16[512,1408]{1,0:T(8,128)(2,1)}, bf16[512,1280]{1,0:T(8,128)(2,1)}, bf16[512,1280]{1,0:T(8,128)(2,1)}) custom-call(s32[3]{0:T(128)} %pad_add_fusion.refs_0_, bf16[512,1408]{1,0:T(8,128)(2,1)} %get-tuple-element.117.refs_7_.refs_1_, bf16[512,1408]{1,0:T(8,128)(2,1)} %get-tuple-element.118.refs_2_, ...), custom_call_target="tpu_custom_call" | custom-call | flops 8257536 | bytes 8257536 | tf_op jit(solution)/shard_map/pallas_call | solution.py:908
  433.2 8.3 %collective-permute-start.44 = (bf16[512,1408]{1,0:T(8,128)(2,1)}, bf16[512,1408]{1,0:T(8,128)(2,1)}, u32[]{:S(2)}, u32[]{:S(2)}) collective-permute-start(bf16[512,1408]{1,0:T(8,128)(2,1)} %get-tuple-element.124), channel_id=1, source_target_pairs={{0,32},{32,64},{64,96},{96,0},{1,33},{33,65},{65,97},{97,1},{2,34}... | collective-permute-start | bytes 4325384 | tf_op jit(solution)/shard_map/ppermute | solution.py:799
  446.5 5.7 %collective-permute-start.48 = (bf16[64,3,704]{2,1,0:T(4,128)(2,1)S(1)}, bf16[64,3,704]{2,1,0:T(4,128)(2,1)S(1)}, u32[]{:S(2)}, u32[]{:S(2)}) collective-permute-start(bf16[64,3,704]{2,1,0:T(4,128)(2,1)S(1)} %add_bitcast_fusion), channel_id=1, source_target_pairs={{0,4},{4,0},{1,5},{5,1},{2,6},{6,2},{3,7},{7,3},{8,12},{12,8},{9,1... | collective-permute-start | bytes 811016 | tf_op jit(solution)/shard_map/ppermute | solution.py:799
  452.5 7.7 %collective-permute-done.48.refs_8_ = bf16[64,3,704]{2,1,0:T(4,128)(2,1)S(1)} collective-permute-done((bf16[64,3,704]{2,1,0:T(4,128)(2,1)S(1)}, bf16[64,3,704]{2,1,0:T(4,128)(2,1)S(1)}, u32[]{:S(2)}, u32[]{:S(2)}) %collective-permute-start.48) | collective-permute-done | bytes 270368 | tf_op jit(solution)/shard_map/ppermute | solution.py:799
  463.7 11.0 %collective-permute-done.51 = f32[16,512]{1,0:T(8,128)S(1)} collective-permute-done((f32[16,512]{1,0:T(8,128)S(1)}, f32[16,512]{1,0:T(8,128)S(1)}, u32[]{:S(2)}, u32[]{:S(2)}) %collective-permute-start.51) | collective-permute-done | bytes 32800 | tf_op jit(solution)/shard_map/ppermute | solution.py:799
  479.5 3.4 collective-permute-done.49
  483.5 5.6 shard_map.304
  499.0 9.2 %collective-permute-done.58.refs_7_ = bf16[128,1280]{1,0:T(8,128)(2,1)S(1)} collective-permute-done((bf16[128,1280]{1,0:T(8,128)(2,1)}, bf16[128,1280]{1,0:T(8,128)(2,1)S(1)}, u32[]{:S(2)}, u32[]{:S(2)}) %collective-permute-start.58) | collective-permute-done | bytes 327712 | tf_op jit(solution)/shard_map/ppermute | solution.py:799
  510.5 4.9 collective-permute-done.59.refs_8_
  520.7 8.3 %collective-permute-start.63 = (f32[16,512]{1,0:T(8,128)S(1)}, f32[16,512]{1,0:T(8,128)S(1)}, u32[]{:S(2)}, u32[]{:S(2)}) collective-permute-start(f32[16,512]{1,0:T(8,128)S(1)} %broadcast_add_fusion.2), channel_id=1, source_target_pairs={{0,24},{8,0},{16,8},{24,16},{1,25},{9,1},{17,9},{25,17},{2,26},{10... | collective-permute-start | bytes 98312 | tf_op jit(solution)/shard_map/ppermute | solution.py:799
  533.8 4.4 collective-permute-start.53
  539.6 5.2 collective-permute-start.67
  (444 shorter events, 210.8 us)
Async XLA Ops:
  7.2 253.3 %all-gather.2.cloned.1.call-start = ((), (), s32[]{:S(2)}) async-start(), calls=%async_computation.5 | async-start | bytes 10027008 | tf_op jit(solution)/shard_map/all_gather | solution.py:1124
  9.9 11.1 %collective-permute-start.1 = (bf16[64,1408]{1,0:T(8,128)(2,1)S(1)}, bf16[64,1408]{1,0:T(8,128)(2,1)S(1)}, u32[]{:S(2)}, u32[]{:S(2)}) collective-permute-start(bf16[64,1408]{1,0:T(8,128)(2,1)S(1)} %fusion.60.refs_1_), channel_id=1, source_target_pairs={{0,4},{4,0},{1,5},{5,1},{2,6},{6,2},{3,7},{7,3},{8,12},{12,8},{9,1... | collective-permute-start | bytes 540680 | tf_op jit(solution)/shard_map/ppermute | solution.py:799
  24.4 12.3 %collective-permute-start.3 = (bf16[128,1408]{1,0:T(8,128)(2,1)}, bf16[128,1408]{1,0:T(8,128)(2,1)S(1)}, u32[]{:S(2)}, u32[]{:S(2)}) collective-permute-start(bf16[128,1408]{1,0:T(8,128)(2,1)} %get-tuple-element.86.refs_1_), channel_id=1, source_target_pairs={{0,32},{32,64},{64,96},{96,0},{1,33},{33,65},{65,97},{97,1},{2,34}... | collective-permute-start | bytes 1081352 | tf_op jit(solution)/shard_map/ppermute | solution.py:799
  25.6 11.1 %collective-permute-start.4 = (bf16[128,1408]{1,0:T(8,128)(2,1)}, bf16[128,1408]{1,0:T(8,128)(2,1)S(1)}, u32[]{:S(2)}, u32[]{:S(2)}) collective-permute-start(bf16[128,1408]{1,0:T(8,128)(2,1)} %get-tuple-element.86.refs_1_), channel_id=1, source_target_pairs={{0,96},{32,0},{64,32},{96,64},{1,97},{33,1},{65,33},{97,65},{2,98}... | collective-permute-start | bytes 1081352 | tf_op jit(solution)/shard_map/ppermute | solution.py:799
  27.0 9.6 %collective-permute-start.5 = (bf16[128,1280]{1,0:T(8,128)(2,1)}, bf16[128,1280]{1,0:T(8,128)(2,1)S(1)}, u32[]{:S(2)}, u32[]{:S(2)}) collective-permute-start(bf16[128,1280]{1,0:T(8,128)(2,1)} %get-tuple-element.87.refs_6_), channel_id=1, source_target_pairs={{0,8},{8,16},{16,24},{24,0},{1,9},{9,17},{17,25},{25,1},{2,10},{10... | collective-permute-start | bytes 983048 | tf_op jit(solution)/shard_map/ppermute | solution.py:799
  53.9 36.2 %collective-permute-start.11 = (bf16[4,128,1408]{2,1,0:T(8,128)(2,1)}, bf16[4,128,1408]{2,1,0:T(8,128)(2,1)}, u32[]{:S(2)}, u32[]{:S(2)}) collective-permute-start(bf16[4,128,1408]{2,1,0:T(8,128)(2,1)} %get-tuple-element.92), channel_id=1, source_target_pairs={{0,8},{8,16},{16,24},{24,0},{1,9},{9,17},{17,25},{25,1},{2,10},{10... | collective-permute-start | bytes 4325384 | tf_op jit(solution)/shard_map/ppermute | solution.py:799
  54.3 35.8 %collective-permute-start.12 = (bf16[4,128,1408]{2,1,0:T(8,128)(2,1)}, bf16[4,128,1408]{2,1,0:T(8,128)(2,1)S(1)}, u32[]{:S(2)}, u32[]{:S(2)}) collective-permute-start(bf16[4,128,1408]{2,1,0:T(8,128)(2,1)} %get-tuple-element.92), channel_id=1, source_target_pairs={{0,24},{8,0},{16,8},{24,16},{1,25},{9,1},{17,9},{25,17},{2,26},{10... | collective-permute-start | bytes 4325384 | tf_op jit(solution)/shard_map/ppermute | solution.py:799
  57.4 32.7 %collective-permute-start.13 = (bf16[4,128,1280]{2,1,0:T(8,128)(2,1)}, bf16[4,128,1280]{2,1,0:T(8,128)(2,1)}, u32[]{:S(2)}, u32[]{:S(2)}) collective-permute-start(bf16[4,128,1280]{2,1,0:T(8,128)(2,1)} %get-tuple-element.93), channel_id=1, source_target_pairs={{0,32},{32,64},{64,96},{96,0},{1,33},{33,65},{65,97},{97,1},{2,34}... | collective-permute-start | bytes 3932168 | tf_op jit(solution)/shard_map/ppermute | solution.py:799
  57.4 32.6 %collective-permute-start.14 = (bf16[4,128,1280]{2,1,0:T(8,128)(2,1)}, bf16[4,128,1280]{2,1,0:T(8,128)(2,1)}, u32[]{:S(2)}, u32[]{:S(2)}) collective-permute-start(bf16[4,128,1280]{2,1,0:T(8,128)(2,1)} %get-tuple-element.93), channel_id=1, source_target_pairs={{0,96},{32,0},{64,32},{96,64},{1,97},{33,1},{65,33},{97,65},{2,98}... | collective-permute-start | bytes 3932168 | tf_op jit(solution)/shard_map/ppermute | solution.py:799
  71.9 31.4 %collective-permute-start = (bf16[2,16,2048]{2,1,0:T(8,128)(2,1)S(1)}, bf16[2,16,2048]{2,1,0:T(8,128)(2,1)S(1)}, u32[]{:S(2)}, u32[]{:S(2)}) collective-permute-start(bf16[2,16,2048]{2,1,0:T(8,128)(2,1)S(1)} %slice.202), channel_id=1, source_target_pairs={{0,4},{4,8},{8,12},{12,16},{16,20},{20,24},{24,28},{28,32},{32,36}... | collective-permute-start | bytes 393224 | tf_op jit(solution)/shard_map/ppermute | solution.py:794
  106.7 15.5 %collective-permute-start.18 = (bf16[2,128,1280]{2,1,0:T(8,128)(2,1)S(1)}, bf16[2,128,1280]{2,1,0:T(8,128)(2,1)S(1)}, u32[]{:S(2)}, u32[]{:S(2)}) collective-permute-start(bf16[2,128,1280]{2,1,0:T(8,128)(2,1)S(1)} %copy-done.74), channel_id=1, source_target_pairs={{0,96},{32,0},{64,32},{96,64},{1,97},{33,1},{65,33},{97,65},{2,98}... | collective-permute-start | bytes 1966088 | tf_op jit(solution)/shard_map/ppermute | solution.py:799
  107.7 19.5 %collective-permute-start.17 = (bf16[2,128,1280]{2,1,0:T(8,128)(2,1)S(1)}, bf16[2,128,1280]{2,1,0:T(8,128)(2,1)S(1)}, u32[]{:S(2)}, u32[]{:S(2)}) collective-permute-start(bf16[2,128,1280]{2,1,0:T(8,128)(2,1)S(1)} %copy-done.73), channel_id=1, source_target_pairs={{0,32},{32,64},{64,96},{96,0},{1,33},{33,65},{65,97},{97,1},{2,34}... | collective-permute-start | bytes 1966088 | tf_op jit(solution)/shard_map/ppermute | solution.py:799
  109.7 24.9 %collective-permute-start.15 = (bf16[2,128,1408]{2,1,0:T(8,128)(2,1)S(1)}, bf16[2,128,1408]{2,1,0:T(8,128)(2,1)S(1)}, u32[]{:S(2)}, u32[]{:S(2)}) collective-permute-start(bf16[2,128,1408]{2,1,0:T(8,128)(2,1)S(1)} %copy-done.71), channel_id=1, source_target_pairs={{0,8},{8,16},{16,24},{24,0},{1,9},{9,17},{17,25},{25,1},{2,10},{10... | collective-permute-start | bytes 2162696 | tf_op jit(solution)/shard_map/ppermute | solution.py:799
  109.8 24.5 %collective-permute-start.16 = (bf16[2,128,1408]{2,1,0:T(8,128)(2,1)S(1)}, bf16[2,128,1408]{2,1,0:T(8,128)(2,1)S(1)}, u32[]{:S(2)}, u32[]{:S(2)}) collective-permute-start(bf16[2,128,1408]{2,1,0:T(8,128)(2,1)S(1)} %copy-done.72), channel_id=1, source_target_pairs={{0,24},{8,0},{16,8},{24,16},{1,25},{9,1},{17,9},{25,17},{2,26},{10... | collective-permute-start | bytes 2162696 | tf_op jit(solution)/shard_map/ppermute | solution.py:799
  152.8 38.5 %all-to-all-start = ((bf16[32,160,128]{2,1,0:T(8,128)(2,1)}), bf16[32,160,128]{2,1,0:T(8,128)(2,1)S(1)}, u32[]{:S(2)}, u32[]{:S(2)}) async-start(bf16[32,160,128]{2,1,0:T(8,128)(2,1)} %get-tuple-element.100), calls=%async_computation | async-start | bytes 2621440 | tf_op jit(solution)/shard_map/all_to_all | solution.py:845
  160.4 48.4 %collective-permute-start.19 = (bf16[256,2048]{1,0:T(8,128)(2,1)S(1)}, bf16[256,2048]{1,0:T(8,128)(2,1)}, u32[]{:S(2)}, u32[]{:S(2)}) collective-permute-start(bf16[256,2048]{1,0:T(8,128)(2,1)S(1)} %bitcast.265), channel_id=1, source_target_pairs={{0,4},{4,0},{1,5},{5,1},{2,6},{6,2},{3,7},{7,3},{8,12},{12,8},{9,1... | collective-permute-start | bytes 3145736 | tf_op jit(solution)/shard_map/ppermute | solution.py:799
  198.3 16.5 %all-to-all-start.1 = ((bf16[32,32,128]{2,1,0:T(8,128)(2,1)}), bf16[32,32,128]{2,1,0:T(8,128)(2,1)S(1)}, u32[]{:S(2)}, u32[]{:S(2)}) async-start(bf16[32,32,128]{2,1,0:T(8,128)(2,1)} %shard_map.293), calls=%async_computation.1 | async-start | bytes 524288 | tf_op jit(solution)/shard_map/all_to_all | solution.py:845
  205.3 239.8 %reduce-scatter.2.cloned.1.call-start = ((), (), s32[]{:S(2)}) async-start(), calls=%async_computation.6 | async-start | bytes 10027008 | tf_op jit(solution)/shard_map/reduce_scatter | solution.py:1198
  239.1 10.9 %collective-permute-start.23 = (bf16[64,2048]{1,0:T(8,128)(2,1)S(1)}, bf16[64,2048]{1,0:T(8,128)(2,1)S(1)}, u32[]{:S(2)}, u32[]{:S(2)}) collective-permute-start(bf16[64,2048]{1,0:T(8,128)(2,1)S(1)} %multiply_convert_fusion.3), channel_id=1, source_target_pairs={{0,2},{1,3},{2,0},{3,1},{4,6},{5,7},{6,4},{7,5},{8,10},{9,11},{10,... | collective-permute-start | bytes 786440 | tf_op jit(solution)/shard_map/ppermute | solution.py:808
  239.3 14.6 %collective-permute-start.24 = (bf16[64,2048]{1,0:T(8,128)(2,1)S(1)}, bf16[64,2048]{1,0:T(8,128)(2,1)S(1)}, u32[]{:S(2)}, u32[]{:S(2)}) collective-permute-start(bf16[64,2048]{1,0:T(8,128)(2,1)S(1)} %multiply_convert_fusion.3), channel_id=1, source_target_pairs={{0,6},{1,7},{2,4},{3,5},{4,2},{5,3},{6,0},{7,1},{8,14},{9,15},{10,... | collective-permute-start | bytes 786440 | tf_op jit(solution)/shard_map/ppermute | solution.py:808
  277.4 9.1 %collective-permute-start.30 = (bf16[64,2048]{1,0:T(8,128)(2,1)S(1)}, bf16[64,2048]{1,0:T(8,128)(2,1)S(1)}, u32[]{:S(2)}, u32[]{:S(2)}) collective-permute-start(bf16[64,2048]{1,0:T(8,128)(2,1)S(1)} %get-tuple-element.273), channel_id=1, source_target_pairs={{0,6},{1,7},{2,4},{3,5},{4,2},{5,3},{6,0},{7,1},{8,14},{9,15},{10,... | collective-permute-start | bytes 786440 | tf_op jit(solution)/shard_map/ppermute | solution.py:808
  278.0 14.9 %collective-permute-start.28 = (bf16[64,2048]{1,0:T(8,128)(2,1)S(1)}, bf16[64,2048]{1,0:T(8,128)(2,1)S(1)}, u32[]{:S(2)}, u32[]{:S(2)}) collective-permute-start(bf16[64,2048]{1,0:T(8,128)(2,1)S(1)} %get-tuple-element.272), channel_id=1, source_target_pairs={{0,4},{1,5},{2,6},{3,7},{4,0},{5,1},{6,2},{7,3},{8,12},{9,13},{10,... | collective-permute-start | bytes 786440 | tf_op jit(solution)/shard_map/ppermute | solution.py:808
  332.0 29.2 %collective-permute-start.33 = (bf16[4,64,2048]{2,1,0:T(8,128)(2,1)}, bf16[4,64,2048]{2,1,0:T(8,128)(2,1)S(1)}, u32[]{:S(2)}, u32[]{:S(2)}) collective-permute-start(bf16[4,64,2048]{2,1,0:T(8,128)(2,1)} %dynamic-slice_bitcast_fusion), channel_id=1, source_target_pairs={{0,1},{1,0},{2,3},{3,2},{4,5},{5,4},{6,7},{7,6},{8,9},{9,8},{10,11... | collective-permute-start | bytes 3145736 | tf_op jit(solution)/shard_map/ppermute | solution.py:808
  332.6 15.1 %all-to-all-start.2 = ((bf16[32,32,128]{2,1,0:T(8,128)(2,1)}), bf16[32,32,128]{2,1,0:T(8,128)(2,1)S(1)}, u32[]{:S(2)}, u32[]{:S(2)}) async-start(bf16[32,32,128]{2,1,0:T(8,128)(2,1)} %get-tuple-element.103.refs_4_), calls=%async_computation.2 | async-start | bytes 524288 | tf_op jit(solution)/shard_map/all_to_all | solution.py:845
  354.4 17.4 %all-to-all-start.3 = ((bf16[32,32,128]{2,1,0:T(8,128)(2,1)}), bf16[32,32,128]{2,1,0:T(8,128)(2,1)}, u32[]{:S(2)}, u32[]{:S(2)}) async-start(bf16[32,32,128]{2,1,0:T(8,128)(2,1)} %shard_map.297), calls=%async_computation.3 | async-start | bytes 524288 | tf_op jit(solution)/shard_map/all_to_all | solution.py:845
  365.3 24.7 %collective-permute-start.36 = (bf16[64,2048]{1,0:T(8,128)(2,1)}, bf16[64,2048]{1,0:T(8,128)(2,1)S(1)}, u32[]{:S(2)}, u32[]{:S(2)}) collective-permute-start(bf16[64,2048]{1,0:T(8,128)(2,1)} %get-tuple-element.270), channel_id=1, source_target_pairs={{0,6},{1,7},{2,4},{3,5},{4,2},{5,3},{6,0},{7,1},{8,14},{9,15},{10,... | collective-permute-start | bytes 786440 | tf_op jit(solution)/shard_map/ppermute | solution.py:808
  367.8 23.6 %collective-permute-start.35 = (bf16[64,2048]{1,0:T(8,128)(2,1)S(1)}, bf16[64,2048]{1,0:T(8,128)(2,1)}, u32[]{:S(2)}, u32[]{:S(2)}) collective-permute-start(bf16[64,2048]{1,0:T(8,128)(2,1)S(1)} %get-tuple-element.271), channel_id=1, source_target_pairs={{0,2},{1,3},{2,0},{3,1},{4,6},{5,7},{6,4},{7,5},{8,10},{9,11},{10,... | collective-permute-start | bytes 786440 | tf_op jit(solution)/shard_map/ppermute | solution.py:808
  367.8 25.1 %collective-permute-start.34 = (bf16[64,2048]{1,0:T(8,128)(2,1)S(1)}, bf16[64,2048]{1,0:T(8,128)(2,1)}, u32[]{:S(2)}, u32[]{:S(2)}) collective-permute-start(bf16[64,2048]{1,0:T(8,128)(2,1)S(1)} %get-tuple-element.269), channel_id=1, source_target_pairs={{0,4},{1,5},{2,6},{3,7},{4,0},{5,1},{6,2},{7,3},{8,12},{9,13},{10,... | collective-permute-start | bytes 786440 | tf_op jit(solution)/shard_map/ppermute | solution.py:808
  387.3 28.3 %collective-permute-start.38 = (bf16[256,1408]{1,0:T(8,128)(2,1)}, bf16[256,1408]{1,0:T(8,128)(2,1)S(1)}, u32[]{:S(2)}, u32[]{:S(2)}) collective-permute-start(bf16[256,1408]{1,0:T(8,128)(2,1)} %get-tuple-element.116.refs_8_), channel_id=1, source_target_pairs={{0,32},{32,64},{64,96},{96,0},{1,33},{33,65},{65,97},{97,1},{2,34}... | collective-permute-start | bytes 2162696 | tf_op jit(solution)/shard_map/ppermute | solution.py:799
  388.9 26.7 %collective-permute-start.39 = (bf16[256,1408]{1,0:T(8,128)(2,1)}, bf16[256,1408]{1,0:T(8,128)(2,1)S(1)}, u32[]{:S(2)}, u32[]{:S(2)}) collective-permute-start(bf16[256,1408]{1,0:T(8,128)(2,1)} %get-tuple-element.119), channel_id=1, source_target_pairs={{0,96},{32,0},{64,32},{96,64},{1,97},{33,1},{65,33},{97,65},{2,98}... | collective-permute-start | bytes 2162696 | tf_op jit(solution)/shard_map/ppermute | solution.py:799
  390.0 23.1 %collective-permute-start.40 = (bf16[256,1280]{1,0:T(8,128)(2,1)}, bf16[256,1280]{1,0:T(8,128)(2,1)S(1)}, u32[]{:S(2)}, u32[]{:S(2)}) collective-permute-start(bf16[256,1280]{1,0:T(8,128)(2,1)} %get-tuple-element.122), channel_id=1, source_target_pairs={{0,8},{8,16},{16,24},{24,0},{1,9},{9,17},{17,25},{25,1},{2,10},{10... | collective-permute-start | bytes 1966088 | tf_op jit(solution)/shard_map/ppermute | solution.py:799
  391.5 24.1 %collective-permute-start.41 = (bf16[256,1280]{1,0:T(8,128)(2,1)}, bf16[256,1280]{1,0:T(8,128)(2,1)S(1)}, u32[]{:S(2)}, u32[]{:S(2)}) collective-permute-start(bf16[256,1280]{1,0:T(8,128)(2,1)} %get-tuple-element.123), channel_id=1, source_target_pairs={{0,24},{8,0},{16,8},{24,16},{1,25},{9,1},{17,9},{25,17},{2,26},{10... | collective-permute-start | bytes 1966088 | tf_op jit(solution)/shard_map/ppermute | solution.py:799
  392.9 10.9 %collective-permute-start.37 = (bf16[32,1536]{1,0:T(8,128)(2,1)S(1)}, bf16[32,1536]{1,0:T(8,128)(2,1)S(1)}, u32[]{:S(2)}, u32[]{:S(2)}) collective-permute-start(bf16[32,1536]{1,0:T(8,128)(2,1)S(1)} %pad_maximum_fusion.12), channel_id=1, source_target_pairs={{4,0},{8,4},{12,8},{16,12},{20,16},{24,20},{28,24},{32,28},{36,32}... | collective-permute-start | bytes 294920 | tf_op jit(solution)/shard_map/ppermute | solution.py:794
  431.7 14.7 %collective-permute-start.43 = (bf16[64,2048]{1,0:T(8,128)(2,1)}, bf16[64,2048]{1,0:T(8,128)(2,1)S(1)}, u32[]{:S(2)}, u32[]{:S(2)}) collective-permute-start(bf16[64,2048]{1,0:T(8,128)(2,1)} %fusion.57), channel_id=1, source_target_pairs={{0,2},{1,3},{2,0},{3,1},{4,6},{5,7},{6,4},{7,5},{8,10},{9,11},{10,... | collective-permute-start | bytes 786440 | tf_op jit(solution)/shard_map/ppermute | solution.py:808
  433.2 50.3 %collective-permute-start.44 = (bf16[512,1408]{1,0:T(8,128)(2,1)}, bf16[512,1408]{1,0:T(8,128)(2,1)}, u32[]{:S(2)}, u32[]{:S(2)}) collective-permute-start(bf16[512,1408]{1,0:T(8,128)(2,1)} %get-tuple-element.124), channel_id=1, source_target_pairs={{0,32},{32,64},{64,96},{96,0},{1,33},{33,65},{65,97},{97,1},{2,34}... | collective-permute-start | bytes 4325384 | tf_op jit(solution)/shard_map/ppermute | solution.py:799
  441.5 42.1 %collective-permute-start.45 = (bf16[512,1408]{1,0:T(8,128)(2,1)}, bf16[512,1408]{1,0:T(8,128)(2,1)}, u32[]{:S(2)}, u32[]{:S(2)}) collective-permute-start(bf16[512,1408]{1,0:T(8,128)(2,1)} %get-tuple-element.126), channel_id=1, source_target_pairs={{0,96},{32,0},{64,32},{96,64},{1,97},{33,1},{65,33},{97,65},{2,98}... | collective-permute-start | bytes 4325384 | tf_op jit(solution)/shard_map/ppermute | solution.py:799
  442.4 41.2 %collective-permute-start.46 = (bf16[512,1280]{1,0:T(8,128)(2,1)}, bf16[512,1280]{1,0:T(8,128)(2,1)}, u32[]{:S(2)}, u32[]{:S(2)}) collective-permute-start(bf16[512,1280]{1,0:T(8,128)(2,1)} %get-tuple-element.128), channel_id=1, source_target_pairs={{0,8},{8,16},{16,24},{24,0},{1,9},{9,17},{17,25},{25,1},{2,10},{10... | collective-permute-start | bytes 3932168 | tf_op jit(solution)/shard_map/ppermute | solution.py:799
  442.4 41.2 %collective-permute-start.47 = (bf16[512,1280]{1,0:T(8,128)(2,1)}, bf16[512,1280]{1,0:T(8,128)(2,1)}, u32[]{:S(2)}, u32[]{:S(2)}) collective-permute-start(bf16[512,1280]{1,0:T(8,128)(2,1)} %get-tuple-element.129), channel_id=1, source_target_pairs={{0,24},{8,0},{16,8},{24,16},{1,25},{9,1},{17,9},{25,17},{2,26},{10... | collective-permute-start | bytes 3932168 | tf_op jit(solution)/shard_map/ppermute | solution.py:799
  446.5 13.6 %collective-permute-start.48 = (bf16[64,3,704]{2,1,0:T(4,128)(2,1)S(1)}, bf16[64,3,704]{2,1,0:T(4,128)(2,1)S(1)}, u32[]{:S(2)}, u32[]{:S(2)}) collective-permute-start(bf16[64,3,704]{2,1,0:T(4,128)(2,1)S(1)} %add_bitcast_fusion), channel_id=1, source_target_pairs={{0,4},{4,0},{1,5},{5,1},{2,6},{6,2},{3,7},{7,3},{8,12},{12,8},{9,1... | collective-permute-start | bytes 811016 | tf_op jit(solution)/shard_map/ppermute | solution.py:799
  462.1 12.6 %collective-permute-start.51 = (f32[16,512]{1,0:T(8,128)S(1)}, f32[16,512]{1,0:T(8,128)S(1)}, u32[]{:S(2)}, u32[]{:S(2)}) collective-permute-start(f32[16,512]{1,0:T(8,128)S(1)} %maximum_add_fusion.1), channel_id=1, source_target_pairs={{0,96},{32,0},{64,32},{96,64},{1,97},{33,1},{65,33},{97,65},{2,98}... | collective-permute-start | bytes 98312 | tf_op jit(solution)/shard_map/ppermute | solution.py:799
  492.0 16.2 %collective-permute-start.58 = (bf16[128,1280]{1,0:T(8,128)(2,1)}, bf16[128,1280]{1,0:T(8,128)(2,1)S(1)}, u32[]{:S(2)}, u32[]{:S(2)}) collective-permute-start(bf16[128,1280]{1,0:T(8,128)(2,1)} %get-tuple-element.140), channel_id=1, source_target_pairs={{0,32},{32,64},{64,96},{96,0},{1,33},{33,65},{65,97},{97,1},{2,34}... | collective-permute-start | bytes 983048 | tf_op jit(solution)/shard_map/ppermute | solution.py:799
  493.1 26.4 %collective-permute-start.52 = (bf16[64,4096]{1,0:T(8,128)(2,1)S(1)}, bf16[64,4096]{1,0:T(8,128)(2,1)S(1)}, u32[]{:S(2)}, u32[]{:S(2)}) collective-permute-start(bf16[64,4096]{1,0:T(8,128)(2,1)S(1)} %broadcast_add_fusion.1), channel_id=1, source_target_pairs={{0,2},{1,3},{2,0},{3,1},{4,6},{5,7},{6,4},{7,5},{8,10},{9,11},{10,... | collective-permute-start | bytes 1572872 | tf_op jit(solution)/shard_map/ppermute | solution.py:808
  496.0 19.5 %collective-permute-start.54 = (bf16[128,1408]{1,0:T(8,128)(2,1)S(1)}, bf16[128,1408]{1,0:T(8,128)(2,1)S(1)}, u32[]{:S(2)}, u32[]{:S(2)}) collective-permute-start(bf16[128,1408]{1,0:T(8,128)(2,1)S(1)} %copy-done.77), channel_id=1, source_target_pairs={{0,16},{8,24},{16,0},{24,8},{1,17},{9,25},{17,1},{25,9},{2,18},{10... | collective-permute-start | bytes 1081352 | tf_op jit(solution)/shard_map/ppermute | solution.py:799
  496.1 19.4 %collective-permute-start.55 = (bf16[128,1408]{1,0:T(8,128)(2,1)S(1)}, bf16[128,1408]{1,0:T(8,128)(2,1)S(1)}, u32[]{:S(2)}, u32[]{:S(2)}) collective-permute-start(bf16[128,1408]{1,0:T(8,128)(2,1)S(1)} %copy-done.76), channel_id=1, source_target_pairs={{0,8},{8,16},{16,24},{24,0},{1,9},{9,17},{17,25},{25,1},{2,10},{10... | collective-permute-start | bytes 1081352 | tf_op jit(solution)/shard_map/ppermute | solution.py:799
  498.9 16.5 %collective-permute-start.56 = (bf16[128,1408]{1,0:T(8,128)(2,1)S(1)}, bf16[128,1408]{1,0:T(8,128)(2,1)S(1)}, u32[]{:S(2)}, u32[]{:S(2)}) collective-permute-start(bf16[128,1408]{1,0:T(8,128)(2,1)S(1)} %copy-done.75), channel_id=1, source_target_pairs={{0,24},{8,0},{16,8},{24,16},{1,25},{9,1},{17,9},{25,17},{2,26},{10... | collective-permute-start | bytes 1081352 | tf_op jit(solution)/shard_map/ppermute | solution.py:799
  519.5 18.7 %collective-permute-start.60 = (bf16[64,2688]{1,0:T(8,128)(2,1)}, bf16[64,2688]{1,0:T(8,128)(2,1)S(1)}, u32[]{:S(2)}, u32[]{:S(2)}) collective-permute-start(bf16[64,2688]{1,0:T(8,128)(2,1)} %get-tuple-element.143), channel_id=1, source_target_pairs={{0,4},{4,0},{1,5},{5,1},{2,6},{6,2},{3,7},{7,3},{8,12},{12,8},{9,1... | collective-permute-start | bytes 1032200 | tf_op jit(solution)/shard_map/ppermute | solution.py:799
  520.7 9.3 %collective-permute-start.63 = (f32[16,512]{1,0:T(8,128)S(1)}, f32[16,512]{1,0:T(8,128)S(1)}, u32[]{:S(2)}, u32[]{:S(2)}) collective-permute-start(f32[16,512]{1,0:T(8,128)S(1)} %broadcast_add_fusion.2), channel_id=1, source_target_pairs={{0,24},{8,0},{16,8},{24,16},{1,25},{9,1},{17,9},{25,17},{2,26},{10... | collective-permute-start | bytes 98312 | tf_op jit(solution)/shard_map/ppermute | solution.py:799
  533.8 15.6 %collective-permute-start.53 = (bf16[2,64,4096]{2,1,0:T(8,128)(2,1)S(1)}, bf16[2,64,4096]{2,1,0:T(8,128)(2,1)S(1)}, u32[]{:S(2)}, u32[]{:S(2)}) collective-permute-start(bf16[2,64,4096]{2,1,0:T(8,128)(2,1)S(1)} %pad_maximum_fusion.6), channel_id=1, source_target_pairs={{0,1},{1,0},{2,3},{3,2},{4,5},{5,4},{6,7},{7,6},{8,9},{9,8},{10,11... | collective-permute-start | bytes 3145736 | tf_op jit(solution)/shard_map/ppermute | solution.py:808
  (109 other events, 711.2 us)
Sparse Core Ops, SparseCore 0:
  98.4 98.0 all-gather.1
  324.1 92.6 reduce-scatter.1

commit v5 on v4

--- a/solution.py
+++ b/solution.py
@@ -987,7 +987,7 @@
     rows, cols = arrays[0].shape[0] // 2, arrays[0].shape[1] + arrays[4].shape[1]
     shapes = [((rows, cols), f32), ((rows, cols), bf16)]
     kept, sent = in_vmem(add_and_halve, shapes, places(), *arrays, deps=deps)
-    return kept + along(sent, "y", 1).astype(f32)
+    return kept + along(sent, "y", 1).astype(f32), sent
 
 
 def pair_up(place_ref, left, left_other, right, right_other, left_out, right_out):
@@ -1230,10 +1230,10 @@
     back_in = norm_pull(own, row_scale(own), gain_in, grad_normed_in)
     both = jnp.concatenate([residual + ffn_out, grad_residual + back_in], axis=1)
     both = both.astype(bf16)
-    small = sum_along(later(small, ffn_other), "x")
-    partials, cross_gate = reduce_cross(partials, (both, ffn_other, small))
-    mixer_w = reduce_end(partials, ())
-    both, chip_got = head_gather(later(both, cross_gate))
+    partials, cross_gate = reduce_cross(partials, (both, ffn_other))
+    small = sum_along(later(small, partials[5]), "x")
+    mixer_w, end_gate = reduce_end(partials, ())
+    both, chip_got = head_gather(later(both, end_gate))
     small = sum_along(sum_along(later(small, chip_got), "z"), "y")
     outputs, grad_in = both[:, :width], both[:, width:].astype(f32)
 

time: 568 us -> 573 us (level)
  starting transfers between devices: 149 us -> 158 us
    ppermute x46, waiting for transfers between devices: 82.4 us -> 72.9 us  [along(): lax.ppermute(array, axis, [(i, (i + by) % count) for i in range(count)])]
    ppermute x46, starting transfers between devices: 74.9 us -> 82.4 us  [along(): lax.ppermute(array, axis, [(i, (i + by) % count) for i in range(count)])]
    unnamed x169 -> x151, local copies, waits for them, and re-layouts: 20.9 us -> 20.6 us
  transfers between devices with their start and end apart: 74 -> 74, of which waited for: 33 -> 32; matrix products, arithmetic and copies ran while one was open for 14% -> 14% of each run, Pallas kernels for 14% -> 14%
where the time goes in v5:
time: 573 us; the launch traced here: 564 us
  waiting for transfers between devices  159 us (28%)
  starting transfers between devices  158 us (28%)
  Pallas kernels  102 us (18%)
  local copies, waits for them, and re-layouts  51.6 us (9%)
  other arithmetic  44 us (8%)
  matrix products  28.6 us (5%)
  between operations  20.7 us (4%)
    ppermute x46, starting transfers between devices, along(): lax.ppermute(array, axis, [(i, (i + by) % count) for i in range(count)])  82.4 us
    ppermute x46, waiting for transfers between devices, along(): lax.ppermute(array, axis, [(i, (i + by) % count) for i in range(count)])  72.9 us
    ppermute x20, waiting for transfers between devices, flipped(): return lax.ppermute(array, axes, [(i, i ^ mask) for i in range(count)])  47.9 us
    all_to_all x4, waiting for transfers between devices, exchange(): return lax.all_to_all(array, axis, split_axis=0, concat_axis=0, tiled=True)  38.7 us
    ppermute x20, starting transfers between devices, flipped(): return lax.ppermute(array, axes, [(i, i ^ mask) for i in range(count)])  31.4 us
    dot_general x9, matrix products, mm(): return jnp.einsum(dims, a, b, preferred_element_type=f32)  28.6 us
    pallas_call x7, Pallas kernels, in_vmem(): pl.pallas_call(ignoring(kernel, 1 + len(arrays), len(deps)), in_specs=[pl...  26.5 us
    all_to_all x4, starting transfers between devices, exchange(): return lax.all_to_all(array, axis, split_axis=0, concat_axis=0, tiled=True)  25.3 us
  transfers between devices with their start and end apart: 74, of which 32 were waited for; matrix products, arithmetic and copies ran while one was open for 14% of the time, Pallas kernels for 14%

profile of v5, /device:TPU:1, one launch (start us, length us, event | category | flops | bytes accessed | tf_op | source)
XLA Modules:
  0.0 564.1 jit_solution(10161659367500574080)
XLA Ops:
  9.9 3.8 collective-permute-start.1
  15.3 5.6 %collective-permute-done.2.refs_4_ = bf16[64,1280]{1,0:T(8,128)(2,1)S(1)} collective-permute-done((bf16[64,1280]{1,0:T(8,128)(2,1)S(1)}, bf16[64,1280]{1,0:T(8,128)(2,1)S(1)}, u32[]{:S(2)}, u32[]{:S(2)}) %collective-permute-start.2) | collective-permute-done | bytes 163872 | tf_op jit(solution)/shard_map/ppermute | solution.py:799
  30.8 5.8 %collective-permute-done.5.refs_3_.refs_7_ = bf16[128,1280]{1,0:T(8,128)(2,1)S(1)} collective-permute-done((bf16[128,1280]{1,0:T(8,128)(2,1)}, bf16[128,1280]{1,0:T(8,128)(2,1)S(1)}, u32[]{:S(2)}, u32[]{:S(2)}) %collective-permute-start.5) | collective-permute-done | bytes 327712 | tf_op jit(solution)/shard_map/ppermute | solution.py:799
  50.5 3.4 shard_map.290
  64.2 3.6 collective-permute-start.26
  71.9 17.0 %collective-permute-start = (bf16[2,16,2048]{2,1,0:T(8,128)(2,1)S(1)}, bf16[2,16,2048]{2,1,0:T(8,128)(2,1)S(1)}, u32[]{:S(2)}, u32[]{:S(2)}) collective-permute-start(bf16[2,16,2048]{2,1,0:T(8,128)(2,1)S(1)} %slice.202), channel_id=1, source_target_pairs={{0,4},{4,8},{8,12},{12,16},{16,20},{20,24},{24,28},{28,32},{32,36}... | collective-permute-start | bytes 393224 | tf_op jit(solution)/shard_map/ppermute | solution.py:794
  91.3 4.2 shard_map.291
  114.1 8.2 %collective-permute-done.18 = bf16[2,128,1280]{2,1,0:T(8,128)(2,1)S(1)} collective-permute-done((bf16[2,128,1280]{2,1,0:T(8,128)(2,1)S(1)}, bf16[2,128,1280]{2,1,0:T(8,128)(2,1)S(1)}, u32[]{:S(2)}, u32[]{:S(2)}) %collective-permute-start.18) | collective-permute-done | bytes 655392 | tf_op jit(solution)/shard_map/ppermute | solution.py:799
  122.3 4.9 collective-permute-done.17
  128.8 5.5 collective-permute-done.16
  141.6 11.1 %shard_map.292 = (bf16[32,160,128]{2,1,0:T(8,128)(2,1)}, bf16[8,128,128]{2,1,0:T(8,128)(2,1)}, f32[8,128,128]{2,1,0:T(8,128)}, bf16[8,128,128]{2,1,0:T(8,128)(2,1)}, f32[8,128,256]{2,1,0:T(8,128)}) custom-call(bf16[288,1536]{1,0:T(8,128)(2,1)} %pad_maximum_fusion.7.pre_ref.rim_ref.refs_0_.refs_1_, ...), custom_call_target="tpu_custom_call" | custom-call | flops 10000000000 | bytes 6000000 | tf_op jit(solution)/shard_map/pallas_call | solution.py:548
  152.8 7.6 %all-to-all-start = ((bf16[32,160,128]{2,1,0:T(8,128)(2,1)}), bf16[32,160,128]{2,1,0:T(8,128)(2,1)S(1)}, u32[]{:S(2)}, u32[]{:S(2)}) async-start(bf16[32,160,128]{2,1,0:T(8,128)(2,1)} %get-tuple-element.100), calls=%async_computation | async-start | bytes 2621440 | tf_op jit(solution)/shard_map/all_to_all | solution.py:845
  163.7 27.6 %all-to-all-done.got_ref.refs_0_ = bf16[32,160,128]{2,1,0:T(8,128)(2,1)S(1)} async-done(((bf16[32,160,128]{2,1,0:T(8,128)(2,1)}), bf16[32,160,128]{2,1,0:T(8,128)(2,1)S(1)}, u32[]{:S(2)}, u32[]{:S(2)}) %all-to-all-start) | async-done | bytes 1310752 | tf_op jit(solution)/shard_map/all_to_all | solution.py:845
  192.4 5.9 %shard_map.293 = bf16[32,32,128]{2,1,0:T(8,128)(2,1)} custom-call(bf16[32,160,128]{2,1,0:T(8,128)(2,1)} %copy-done.18), custom_call_target="tpu_custom_call" | custom-call | flops 1000000000 | bytes 3000000 | tf_op jit(solution)/shard_map/pallas_call | solution.py:573
  198.3 7.0 %all-to-all-start.1 = ((bf16[32,32,128]{2,1,0:T(8,128)(2,1)}), bf16[32,32,128]{2,1,0:T(8,128)(2,1)S(1)}, u32[]{:S(2)}, u32[]{:S(2)}) async-start(bf16[32,32,128]{2,1,0:T(8,128)(2,1)} %shard_map.293), calls=%async_computation.1 | async-start | bytes 524288 | tf_op jit(solution)/shard_map/all_to_all | solution.py:845
  208.8 6.0 %all-to-all-done.1 = bf16[32,32,128]{2,1,0:T(8,128)(2,1)S(1)} async-done(((bf16[32,32,128]{2,1,0:T(8,128)(2,1)}), bf16[32,32,128]{2,1,0:T(8,128)(2,1)S(1)}, u32[]{:S(2)}, u32[]{:S(2)}) %all-to-all-start.1) | async-done | bytes 262176 | tf_op jit(solution)/shard_map/all_to_all | solution.py:845
  221.4 6.1 %collective-permute-start.20 = (bf16[2,64,2048]{2,1,0:T(8,128)(2,1)S(1)}, bf16[2,64,2048]{2,1,0:T(8,128)(2,1)S(1)}, u32[]{:S(2)}, u32[]{:S(2)}) collective-permute-start(bf16[2,64,2048]{2,1,0:T(8,128)(2,1)S(1)} %dynamic-slice_bitcast_fusion.3), channel_id=1, source_target_pairs={{0,1},{1,0},{2,3},{3,2},{4,5},{5,4},{6,7},{7,6},{8,9},{9,8},{10,11... | collective-permute-start | bytes 1572872 | tf_op jit(solution)/shard_map/ppermute | solution.py:808
  230.7 7.4 %collective-permute-done.21 = bf16[64,2048]{1,0:T(8,128)(2,1)S(1)} collective-permute-done((bf16[64,2048]{1,0:T(8,128)(2,1)S(1)}, bf16[64,2048]{1,0:T(8,128)(2,1)S(1)}, u32[]{:S(2)}, u32[]{:S(2)}) %collective-permute-start.21) | collective-permute-done | bytes 262176 | tf_op jit(solution)/shard_map/ppermute | solution.py:808
  241.8 4.9 collective-permute-done.22
  250.1 3.8 collective-permute-done.24
  260.5 6.3 %fusion.2 = f32[512,1536]{1,0:T(8,128)S(1)} fusion(bf16[512,2048]{1,0:T(8,128)(2,1)} %bitcast.262, bf16[2048,2304]{1,0:T(8,128)(2,1)} %all-gather.2.cloned.1.call-done), kind=kOutput, calls=%fused_computation.2 | convolution fusion | flops 3221225472 | bytes 11534336 | tf_op jit(solution)/shard_map/ij,jk->ik/dot_general | solution.py:1045
  270.4 3.7 fusion.8
  281.3 5.1 collective-permute-done.30
  286.4 6.5 %collective-permute-done.28 = bf16[64,2048]{1,0:T(8,128)(2,1)S(1)} collective-permute-done((bf16[64,2048]{1,0:T(8,128)(2,1)S(1)}, bf16[64,2048]{1,0:T(8,128)(2,1)S(1)}, u32[]{:S(2)}, u32[]{:S(2)}) %collective-permute-start.28) | collective-permute-done | bytes 262176 | tf_op jit(solution)/shard_map/ppermute | solution.py:808
  295.3 6.5 %collective-permute-done.31 = bf16[64,2048]{1,0:T(8,128)(2,1)S(1)} collective-permute-done((bf16[64,2048]{1,0:T(8,128)(2,1)S(1)}, bf16[64,2048]{1,0:T(8,128)(2,1)S(1)}, u32[]{:S(2)}, u32[]{:S(2)}) %collective-permute-start.31) | collective-permute-done | bytes 262176 | tf_op jit(solution)/shard_map/ppermute | solution.py:808
  307.7 3.5 fusion.19.gg_ref
  314.2 9.8 %shard_map.303 = bf16[2048,2304]{1,0:T(8,128)(2,1)} custom-call(bf16[512,2048]{1,0:T(8,128)(2,1)} %bitcast.263, bf16[512,2048]{1,0:T(8,128)(2,1)} %pad_maximum_fusion.1.refs_1_, bf16[512,1536]{1,0:T(8,128)(2,1)} %pad_maximum_fusion.3.refs_2_, bf16[512,768]{1,0:T(8,128)(2,1)} %get-tuple-element.264.refs_3_, bf16[32,32,128]{2,1,0:T(8,128)(2,1)} %get-tuple-element.103.refs_4_), custom_call_target="tpu_custom_call" | custom-call | flops 4831838208 | bytes 9437184 | tf_op jit(solution)/shard_map/pallas_call | solution.py:730
  326.0 3.7 convolution_convert_fusion
  332.7 3.9 all-to-all-start.2
  336.5 7.9 %shard_map.296 = (bf16[288,512]{1,0:T(8,128)(2,1)}, f32[4,512]{1,0:T(4,128)}, bf16[8,128,128]{2,1,0:T(8,128)(2,1)}, f32[8,128,128]{2,1,0:T(8,128)}, f32[8,128,12...) custom-call(bf16[288,1536]{1,0:T(8,128)(2,1)} %pad_maximum_fusion.7.pre_ref.rim_ref.refs_0_.refs_1_, ...), custom_call_target="tpu_custom_call" | custom-call | flops 5000000000 | bytes 10000000 | tf_op jit(solution)/shard_map/pallas_call | solution.py:649
  348.4 5.9 %shard_map.297 = bf16[32,32,128]{2,1,0:T(8,128)(2,1)} custom-call(bf16[32,160,128]{2,1,0:T(8,128)(2,1)} %copy-done.18, bf16[32,32,128]{2,1,0:T(8,128)(2,1)} %copy-done.46, bf16[288,512]{1,0:T(8,128)(2,1)} %get-tuple-element.106.refs_2_.refs_4_.refs_1_), custom_call_target="tpu_custom_call" | custom-call | flops 1000000000 | bytes 3000000 | tf_op jit(solution)/shard_map/pallas_call | solution.py:583
  354.4 6.8 %all-to-all-start.3 = ((bf16[32,32,128]{2,1,0:T(8,128)(2,1)}), bf16[32,32,128]{2,1,0:T(8,128)(2,1)}, u32[]{:S(2)}, u32[]{:S(2)}) async-start(bf16[32,32,128]{2,1,0:T(8,128)(2,1)} %shard_map.297), calls=%async_computation.3 | async-start | bytes 524288 | tf_op jit(solution)/shard_map/all_to_all | solution.py:845
  371.9 10.2 %shard_map.298 = (bf16[288,1024]{1,0:T(8,128)(2,1)}, bf16[256,128]{1,0:T(8,128)(2,1)}, f32[4,1024]{1,0:T(4,128)}, f32[8,128]{1,0:T(8,128)}) custom-call(bf16[288,1536]{1,0:T(8,128)(2,1)} %pad_maximum_fusion.7.pre_ref.rim_ref.refs_0_.refs_1_, bf16[288,1536]{1,0:T(8,128)(2,1)} %pad_maximum_fusion.7.pre_ref.rim_ref.refs_0_.refs_1_, ...), custom_call_target="tpu_custom_call" | custom-call | flops 5000000000 | bytes 10000000 | tf_op jit(solution)/shard_map/pallas_call | solution.py:691
  382.1 4.5 shard_map.299
  396.4 7.4 %shard_map.300 = (bf16[512,1408]{1,0:T(8,128)(2,1)}, bf16[512,1408]{1,0:T(8,128)(2,1)}, bf16[512,1408]{1,0:T(8,128)(2,1)}, bf16[512,1280]{1,0:T(8,128)(2,1)}, bf...) custom-call(s32[2]{0:T(128)} %pad_add_fusion.1.refs_0_, bf16[288,2048]{1,0:T(8,128)(2,1)} %copy-done.20, ...), custom_call_target="tpu_custom_call" | custom-call | flops 2684354560 | bytes 10485760 | tf_op jit(solution)/shard_map/pallas_call | solution.py:753
  404.4 7.6 %shard_map.301.refs_9_ = bf16[256,2048]{1,0:T(8,128)(2,1)} custom-call(bf16[32,1536]{1,0:T(8,128)(2,1)} %copy-done.56, bf16[288,512]{1,0:T(8,128)(2,1)} %get-tuple-element.106.refs_2_.refs_4_.refs_1_, bf16[288,1024]{1,0:T(8,128)(2,1)} %get-tuple-element.113.refs_5_.refs_2_, bf16[256,128]{1,0:T(8,128)(2,1)} %get-tuple-element.114.refs_6_.refs_3_, ...), custom_call_target="tpu_custom_call" | custom-call | flops 2684354560 | bytes 10485760 | tf_op jit(solution)/shard_map/pallas_call | solution.py:768
  416.8 6.1 %shard_map.302 = (bf16[512,1408]{1,0:T(8,128)(2,1)}, bf16[512,1408]{1,0:T(8,128)(2,1)}, bf16[512,1280]{1,0:T(8,128)(2,1)}, bf16[512,1280]{1,0:T(8,128)(2,1)}) custom-call(s32[3]{0:T(128)} %pad_add_fusion.refs_0_, bf16[512,1408]{1,0:T(8,128)(2,1)} %get-tuple-element.117.refs_7_.refs_1_, bf16[512,1408]{1,0:T(8,128)(2,1)} %get-tuple-element.118.refs_2_, ...), custom_call_target="tpu_custom_call" | custom-call | flops 8257536 | bytes 8257536 | tf_op jit(solution)/shard_map/pallas_call | solution.py:908
  431.8 8.3 %collective-permute-start.44 = (bf16[512,1408]{1,0:T(8,128)(2,1)}, bf16[512,1408]{1,0:T(8,128)(2,1)}, u32[]{:S(2)}, u32[]{:S(2)}) collective-permute-start(bf16[512,1408]{1,0:T(8,128)(2,1)} %get-tuple-element.124), channel_id=1, source_target_pairs={{0,32},{32,64},{64,96},{96,0},{1,33},{33,65},{65,97},{97,1},{2,34}... | collective-permute-start | bytes 4325384 | tf_op jit(solution)/shard_map/ppermute | solution.py:799
  446.9 5.7 %collective-permute-start.48 = (bf16[64,3,704]{2,1,0:T(4,128)(2,1)S(1)}, bf16[64,3,704]{2,1,0:T(4,128)(2,1)S(1)}, u32[]{:S(2)}, u32[]{:S(2)}) collective-permute-start(bf16[64,3,704]{2,1,0:T(4,128)(2,1)S(1)} %add_bitcast_fusion), channel_id=1, source_target_pairs={{0,4},{4,0},{1,5},{5,1},{2,6},{6,2},{3,7},{7,3},{8,12},{12,8},{9,1... | collective-permute-start | bytes 811016 | tf_op jit(solution)/shard_map/ppermute | solution.py:799
  453.4 18.7 %collective-permute-done.46.refs_5_ = bf16[512,1280]{1,0:T(8,128)(2,1)} collective-permute-done((bf16[512,1280]{1,0:T(8,128)(2,1)}, bf16[512,1280]{1,0:T(8,128)(2,1)}, u32[]{:S(2)}, u32[]{:S(2)}) %collective-permute-start.46) | collective-permute-done | bytes 1310752 | tf_op jit(solution)/shard_map/ppermute | solution.py:799
  473.5 5.6 shard_map.304
  494.4 6.4 %collective-permute-done.53.refs_7_ = bf16[128,1280]{1,0:T(8,128)(2,1)} collective-permute-done((bf16[128,1280]{1,0:T(8,128)(2,1)}, bf16[128,1280]{1,0:T(8,128)(2,1)}, u32[]{:S(2)}, u32[]{:S(2)}) %collective-permute-start.53) | collective-permute-done | bytes 327712 | tf_op jit(solution)/shard_map/ppermute | solution.py:799
  508.2 5.1 collective-permute-start.57
  514.1 4.0 collective-permute-done.57
  521.1 6.1 %collective-permute-done.55 = bf16[64,4096]{1,0:T(8,128)(2,1)S(1)} collective-permute-done((bf16[64,4096]{1,0:T(8,128)(2,1)S(1)}, bf16[64,4096]{1,0:T(8,128)(2,1)S(1)}, u32[]{:S(2)}, u32[]{:S(2)}) %collective-permute-start.55) | collective-permute-done | bytes 524320 | tf_op jit(solution)/shard_map/ppermute | solution.py:808
  529.9 3.7 collective-permute-start.62
  538.8 6.1 %collective-permute-start.56 = (bf16[2,64,4096]{2,1,0:T(8,128)(2,1)S(1)}, bf16[2,64,4096]{2,1,0:T(8,128)(2,1)S(1)}, u32[]{:S(2)}, u32[]{:S(2)}) collective-permute-start(bf16[2,64,4096]{2,1,0:T(8,128)(2,1)S(1)} %pad_maximum_fusion.6), channel_id=1, source_target_pairs={{0,1},{1,0},{2,3},{3,2},{4,5},{5,4},{6,7},{7,6},{8,9},{9,8},{10,11... | collective-permute-start | bytes 3145736 | tf_op jit(solution)/shard_map/ppermute | solution.py:808
  545.1 4.3 collective-permute-start.67
  (425 shorter events, 214.4 us)
Async XLA Ops:
  7.2 253.3 %all-gather.2.cloned.1.call-start = ((), (), s32[]{:S(2)}) async-start(), calls=%async_computation.5 | async-start | bytes 10027008 | tf_op jit(solution)/shard_map/all_gather | solution.py:1124
  9.9 11.1 %collective-permute-start.1 = (bf16[64,1408]{1,0:T(8,128)(2,1)S(1)}, bf16[64,1408]{1,0:T(8,128)(2,1)S(1)}, u32[]{:S(2)}, u32[]{:S(2)}) collective-permute-start(bf16[64,1408]{1,0:T(8,128)(2,1)S(1)} %fusion.60.refs_1_), channel_id=1, source_target_pairs={{0,4},{4,0},{1,5},{5,1},{2,6},{6,2},{3,7},{7,3},{8,12},{12,8},{9,1... | collective-permute-start | bytes 540680 | tf_op jit(solution)/shard_map/ppermute | solution.py:799
  24.4 12.3 %collective-permute-start.3 = (bf16[128,1408]{1,0:T(8,128)(2,1)}, bf16[128,1408]{1,0:T(8,128)(2,1)S(1)}, u32[]{:S(2)}, u32[]{:S(2)}) collective-permute-start(bf16[128,1408]{1,0:T(8,128)(2,1)} %get-tuple-element.86.refs_1_), channel_id=1, source_target_pairs={{0,32},{32,64},{64,96},{96,0},{1,33},{33,65},{65,97},{97,1},{2,34}... | collective-permute-start | bytes 1081352 | tf_op jit(solution)/shard_map/ppermute | solution.py:799
  25.6 11.1 %collective-permute-start.4 = (bf16[128,1408]{1,0:T(8,128)(2,1)}, bf16[128,1408]{1,0:T(8,128)(2,1)S(1)}, u32[]{:S(2)}, u32[]{:S(2)}) collective-permute-start(bf16[128,1408]{1,0:T(8,128)(2,1)} %get-tuple-element.86.refs_1_), channel_id=1, source_target_pairs={{0,96},{32,0},{64,32},{96,64},{1,97},{33,1},{65,33},{97,65},{2,98}... | collective-permute-start | bytes 1081352 | tf_op jit(solution)/shard_map/ppermute | solution.py:799
  53.9 36.2 %collective-permute-start.11 = (bf16[4,128,1408]{2,1,0:T(8,128)(2,1)}, bf16[4,128,1408]{2,1,0:T(8,128)(2,1)}, u32[]{:S(2)}, u32[]{:S(2)}) collective-permute-start(bf16[4,128,1408]{2,1,0:T(8,128)(2,1)} %get-tuple-element.92), channel_id=1, source_target_pairs={{0,8},{8,16},{16,24},{24,0},{1,9},{9,17},{17,25},{25,1},{2,10},{10... | collective-permute-start | bytes 4325384 | tf_op jit(solution)/shard_map/ppermute | solution.py:799
  54.4 35.8 %collective-permute-start.12 = (bf16[4,128,1408]{2,1,0:T(8,128)(2,1)}, bf16[4,128,1408]{2,1,0:T(8,128)(2,1)S(1)}, u32[]{:S(2)}, u32[]{:S(2)}) collective-permute-start(bf16[4,128,1408]{2,1,0:T(8,128)(2,1)} %get-tuple-element.92), channel_id=1, source_target_pairs={{0,24},{8,0},{16,8},{24,16},{1,25},{9,1},{17,9},{25,17},{2,26},{10... | collective-permute-start | bytes 4325384 | tf_op jit(solution)/shard_map/ppermute | solution.py:799
  57.4 32.7 %collective-permute-start.13 = (bf16[4,128,1280]{2,1,0:T(8,128)(2,1)}, bf16[4,128,1280]{2,1,0:T(8,128)(2,1)}, u32[]{:S(2)}, u32[]{:S(2)}) collective-permute-start(bf16[4,128,1280]{2,1,0:T(8,128)(2,1)} %get-tuple-element.93), channel_id=1, source_target_pairs={{0,32},{32,64},{64,96},{96,0},{1,33},{33,65},{65,97},{97,1},{2,34}... | collective-permute-start | bytes 3932168 | tf_op jit(solution)/shard_map/ppermute | solution.py:799
  57.5 32.6 %collective-permute-start.14 = (bf16[4,128,1280]{2,1,0:T(8,128)(2,1)}, bf16[4,128,1280]{2,1,0:T(8,128)(2,1)}, u32[]{:S(2)}, u32[]{:S(2)}) collective-permute-start(bf16[4,128,1280]{2,1,0:T(8,128)(2,1)} %get-tuple-element.93), channel_id=1, source_target_pairs={{0,96},{32,0},{64,32},{96,64},{1,97},{33,1},{65,33},{97,65},{2,98}... | collective-permute-start | bytes 3932168 | tf_op jit(solution)/shard_map/ppermute | solution.py:799
  71.9 31.5 %collective-permute-start = (bf16[2,16,2048]{2,1,0:T(8,128)(2,1)S(1)}, bf16[2,16,2048]{2,1,0:T(8,128)(2,1)S(1)}, u32[]{:S(2)}, u32[]{:S(2)}) collective-permute-start(bf16[2,16,2048]{2,1,0:T(8,128)(2,1)S(1)} %slice.202), channel_id=1, source_target_pairs={{0,4},{4,8},{8,12},{12,16},{16,20},{20,24},{24,28},{28,32},{32,36}... | collective-permute-start | bytes 393224 | tf_op jit(solution)/shard_map/ppermute | solution.py:794
  106.8 15.5 %collective-permute-start.18 = (bf16[2,128,1280]{2,1,0:T(8,128)(2,1)S(1)}, bf16[2,128,1280]{2,1,0:T(8,128)(2,1)S(1)}, u32[]{:S(2)}, u32[]{:S(2)}) collective-permute-start(bf16[2,128,1280]{2,1,0:T(8,128)(2,1)S(1)} %copy-done.68), channel_id=1, source_target_pairs={{0,96},{32,0},{64,32},{96,64},{1,97},{33,1},{65,33},{97,65},{2,98}... | collective-permute-start | bytes 1966088 | tf_op jit(solution)/shard_map/ppermute | solution.py:799
  107.7 19.5 %collective-permute-start.17 = (bf16[2,128,1280]{2,1,0:T(8,128)(2,1)S(1)}, bf16[2,128,1280]{2,1,0:T(8,128)(2,1)S(1)}, u32[]{:S(2)}, u32[]{:S(2)}) collective-permute-start(bf16[2,128,1280]{2,1,0:T(8,128)(2,1)S(1)} %copy-done.67), channel_id=1, source_target_pairs={{0,32},{32,64},{64,96},{96,0},{1,33},{33,65},{65,97},{97,1},{2,34}... | collective-permute-start | bytes 1966088 | tf_op jit(solution)/shard_map/ppermute | solution.py:799
  109.8 24.8 %collective-permute-start.15 = (bf16[2,128,1408]{2,1,0:T(8,128)(2,1)S(1)}, bf16[2,128,1408]{2,1,0:T(8,128)(2,1)S(1)}, u32[]{:S(2)}, u32[]{:S(2)}) collective-permute-start(bf16[2,128,1408]{2,1,0:T(8,128)(2,1)S(1)} %copy-done.65), channel_id=1, source_target_pairs={{0,8},{8,16},{16,24},{24,0},{1,9},{9,17},{17,25},{25,1},{2,10},{10... | collective-permute-start | bytes 2162696 | tf_op jit(solution)/shard_map/ppermute | solution.py:799
  109.8 24.5 %collective-permute-start.16 = (bf16[2,128,1408]{2,1,0:T(8,128)(2,1)S(1)}, bf16[2,128,1408]{2,1,0:T(8,128)(2,1)S(1)}, u32[]{:S(2)}, u32[]{:S(2)}) collective-permute-start(bf16[2,128,1408]{2,1,0:T(8,128)(2,1)S(1)} %copy-done.66), channel_id=1, source_target_pairs={{0,24},{8,0},{16,8},{24,16},{1,25},{9,1},{17,9},{25,17},{2,26},{10... | collective-permute-start | bytes 2162696 | tf_op jit(solution)/shard_map/ppermute | solution.py:799
  152.8 38.5 %all-to-all-start = ((bf16[32,160,128]{2,1,0:T(8,128)(2,1)}), bf16[32,160,128]{2,1,0:T(8,128)(2,1)S(1)}, u32[]{:S(2)}, u32[]{:S(2)}) async-start(bf16[32,160,128]{2,1,0:T(8,128)(2,1)} %get-tuple-element.100), calls=%async_computation | async-start | bytes 2621440 | tf_op jit(solution)/shard_map/all_to_all | solution.py:845
  160.4 48.4 %collective-permute-start.19 = (bf16[256,2048]{1,0:T(8,128)(2,1)S(1)}, bf16[256,2048]{1,0:T(8,128)(2,1)}, u32[]{:S(2)}, u32[]{:S(2)}) collective-permute-start(bf16[256,2048]{1,0:T(8,128)(2,1)S(1)} %bitcast.265), channel_id=1, source_target_pairs={{0,4},{4,0},{1,5},{5,1},{2,6},{6,2},{3,7},{7,3},{8,12},{12,8},{9,1... | collective-permute-start | bytes 3145736 | tf_op jit(solution)/shard_map/ppermute | solution.py:799
  198.3 16.5 %all-to-all-start.1 = ((bf16[32,32,128]{2,1,0:T(8,128)(2,1)}), bf16[32,32,128]{2,1,0:T(8,128)(2,1)S(1)}, u32[]{:S(2)}, u32[]{:S(2)}) async-start(bf16[32,32,128]{2,1,0:T(8,128)(2,1)} %shard_map.293), calls=%async_computation.1 | async-start | bytes 524288 | tf_op jit(solution)/shard_map/all_to_all | solution.py:845
  205.3 240.2 %reduce-scatter.2.cloned.1.call-start = ((), (), s32[]{:S(2)}) async-start(), calls=%async_computation.6 | async-start | bytes 10027008 | tf_op jit(solution)/shard_map/reduce_scatter | solution.py:1198
  239.1 10.9 %collective-permute-start.23 = (bf16[64,2048]{1,0:T(8,128)(2,1)S(1)}, bf16[64,2048]{1,0:T(8,128)(2,1)S(1)}, u32[]{:S(2)}, u32[]{:S(2)}) collective-permute-start(bf16[64,2048]{1,0:T(8,128)(2,1)S(1)} %multiply_convert_fusion.3), channel_id=1, source_target_pairs={{0,2},{1,3},{2,0},{3,1},{4,6},{5,7},{6,4},{7,5},{8,10},{9,11},{10,... | collective-permute-start | bytes 786440 | tf_op jit(solution)/shard_map/ppermute | solution.py:808
  239.3 14.6 %collective-permute-start.24 = (bf16[64,2048]{1,0:T(8,128)(2,1)S(1)}, bf16[64,2048]{1,0:T(8,128)(2,1)S(1)}, u32[]{:S(2)}, u32[]{:S(2)}) collective-permute-start(bf16[64,2048]{1,0:T(8,128)(2,1)S(1)} %multiply_convert_fusion.3), channel_id=1, source_target_pairs={{0,6},{1,7},{2,4},{3,5},{4,2},{5,3},{6,0},{7,1},{8,14},{9,15},{10,... | collective-permute-start | bytes 786440 | tf_op jit(solution)/shard_map/ppermute | solution.py:808
  278.0 14.9 %collective-permute-start.28 = (bf16[64,2048]{1,0:T(8,128)(2,1)S(1)}, bf16[64,2048]{1,0:T(8,128)(2,1)S(1)}, u32[]{:S(2)}, u32[]{:S(2)}) collective-permute-start(bf16[64,2048]{1,0:T(8,128)(2,1)S(1)} %get-tuple-element.272), channel_id=1, source_target_pairs={{0,4},{1,5},{2,6},{3,7},{4,0},{5,1},{6,2},{7,3},{8,12},{9,13},{10,... | collective-permute-start | bytes 786440 | tf_op jit(solution)/shard_map/ppermute | solution.py:808
  332.0 29.2 %collective-permute-start.33 = (bf16[4,64,2048]{2,1,0:T(8,128)(2,1)}, bf16[4,64,2048]{2,1,0:T(8,128)(2,1)S(1)}, u32[]{:S(2)}, u32[]{:S(2)}) collective-permute-start(bf16[4,64,2048]{2,1,0:T(8,128)(2,1)} %dynamic-slice_bitcast_fusion), channel_id=1, source_target_pairs={{0,1},{1,0},{2,3},{3,2},{4,5},{5,4},{6,7},{7,6},{8,9},{9,8},{10,11... | collective-permute-start | bytes 3145736 | tf_op jit(solution)/shard_map/ppermute | solution.py:808
  332.7 15.1 %all-to-all-start.2 = ((bf16[32,32,128]{2,1,0:T(8,128)(2,1)}), bf16[32,32,128]{2,1,0:T(8,128)(2,1)S(1)}, u32[]{:S(2)}, u32[]{:S(2)}) async-start(bf16[32,32,128]{2,1,0:T(8,128)(2,1)} %get-tuple-element.103.refs_4_), calls=%async_computation.2 | async-start | bytes 524288 | tf_op jit(solution)/shard_map/all_to_all | solution.py:845
  354.4 17.5 %all-to-all-start.3 = ((bf16[32,32,128]{2,1,0:T(8,128)(2,1)}), bf16[32,32,128]{2,1,0:T(8,128)(2,1)}, u32[]{:S(2)}, u32[]{:S(2)}) async-start(bf16[32,32,128]{2,1,0:T(8,128)(2,1)} %shard_map.297), calls=%async_computation.3 | async-start | bytes 524288 | tf_op jit(solution)/shard_map/all_to_all | solution.py:845
  365.4 24.7 %collective-permute-start.36 = (bf16[64,2048]{1,0:T(8,128)(2,1)}, bf16[64,2048]{1,0:T(8,128)(2,1)S(1)}, u32[]{:S(2)}, u32[]{:S(2)}) collective-permute-start(bf16[64,2048]{1,0:T(8,128)(2,1)} %get-tuple-element.270), channel_id=1, source_target_pairs={{0,6},{1,7},{2,4},{3,5},{4,2},{5,3},{6,0},{7,1},{8,14},{9,15},{10,... | collective-permute-start | bytes 786440 | tf_op jit(solution)/shard_map/ppermute | solution.py:808
  367.9 23.4 %collective-permute-start.35 = (bf16[64,2048]{1,0:T(8,128)(2,1)S(1)}, bf16[64,2048]{1,0:T(8,128)(2,1)}, u32[]{:S(2)}, u32[]{:S(2)}) collective-permute-start(bf16[64,2048]{1,0:T(8,128)(2,1)S(1)} %get-tuple-element.271), channel_id=1, source_target_pairs={{0,2},{1,3},{2,0},{3,1},{4,6},{5,7},{6,4},{7,5},{8,10},{9,11},{10,... | collective-permute-start | bytes 786440 | tf_op jit(solution)/shard_map/ppermute | solution.py:808
  367.9 25.0 %collective-permute-start.34 = (bf16[64,2048]{1,0:T(8,128)(2,1)S(1)}, bf16[64,2048]{1,0:T(8,128)(2,1)}, u32[]{:S(2)}, u32[]{:S(2)}) collective-permute-start(bf16[64,2048]{1,0:T(8,128)(2,1)S(1)} %get-tuple-element.269), channel_id=1, source_target_pairs={{0,4},{1,5},{2,6},{3,7},{4,0},{5,1},{6,2},{7,3},{8,12},{9,13},{10,... | collective-permute-start | bytes 786440 | tf_op jit(solution)/shard_map/ppermute | solution.py:808
  387.4 28.0 %collective-permute-start.38 = (bf16[256,1408]{1,0:T(8,128)(2,1)}, bf16[256,1408]{1,0:T(8,128)(2,1)S(1)}, u32[]{:S(2)}, u32[]{:S(2)}) collective-permute-start(bf16[256,1408]{1,0:T(8,128)(2,1)} %get-tuple-element.116.refs_8_), channel_id=1, source_target_pairs={{0,32},{32,64},{64,96},{96,0},{1,33},{33,65},{65,97},{97,1},{2,34}... | collective-permute-start | bytes 2162696 | tf_op jit(solution)/shard_map/ppermute | solution.py:799
  388.9 26.5 %collective-permute-start.39 = (bf16[256,1408]{1,0:T(8,128)(2,1)}, bf16[256,1408]{1,0:T(8,128)(2,1)S(1)}, u32[]{:S(2)}, u32[]{:S(2)}) collective-permute-start(bf16[256,1408]{1,0:T(8,128)(2,1)} %get-tuple-element.119), channel_id=1, source_target_pairs={{0,96},{32,0},{64,32},{96,64},{1,97},{33,1},{65,33},{97,65},{2,98}... | collective-permute-start | bytes 2162696 | tf_op jit(solution)/shard_map/ppermute | solution.py:799
  390.1 22.5 %collective-permute-start.40 = (bf16[256,1280]{1,0:T(8,128)(2,1)}, bf16[256,1280]{1,0:T(8,128)(2,1)S(1)}, u32[]{:S(2)}, u32[]{:S(2)}) collective-permute-start(bf16[256,1280]{1,0:T(8,128)(2,1)} %get-tuple-element.122), channel_id=1, source_target_pairs={{0,8},{8,16},{16,24},{24,0},{1,9},{9,17},{17,25},{25,1},{2,10},{10... | collective-permute-start | bytes 1966088 | tf_op jit(solution)/shard_map/ppermute | solution.py:799
  391.3 24.1 %collective-permute-start.41 = (bf16[256,1280]{1,0:T(8,128)(2,1)}, bf16[256,1280]{1,0:T(8,128)(2,1)S(1)}, u32[]{:S(2)}, u32[]{:S(2)}) collective-permute-start(bf16[256,1280]{1,0:T(8,128)(2,1)} %get-tuple-element.123), channel_id=1, source_target_pairs={{0,24},{8,0},{16,8},{24,16},{1,25},{9,1},{17,9},{25,17},{2,26},{10... | collective-permute-start | bytes 1966088 | tf_op jit(solution)/shard_map/ppermute | solution.py:799
  392.8 10.9 %collective-permute-start.37 = (bf16[32,1536]{1,0:T(8,128)(2,1)S(1)}, bf16[32,1536]{1,0:T(8,128)(2,1)S(1)}, u32[]{:S(2)}, u32[]{:S(2)}) collective-permute-start(bf16[32,1536]{1,0:T(8,128)(2,1)S(1)} %pad_maximum_fusion.12), channel_id=1, source_target_pairs={{4,0},{8,4},{12,8},{16,12},{20,16},{24,20},{28,24},{32,28},{36,32}... | collective-permute-start | bytes 294920 | tf_op jit(solution)/shard_map/ppermute | solution.py:794
  431.1 12.9 %collective-permute-start.43 = (bf16[64,2048]{1,0:T(8,128)(2,1)S(1)}, bf16[64,2048]{1,0:T(8,128)(2,1)S(1)}, u32[]{:S(2)}, u32[]{:S(2)}) collective-permute-start(bf16[64,2048]{1,0:T(8,128)(2,1)S(1)} %fusion.57), channel_id=1, source_target_pairs={{0,2},{1,3},{2,0},{3,1},{4,6},{5,7},{6,4},{7,5},{8,10},{9,11},{10,... | collective-permute-start | bytes 786440 | tf_op jit(solution)/shard_map/ppermute | solution.py:808
  431.8 40.9 %collective-permute-start.44 = (bf16[512,1408]{1,0:T(8,128)(2,1)}, bf16[512,1408]{1,0:T(8,128)(2,1)}, u32[]{:S(2)}, u32[]{:S(2)}) collective-permute-start(bf16[512,1408]{1,0:T(8,128)(2,1)} %get-tuple-element.124), channel_id=1, source_target_pairs={{0,32},{32,64},{64,96},{96,0},{1,33},{33,65},{65,97},{97,1},{2,34}... | collective-permute-start | bytes 4325384 | tf_op jit(solution)/shard_map/ppermute | solution.py:799
  440.2 32.6 %collective-permute-start.45 = (bf16[512,1408]{1,0:T(8,128)(2,1)}, bf16[512,1408]{1,0:T(8,128)(2,1)}, u32[]{:S(2)}, u32[]{:S(2)}) collective-permute-start(bf16[512,1408]{1,0:T(8,128)(2,1)} %get-tuple-element.126), channel_id=1, source_target_pairs={{0,96},{32,0},{64,32},{96,64},{1,97},{33,1},{65,33},{97,65},{2,98}... | collective-permute-start | bytes 4325384 | tf_op jit(solution)/shard_map/ppermute | solution.py:799
  441.2 30.9 %collective-permute-start.46 = (bf16[512,1280]{1,0:T(8,128)(2,1)}, bf16[512,1280]{1,0:T(8,128)(2,1)}, u32[]{:S(2)}, u32[]{:S(2)}) collective-permute-start(bf16[512,1280]{1,0:T(8,128)(2,1)} %get-tuple-element.128), channel_id=1, source_target_pairs={{0,8},{8,16},{16,24},{24,0},{1,9},{9,17},{17,25},{25,1},{2,10},{10... | collective-permute-start | bytes 3932168 | tf_op jit(solution)/shard_map/ppermute | solution.py:799
  441.3 30.9 %collective-permute-start.47 = (bf16[512,1280]{1,0:T(8,128)(2,1)}, bf16[512,1280]{1,0:T(8,128)(2,1)}, u32[]{:S(2)}, u32[]{:S(2)}) collective-permute-start(bf16[512,1280]{1,0:T(8,128)(2,1)} %get-tuple-element.129), channel_id=1, source_target_pairs={{0,24},{8,0},{16,8},{24,16},{1,25},{9,1},{17,9},{25,17},{2,26},{10... | collective-permute-start | bytes 3932168 | tf_op jit(solution)/shard_map/ppermute | solution.py:799
  446.9 25.8 %collective-permute-start.48 = (bf16[64,3,704]{2,1,0:T(4,128)(2,1)S(1)}, bf16[64,3,704]{2,1,0:T(4,128)(2,1)S(1)}, u32[]{:S(2)}, u32[]{:S(2)}) collective-permute-start(bf16[64,3,704]{2,1,0:T(4,128)(2,1)S(1)} %add_bitcast_fusion), channel_id=1, source_target_pairs={{0,4},{4,0},{1,5},{5,1},{2,6},{6,2},{3,7},{7,3},{8,12},{12,8},{9,1... | collective-permute-start | bytes 811016 | tf_op jit(solution)/shard_map/ppermute | solution.py:799
  479.1 23.3 %collective-permute-start.49 = (bf16[128,1408]{1,0:T(8,128)(2,1)}, bf16[128,1408]{1,0:T(8,128)(2,1)S(1)}, u32[]{:S(2)}, u32[]{:S(2)}) collective-permute-start(bf16[128,1408]{1,0:T(8,128)(2,1)} %get-tuple-element.131), channel_id=1, source_target_pairs={{0,16},{8,24},{16,0},{24,8},{1,17},{9,25},{17,1},{25,9},{2,18},{10... | collective-permute-start | bytes 1081352 | tf_op jit(solution)/shard_map/ppermute | solution.py:799
  479.8 23.5 %collective-permute-start.50 = (bf16[128,1408]{1,0:T(8,128)(2,1)}, bf16[128,1408]{1,0:T(8,128)(2,1)S(1)}, u32[]{:S(2)}, u32[]{:S(2)}) collective-permute-start(bf16[128,1408]{1,0:T(8,128)(2,1)} %get-tuple-element.132), channel_id=1, source_target_pairs={{0,8},{8,16},{16,24},{24,0},{1,9},{9,17},{17,25},{25,1},{2,10},{10... | collective-permute-start | bytes 1081352 | tf_op jit(solution)/shard_map/ppermute | solution.py:799
  481.6 21.7 %collective-permute-start.51 = (bf16[128,1408]{1,0:T(8,128)(2,1)}, bf16[128,1408]{1,0:T(8,128)(2,1)}, u32[]{:S(2)}, u32[]{:S(2)}) collective-permute-start(bf16[128,1408]{1,0:T(8,128)(2,1)} %get-tuple-element.133), channel_id=1, source_target_pairs={{0,24},{8,0},{16,8},{24,16},{1,25},{9,1},{17,9},{25,17},{2,26},{10... | collective-permute-start | bytes 1081352 | tf_op jit(solution)/shard_map/ppermute | solution.py:799
  484.0 16.8 %collective-permute-start.53 = (bf16[128,1280]{1,0:T(8,128)(2,1)}, bf16[128,1280]{1,0:T(8,128)(2,1)}, u32[]{:S(2)}, u32[]{:S(2)}) collective-permute-start(bf16[128,1280]{1,0:T(8,128)(2,1)} %get-tuple-element.136), channel_id=1, source_target_pairs={{0,32},{32,64},{64,96},{96,0},{1,33},{33,65},{65,97},{97,1},{2,34}... | collective-permute-start | bytes 983048 | tf_op jit(solution)/shard_map/ppermute | solution.py:799
  490.8 10.0 %collective-permute-start.54 = (bf16[128,1280]{1,0:T(8,128)(2,1)S(1)}, bf16[128,1280]{1,0:T(8,128)(2,1)S(1)}, u32[]{:S(2)}, u32[]{:S(2)}) collective-permute-start(bf16[128,1280]{1,0:T(8,128)(2,1)S(1)} %copy-done.69), channel_id=1, source_target_pairs={{0,96},{32,0},{64,32},{96,64},{1,97},{33,1},{65,33},{97,65},{2,98}... | collective-permute-start | bytes 983048 | tf_op jit(solution)/shard_map/ppermute | solution.py:799
  500.8 27.6 %collective-permute-start.60 = (f32[16,512]{1,0:T(8,128)S(1)}, f32[16,512]{1,0:T(8,128)S(1)}, u32[]{:S(2)}, u32[]{:S(2)}) collective-permute-start(f32[16,512]{1,0:T(8,128)S(1)} %maximum_add_fusion.1), channel_id=1, source_target_pairs={{0,96},{32,0},{64,32},{96,64},{1,97},{33,1},{65,33},{97,65},{2,98}... | collective-permute-start | bytes 98312 | tf_op jit(solution)/shard_map/ppermute | solution.py:799
  500.8 27.6 %collective-permute-start.59 = (f32[16,512]{1,0:T(8,128)S(1)}, f32[16,512]{1,0:T(8,128)S(1)}, u32[]{:S(2)}, u32[]{:S(2)}) collective-permute-start(f32[16,512]{1,0:T(8,128)S(1)} %maximum_add_fusion.1), channel_id=1, source_target_pairs={{0,64},{32,96},{64,0},{96,32},{1,65},{33,97},{65,1},{97,33},{2,66}... | collective-permute-start | bytes 98312 | tf_op jit(solution)/shard_map/ppermute | solution.py:799
  502.5 25.9 %collective-permute-start.58 = (f32[16,512]{1,0:T(8,128)S(1)}, f32[16,512]{1,0:T(8,128)S(1)}, u32[]{:S(2)}, u32[]{:S(2)}) collective-permute-start(f32[16,512]{1,0:T(8,128)S(1)} %maximum_add_fusion.1), channel_id=1, source_target_pairs={{0,32},{32,64},{64,96},{96,0},{1,33},{33,65},{65,97},{97,1},{2,34}... | collective-permute-start | bytes 98312 | tf_op jit(solution)/shard_map/ppermute | solution.py:799
  508.2 9.9 %collective-permute-start.57 = (bf16[64,2688]{1,0:T(8,128)(2,1)}, bf16[64,2688]{1,0:T(8,128)(2,1)S(1)}, u32[]{:S(2)}, u32[]{:S(2)}) collective-permute-start(bf16[64,2688]{1,0:T(8,128)(2,1)} %get-tuple-element.138), channel_id=1, source_target_pairs={{0,4},{4,0},{1,5},{5,1},{2,6},{6,2},{3,7},{7,3},{8,12},{12,8},{9,1... | collective-permute-start | bytes 1032200 | tf_op jit(solution)/shard_map/ppermute | solution.py:799
  514.0 13.1 %collective-permute-start.55 = (bf16[64,4096]{1,0:T(8,128)(2,1)S(1)}, bf16[64,4096]{1,0:T(8,128)(2,1)S(1)}, u32[]{:S(2)}, u32[]{:S(2)}) collective-permute-start(bf16[64,4096]{1,0:T(8,128)(2,1)S(1)} %broadcast_add_fusion.1), channel_id=1, source_target_pairs={{0,2},{1,3},{2,0},{3,1},{4,6},{5,7},{6,4},{7,5},{8,10},{9,11},{10,... | collective-permute-start | bytes 1572872 | tf_op jit(solution)/shard_map/ppermute | solution.py:808
  538.8 14.7 %collective-permute-start.56 = (bf16[2,64,4096]{2,1,0:T(8,128)(2,1)S(1)}, bf16[2,64,4096]{2,1,0:T(8,128)(2,1)S(1)}, u32[]{:S(2)}, u32[]{:S(2)}) collective-permute-start(bf16[2,64,4096]{2,1,0:T(8,128)(2,1)S(1)} %pad_maximum_fusion.6), channel_id=1, source_target_pairs={{0,1},{1,0},{2,3},{3,2},{4,5},{5,4},{6,7},{7,6},{8,9},{9,8},{10,11... | collective-permute-start | bytes 3145736 | tf_op jit(solution)/shard_map/ppermute | solution.py:808
  (100 other events, 594.9 us)
Sparse Core Ops, SparseCore 0:
  98.5 98.0 all-gather.1
  324.2 92.3 reduce-scatter.1

commit v6 on v5

--- a/solution.py
+++ b/solution.py
@@ -1233,7 +1233,7 @@
     partials, cross_gate = reduce_cross(partials, (both, ffn_other))
     small = sum_along(later(small, partials[5]), "x")
     mixer_w, end_gate = reduce_end(partials, ())
-    both, chip_got = head_gather(later(both, end_gate))
+    both, chip_got = head_gather(later(both, cross_gate))
     small = sum_along(sum_along(later(small, chip_got), "z"), "y")
     outputs, grad_in = both[:, :width], both[:, width:].astype(f32)
 

time: 573 us -> 564 us (0.984)
  starting transfers between devices: 158 us -> 152 us
    ppermute x20, waiting for transfers between devices: 47.9 us -> 41.8 us  [flipped(): return lax.ppermute(array, axes, [(i, i ^ mask) for i in range(count)])]
    unnamed x151 -> x157, local copies, waits for them, and re-layouts: 20.6 us -> 20.5 us
  transfers between devices with their start and end apart: 74 -> 74, of which waited for: 32 -> 30; matrix products, arithmetic and copies ran while one was open for 14% -> 14% of each run, Pallas kernels for 14% -> 14%
where the time goes in v6:
time: 564 us; the launch traced here: 556 us
  waiting for transfers between devices  156 us (28%)
  starting transfers between devices  152 us (27%)
  Pallas kernels  102 us (18%)
  local copies, waits for them, and re-layouts  52.2 us (9%)
  other arithmetic  44.4 us (8%)
  matrix products  28.6 us (5%)
  between operations  20.8 us (4%)
    ppermute x46, starting transfers between devices, along(): lax.ppermute(array, axis, [(i, (i + by) % count) for i in range(count)])  77.6 us
    ppermute x46, waiting for transfers between devices, along(): lax.ppermute(array, axis, [(i, (i + by) % count) for i in range(count)])  75 us
    ppermute x20, waiting for transfers between devices, flipped(): return lax.ppermute(array, axes, [(i, i ^ mask) for i in range(count)])  41.8 us
    all_to_all x4, waiting for transfers between devices, exchange(): return lax.all_to_all(array, axis, split_axis=0, concat_axis=0, tiled=True)  38.9 us
    ppermute x20, starting transfers between devices, flipped(): return lax.ppermute(array, axes, [(i, i ^ mask) for i in range(count)])  30.5 us
    dot_general x9, matrix products, mm(): return jnp.einsum(dims, a, b, preferred_element_type=f32)  28.6 us
    pallas_call x7, Pallas kernels, in_vmem(): pl.pallas_call(ignoring(kernel, 1 + len(arrays), len(deps)), in_specs=[pl...  26.5 us
    all_to_all x4, starting transfers between devices, exchange(): return lax.all_to_all(array, axis, split_axis=0, concat_axis=0, tiled=True)  25.2 us
  transfers between devices with their start and end apart: 74, of which 30 were waited for; matrix products, arithmetic and copies ran while one was open for 14% of the time, Pallas kernels for 14%

profile of v6, /device:TPU:1, one launch (start us, length us, event | category | flops | bytes accessed | tf_op | source)
XLA Modules:
  0.0 555.6 jit_solution(15389263039652587295)
XLA Ops:
  9.9 3.8 collective-permute-start.1
  15.3 5.6 %collective-permute-done.2.refs_4_ = bf16[64,1280]{1,0:T(8,128)(2,1)S(1)} collective-permute-done((bf16[64,1280]{1,0:T(8,128)(2,1)S(1)}, bf16[64,1280]{1,0:T(8,128)(2,1)S(1)}, u32[]{:S(2)}, u32[]{:S(2)}) %collective-permute-start.2) | collective-permute-done | bytes 163872 | tf_op jit(solution)/shard_map/ppermute | solution.py:799
  30.8 5.8 %collective-permute-done.5.refs_3_.refs_7_ = bf16[128,1280]{1,0:T(8,128)(2,1)S(1)} collective-permute-done((bf16[128,1280]{1,0:T(8,128)(2,1)}, bf16[128,1280]{1,0:T(8,128)(2,1)S(1)}, u32[]{:S(2)}, u32[]{:S(2)}) %collective-permute-start.5) | collective-permute-done | bytes 327712 | tf_op jit(solution)/shard_map/ppermute | solution.py:799
  50.5 3.4 shard_map.290
  64.2 3.6 collective-permute-start.26
  71.9 17.0 %collective-permute-start = (bf16[2,16,2048]{2,1,0:T(8,128)(2,1)S(1)}, bf16[2,16,2048]{2,1,0:T(8,128)(2,1)S(1)}, u32[]{:S(2)}, u32[]{:S(2)}) collective-permute-start(bf16[2,16,2048]{2,1,0:T(8,128)(2,1)S(1)} %slice.202), channel_id=1, source_target_pairs={{0,4},{4,8},{8,12},{12,16},{16,20},{20,24},{24,28},{28,32},{32,36}... | collective-permute-start | bytes 393224 | tf_op jit(solution)/shard_map/ppermute | solution.py:794
  91.3 4.2 shard_map.291
  114.1 8.2 %collective-permute-done.18 = bf16[2,128,1280]{2,1,0:T(8,128)(2,1)S(1)} collective-permute-done((bf16[2,128,1280]{2,1,0:T(8,128)(2,1)S(1)}, bf16[2,128,1280]{2,1,0:T(8,128)(2,1)S(1)}, u32[]{:S(2)}, u32[]{:S(2)}) %collective-permute-start.18) | collective-permute-done | bytes 655392 | tf_op jit(solution)/shard_map/ppermute | solution.py:799
  122.3 4.9 collective-permute-done.17
  128.8 5.5 collective-permute-done.16
  141.6 11.1 %shard_map.292 = (bf16[32,160,128]{2,1,0:T(8,128)(2,1)}, bf16[8,128,128]{2,1,0:T(8,128)(2,1)}, f32[8,128,128]{2,1,0:T(8,128)}, bf16[8,128,128]{2,1,0:T(8,128)(2,1)}, f32[8,128,256]{2,1,0:T(8,128)}) custom-call(bf16[288,1536]{1,0:T(8,128)(2,1)} %pad_maximum_fusion.7.pre_ref.rim_ref.refs_0_.refs_1_, ...), custom_call_target="tpu_custom_call" | custom-call | flops 10000000000 | bytes 6000000 | tf_op jit(solution)/shard_map/pallas_call | solution.py:548
  152.8 7.6 %all-to-all-start = ((bf16[32,160,128]{2,1,0:T(8,128)(2,1)}), bf16[32,160,128]{2,1,0:T(8,128)(2,1)S(1)}, u32[]{:S(2)}, u32[]{:S(2)}) async-start(bf16[32,160,128]{2,1,0:T(8,128)(2,1)} %get-tuple-element.100), calls=%async_computation | async-start | bytes 2621440 | tf_op jit(solution)/shard_map/all_to_all | solution.py:845
  163.7 27.6 %all-to-all-done.got_ref.refs_0_ = bf16[32,160,128]{2,1,0:T(8,128)(2,1)S(1)} async-done(((bf16[32,160,128]{2,1,0:T(8,128)(2,1)}), bf16[32,160,128]{2,1,0:T(8,128)(2,1)S(1)}, u32[]{:S(2)}, u32[]{:S(2)}) %all-to-all-start) | async-done | bytes 1310752 | tf_op jit(solution)/shard_map/all_to_all | solution.py:845
  192.4 5.9 %shard_map.293 = bf16[32,32,128]{2,1,0:T(8,128)(2,1)} custom-call(bf16[32,160,128]{2,1,0:T(8,128)(2,1)} %copy-done.18), custom_call_target="tpu_custom_call" | custom-call | flops 1000000000 | bytes 3000000 | tf_op jit(solution)/shard_map/pallas_call | solution.py:573
  198.2 7.0 %all-to-all-start.1 = ((bf16[32,32,128]{2,1,0:T(8,128)(2,1)}), bf16[32,32,128]{2,1,0:T(8,128)(2,1)S(1)}, u32[]{:S(2)}, u32[]{:S(2)}) async-start(bf16[32,32,128]{2,1,0:T(8,128)(2,1)} %shard_map.293), calls=%async_computation.1 | async-start | bytes 524288 | tf_op jit(solution)/shard_map/all_to_all | solution.py:845
  205.3 3.4 fusion.17.refs_3_.og_ref
  208.7 6.0 %all-to-all-done.1 = bf16[32,32,128]{2,1,0:T(8,128)(2,1)S(1)} async-done(((bf16[32,32,128]{2,1,0:T(8,128)(2,1)}), bf16[32,32,128]{2,1,0:T(8,128)(2,1)S(1)}, u32[]{:S(2)}, u32[]{:S(2)}) %all-to-all-start.1) | async-done | bytes 262176 | tf_op jit(solution)/shard_map/all_to_all | solution.py:845
  221.4 6.1 %collective-permute-start.20 = (bf16[2,64,2048]{2,1,0:T(8,128)(2,1)S(1)}, bf16[2,64,2048]{2,1,0:T(8,128)(2,1)S(1)}, u32[]{:S(2)}, u32[]{:S(2)}) collective-permute-start(bf16[2,64,2048]{2,1,0:T(8,128)(2,1)S(1)} %dynamic-slice_bitcast_fusion.3), channel_id=1, source_target_pairs={{0,1},{1,0},{2,3},{3,2},{4,5},{5,4},{6,7},{7,6},{8,9},{9,8},{10,11... | collective-permute-start | bytes 1572872 | tf_op jit(solution)/shard_map/ppermute | solution.py:808
  230.7 7.4 %collective-permute-done.21 = bf16[64,2048]{1,0:T(8,128)(2,1)S(1)} collective-permute-done((bf16[64,2048]{1,0:T(8,128)(2,1)S(1)}, bf16[64,2048]{1,0:T(8,128)(2,1)S(1)}, u32[]{:S(2)}, u32[]{:S(2)}) %collective-permute-start.21) | collective-permute-done | bytes 262176 | tf_op jit(solution)/shard_map/ppermute | solution.py:808
  241.7 4.9 collective-permute-done.22
  250.0 3.8 collective-permute-done.24
  260.5 6.3 %fusion.2 = f32[512,1536]{1,0:T(8,128)S(1)} fusion(bf16[512,2048]{1,0:T(8,128)(2,1)} %bitcast.262, bf16[2048,2304]{1,0:T(8,128)(2,1)} %all-gather.2.cloned.1.call-done), kind=kOutput, calls=%fused_computation.2 | convolution fusion | flops 3221225472 | bytes 11534336 | tf_op jit(solution)/shard_map/ij,jk->ik/dot_general | solution.py:1045
  270.4 3.7 fusion.8
  277.9 3.3 collective-permute-start.28
  281.3 5.1 collective-permute-done.30
  286.4 6.5 %collective-permute-done.28 = bf16[64,2048]{1,0:T(8,128)(2,1)S(1)} collective-permute-done((bf16[64,2048]{1,0:T(8,128)(2,1)S(1)}, bf16[64,2048]{1,0:T(8,128)(2,1)S(1)}, u32[]{:S(2)}, u32[]{:S(2)}) %collective-permute-start.28) | collective-permute-done | bytes 262176 | tf_op jit(solution)/shard_map/ppermute | solution.py:808
  295.2 6.5 %collective-permute-done.31 = bf16[64,2048]{1,0:T(8,128)(2,1)S(1)} collective-permute-done((bf16[64,2048]{1,0:T(8,128)(2,1)S(1)}, bf16[64,2048]{1,0:T(8,128)(2,1)S(1)}, u32[]{:S(2)}, u32[]{:S(2)}) %collective-permute-start.31) | collective-permute-done | bytes 262176 | tf_op jit(solution)/shard_map/ppermute | solution.py:808
  307.6 3.5 fusion.19.gg_ref
  314.1 9.8 %shard_map.303 = bf16[2048,2304]{1,0:T(8,128)(2,1)} custom-call(bf16[512,2048]{1,0:T(8,128)(2,1)} %bitcast.263, bf16[512,2048]{1,0:T(8,128)(2,1)} %pad_maximum_fusion.1.refs_1_, bf16[512,1536]{1,0:T(8,128)(2,1)} %pad_maximum_fusion.3.refs_2_, bf16[512,768]{1,0:T(8,128)(2,1)} %get-tuple-element.264.refs_3_, bf16[32,32,128]{2,1,0:T(8,128)(2,1)} %get-tuple-element.103.refs_4_), custom_call_target="tpu_custom_call" | custom-call | flops 4831838208 | bytes 9437184 | tf_op jit(solution)/shard_map/pallas_call | solution.py:730
  325.9 3.7 convolution_convert_fusion
  332.6 3.9 all-to-all-start.2
  336.5 7.9 %shard_map.296 = (bf16[288,512]{1,0:T(8,128)(2,1)}, f32[4,512]{1,0:T(4,128)}, bf16[8,128,128]{2,1,0:T(8,128)(2,1)}, f32[8,128,128]{2,1,0:T(8,128)}, f32[8,128,12...) custom-call(bf16[288,1536]{1,0:T(8,128)(2,1)} %pad_maximum_fusion.7.pre_ref.rim_ref.refs_0_.refs_1_, ...), custom_call_target="tpu_custom_call" | custom-call | flops 5000000000 | bytes 10000000 | tf_op jit(solution)/shard_map/pallas_call | solution.py:649
  348.5 5.9 %shard_map.297 = bf16[32,32,128]{2,1,0:T(8,128)(2,1)} custom-call(bf16[32,160,128]{2,1,0:T(8,128)(2,1)} %copy-done.18, bf16[32,32,128]{2,1,0:T(8,128)(2,1)} %copy-done.49, bf16[288,512]{1,0:T(8,128)(2,1)} %get-tuple-element.106.refs_2_.refs_4_.refs_1_), custom_call_target="tpu_custom_call" | custom-call | flops 1000000000 | bytes 3000000 | tf_op jit(solution)/shard_map/pallas_call | solution.py:583
  354.4 6.8 %all-to-all-start.3 = ((bf16[32,32,128]{2,1,0:T(8,128)(2,1)}), bf16[32,32,128]{2,1,0:T(8,128)(2,1)}, u32[]{:S(2)}, u32[]{:S(2)}) async-start(bf16[32,32,128]{2,1,0:T(8,128)(2,1)} %shard_map.297), calls=%async_computation.3 | async-start | bytes 524288 | tf_op jit(solution)/shard_map/all_to_all | solution.py:845
  371.9 10.2 %shard_map.298 = (bf16[288,1024]{1,0:T(8,128)(2,1)}, bf16[256,128]{1,0:T(8,128)(2,1)}, f32[4,1024]{1,0:T(4,128)}, f32[8,128]{1,0:T(8,128)}) custom-call(bf16[288,1536]{1,0:T(8,128)(2,1)} %pad_maximum_fusion.7.pre_ref.rim_ref.refs_0_.refs_1_, bf16[288,1536]{1,0:T(8,128)(2,1)} %pad_maximum_fusion.7.pre_ref.rim_ref.refs_0_.refs_1_, ...), custom_call_target="tpu_custom_call" | custom-call | flops 5000000000 | bytes 10000000 | tf_op jit(solution)/shard_map/pallas_call | solution.py:691
  382.1 4.5 shard_map.299
  396.4 7.4 %shard_map.300 = (bf16[512,1408]{1,0:T(8,128)(2,1)}, bf16[512,1408]{1,0:T(8,128)(2,1)}, bf16[512,1408]{1,0:T(8,128)(2,1)}, bf16[512,1280]{1,0:T(8,128)(2,1)}, bf...) custom-call(s32[2]{0:T(128)} %pad_add_fusion.1.refs_0_, bf16[288,2048]{1,0:T(8,128)(2,1)} %copy-done.20, ...), custom_call_target="tpu_custom_call" | custom-call | flops 2684354560 | bytes 10485760 | tf_op jit(solution)/shard_map/pallas_call | solution.py:753
  404.4 7.6 %shard_map.301.refs_9_ = bf16[256,2048]{1,0:T(8,128)(2,1)} custom-call(bf16[32,1536]{1,0:T(8,128)(2,1)} %copy-done.59, bf16[288,512]{1,0:T(8,128)(2,1)} %get-tuple-element.106.refs_2_.refs_4_.refs_1_, bf16[288,1024]{1,0:T(8,128)(2,1)} %get-tuple-element.113.refs_5_.refs_2_, bf16[256,128]{1,0:T(8,128)(2,1)} %get-tuple-element.114.refs_6_.refs_3_, ...), custom_call_target="tpu_custom_call" | custom-call | flops 2684354560 | bytes 10485760 | tf_op jit(solution)/shard_map/pallas_call | solution.py:768
  417.0 6.1 %shard_map.302 = (bf16[512,1408]{1,0:T(8,128)(2,1)}, bf16[512,1408]{1,0:T(8,128)(2,1)}, bf16[512,1280]{1,0:T(8,128)(2,1)}, bf16[512,1280]{1,0:T(8,128)(2,1)}) custom-call(s32[3]{0:T(128)} %pad_add_fusion.refs_0_, bf16[512,1408]{1,0:T(8,128)(2,1)} %get-tuple-element.117.refs_7_.refs_1_, bf16[512,1408]{1,0:T(8,128)(2,1)} %get-tuple-element.118.refs_2_, ...), custom_call_target="tpu_custom_call" | custom-call | flops 8257536 | bytes 8257536 | tf_op jit(solution)/shard_map/pallas_call | solution.py:908
  431.9 7.7 %collective-permute-start.44 = (bf16[512,1408]{1,0:T(8,128)(2,1)}, bf16[512,1408]{1,0:T(8,128)(2,1)}, u32[]{:S(2)}, u32[]{:S(2)}) collective-permute-start(bf16[512,1408]{1,0:T(8,128)(2,1)} %get-tuple-element.124), channel_id=1, source_target_pairs={{0,32},{32,64},{64,96},{96,0},{1,33},{33,65},{65,97},{97,1},{2,34}... | collective-permute-start | bytes 4325384 | tf_op jit(solution)/shard_map/ppermute | solution.py:799
  446.9 5.1 collective-permute-start.48
  452.9 19.3 %collective-permute-done.46.refs_5_ = bf16[512,1280]{1,0:T(8,128)(2,1)} collective-permute-done((bf16[512,1280]{1,0:T(8,128)(2,1)}, bf16[512,1280]{1,0:T(8,128)(2,1)}, u32[]{:S(2)}, u32[]{:S(2)}) %collective-permute-start.46) | collective-permute-done | bytes 1310752 | tf_op jit(solution)/shard_map/ppermute | solution.py:799
  473.5 5.6 %shard_map.304 = (bf16[128,1408]{1,0:T(8,128)(2,1)}, bf16[128,1408]{1,0:T(8,128)(2,1)}, bf16[128,1408]{1,0:T(8,128)(2,1)}, bf16[128,1408]{1,0:T(8,128)(2,1)}, bf...) custom-call(s32[3]{0:T(128)} %pad_add_fusion.refs_0_, ...), custom_call_target="tpu_custom_call" | custom-call | flops 8257536 | bytes 8257536 | tf_op jit(solution)/shard_map/pallas_call | solution.py:908
  492.0 6.9 %collective-permute-done.55.refs_7_ = bf16[128,1280]{1,0:T(8,128)(2,1)S(1)} collective-permute-done((bf16[128,1280]{1,0:T(8,128)(2,1)}, bf16[128,1280]{1,0:T(8,128)(2,1)S(1)}, u32[]{:S(2)}, u32[]{:S(2)}) %collective-permute-start.55) | collective-permute-done | bytes 327712 | tf_op jit(solution)/shard_map/ppermute | solution.py:799
  501.2 5.4 collective-permute-done.56.refs_8_
  520.2 4.1 collective-permute-start.63
  529.1 4.7 collective-permute-start.50
  535.2 5.2 collective-permute-start.67
  (431 shorter events, 209.3 us)
Async XLA Ops:
  7.2 253.2 %all-gather.2.cloned.1.call-start = ((), (), s32[]{:S(2)}) async-start(), calls=%async_computation.5 | async-start | bytes 10027008 | tf_op jit(solution)/shard_map/all_gather | solution.py:1124
  9.9 11.1 %collective-permute-start.1 = (bf16[64,1408]{1,0:T(8,128)(2,1)S(1)}, bf16[64,1408]{1,0:T(8,128)(2,1)S(1)}, u32[]{:S(2)}, u32[]{:S(2)}) collective-permute-start(bf16[64,1408]{1,0:T(8,128)(2,1)S(1)} %fusion.60.refs_1_), channel_id=1, source_target_pairs={{0,4},{4,0},{1,5},{5,1},{2,6},{6,2},{3,7},{7,3},{8,12},{12,8},{9,1... | collective-permute-start | bytes 540680 | tf_op jit(solution)/shard_map/ppermute | solution.py:799
  24.4 12.3 %collective-permute-start.3 = (bf16[128,1408]{1,0:T(8,128)(2,1)}, bf16[128,1408]{1,0:T(8,128)(2,1)S(1)}, u32[]{:S(2)}, u32[]{:S(2)}) collective-permute-start(bf16[128,1408]{1,0:T(8,128)(2,1)} %get-tuple-element.86.refs_1_), channel_id=1, source_target_pairs={{0,32},{32,64},{64,96},{96,0},{1,33},{33,65},{65,97},{97,1},{2,34}... | collective-permute-start | bytes 1081352 | tf_op jit(solution)/shard_map/ppermute | solution.py:799
  25.6 11.1 %collective-permute-start.4 = (bf16[128,1408]{1,0:T(8,128)(2,1)}, bf16[128,1408]{1,0:T(8,128)(2,1)S(1)}, u32[]{:S(2)}, u32[]{:S(2)}) collective-permute-start(bf16[128,1408]{1,0:T(8,128)(2,1)} %get-tuple-element.86.refs_1_), channel_id=1, source_target_pairs={{0,96},{32,0},{64,32},{96,64},{1,97},{33,1},{65,33},{97,65},{2,98}... | collective-permute-start | bytes 1081352 | tf_op jit(solution)/shard_map/ppermute | solution.py:799
  27.0 9.6 %collective-permute-start.5 = (bf16[128,1280]{1,0:T(8,128)(2,1)}, bf16[128,1280]{1,0:T(8,128)(2,1)S(1)}, u32[]{:S(2)}, u32[]{:S(2)}) collective-permute-start(bf16[128,1280]{1,0:T(8,128)(2,1)} %get-tuple-element.87.refs_6_), channel_id=1, source_target_pairs={{0,8},{8,16},{16,24},{24,0},{1,9},{9,17},{17,25},{25,1},{2,10},{10... | collective-permute-start | bytes 983048 | tf_op jit(solution)/shard_map/ppermute | solution.py:799
  53.9 36.2 %collective-permute-start.11 = (bf16[4,128,1408]{2,1,0:T(8,128)(2,1)}, bf16[4,128,1408]{2,1,0:T(8,128)(2,1)}, u32[]{:S(2)}, u32[]{:S(2)}) collective-permute-start(bf16[4,128,1408]{2,1,0:T(8,128)(2,1)} %get-tuple-element.92), channel_id=1, source_target_pairs={{0,8},{8,16},{16,24},{24,0},{1,9},{9,17},{17,25},{25,1},{2,10},{10... | collective-permute-start | bytes 4325384 | tf_op jit(solution)/shard_map/ppermute | solution.py:799
  54.3 35.8 %collective-permute-start.12 = (bf16[4,128,1408]{2,1,0:T(8,128)(2,1)}, bf16[4,128,1408]{2,1,0:T(8,128)(2,1)S(1)}, u32[]{:S(2)}, u32[]{:S(2)}) collective-permute-start(bf16[4,128,1408]{2,1,0:T(8,128)(2,1)} %get-tuple-element.92), channel_id=1, source_target_pairs={{0,24},{8,0},{16,8},{24,16},{1,25},{9,1},{17,9},{25,17},{2,26},{10... | collective-permute-start | bytes 4325384 | tf_op jit(solution)/shard_map/ppermute | solution.py:799
  57.4 32.7 %collective-permute-start.13 = (bf16[4,128,1280]{2,1,0:T(8,128)(2,1)}, bf16[4,128,1280]{2,1,0:T(8,128)(2,1)}, u32[]{:S(2)}, u32[]{:S(2)}) collective-permute-start(bf16[4,128,1280]{2,1,0:T(8,128)(2,1)} %get-tuple-element.93), channel_id=1, source_target_pairs={{0,32},{32,64},{64,96},{96,0},{1,33},{33,65},{65,97},{97,1},{2,34}... | collective-permute-start | bytes 3932168 | tf_op jit(solution)/shard_map/ppermute | solution.py:799
  57.4 32.6 %collective-permute-start.14 = (bf16[4,128,1280]{2,1,0:T(8,128)(2,1)}, bf16[4,128,1280]{2,1,0:T(8,128)(2,1)}, u32[]{:S(2)}, u32[]{:S(2)}) collective-permute-start(bf16[4,128,1280]{2,1,0:T(8,128)(2,1)} %get-tuple-element.93), channel_id=1, source_target_pairs={{0,96},{32,0},{64,32},{96,64},{1,97},{33,1},{65,33},{97,65},{2,98}... | collective-permute-start | bytes 3932168 | tf_op jit(solution)/shard_map/ppermute | solution.py:799
  71.9 31.5 %collective-permute-start = (bf16[2,16,2048]{2,1,0:T(8,128)(2,1)S(1)}, bf16[2,16,2048]{2,1,0:T(8,128)(2,1)S(1)}, u32[]{:S(2)}, u32[]{:S(2)}) collective-permute-start(bf16[2,16,2048]{2,1,0:T(8,128)(2,1)S(1)} %slice.202), channel_id=1, source_target_pairs={{0,4},{4,8},{8,12},{12,16},{16,20},{20,24},{24,28},{28,32},{32,36}... | collective-permute-start | bytes 393224 | tf_op jit(solution)/shard_map/ppermute | solution.py:794
  106.7 15.5 %collective-permute-start.18 = (bf16[2,128,1280]{2,1,0:T(8,128)(2,1)S(1)}, bf16[2,128,1280]{2,1,0:T(8,128)(2,1)S(1)}, u32[]{:S(2)}, u32[]{:S(2)}) collective-permute-start(bf16[2,128,1280]{2,1,0:T(8,128)(2,1)S(1)} %copy-done.72), channel_id=1, source_target_pairs={{0,96},{32,0},{64,32},{96,64},{1,97},{33,1},{65,33},{97,65},{2,98}... | collective-permute-start | bytes 1966088 | tf_op jit(solution)/shard_map/ppermute | solution.py:799
  107.7 19.5 %collective-permute-start.17 = (bf16[2,128,1280]{2,1,0:T(8,128)(2,1)S(1)}, bf16[2,128,1280]{2,1,0:T(8,128)(2,1)S(1)}, u32[]{:S(2)}, u32[]{:S(2)}) collective-permute-start(bf16[2,128,1280]{2,1,0:T(8,128)(2,1)S(1)} %copy-done.71), channel_id=1, source_target_pairs={{0,32},{32,64},{64,96},{96,0},{1,33},{33,65},{65,97},{97,1},{2,34}... | collective-permute-start | bytes 1966088 | tf_op jit(solution)/shard_map/ppermute | solution.py:799
  109.7 24.8 %collective-permute-start.15 = (bf16[2,128,1408]{2,1,0:T(8,128)(2,1)S(1)}, bf16[2,128,1408]{2,1,0:T(8,128)(2,1)S(1)}, u32[]{:S(2)}, u32[]{:S(2)}) collective-permute-start(bf16[2,128,1408]{2,1,0:T(8,128)(2,1)S(1)} %copy-done.69), channel_id=1, source_target_pairs={{0,8},{8,16},{16,24},{24,0},{1,9},{9,17},{17,25},{25,1},{2,10},{10... | collective-permute-start | bytes 2162696 | tf_op jit(solution)/shard_map/ppermute | solution.py:799
  109.8 24.5 %collective-permute-start.16 = (bf16[2,128,1408]{2,1,0:T(8,128)(2,1)S(1)}, bf16[2,128,1408]{2,1,0:T(8,128)(2,1)S(1)}, u32[]{:S(2)}, u32[]{:S(2)}) collective-permute-start(bf16[2,128,1408]{2,1,0:T(8,128)(2,1)S(1)} %copy-done.70), channel_id=1, source_target_pairs={{0,24},{8,0},{16,8},{24,16},{1,25},{9,1},{17,9},{25,17},{2,26},{10... | collective-permute-start | bytes 2162696 | tf_op jit(solution)/shard_map/ppermute | solution.py:799
  152.8 38.5 %all-to-all-start = ((bf16[32,160,128]{2,1,0:T(8,128)(2,1)}), bf16[32,160,128]{2,1,0:T(8,128)(2,1)S(1)}, u32[]{:S(2)}, u32[]{:S(2)}) async-start(bf16[32,160,128]{2,1,0:T(8,128)(2,1)} %get-tuple-element.100), calls=%async_computation | async-start | bytes 2621440 | tf_op jit(solution)/shard_map/all_to_all | solution.py:845
  160.4 48.4 %collective-permute-start.19 = (bf16[256,2048]{1,0:T(8,128)(2,1)S(1)}, bf16[256,2048]{1,0:T(8,128)(2,1)}, u32[]{:S(2)}, u32[]{:S(2)}) collective-permute-start(bf16[256,2048]{1,0:T(8,128)(2,1)S(1)} %bitcast.265), channel_id=1, source_target_pairs={{0,4},{4,0},{1,5},{5,1},{2,6},{6,2},{3,7},{7,3},{8,12},{12,8},{9,1... | collective-permute-start | bytes 3145736 | tf_op jit(solution)/shard_map/ppermute | solution.py:799
  198.2 16.5 %all-to-all-start.1 = ((bf16[32,32,128]{2,1,0:T(8,128)(2,1)}), bf16[32,32,128]{2,1,0:T(8,128)(2,1)S(1)}, u32[]{:S(2)}, u32[]{:S(2)}) async-start(bf16[32,32,128]{2,1,0:T(8,128)(2,1)} %shard_map.293), calls=%async_computation.1 | async-start | bytes 524288 | tf_op jit(solution)/shard_map/all_to_all | solution.py:845
  205.2 240.2 %reduce-scatter.2.cloned.1.call-start = ((), (), s32[]{:S(2)}) async-start(), calls=%async_computation.6 | async-start | bytes 10027008 | tf_op jit(solution)/shard_map/reduce_scatter | solution.py:1198
  239.1 10.9 %collective-permute-start.23 = (bf16[64,2048]{1,0:T(8,128)(2,1)S(1)}, bf16[64,2048]{1,0:T(8,128)(2,1)S(1)}, u32[]{:S(2)}, u32[]{:S(2)}) collective-permute-start(bf16[64,2048]{1,0:T(8,128)(2,1)S(1)} %multiply_convert_fusion.3), channel_id=1, source_target_pairs={{0,2},{1,3},{2,0},{3,1},{4,6},{5,7},{6,4},{7,5},{8,10},{9,11},{10,... | collective-permute-start | bytes 786440 | tf_op jit(solution)/shard_map/ppermute | solution.py:808
  239.2 14.6 %collective-permute-start.24 = (bf16[64,2048]{1,0:T(8,128)(2,1)S(1)}, bf16[64,2048]{1,0:T(8,128)(2,1)S(1)}, u32[]{:S(2)}, u32[]{:S(2)}) collective-permute-start(bf16[64,2048]{1,0:T(8,128)(2,1)S(1)} %multiply_convert_fusion.3), channel_id=1, source_target_pairs={{0,6},{1,7},{2,4},{3,5},{4,2},{5,3},{6,0},{7,1},{8,14},{9,15},{10,... | collective-permute-start | bytes 786440 | tf_op jit(solution)/shard_map/ppermute | solution.py:808
  277.9 14.9 %collective-permute-start.28 = (bf16[64,2048]{1,0:T(8,128)(2,1)S(1)}, bf16[64,2048]{1,0:T(8,128)(2,1)S(1)}, u32[]{:S(2)}, u32[]{:S(2)}) collective-permute-start(bf16[64,2048]{1,0:T(8,128)(2,1)S(1)} %get-tuple-element.272), channel_id=1, source_target_pairs={{0,4},{1,5},{2,6},{3,7},{4,0},{5,1},{6,2},{7,3},{8,12},{9,13},{10,... | collective-permute-start | bytes 786440 | tf_op jit(solution)/shard_map/ppermute | solution.py:808
  332.0 29.2 %collective-permute-start.33 = (bf16[4,64,2048]{2,1,0:T(8,128)(2,1)}, bf16[4,64,2048]{2,1,0:T(8,128)(2,1)S(1)}, u32[]{:S(2)}, u32[]{:S(2)}) collective-permute-start(bf16[4,64,2048]{2,1,0:T(8,128)(2,1)} %dynamic-slice_bitcast_fusion), channel_id=1, source_target_pairs={{0,1},{1,0},{2,3},{3,2},{4,5},{5,4},{6,7},{7,6},{8,9},{9,8},{10,11... | collective-permute-start | bytes 3145736 | tf_op jit(solution)/shard_map/ppermute | solution.py:808
  332.6 15.1 %all-to-all-start.2 = ((bf16[32,32,128]{2,1,0:T(8,128)(2,1)}), bf16[32,32,128]{2,1,0:T(8,128)(2,1)S(1)}, u32[]{:S(2)}, u32[]{:S(2)}) async-start(bf16[32,32,128]{2,1,0:T(8,128)(2,1)} %get-tuple-element.103.refs_4_), calls=%async_computation.2 | async-start | bytes 524288 | tf_op jit(solution)/shard_map/all_to_all | solution.py:845
  354.4 17.6 %all-to-all-start.3 = ((bf16[32,32,128]{2,1,0:T(8,128)(2,1)}), bf16[32,32,128]{2,1,0:T(8,128)(2,1)}, u32[]{:S(2)}, u32[]{:S(2)}) async-start(bf16[32,32,128]{2,1,0:T(8,128)(2,1)} %shard_map.297), calls=%async_computation.3 | async-start | bytes 524288 | tf_op jit(solution)/shard_map/all_to_all | solution.py:845
  365.3 24.8 %collective-permute-start.36 = (bf16[64,2048]{1,0:T(8,128)(2,1)}, bf16[64,2048]{1,0:T(8,128)(2,1)S(1)}, u32[]{:S(2)}, u32[]{:S(2)}) collective-permute-start(bf16[64,2048]{1,0:T(8,128)(2,1)} %get-tuple-element.270), channel_id=1, source_target_pairs={{0,6},{1,7},{2,4},{3,5},{4,2},{5,3},{6,0},{7,1},{8,14},{9,15},{10,... | collective-permute-start | bytes 786440 | tf_op jit(solution)/shard_map/ppermute | solution.py:808
  367.8 23.2 %collective-permute-start.35 = (bf16[64,2048]{1,0:T(8,128)(2,1)S(1)}, bf16[64,2048]{1,0:T(8,128)(2,1)}, u32[]{:S(2)}, u32[]{:S(2)}) collective-permute-start(bf16[64,2048]{1,0:T(8,128)(2,1)S(1)} %get-tuple-element.271), channel_id=1, source_target_pairs={{0,2},{1,3},{2,0},{3,1},{4,6},{5,7},{6,4},{7,5},{8,10},{9,11},{10,... | collective-permute-start | bytes 786440 | tf_op jit(solution)/shard_map/ppermute | solution.py:808
  367.8 25.1 %collective-permute-start.34 = (bf16[64,2048]{1,0:T(8,128)(2,1)S(1)}, bf16[64,2048]{1,0:T(8,128)(2,1)}, u32[]{:S(2)}, u32[]{:S(2)}) collective-permute-start(bf16[64,2048]{1,0:T(8,128)(2,1)S(1)} %get-tuple-element.269), channel_id=1, source_target_pairs={{0,4},{1,5},{2,6},{3,7},{4,0},{5,1},{6,2},{7,3},{8,12},{9,13},{10,... | collective-permute-start | bytes 786440 | tf_op jit(solution)/shard_map/ppermute | solution.py:808
  387.5 28.2 %collective-permute-start.38 = (bf16[256,1408]{1,0:T(8,128)(2,1)}, bf16[256,1408]{1,0:T(8,128)(2,1)S(1)}, u32[]{:S(2)}, u32[]{:S(2)}) collective-permute-start(bf16[256,1408]{1,0:T(8,128)(2,1)} %get-tuple-element.116.refs_8_), channel_id=1, source_target_pairs={{0,32},{32,64},{64,96},{96,0},{1,33},{33,65},{65,97},{97,1},{2,34}... | collective-permute-start | bytes 2162696 | tf_op jit(solution)/shard_map/ppermute | solution.py:799
  388.8 26.9 %collective-permute-start.39 = (bf16[256,1408]{1,0:T(8,128)(2,1)}, bf16[256,1408]{1,0:T(8,128)(2,1)S(1)}, u32[]{:S(2)}, u32[]{:S(2)}) collective-permute-start(bf16[256,1408]{1,0:T(8,128)(2,1)} %get-tuple-element.119), channel_id=1, source_target_pairs={{0,96},{32,0},{64,32},{96,64},{1,97},{33,1},{65,33},{97,65},{2,98}... | collective-permute-start | bytes 2162696 | tf_op jit(solution)/shard_map/ppermute | solution.py:799
  390.1 22.4 %collective-permute-start.40 = (bf16[256,1280]{1,0:T(8,128)(2,1)}, bf16[256,1280]{1,0:T(8,128)(2,1)S(1)}, u32[]{:S(2)}, u32[]{:S(2)}) collective-permute-start(bf16[256,1280]{1,0:T(8,128)(2,1)} %get-tuple-element.122), channel_id=1, source_target_pairs={{0,8},{8,16},{16,24},{24,0},{1,9},{9,17},{17,25},{25,1},{2,10},{10... | collective-permute-start | bytes 1966088 | tf_op jit(solution)/shard_map/ppermute | solution.py:799
  391.1 24.6 %collective-permute-start.41 = (bf16[256,1280]{1,0:T(8,128)(2,1)}, bf16[256,1280]{1,0:T(8,128)(2,1)S(1)}, u32[]{:S(2)}, u32[]{:S(2)}) collective-permute-start(bf16[256,1280]{1,0:T(8,128)(2,1)} %get-tuple-element.123), channel_id=1, source_target_pairs={{0,24},{8,0},{16,8},{24,16},{1,25},{9,1},{17,9},{25,17},{2,26},{10... | collective-permute-start | bytes 1966088 | tf_op jit(solution)/shard_map/ppermute | solution.py:799
  392.9 10.9 %collective-permute-start.37 = (bf16[32,1536]{1,0:T(8,128)(2,1)S(1)}, bf16[32,1536]{1,0:T(8,128)(2,1)S(1)}, u32[]{:S(2)}, u32[]{:S(2)}) collective-permute-start(bf16[32,1536]{1,0:T(8,128)(2,1)S(1)} %pad_maximum_fusion.12), channel_id=1, source_target_pairs={{4,0},{8,4},{12,8},{16,12},{20,16},{24,20},{28,24},{32,28},{36,32}... | collective-permute-start | bytes 294920 | tf_op jit(solution)/shard_map/ppermute | solution.py:794
  431.1 12.8 %collective-permute-start.43 = (bf16[64,2048]{1,0:T(8,128)(2,1)S(1)}, bf16[64,2048]{1,0:T(8,128)(2,1)S(1)}, u32[]{:S(2)}, u32[]{:S(2)}) collective-permute-start(bf16[64,2048]{1,0:T(8,128)(2,1)S(1)} %fusion.57), channel_id=1, source_target_pairs={{0,2},{1,3},{2,0},{3,1},{4,6},{5,7},{6,4},{7,5},{8,10},{9,11},{10,... | collective-permute-start | bytes 786440 | tf_op jit(solution)/shard_map/ppermute | solution.py:808
  431.9 40.9 %collective-permute-start.44 = (bf16[512,1408]{1,0:T(8,128)(2,1)}, bf16[512,1408]{1,0:T(8,128)(2,1)}, u32[]{:S(2)}, u32[]{:S(2)}) collective-permute-start(bf16[512,1408]{1,0:T(8,128)(2,1)} %get-tuple-element.124), channel_id=1, source_target_pairs={{0,32},{32,64},{64,96},{96,0},{1,33},{33,65},{65,97},{97,1},{2,34}... | collective-permute-start | bytes 4325384 | tf_op jit(solution)/shard_map/ppermute | solution.py:799
  439.6 33.1 %collective-permute-start.45 = (bf16[512,1408]{1,0:T(8,128)(2,1)}, bf16[512,1408]{1,0:T(8,128)(2,1)}, u32[]{:S(2)}, u32[]{:S(2)}) collective-permute-start(bf16[512,1408]{1,0:T(8,128)(2,1)} %get-tuple-element.126), channel_id=1, source_target_pairs={{0,96},{32,0},{64,32},{96,64},{1,97},{33,1},{65,33},{97,65},{2,98}... | collective-permute-start | bytes 4325384 | tf_op jit(solution)/shard_map/ppermute | solution.py:799
  441.2 30.9 %collective-permute-start.46 = (bf16[512,1280]{1,0:T(8,128)(2,1)}, bf16[512,1280]{1,0:T(8,128)(2,1)}, u32[]{:S(2)}, u32[]{:S(2)}) collective-permute-start(bf16[512,1280]{1,0:T(8,128)(2,1)} %get-tuple-element.128), channel_id=1, source_target_pairs={{0,8},{8,16},{16,24},{24,0},{1,9},{9,17},{17,25},{25,1},{2,10},{10... | collective-permute-start | bytes 3932168 | tf_op jit(solution)/shard_map/ppermute | solution.py:799
  441.3 30.9 %collective-permute-start.47 = (bf16[512,1280]{1,0:T(8,128)(2,1)}, bf16[512,1280]{1,0:T(8,128)(2,1)}, u32[]{:S(2)}, u32[]{:S(2)}) collective-permute-start(bf16[512,1280]{1,0:T(8,128)(2,1)} %get-tuple-element.129), channel_id=1, source_target_pairs={{0,24},{8,0},{16,8},{24,16},{1,25},{9,1},{17,9},{25,17},{2,26},{10... | collective-permute-start | bytes 3932168 | tf_op jit(solution)/shard_map/ppermute | solution.py:799
  446.9 25.8 %collective-permute-start.48 = (bf16[64,3,704]{2,1,0:T(4,128)(2,1)S(1)}, bf16[64,3,704]{2,1,0:T(4,128)(2,1)S(1)}, u32[]{:S(2)}, u32[]{:S(2)}) collective-permute-start(bf16[64,3,704]{2,1,0:T(4,128)(2,1)S(1)} %add_bitcast_fusion), channel_id=1, source_target_pairs={{0,4},{4,0},{1,5},{5,1},{2,6},{6,2},{3,7},{7,3},{8,12},{12,8},{9,1... | collective-permute-start | bytes 811016 | tf_op jit(solution)/shard_map/ppermute | solution.py:799
  481.1 37.2 %collective-permute-start.49 = (bf16[64,4096]{1,0:T(8,128)(2,1)S(1)}, bf16[64,4096]{1,0:T(8,128)(2,1)}, u32[]{:S(2)}, u32[]{:S(2)}) collective-permute-start(bf16[64,4096]{1,0:T(8,128)(2,1)S(1)} %broadcast_add_fusion.1), channel_id=1, source_target_pairs={{0,2},{1,3},{2,0},{3,1},{4,6},{5,7},{6,4},{7,5},{8,10},{9,11},{10,... | collective-permute-start | bytes 1572872 | tf_op jit(solution)/shard_map/ppermute | solution.py:808
  483.7 24.3 %collective-permute-start.51 = (bf16[128,1408]{1,0:T(8,128)(2,1)}, bf16[128,1408]{1,0:T(8,128)(2,1)S(1)}, u32[]{:S(2)}, u32[]{:S(2)}) collective-permute-start(bf16[128,1408]{1,0:T(8,128)(2,1)} %get-tuple-element.131), channel_id=1, source_target_pairs={{0,16},{8,24},{16,0},{24,8},{1,17},{9,25},{17,1},{25,9},{2,18},{10... | collective-permute-start | bytes 1081352 | tf_op jit(solution)/shard_map/ppermute | solution.py:799
  483.8 26.2 %collective-permute-start.52 = (bf16[128,1408]{1,0:T(8,128)(2,1)}, bf16[128,1408]{1,0:T(8,128)(2,1)S(1)}, u32[]{:S(2)}, u32[]{:S(2)}) collective-permute-start(bf16[128,1408]{1,0:T(8,128)(2,1)} %get-tuple-element.132), channel_id=1, source_target_pairs={{0,8},{8,16},{16,24},{24,0},{1,9},{9,17},{17,25},{25,1},{2,10},{10... | collective-permute-start | bytes 1081352 | tf_op jit(solution)/shard_map/ppermute | solution.py:799
  485.1 13.8 %collective-permute-start.55 = (bf16[128,1280]{1,0:T(8,128)(2,1)}, bf16[128,1280]{1,0:T(8,128)(2,1)S(1)}, u32[]{:S(2)}, u32[]{:S(2)}) collective-permute-start(bf16[128,1280]{1,0:T(8,128)(2,1)} %get-tuple-element.136), channel_id=1, source_target_pairs={{0,32},{32,64},{64,96},{96,0},{1,33},{33,65},{65,97},{97,1},{2,34}... | collective-permute-start | bytes 983048 | tf_op jit(solution)/shard_map/ppermute | solution.py:799
  490.6 21.4 %collective-permute-start.53 = (bf16[128,1408]{1,0:T(8,128)(2,1)}, bf16[128,1408]{1,0:T(8,128)(2,1)S(1)}, u32[]{:S(2)}, u32[]{:S(2)}) collective-permute-start(bf16[128,1408]{1,0:T(8,128)(2,1)} %get-tuple-element.133), channel_id=1, source_target_pairs={{0,24},{8,0},{16,8},{24,16},{1,25},{9,1},{17,9},{25,17},{2,26},{10... | collective-permute-start | bytes 1081352 | tf_op jit(solution)/shard_map/ppermute | solution.py:799
  506.6 13.5 %collective-permute-start.60 = (f32[16,512]{1,0:T(8,128)S(1)}, f32[16,512]{1,0:T(8,128)S(1)}, u32[]{:S(2)}, u32[]{:S(2)}) collective-permute-start(f32[16,512]{1,0:T(8,128)S(1)} %maximum_add_fusion.1), channel_id=1, source_target_pairs={{0,96},{32,0},{64,32},{96,64},{1,97},{33,1},{65,33},{97,65},{2,98}... | collective-permute-start | bytes 98312 | tf_op jit(solution)/shard_map/ppermute | solution.py:799
  508.1 12.1 %collective-permute-start.59 = (f32[16,512]{1,0:T(8,128)S(1)}, f32[16,512]{1,0:T(8,128)S(1)}, u32[]{:S(2)}, u32[]{:S(2)}) collective-permute-start(f32[16,512]{1,0:T(8,128)S(1)} %maximum_add_fusion.1), channel_id=1, source_target_pairs={{0,64},{32,96},{64,0},{96,32},{1,65},{33,97},{65,1},{97,33},{2,66}... | collective-permute-start | bytes 98312 | tf_op jit(solution)/shard_map/ppermute | solution.py:799
  510.0 10.2 %collective-permute-start.58 = (f32[16,512]{1,0:T(8,128)S(1)}, f32[16,512]{1,0:T(8,128)S(1)}, u32[]{:S(2)}, u32[]{:S(2)}) collective-permute-start(f32[16,512]{1,0:T(8,128)S(1)} %maximum_add_fusion.1), channel_id=1, source_target_pairs={{0,32},{32,64},{64,96},{96,0},{1,33},{33,65},{65,97},{97,1},{2,34}... | collective-permute-start | bytes 98312 | tf_op jit(solution)/shard_map/ppermute | solution.py:799
  515.7 18.1 %collective-permute-start.57 = (bf16[64,2688]{1,0:T(8,128)(2,1)}, bf16[64,2688]{1,0:T(8,128)(2,1)S(1)}, u32[]{:S(2)}, u32[]{:S(2)}) collective-permute-start(bf16[64,2688]{1,0:T(8,128)(2,1)} %get-tuple-element.139), channel_id=1, source_target_pairs={{0,4},{4,0},{1,5},{5,1},{2,6},{6,2},{3,7},{7,3},{8,12},{12,8},{9,1... | collective-permute-start | bytes 1032200 | tf_op jit(solution)/shard_map/ppermute | solution.py:799
  529.1 16.0 %collective-permute-start.50 = (bf16[2,64,4096]{2,1,0:T(8,128)(2,1)S(1)}, bf16[2,64,4096]{2,1,0:T(8,128)(2,1)S(1)}, u32[]{:S(2)}, u32[]{:S(2)}) collective-permute-start(bf16[2,64,4096]{2,1,0:T(8,128)(2,1)S(1)} %pad_maximum_fusion.6), channel_id=1, source_target_pairs={{0,1},{1,0},{2,3},{3,2},{4,5},{5,4},{6,7},{7,6},{8,9},{9,8},{10,11... | collective-permute-start | bytes 3145736 | tf_op jit(solution)/shard_map/ppermute | solution.py:808
  (103 other events, 642.8 us)
Sparse Core Ops, SparseCore 0:
  98.4 98.0 all-gather.1
  324.1 92.4 reduce-scatter.1
